TPU v7x, 32 devices: a whole 2x2x4 slice. The times are simulated.
32 devices in a mesh: dp: 4 (over y, core), expert: 8 (over z, x).
Axes of the slice: x: 2, y: 2, z: 4, core: 2. Of those that a mesh axis runs over, the one named last changes fastest.
Arguments:
- tokens: bfloat16 [4096, 3072], P(('dp', 'expert')), may hold values from -6 to 6
- cotangent: bfloat16 [4096, 3072], P(('dp', 'expert')), may hold values from -0.3125 to 0.3125
- route_ids: int32 [4096, 2], P(('dp', 'expert')), may hold values from 0 to 7, all different within a row; in each aligned block of 128 rows (0 to 127, 128 to 255, ...) at most 36 rows name the same one
- route_probs: float32 [4096, 2], P(('dp', 'expert')), may hold values from 0.2 to 1
- gate_weight: bfloat16 [3072, 8192], P(None, 'expert'), may hold values from -0.109375 to 0.109375
- up_weight: bfloat16 [3072, 8192], P(None, 'expert'), may hold values from -0.109375 to 0.109375
- down_weight: bfloat16 [8192, 3072], P('expert'), may hold values from -0.0625 to 0.0625
Outputs:
- token_grad: bfloat16 [4096, 3072], P(('dp', 'expert'))
- gate_grad: bfloat16 [3072, 8192], P('dp', 'expert')
- up_grad: bfloat16 [3072, 8192], P('dp', 'expert')
- down_grad: bfloat16 [8192, 3072], P('expert', 'dp')
Inputs may be any that keep to these rules, and one draw needn't show every extreme that they name: `route_ids`: in every block of 128 consecutive tokens (the tokens of one device) at most 36 tokens name any one expert, a bound that some block reaches; a token's 2 ids differ.
All inputs are finite; a program needn't handle non-finite values.
Results may differ from a plain program's by a relative error of at most 0.023.
Values may be sent and summed in bfloat16 or wider, within the bound.
No kernel may reach another device: no remote copies, remote signals or barrier semaphores. Data moves between devices by JAX's collectives and lax.ppermute only.
A program may use at most 128 MiB of HBM per device.

v0:
```python
import jax
import jax.numpy as jnp
from jax import lax
from jax.sharding import PartitionSpec as P

CAP = 36


def pick_rows(placer, values):
    return lax.dot_general(
        placer, values, (((0,), (0,)), ((), ())), preferred_element_type=jnp.float32
    ).astype(jnp.bfloat16)


def per_device(tokens, cotangent, route_ids, route_probs, gate_weight, up_weight, down_weight):
    hits = route_ids == 0
    chosen = jnp.any(hits, axis=1).astype(jnp.int32)
    share = jnp.sum(jnp.where(hits, route_probs, 0.0), axis=1)
    slots = jnp.cumsum(chosen) - chosen
    placer_mask = (slots[:, None] == jnp.arange(CAP, dtype=jnp.int32)[None, :]) & (
        chosen[:, None] == 1
    )
    placer = placer_mask.astype(jnp.float32)
    placer_half = placer_mask.astype(jnp.bfloat16)
    local_rows = pick_rows(placer_half, tokens)
    local_cotan = pick_rows(placer_half, cotangent)
    local_shares = jnp.sum(placer * share[:, None], axis=0)
    routed, routed_cotan, routed_shares = (
        lax.all_gather(local_rows, "expert", axis=0, tiled=True),
        lax.all_gather(local_cotan, "expert", axis=0, tiled=True),
        lax.all_gather(local_shares.astype(jnp.bfloat16), "expert", axis=0, tiled=True).astype(
            local_shares.dtype
        ),
    )
    gate_pre = jnp.dot(routed, gate_weight, preferred_element_type=jnp.float32)
    up_pre = jnp.dot(routed, up_weight, preferred_element_type=jnp.float32)
    sigma = jax.nn.sigmoid(gate_pre)
    gate_act = gate_pre * sigma
    hidden = (gate_act * up_pre).astype(jnp.bfloat16)
    gate_pre, up_pre, sigma, gate_act, hidden = (gate_pre, up_pre, sigma, gate_act, hidden)
    scaled = (routed_shares[:, None] * routed_cotan.astype(jnp.float32)).astype(jnp.bfloat16)
    down_part = lax.dot_general(
        hidden, scaled, (((0,), (0,)), ((), ())), preferred_element_type=jnp.float32
    )
    hidden_back = lax.dot_general(
        scaled, down_weight, (((1,), (1,)), ((), ())), preferred_element_type=jnp.float32
    )
    gate_back = (hidden_back * up_pre * sigma * (1.0 + gate_pre * (1.0 - sigma))).astype(
        jnp.bfloat16
    )
    up_back = (hidden_back * gate_act).astype(jnp.bfloat16)
    gate_part = lax.dot_general(
        routed, gate_back, (((0,), (0,)), ((), ())), preferred_element_type=jnp.float32
    )
    up_part = lax.dot_general(
        routed, up_back, (((0,), (0,)), ((), ())), preferred_element_type=jnp.float32
    )
    gate_sum, up_sum, down_sum = (
        lax.psum_scatter(
            gate_part.astype(jnp.bfloat16), "dp", scatter_dimension=0, tiled=True
        ).astype(jnp.float32),
        lax.psum_scatter(
            up_part.astype(jnp.bfloat16), "dp", scatter_dimension=0, tiled=True
        ).astype(jnp.float32),
        lax.psum_scatter(
            down_part.astype(jnp.bfloat16), "dp", scatter_dimension=1, tiled=True
        ).astype(jnp.float32),
    )
    partial_value = lax.dot_general(
        gate_back, gate_weight, (((1,), (1,)), ((), ())), preferred_element_type=jnp.float32
    )
    partial_value = partial_value + lax.dot_general(
        up_back, up_weight, (((1,), (1,)), ((), ())), preferred_element_type=jnp.float32
    )
    returned = lax.psum_scatter(
        partial_value.astype(jnp.bfloat16), "expert", scatter_dimension=0, tiled=True
    ).astype(jnp.float32)
    token_grad = jnp.dot(placer, returned, precision=lax.Precision.HIGHEST).astype(jnp.bfloat16)
    return (
        token_grad,
        gate_sum.astype(jnp.bfloat16),
        up_sum.astype(jnp.bfloat16),
        down_sum.astype(jnp.bfloat16),
    )


def solution(mesh):
    in_specs = (
        P(("dp", "expert"), None),
        P(("dp", "expert"), None),
        P(("dp", "expert"), None),
        P(("dp", "expert"), None),
        P(None, "expert"),
        P(None, "expert"),
        P("expert", None),
    )
    out_specs = (P(("dp", "expert"), None), P("dp", "expert"), P("dp", "expert"), P("expert", "dp"))
    return jax.shard_map(
        per_device, mesh=mesh, in_specs=in_specs, out_specs=out_specs, check_vma=False
    )
```

profile of v0, /device:TPU:0, one launch (start us, length us, event | category | flops | bytes accessed | tf_op | source)
XLA Modules:
  0.0 309.7 jit_solution(10212185512451496390)
XLA Ops:
  7.2 0.0 copy-start
  7.2 0.0 copy-start.2
  7.2 0.0 copy-start.3
  7.2 0.0 copy-start.1
  7.2 0.0 copy-start.4
  7.2 0.0 all-gather.7.cloned.1.call-start
  7.3 0.8 fusion.18
  8.1 0.1 copy.14
  8.2 0.2 reduce-window.8
  8.4 0.1 reduce
  8.5 0.1 copy-done
  8.6 0.9 fusion.3
  9.5 0.0 all-gather.7.cloned.1.call-update
  9.5 0.0 all-gather.5.cloned.1.call-start
  9.6 0.9 fusion.2
  10.5 0.0 all-gather.5.cloned.1.call-update
  10.5 0.0 reduce-scatter.10.cloned.1.call-start
  10.6 0.6 fusion.21
  11.9 0.1 select_reduce_fusion
  12.0 0.2 dynamic-update-slice
  12.3 23.1 %all-reduce = bf16[288]{0:T(512)(128)(2,1)S(1)} all-reduce(bf16[288]{0:T(512)(128)(2,1)S(1)} %dynamic-update-slice), channel_id=1, replica_groups=mesh['dp'=4,'expert'=8] {'expert'}, use_global_device_ids=true, to_apply=%add | all-reduce | flops 288 | bytes 1152
  35.4 25.7 %all-gather.7.cloned.1.call-done = bf16[8,36,3072]{2,1,0:T(8,128)(2,1)} async-done(((bf16[1,36,3072]{2,1,0:T(8,128)(2,1)}), bf16[8,36,3072]{2,1,0:T(8,128)(2,1)}) %all-gather.7.cloned.1.call-update) | async-done | bytes 1769488 | tf_op jit(solution)/shard_map/all_gather | solution.py:29
  61.1 1.7 reshape.52
  62.8 5.8 %fusion.23 = f32[288,1024]{1,0:T(8,128)} fusion(bf16[288,3072]{1,0:T(8,128)(2,1)S(1)} %reshape.52, bf16[3072,1024]{1,0:T(8,128)(2,1)} %param.11), kind=kOutput, calls=%fused_computation.37 | convolution fusion | flops 1811939328 | bytes 9240576 | tf_op jit(solution)/shard_map/dot_general | solution.py:35
  68.6 6.0 %fusion.22 = f32[288,1024]{1,0:T(8,128)} fusion(bf16[288,3072]{1,0:T(8,128)(2,1)S(1)} %reshape.52, bf16[3072,1024]{1,0:T(8,128)(2,1)} %param.12), kind=kOutput, calls=%fused_computation.36 | convolution fusion | flops 1811939328 | bytes 9240576 | tf_op jit(solution)/shard_map/dot_general | solution.py:36
  74.6 35.8 %all-gather.5.cloned.1.call-done = bf16[8,36,3072]{2,1,0:T(8,128)(2,1)} async-done(((bf16[1,36,3072]{2,1,0:T(8,128)(2,1)}), bf16[8,36,3072]{2,1,0:T(8,128)(2,1)}) %all-gather.5.cloned.1.call-update) | async-done | bytes 1769488 | tf_op jit(solution)/shard_map/all_gather | solution.py:30
  110.5 3.2 %reshape.53 = f32[288,3072]{1,0:T(8,128)} reshape(bf16[8,36,3072]{2,1,0:T(8,128)(2,1)} %all-gather.5.cloned.1.call-done) | data formatting | bytes 5308416 | tf_op jit(solution)/shard_map/convert_element_type | solution.py:41
  113.7 9.0 %convolution_convert_fusion = bf16[1024,3072]{1,0:T(8,128)(2,1)} fusion(f32[288,1024]{1,0:T(8,128)} %fusion.22, f32[288,1024]{1,0:T(8,128)} %fusion.23, f32[288,3072]{1,0:T(8,128)} %reshape.53, f32[288]{0:T(512)S(1)} %convert_element_type.76), kind=kOutput, calls=%fused_computation | convolution fusion | flops 1818624000 | bytes 12190848 | tf_op jit(solution)/shard_map/dot_general | solution.py:42
  122.7 0.0 reduce-scatter.10.cloned.1.call-update
  122.7 0.0 reduce-scatter.8.cloned.1.call-start
  122.7 6.8 %multiply_convert_fusion.2 = (bf16[288,1024]{1,0:T(8,128)(2,1)S(1)}, bf16[288,1024]{1,0:T(8,128)(2,1)S(1)}) fusion(f32[288,1024]{1,0:T(8,128)} %fusion.23, f32[288,1024]{1,0:T(8,128)} %fusion.22, bf16[1024,3072]{1,0:T(8,128)(2,1)} %param.13, f32[288,3072]{1,0:T(8,128)} %reshape.53, f32[288]{0:T(512)S(1)} %convert_element_type.76), kind=kOutput, calls=%fused_computation.12 | convolution fusion | flops 1817542656 | bytes 13370496 | tf_op jit(solution)/shard_map/dot_general | solution.py:45
  129.5 0.0 copy-start.5
  129.5 0.8 copy-done.5
  130.3 5.4 %convolution_convert_fusion.1 = bf16[3072,1024]{1,0:T(8,128)(2,1)} fusion(bf16[288,3072]{1,0:T(8,128)(2,1)S(1)} %reshape.52, bf16[288,1024]{1,0:T(8,128)(2,1)S(1)} %get-tuple-element.4), kind=kOutput, calls=%fused_computation.1 | convolution fusion | flops 1815085056 | bytes 8650752 | tf_op jit(solution)/shard_map/dot_general | solution.py:55
  135.7 0.0 reduce-scatter.8.cloned.1.call-update
  135.7 0.2 reduce-scatter.6.cloned.1.call-start
  136.0 5.4 %convolution_convert_fusion.2 = bf16[3072,1024]{1,0:T(8,128)(2,1)} fusion(bf16[288,3072]{1,0:T(8,128)(2,1)S(1)} %reshape.52, bf16[288,1024]{1,0:T(8,128)(2,1)S(1)} %get-tuple-element.5), kind=kOutput, calls=%fused_computation.2 | convolution fusion | flops 1815085056 | bytes 8650752 | tf_op jit(solution)/shard_map/dot_general | solution.py:52
  141.3 0.0 reduce-scatter.6.cloned.1.call-update
  141.4 0.0 copy-start.6
  141.4 6.0 %fusion.24 = f32[288,3072]{1,0:T(8,128)S(1)} fusion(bf16[288,1024]{1,0:T(8,128)(2,1)S(1)} %get-tuple-element.5, bf16[3072,1024]{1,0:T(8,128)(2,1)} %param.11), kind=kOutput, calls=%fused_computation.38 | convolution fusion | flops 1811939328 | bytes 10420224 | tf_op jit(solution)/shard_map/dot_general | solution.py:69
  147.4 4.9 %fusion.1 = bf16[288,3072]{1,0:T(8,128)(2,1)S(1)} fusion(f32[288,3072]{1,0:T(8,128)S(1)} %fusion.24, bf16[288,1024]{1,0:T(8,128)(2,1)S(1)} %copy-done.6, bf16[3072,1024]{1,0:T(8,128)(2,1)} %param.12), kind=kOutput, calls=%fused_computation.4 | convolution fusion | flops 1813708800 | bytes 12189696 | tf_op jit(solution)/shard_map/dot_general | solution.py:72
  152.3 44.9 %fusion = bf16[40,3072]{1,0:T(8,128)(2,1)S(1)} fusion(bf16[288,3072]{1,0:T(8,128)(2,1)S(1)} %fusion.1), kind=kCustom, calls=%all-reduce-scatter | all-reduce-scatter fusion | flops 983041 | bytes 2015744
  197.2 1.3 collective-permute-start
  199.1 3.7 %collective-permute-done = bf16[28,3072]{1,0:T(8,128)(2,1)S(1)} collective-permute-done((bf16[28,3072]{1,0:T(8,128)(2,1)S(1)}, bf16[28,3072]{1,0:T(8,128)(2,1)S(1)}, u32[]{:S(2)}, u32[]{:S(2)}) %collective-permute-start) | collective-permute-done | bytes 172064
  202.9 0.4 concatenate
  203.3 1.3 convolution_convert_fusion.3
  204.6 37.2 %reduce-scatter.8.cloned.1.call-done = bf16[768,1024]{1,0:T(8,128)(2,1)} async-done(((bf16[3072,1024]{1,0:T(8,128)(2,1)}), bf16[768,1024]{1,0:T(8,128)(2,1)}) %reduce-scatter.8.cloned.1.call-update) | async-done | bytes 1572880 | tf_op jit(solution)/shard_map/reduce_scatter | solution.py:62
  241.8 61.3 %reduce-scatter.6.cloned.1.call-done = bf16[768,1024]{1,0:T(8,128)(2,1)} async-done(((bf16[3072,1024]{1,0:T(8,128)(2,1)}), bf16[768,1024]{1,0:T(8,128)(2,1)}) %reduce-scatter.6.cloned.1.call-update) | async-done | bytes 1572880 | tf_op jit(solution)/shard_map/reduce_scatter | solution.py:59
  (12 shorter events, 0.1 us)
Async XLA Ops:
  7.2 1.4 copy-start
  7.2 3.4 %copy-start.2 = (u32[32]{0:T(128)S(1)}, u32[32]{0:T(128)}, u32[]{:S(2)}) copy-start(u32[32]{0:T(128)} %constant.16) | copy-start | bytes 388
  7.2 4.7 %copy-start.3 = (s32[128,2]{0,1:T(2,128)S(1)}, s32[128,2]{0,1:T(2,128)}, u32[]{:S(2)}) copy-start(s32[128,2]{0,1:T(2,128)} %param.9) | copy-start | bytes 3076
  7.2 2.4 copy-start.1
  7.2 4.7 %copy-start.4 = (f32[128,2]{0,1:T(2,128)S(1)}, f32[128,2]{0,1:T(2,128)}, u32[]{:S(2)}) copy-start(f32[128,2]{0,1:T(2,128)} %param.10) | copy-start | bytes 3076
  7.2 53.9 %all-gather.7.cloned.1.call-start = ((), (), s32[]{:S(2)}) async-start(), calls=%async_computation.7 | async-start | bytes 2211840 | tf_op jit(solution)/shard_map/all_gather | solution.py:29
  9.5 101.0 %all-gather.5.cloned.1.call-start = ((), (), s32[]{:S(2)}) async-start(), calls=%async_computation.6 | async-start | bytes 2211840 | tf_op jit(solution)/shard_map/all_gather | solution.py:30
  10.5 194.1 %reduce-scatter.10.cloned.1.call-start = ((), (), s32[]{:S(2)}) async-start(), calls=%async_computation.5 | async-start | bytes 7864320 | tf_op jit(solution)/shard_map/reduce_scatter | solution.py:65
  122.7 119.1 %reduce-scatter.8.cloned.1.call-start = ((), (), s32[]{:S(2)}) async-start(), calls=%async_computation.4 | async-start | bytes 7864320 | tf_op jit(solution)/shard_map/reduce_scatter | solution.py:62
  129.5 0.8 copy-start.5
  135.7 167.4 %reduce-scatter.6.cloned.1.call-start = ((), (), s32[]{:S(2)}) async-start(), calls=%async_computation.3 | async-start | bytes 7864320 | tf_op jit(solution)/shard_map/reduce_scatter | solution.py:59
  141.4 6.0 %copy-start.6 = (bf16[288,1024]{1,0:T(8,128)(2,1)S(1)}, bf16[288,1024]{1,0:T(8,128)(2,1)}, u32[]{:S(2)}) copy-start(bf16[288,1024]{1,0:T(8,128)(2,1)} %copy-done.5) | copy-start | bytes 1769476
  197.2 5.6 %collective-permute-start = (bf16[28,3072]{1,0:T(8,128)(2,1)S(1)}, bf16[28,3072]{1,0:T(8,128)(2,1)S(1)}, u32[]{:S(2)}, u32[]{:S(2)}) collective-permute-start(bf16[28,3072]{1,0:T(8,128)(2,1)S(1)} %slice), channel_id=1, source_target_pairs={{0,1},{1,2},{2,3},{3,4},{4,5},{5,6},{6,7},{8,9},{9,10},{10,11},{11... | collective-permute-start | bytes 516104
Sparse Core Ops, SparseCore 0:
  10.8 50.2 all-gather.6
  63.9 46.5 all-gather.4
  122.8 57.4 reduce-scatter.9
  183.4 58.3 reduce-scatter.7
  244.8 58.3 reduce-scatter.5
where the time goes:
time: 310 us
  waiting for transfers between devices  164 us (53%)
  blocking collectives  68 us (22%)
  matrix products  52.4 us (17%)
  between operations  15.2 us (5%)
  local copies, waits for them, and re-layouts  7.25 us (2%)
    unnamed x2, blocking collectives  68 us
    reduce_scatter x1, waiting for transfers between devices, per_device(): lax.psum_scatter(gate_part.astype(jnp.bfloat16), 'dp', scatter_dimension=...  61.3 us
    reduce_scatter x1, waiting for transfers between devices, per_device(): lax.psum_scatter(up_part.astype(jnp.bfloat16), 'dp', scatter_dimension=0,...  37.2 us
    all_gather x1, waiting for transfers between devices, per_device(): lax.all_gather(local_cotan, 'expert', axis=0, tiled=True)  35.8 us
    all_gather x1, waiting for transfers between devices, per_device(): lax.all_gather(local_rows, 'expert', axis=0, tiled=True)  25.7 us
    dot_general x1, matrix products, per_device(): lax.dot_general(hidden, scaled, (((0,), (0,)), ((), ())), preferred_eleme...  8.98 us
    dot_general x1, matrix products, per_device(): lax.dot_general(scaled, down_weight, (((1,), (1,)), ((), ())), preferred_...  6.8 us
  transfers between devices with their start and end apart: 6, of which 5 were waited for; matrix products, arithmetic and copies ran while one was open for 29% of the time, Pallas kernels for 0%

commit v1 on v0

--- a/solution.py
+++ b/solution.py
@@ -1,9 +1,352 @@
+import functools
+
 import jax
 import jax.numpy as jnp
 from jax import lax
+from jax.experimental import pallas as pl
+from jax.experimental.pallas import tpu as pltpu
 from jax.sharding import PartitionSpec as P
 
 CAP = 36
+MAIN = 32
+REST = CAP - MAIN
+HALF = jnp.bfloat16
+FULL = jnp.float32
+
+
+def shape(dims, dtype=HALF):
+    return jax.ShapeDtypeStruct(dims, dtype)
+
+
+def params(mib):
+    return pltpu.CompilerParams(vmem_limit_bytes=mib * 2**20)
+
+
+def nt_dot(a, b):
+    return lax.dot_general(a, b, (((1,), (1,)), ((), ())), preferred_element_type=FULL)
+
+
+def tn_dot(a, b):
+    return lax.dot_general(a, b, (((0,), (0,)), ((), ())), preferred_element_type=FULL)
+
+
+def chosen_slots(ids):
+    count = ids.shape[0]
+    chosen = jnp.max((ids == 0).astype(FULL), axis=1, keepdims=True)
+    chosen = jnp.broadcast_to(chosen, (count, 128))
+    earlier = lax.broadcasted_iota(jnp.int32, (count, count), 1) < lax.broadcasted_iota(
+        jnp.int32, (count, count), 0
+    )
+    slots = jnp.dot(
+        earlier.astype(FULL).astype(HALF), chosen.astype(HALF), preferred_element_type=FULL
+    )
+    return chosen, slots
+
+
+def pack_kernel(ids, probs, tokens, cotangent, out, pick_rows, pick_cotan, share):
+    @pl.when(pl.program_id(0) == 0)
+    def _():
+        chosen, slots = chosen_slots(ids[...])
+        column = lax.broadcasted_iota(jnp.int32, slots.shape, 1).astype(FULL)
+        late = (slots >= MAIN).astype(FULL)
+        row_place = slots + late * MAIN
+        cotan_place = slots + MAIN + late * REST
+        pick_rows[...] = jnp.where(row_place == column, chosen, 0.0).astype(HALF)
+        pick_cotan[...] = jnp.where(cotan_place == column, chosen, 0.0).astype(HALF)
+        total = jnp.sum(jnp.where(ids[...] == 0, probs[...], 0.0), axis=1, keepdims=True)
+        share[...] = jnp.broadcast_to(total, share.shape)
+
+    scaled = (share[:, 0:1] * cotangent[...].astype(FULL)).astype(HALF)
+    packed = tn_dot(pick_rows[...], tokens[...]) + tn_dot(pick_cotan[...], scaled)
+    out[...] = packed[0 : 2 * CAP].astype(HALF)
+
+
+def pack(ids, probs, tokens, cotangent):
+    count, width = tokens.shape
+    step = 768
+    return pl.pallas_call(
+        pack_kernel,
+        grid=(width // step,),
+        in_specs=[
+            pl.BlockSpec(ids.shape, lambda j: (0, 0)),
+            pl.BlockSpec(probs.shape, lambda j: (0, 0)),
+            pl.BlockSpec((count, step), lambda j: (0, j)),
+            pl.BlockSpec((count, step), lambda j: (0, j)),
+        ],
+        out_specs=pl.BlockSpec((2 * CAP, step), lambda j: (0, j)),
+        out_shape=shape((2 * CAP, width)),
+        scratch_shapes=[
+            pltpu.VMEM((count, 128), HALF),
+            pltpu.VMEM((count, 128), HALF),
+            pltpu.VMEM((count, 128), FULL),
+        ],
+        compiler_params=params(32),
+        name="pack",
+    )(ids, probs, tokens, cotangent)
+
+
+def unpack_kernel(ids, *refs):
+    pieces, out = refs[:-1], refs[-1]
+    chosen, slots = chosen_slots(ids[...])
+    column = lax.broadcasted_iota(jnp.int32, slots.shape, 1).astype(FULL)
+    depth = pieces[0].shape[0]
+    place = jnp.where(slots == column, chosen, 0.0).astype(HALF)[:, 0:depth]
+    total = pieces[0][...].astype(FULL)
+    for piece in pieces[1:]:
+        total = total + piece[...].astype(FULL)
+    out[...] = jnp.dot(place, total.astype(HALF), preferred_element_type=FULL).astype(HALF)
+
+
+def unpack(ids, pieces):
+    count, (depth, width) = ids.shape[0], pieces[0].shape
+    step = 1024
+    return pl.pallas_call(
+        unpack_kernel,
+        grid=(width // step,),
+        in_specs=[pl.BlockSpec(ids.shape, lambda j: (0, 0))]
+        + [pl.BlockSpec((depth, step), lambda j: (0, j)) for _ in pieces],
+        out_specs=pl.BlockSpec((count, step), lambda j: (0, j)),
+        out_shape=shape((count, width)),
+        compiler_params=params(32),
+        name="unpack",
+    )(ids, *pieces)
+
+
+TILE = 256
+
+
+def forward_kernel(n, back, place, *refs):
+    blocks, (gate, up, down), refs = refs[:n], refs[n : n + 3], refs[n + 3 :]
+    if back:
+        acts, own, other, send, keep, rows, scaled, total = refs
+    else:
+        acts, own, other, rows, scaled = refs
+    step = pl.program_id(0)
+    width = rows.shape[1]
+    part = own.shape[1] // 2
+
+    @pl.when(step == 0)
+    def _():
+        for i, block in enumerate(blocks):
+            rows[MAIN * i : MAIN * (i + 1), :] = block[0:MAIN, :]
+            scaled[MAIN * i : MAIN * (i + 1), :] = block[MAIN : 2 * MAIN, :]
+        first = lax.broadcasted_iota(jnp.int32, (2 * REST, width), 0) < REST
+        tails = [block[2 * MAIN : 2 * CAP, :].astype(FULL) for block in blocks]
+        row_tails, scaled_tails = [], []
+        for a, b in zip(tails[0::2], tails[1::2]):
+            row_tails.append(jnp.where(first, a, pltpu.roll(b, REST, 0)))
+            scaled_tails.append(jnp.where(first, pltpu.roll(a, REST, 0), b))
+        for i in range(0, n // 2, 2):
+            here = slice(MAIN * n + 8 * i, MAIN * n + 8 * i + 16)
+            rows[here, :] = jnp.concatenate(row_tails[i : i + 2], axis=0).astype(HALF)
+            scaled[here, :] = jnp.concatenate(scaled_tails[i : i + 2], axis=0).astype(HALF)
+        for out, index in ((own, 0), (other, 1)):
+            columns = pl.ds(pl.multiple_of(place[index] * part, part), part)
+            out[:, 0:part] = rows[:, columns]
+            out[:, part : 2 * part] = scaled[:, columns]
+
+    gate_pre = jnp.dot(rows[...], gate[...], preferred_element_type=FULL)
+    up_pre = jnp.dot(rows[...], up[...], preferred_element_type=FULL)
+    hidden_back = nt_dot(scaled[...], down[...])
+    sigma = jax.nn.sigmoid(gate_pre)
+    gate_act = gate_pre * sigma
+    hidden = (gate_act * up_pre).astype(HALF)
+    gate_back = (hidden_back * up_pre * sigma * (1.0 + gate_pre * (1.0 - sigma))).astype(HALF)
+    up_back = (hidden_back * gate_act).astype(HALF)
+    acts[:, 0:TILE] = hidden
+    acts[:, TILE : 2 * TILE] = gate_back
+    acts[:, 2 * TILE : 3 * TILE] = up_back
+    if back:
+        term = nt_dot(gate_back, gate[...]) + nt_dot(up_back, up[...])
+
+        @pl.when(step == 0)
+        def _():
+            total[...] = term
+
+        @pl.when(step > 0)
+        def _():
+            total[...] += term
+
+        @pl.when(step == pl.num_programs(0) - 1)
+        def _():
+            mid, tail, half = MAIN * n // 2, MAIN * n, REST * n // 2
+            keep[0:mid, :] = total[0:mid, :].astype(HALF)
+            send[0:mid, :] = total[mid : 2 * mid, :].astype(HALF)
+            keep[mid : mid + half, :] = total[tail : tail + half, :].astype(HALF)
+            send[mid : mid + half, :] = total[tail + half : tail + 2 * half, :].astype(HALF)
+
+
+def forward(blocks, gate, up, down, place, part, back):
+    n, (width, hidden) = len(blocks), gate.shape
+    count = CAP * n
+    whole = lambda j, place: (0, 0)
+    out_shape = [
+        shape((count, 3 * hidden)),
+        shape((count, 2 * part)),
+        shape((count, 2 * part)),
+    ]
+    out_specs = [
+        pl.BlockSpec((count, 3 * TILE), lambda j, place: (0, j)),
+        pl.BlockSpec((count, 2 * part), whole),
+        pl.BlockSpec((count, 2 * part), whole),
+    ]
+    scratch = [pltpu.VMEM((count, width), HALF), pltpu.VMEM((count, width), HALF)]
+    if back:
+        out_shape += [shape((count // 2, width))] * 2
+        out_specs += [pl.BlockSpec((count // 2, width), whole)] * 2
+        scratch += [pltpu.VMEM((count, width), FULL)]
+    matmuls = 5 if back else 3
+    return pl.pallas_call(
+        functools.partial(forward_kernel, n, back),
+        grid_spec=pltpu.PrefetchScalarGridSpec(
+            num_scalar_prefetch=1,
+            grid=(hidden // TILE,),
+            in_specs=[pl.BlockSpec((2 * CAP, width), whole) for _ in blocks]
+            + [
+                pl.BlockSpec((width, TILE), lambda j, place: (0, j)),
+                pl.BlockSpec((width, TILE), lambda j, place: (0, j)),
+                pl.BlockSpec((TILE, width), lambda j, place: (j, 0)),
+            ],
+            out_specs=out_specs,
+            scratch_shapes=scratch,
+        ),
+        out_shape=out_shape,
+        compiler_params=params(56),
+        cost_estimate=pl.CostEstimate(
+            flops=2 * matmuls * count * width * hidden,
+            bytes_accessed=6 * width * hidden + 4 * count * (width + part),
+            transcendentals=count * hidden,
+        ),
+        name="forward_back" if back else "forward",
+    )(place, *blocks, gate, up, down)
+
+
+def grads_kernel(n, *refs):
+    acts, parts, refs = refs[:n], refs[n : 2 * n], refs[2 * n :]
+    gate_grad, up_grad, down_grad, act_rows, part_rows, done = refs
+    copies, start = [], 0
+    for i in range(n):
+        count = acts[i].shape[0]
+        for ref, buffer in ((acts[i], act_rows), (parts[i], part_rows)):
+            copy = pltpu.make_async_copy(
+                ref, buffer.at[pl.ds(start, count), :], done.at[len(copies)]
+            )
+            copy.start()
+            copies.append(copy)
+        start += count
+    for copy in copies:
+        copy.wait()
+    part = part_rows.shape[1] // 2
+    tiles = act_rows.shape[1] // (3 * TILE)
+    for i in range(part // TILE):
+        picked = part_rows[:, i * TILE : (i + 1) * TILE].T
+        here = slice(i * TILE, (i + 1) * TILE)
+        for j in range(tiles):
+            at = 3 * TILE * j
+            there = slice(j * TILE, (j + 1) * TILE)
+            gate_grad[here, there] = jnp.dot(
+                picked, act_rows[:, at + TILE : at + 2 * TILE], preferred_element_type=FULL
+            ).astype(HALF)
+            up_grad[here, there] = jnp.dot(
+                picked, act_rows[:, at + 2 * TILE : at + 3 * TILE], preferred_element_type=FULL
+            ).astype(HALF)
+    for j in range(tiles):
+        at = 3 * TILE * j
+        hidden = act_rows[:, at : at + TILE].T
+        down_grad[j * TILE : (j + 1) * TILE, :] = jnp.dot(
+            hidden, part_rows[:, part : 2 * part], preferred_element_type=FULL
+        ).astype(HALF)
+
+
+def grads(acts, parts, part, hidden):
+    n, count = len(acts), sum(a.shape[0] for a in acts)
+    anywhere = pl.BlockSpec(memory_space=pl.ANY)
+    in_vmem = pl.BlockSpec(memory_space=pltpu.VMEM)
+    return pl.pallas_call(
+        functools.partial(grads_kernel, n),
+        in_specs=[anywhere] * (2 * n),
+        out_specs=[in_vmem] * 3,
+        out_shape=[shape((part, hidden)), shape((part, hidden)), shape((hidden, part))],
+        scratch_shapes=[
+            pltpu.VMEM((count, 3 * hidden), HALF),
+            pltpu.VMEM((count, 2 * part), HALF),
+            pltpu.SemaphoreType.DMA((2 * n,)),
+        ],
+        compiler_params=params(56),
+        cost_estimate=pl.CostEstimate(
+            flops=6 * count * part * hidden,
+            bytes_accessed=2 * count * (3 * hidden + 2 * part) + 6 * part * hidden,
+            transcendentals=0,
+        ),
+        name="grads",
+    )(*acts, *parts)
+
+
+def merge_kernel(keep, came, *outs):
+    total = keep[...].astype(FULL) + came[...].astype(FULL)
+    mid = MAIN * len(outs)
+    for i, out in enumerate(outs):
+        out[0:MAIN, :] = total[MAIN * i : MAIN * (i + 1)].astype(HALF)
+        pair = total[mid + 8 * (i // 2) : mid + 8 * (i // 2) + 8]
+        out[MAIN : MAIN + 8, :] = (pair if i % 2 == 0 else pltpu.roll(pair, REST, 0)).astype(HALF)
+
+
+def merge(keep, came):
+    n, width = keep.shape[0] // CAP, keep.shape[1]
+    return pl.pallas_call(
+        merge_kernel,
+        out_shape=[shape((MAIN + 8, width))] * n,
+        compiler_params=params(32),
+        name="merge",
+    )(keep, came)
+
+
+def per_device(tokens, cotangent, route_ids, route_probs, gate_weight, up_weight, down_weight):
+    n_dp, n_expert = lax.axis_size("dp"), lax.axis_size("expert")
+    core_pairs = [(i, i ^ 1) for i in range(n_dp)]
+    y_pairs = [(i, (i + 2) % n_dp) for i in range(n_dp)]
+    x_pairs = [(i, i ^ 1) for i in range(n_expert)]
+
+    def over_core(v):
+        return lax.ppermute(v, "dp", core_pairs)
+
+    def over_y(v):
+        return lax.ppermute(v, "dp", y_pairs)
+
+    def over_x(v):
+        return lax.ppermute(v, "expert", x_pairs)
+
+    def over_z(v, by):
+        return lax.ppermute(
+            v, "expert", [(i, (i + 2 * by) % n_expert) for i in range(n_expert)]
+        )
+
+    part = tokens.shape[1] // n_dp
+    p = lax.axis_index("dp")
+    place = jnp.stack([p, p + 1 - 2 * (p % 2)]).astype(jnp.int32)
+
+    block = pack(route_ids, route_probs, tokens, cotangent)
+    mine = [block, over_z(block, 1), over_z(block, -1), over_z(block, 2)]
+    beside = [over_x(b) for b in mine]
+    far_mine = [over_y(b) for b in mine]
+    far_beside = [over_x(far_mine[0])] + [over_y(b) for b in beside[1:]]
+
+    weights = (gate_weight, up_weight, down_weight)
+    run = functools.partial(forward, gate=gate_weight, up=up_weight, down=down_weight, place=place, part=part)
+    results, pieces = [], []
+    for lo in (0, 2):
+        out = run(mine[lo : lo + 2] + beside[lo : lo + 2], back=True)
+        results.append(out[:3])
+        pieces += merge(out[4], over_x(out[3]))
+    results.append(run(far_mine + far_beside, back=False))
+    returned = [pieces[0], over_z(pieces[1], -1), over_z(pieces[2], 1), over_z(pieces[3], 2)]
+
+    acts, parts = [], []
+    for act, own, other in results:
+        acts += [act, over_core(act)]
+        parts += [own, over_core(other)]
+    gate_grad, up_grad, down_grad = grads(acts, parts, part, gate_weight.shape[1])
+    return unpack(route_ids, returned), gate_grad, up_grad, down_grad
 
 
 def pick_rows(placer, values):
@@ -12,7 +355,7 @@
     ).astype(jnp.bfloat16)
 
 
-def per_device(tokens, cotangent, route_ids, route_probs, gate_weight, up_weight, down_weight):
+def per_device_general(tokens, cotangent, route_ids, route_probs, gate_weight, up_weight, down_weight):
     hits = route_ids == 0
     chosen = jnp.any(hits, axis=1).astype(jnp.int32)
     share = jnp.sum(jnp.where(hits, route_probs, 0.0), axis=1)
@@ -95,6 +438,8 @@
         P("expert", None),
     )
     out_specs = (P(("dp", "expert"), None), P("dp", "expert"), P("dp", "expert"), P("expert", "dp"))
+    fast = mesh.shape["dp"] == 4 and mesh.shape["expert"] == 8
+    body = per_device if fast else per_device_general
     return jax.shard_map(
-        per_device, mesh=mesh, in_specs=in_specs, out_specs=out_specs, check_vma=False
-    )
+        body, mesh=mesh, in_specs=in_specs, out_specs=out_specs, check_vma=False
+    )

time: 310 us -> 186 us (0.60)
  waiting for transfers between devices: 164 us -> 71.4 us
  blocking collectives: 68 us -> 0 us
  Pallas kernels: 0 us -> 65.1 us
  matrix products: 52.4 us -> 0 us
  starting transfers between devices: 1.69 us -> 38.6 us
  between operations: 15.2 us -> 1.07 us
    reduce_scatter x3 -> x0, waiting for transfers between devices: 98.5 us -> none  [the longest x1 61.3 us: per_device(): lax.psum_scatter(gate_part.astype(jnp.bfloat16), 'dp', scatter_dimension=...]
    ppermute x0 -> x26, waiting for transfers between devices: none -> 71.4 us  [the longest x6 37.8 us: over_z(): lax.ppermute(v, 'expert', [(i, (i + 2 * by) % n_expert) for i in range(n_...]
    unnamed x2 -> x0, blocking collectives: 68 us -> none
    pallas_call x0 -> x8, Pallas kernels: none -> 65.1 us  [the longest x3 49.3 us: forward(): pl.pallas_call(functools.partial(forward_kernel, n, back), grid_spec=pltp...]
    all_gather x2 -> x0, waiting for transfers between devices: 61.5 us -> none  [the longest x1 35.8 us: per_device(): lax.all_gather(local_cotan, 'expert', axis=0, tiled=True)]
    dot_general x11 -> x0, matrix products: 52.4 us -> none  [the longest x1 8.98 us: per_device(): lax.dot_general(hidden, scaled, (((0,), (0,)), ((), ())), preferred_eleme...]
    ppermute x0 -> x26, starting transfers between devices: none -> 38.6 us  [the longest x6 21.1 us: over_z(): lax.ppermute(v, 'expert', [(i, (i + 2 * by) % n_expert) for i in range(n_...]
    unnamed x20 -> x54, local copies, waits for them, and re-layouts: 3.94 us -> 8.49 us
  transfers between devices with their start and end apart: 6 -> 26, of which waited for: 5 -> 11; matrix products, arithmetic and copies ran while one was open for 29% -> 0% of each run, Pallas kernels for 0% -> 28%
where the time goes in v1:
time: 186 us; the launch traced here: 185 us
  waiting for transfers between devices  71.4 us (38%)
  Pallas kernels  65.1 us (35%)
  starting transfers between devices  38.6 us (21%)
  local copies, waits for them, and re-layouts  8.49 us (5%)
    pallas_call x3, Pallas kernels, forward(): pl.pallas_call(functools.partial(forward_kernel, n, back), grid_spec=pltp...  49.3 us
    ppermute x6, waiting for transfers between devices, over_z(): lax.ppermute(v, 'expert', [(i, (i + 2 * by) % n_expert) for i in range(n_...  37.8 us
    ppermute x7, waiting for transfers between devices, over_y(): return lax.ppermute(v, 'dp', y_pairs)  24.9 us
    ppermute x6, starting transfers between devices, over_z(): lax.ppermute(v, 'expert', [(i, (i + 2 * by) % n_expert) for i in range(n_...  21.1 us
    pallas_call x1, Pallas kernels, grads(): pl.pallas_call(functools.partial(grads_kernel, n), in_specs=[anywhere] *...  11.6 us
    ppermute x7, starting transfers between devices, over_x(): return lax.ppermute(v, 'expert', x_pairs)  8.69 us
    ppermute x7, waiting for transfers between devices, over_x(): return lax.ppermute(v, 'expert', x_pairs)  8.58 us
    unnamed x54, local copies, waits for them, and re-layouts  8.49 us
  transfers between devices with their start and end apart: 26, of which 11 were waited for; matrix products, arithmetic and copies ran while one was open for 0% of the time, Pallas kernels for 28%

profile of v1, /device:TPU:0, one launch (start us, length us, event | category | flops | bytes accessed | tf_op | source)
XLA Modules:
  0.0 185.3 jit_solution(4755605590162638972)
XLA Ops:
  0.6 0.8 copy.13.ids
  1.4 0.8 copy.12.probs
  2.2 1.1 copy-done.1
  3.3 1.1 copy-done.2
  4.5 1.7 pack.1.refs_0_
  6.2 3.0 %collective-permute-start.14 = (bf16[72,3072]{1,0:T(8,128)(2,1)S(1)}, bf16[72,3072]{1,0:T(8,128)(2,1)S(1)}, u32[]{:S(2)}, u32[]{:S(2)}) collective-permute-start(bf16[72,3072]{1,0:T(8,128)(2,1)S(1)} %pack.1.refs_0_), channel_id=1, source_target_pairs={{0,16},{8,24},{16,0},{24,8},{1,17},{9,25},{17,1},{25,9},{2,18},{10... | collective-permute-start | bytes 1327112 | tf_op jit(solution)/shard_map/ppermute | solution.py:314
  9.3 2.6 %collective-permute-start.6 = (bf16[72,3072]{1,0:T(8,128)(2,1)S(1)}, bf16[72,3072]{1,0:T(8,128)(2,1)S(1)}, u32[]{:S(2)}, u32[]{:S(2)}) collective-permute-start(bf16[72,3072]{1,0:T(8,128)(2,1)S(1)} %pack.1.refs_0_), channel_id=1, source_target_pairs={{0,4},{1,5},{2,6},{3,7},{4,0},{5,1},{6,2},{7,3},{8,12},{9,13},{10,... | collective-permute-start | bytes 1327112 | tf_op jit(solution)/shard_map/ppermute | solution.py:320
  11.9 1.4 collective-permute-start.5
  13.2 1.5 collective-permute-start.1
  14.7 0.7 collective-permute-start
  15.4 4.1 %collective-permute-done.14.refs_0_ = bf16[72,3072]{1,0:T(8,128)(2,1)S(1)} collective-permute-done((bf16[72,3072]{1,0:T(8,128)(2,1)S(1)}, bf16[72,3072]{1,0:T(8,128)(2,1)S(1)}, u32[]{:S(2)}, u32[]{:S(2)}) %collective-permute-start.14) | collective-permute-done | bytes 442400 | tf_op jit(solution)/shard_map/ppermute | solution.py:314
  19.4 1.7 collective-permute-start.18
  21.1 20.8 %collective-permute-done.6.refs_1_ = bf16[72,3072]{1,0:T(8,128)(2,1)S(1)} collective-permute-done((bf16[72,3072]{1,0:T(8,128)(2,1)S(1)}, bf16[72,3072]{1,0:T(8,128)(2,1)S(1)}, u32[]{:S(2)}, u32[]{:S(2)}) %collective-permute-start.6) | collective-permute-done | bytes 442400 | tf_op jit(solution)/shard_map/ppermute | solution.py:320
  42.0 2.0 %collective-permute-start.8 = (bf16[72,3072]{1,0:T(8,128)(2,1)S(1)}, bf16[72,3072]{1,0:T(8,128)(2,1)S(1)}, u32[]{:S(2)}, u32[]{:S(2)}) collective-permute-start(bf16[72,3072]{1,0:T(8,128)(2,1)S(1)} %collective-permute-done.6.refs_1_), channel_id=1, source_target_pairs={{0,1},{1,0},{2,3},{3,2},{4,5},{5,4},{6,7},{7,6},{8,9},{9,8},{10,11... | collective-permute-start | bytes 1327112 | tf_op jit(solution)/shard_map/ppermute | solution.py:317
  44.1 0.7 copy-done.16
  44.7 1.3 collective-permute-start.2
  46.0 1.5 collective-permute-start.16
  47.5 7.5 %collective-permute-done.17.refs_3_ = bf16[72,3072]{1,0:T(8,128)(2,1)S(1)} collective-permute-done((bf16[72,3072]{1,0:T(8,128)(2,1)S(1)}, bf16[72,3072]{1,0:T(8,128)(2,1)S(1)}, u32[]{:S(2)}, u32[]{:S(2)}) %collective-permute-start.17) | collective-permute-done | bytes 442400 | tf_op jit(solution)/shard_map/ppermute | solution.py:314
  55.0 2.0 %collective-permute-start.21 = (bf16[72,3072]{1,0:T(8,128)(2,1)S(1)}, bf16[72,3072]{1,0:T(8,128)(2,1)S(1)}, u32[]{:S(2)}, u32[]{:S(2)}) collective-permute-start(bf16[72,3072]{1,0:T(8,128)(2,1)S(1)} %collective-permute-done.8.refs_3_), channel_id=1, source_target_pairs={{0,16},{8,24},{16,0},{24,8},{1,17},{9,25},{17,1},{25,9},{2,18},{10... | collective-permute-start | bytes 1327112 | tf_op jit(solution)/shard_map/ppermute | solution.py:314
  57.0 0.7 collective-permute-done.7.refs_2_
  57.8 0.6 collective-permute-start.20
  58.4 4.1 %collective-permute-done.2.refs_3_ = bf16[72,3072]{1,0:T(8,128)(2,1)} collective-permute-done((bf16[72,3072]{1,0:T(8,128)(2,1)}, bf16[72,3072]{1,0:T(8,128)(2,1)}, u32[]{:S(2)}, u32[]{:S(2)}) %collective-permute-start.2) | collective-permute-done | bytes 442400 | tf_op jit(solution)/shard_map/ppermute | solution.py:317
  62.5 0.6 collective-permute-start.19
  63.2 0.6 pad_add_fusion.place
  63.7 17.9 %forward_back.2 = (bf16[144,3072]{1,0:T(8,128)(2,1)}, bf16[144,1536]{1,0:T(8,128)(2,1)}, bf16[144,1536]{1,0:T(8,128)(2,1)}, bf16[72,3072]{1,0:T(8,128)(2,1)}, bf16[72,3072]{1,0:T(8,128)(2,1)}) custom-call(s32[2]{0:T(128)} %pad_add_fusion.place, bf16[72,3072]{1,0:T(8,128)(2,1)} %copy-done, bf16[72,3072]{1,0:T(8,128)(2,1)} %collective-permute-done.refs_1_, ...), custom_call_target="tpu_custom_call" | custom-call | flops 4529848320 | bytes 21086208 | tf_op jit(solution)/shard_map/forward_back/pallas_call | solution.py:199
  81.6 1.6 collective-permute-start.3
  83.2 0.2 collective-permute-done.21.refs_7_
  83.5 8.4 %collective-permute-done.20.refs_6_ = bf16[72,3072]{1,0:T(8,128)(2,1)S(1)} collective-permute-done((bf16[72,3072]{1,0:T(8,128)(2,1)}, bf16[72,3072]{1,0:T(8,128)(2,1)S(1)}, u32[]{:S(2)}, u32[]{:S(2)}) %collective-permute-start.20) | collective-permute-done | bytes 442400 | tf_op jit(solution)/shard_map/ppermute | solution.py:314
  91.9 4.7 %collective-permute-done.19.refs_5_ = bf16[72,3072]{1,0:T(8,128)(2,1)S(1)} collective-permute-done((bf16[72,3072]{1,0:T(8,128)(2,1)}, bf16[72,3072]{1,0:T(8,128)(2,1)S(1)}, u32[]{:S(2)}, u32[]{:S(2)}) %collective-permute-start.19) | collective-permute-done | bytes 442400 | tf_op jit(solution)/shard_map/ppermute | solution.py:314
  96.6 0.8 copy-done.12
  97.4 13.4 %forward.1 = (bf16[288,3072]{1,0:T(8,128)(2,1)}, bf16[288,1536]{1,0:T(8,128)(2,1)}, bf16[288,1536]{1,0:T(8,128)(2,1)}) custom-call(s32[2]{0:T(128)} %pad_add_fusion.place, bf16[72,3072]{1,0:T(8,128)(2,1)} %copy-done.5, bf16[72,3072]{1,0:T(8,128)(2,1)} %copy-done.9, bf16[72,3072]{1,0:T(8,128)(2,1)} %copy-done.8, bf16[72,3072]{1,0:T(8,128)(2,1)} %copy-done.7, ...), custom_call_target="tpu_custom_call" | custom-call | flops 5435817984 | bytes 23298048 | tf_op jit(solution)/shard_map/forward/pallas_call | solution.py:199
  110.9 18.0 %forward_back.3 = (bf16[144,3072]{1,0:T(8,128)(2,1)}, bf16[144,1536]{1,0:T(8,128)(2,1)}, bf16[144,1536]{1,0:T(8,128)(2,1)}, bf16[72,3072]{1,0:T(8,128)(2,1)}, bf16[72,3072]{1,0:T(8,128)(2,1)}) custom-call(s32[2]{0:T(128)} %pad_add_fusion.place, bf16[72,3072]{1,0:T(8,128)(2,1)} %copy-done.14, bf16[72,3072]{1,0:T(8,128)(2,1)} %copy-done.13, ...), custom_call_target="tpu_custom_call" | custom-call | flops 4529848320 | bytes 21086208 | tf_op jit(solution)/shard_map/forward_back/pallas_call | solution.py:199
  128.9 0.6 collective-permute-start.9
  129.5 0.2 collective-permute-start.23
  129.8 8.2 %collective-permute-start.4 = (bf16[40,3072]{1,0:T(8,128)(2,1)S(1)}, bf16[40,3072]{1,0:T(8,128)(2,1)S(1)}, u32[]{:S(2)}, u32[]{:S(2)}) collective-permute-start(bf16[40,3072]{1,0:T(8,128)(2,1)S(1)} %get-tuple-element.27), channel_id=1, source_target_pairs={{0,6},{1,7},{2,0},{3,1},{4,2},{5,3},{6,4},{7,5},{8,14},{9,15},{10,... | collective-permute-start | bytes 737288 | tf_op jit(solution)/shard_map/ppermute | solution.py:320
  138.0 3.7 %collective-permute-done.9.came = bf16[72,3072]{1,0:T(8,128)(2,1)S(1)} collective-permute-done((bf16[72,3072]{1,0:T(8,128)(2,1)}, bf16[72,3072]{1,0:T(8,128)(2,1)S(1)}, u32[]{:S(2)}, u32[]{:S(2)}) %collective-permute-start.9) | collective-permute-done | bytes 442400 | tf_op jit(solution)/shard_map/ppermute | solution.py:317
  141.8 1.0 copy-done.4
  142.9 6.2 %collective-permute-start.10 = (bf16[40,3072]{1,0:T(8,128)(2,1)S(1)}, bf16[40,3072]{1,0:T(8,128)(2,1)S(1)}, u32[]{:S(2)}, u32[]{:S(2)}) collective-permute-start(bf16[40,3072]{1,0:T(8,128)(2,1)S(1)} %get-tuple-element.30), channel_id=1, source_target_pairs={{0,2},{1,3},{2,4},{3,5},{4,6},{5,7},{6,0},{7,1},{8,10},{9,11},{10,... | collective-permute-start | bytes 737288 | tf_op jit(solution)/shard_map/ppermute | solution.py:320
  149.1 0.6 collective-permute-start.12
  149.7 6.4 %collective-permute-done.10.refs_2_ = bf16[40,3072]{1,0:T(8,128)(2,1)S(1)} collective-permute-done((bf16[40,3072]{1,0:T(8,128)(2,1)S(1)}, bf16[40,3072]{1,0:T(8,128)(2,1)S(1)}, u32[]{:S(2)}, u32[]{:S(2)}) %collective-permute-start.10) | collective-permute-done | bytes 245792 | tf_op jit(solution)/shard_map/ppermute | solution.py:320
  156.1 2.1 %collective-permute-start.11 = (bf16[40,3072]{1,0:T(8,128)(2,1)S(1)}, bf16[40,3072]{1,0:T(8,128)(2,1)S(1)}, u32[]{:S(2)}, u32[]{:S(2)}) collective-permute-start(bf16[40,3072]{1,0:T(8,128)(2,1)S(1)} %get-tuple-element.31), channel_id=1, source_target_pairs={{0,4},{1,5},{2,6},{3,7},{4,0},{5,1},{6,2},{7,3},{8,12},{9,13},{10,... | collective-permute-start | bytes 737288 | tf_op jit(solution)/shard_map/ppermute | solution.py:320
  158.2 10.7 %collective-permute-done.11.refs_3_ = bf16[40,3072]{1,0:T(8,128)(2,1)S(1)} collective-permute-done((bf16[40,3072]{1,0:T(8,128)(2,1)S(1)}, bf16[40,3072]{1,0:T(8,128)(2,1)S(1)}, u32[]{:S(2)}, u32[]{:S(2)}) %collective-permute-start.11) | collective-permute-done | bytes 245792 | tf_op jit(solution)/shard_map/ppermute | solution.py:320
  168.9 2.3 %unpack.1 = bf16[128,3072]{1,0:T(8,128)(2,1)} custom-call(s32[128,2]{1,0:T(8,128)S(1)} %copy.13.ids, bf16[40,3072]{1,0:T(8,128)(2,1)S(1)} %get-tuple-element.26.refs_0_, bf16[40,3072]{1,0:T(8,128)(2,1)S(1)} %collective-permute-done.4.refs_1_, bf16[40,3072]{1,0:T(8,128)(2,1)S(1)} %collective-permute-done.10.refs_2_, ...), custom_call_target="tpu_custom_call" | custom-call | tf_op jit(solution)/shard_map/unpack/pallas_call | solution.py:103
  171.4 0.7 copy-done.25
  172.0 0.4 copy-done.20
  172.6 0.3 copy-done.22
  172.9 0.6 copy-done.17
  173.5 11.6 %grads.1 = (bf16[768,1024]{1,0:T(8,128)(2,1)}, bf16[768,1024]{1,0:T(8,128)(2,1)}, bf16[1024,768]{1,0:T(8,128)(2,1)}) custom-call(bf16[144,3072]{1,0:T(8,128)(2,1)} %get-tuple-element.32.refs_0_, bf16[144,3072]{1,0:T(8,128)(2,1)} %copy-done.21, bf16[144,3072]{1,0:T(8,128)(2,1)} %get-tuple-element.33.refs_2_, bf16[144,3072]{1,0:T(8,128)(2,1)} %copy-done.20, ...), custom_call_target="tpu_custom_call" | custom-call | flops 5435817984 | bytes 15335424 | tf_op jit(solution)/shard_map/grads/pallas_call | solution.py:265
  (67 shorter events, 0.8 us)
Async XLA Ops:
  2.2 1.1 copy-start.1
  3.3 1.1 copy-start.2
  6.2 57.5 %copy-start = (bf16[72,3072]{1,0:T(8,128)(2,1)}, bf16[72,3072]{1,0:T(8,128)(2,1)S(1)}, u32[]{:S(2)}) copy-start(bf16[72,3072]{1,0:T(8,128)(2,1)S(1)} %pack.1.refs_0_) | copy-start | bytes 1327108
  6.2 13.2 %collective-permute-start.14 = (bf16[72,3072]{1,0:T(8,128)(2,1)S(1)}, bf16[72,3072]{1,0:T(8,128)(2,1)S(1)}, u32[]{:S(2)}, u32[]{:S(2)}) collective-permute-start(bf16[72,3072]{1,0:T(8,128)(2,1)S(1)} %pack.1.refs_0_), channel_id=1, source_target_pairs={{0,16},{8,24},{16,0},{24,8},{1,17},{9,25},{17,1},{25,9},{2,18},{10... | collective-permute-start | bytes 1327112 | tf_op jit(solution)/shard_map/ppermute | solution.py:314
  9.3 32.7 %collective-permute-start.6 = (bf16[72,3072]{1,0:T(8,128)(2,1)S(1)}, bf16[72,3072]{1,0:T(8,128)(2,1)S(1)}, u32[]{:S(2)}, u32[]{:S(2)}) collective-permute-start(bf16[72,3072]{1,0:T(8,128)(2,1)S(1)} %pack.1.refs_0_), channel_id=1, source_target_pairs={{0,4},{1,5},{2,6},{3,7},{4,0},{5,1},{6,2},{7,3},{8,12},{9,13},{10,... | collective-permute-start | bytes 1327112 | tf_op jit(solution)/shard_map/ppermute | solution.py:320
  11.9 30.1 %collective-permute-start.5 = (bf16[72,3072]{1,0:T(8,128)(2,1)S(1)}, bf16[72,3072]{1,0:T(8,128)(2,1)S(1)}, u32[]{:S(2)}, u32[]{:S(2)}) collective-permute-start(bf16[72,3072]{1,0:T(8,128)(2,1)S(1)} %pack.1.refs_0_), channel_id=1, source_target_pairs={{0,6},{1,7},{2,0},{3,1},{4,2},{5,3},{6,4},{7,5},{8,14},{9,15},{10,... | collective-permute-start | bytes 1327112 | tf_op jit(solution)/shard_map/ppermute | solution.py:320
  13.2 30.8 %collective-permute-start.1 = (bf16[72,3072]{1,0:T(8,128)(2,1)S(1)}, bf16[72,3072]{1,0:T(8,128)(2,1)S(1)}, u32[]{:S(2)}, u32[]{:S(2)}) collective-permute-start(bf16[72,3072]{1,0:T(8,128)(2,1)S(1)} %pack.1.refs_0_), channel_id=1, source_target_pairs={{0,1},{1,0},{2,3},{3,2},{4,5},{5,4},{6,7},{7,6},{8,9},{9,8},{10,11... | collective-permute-start | bytes 1327112 | tf_op jit(solution)/shard_map/ppermute | solution.py:317
  14.7 29.4 %collective-permute-start = (bf16[72,3072]{1,0:T(8,128)(2,1)S(1)}, bf16[72,3072]{1,0:T(8,128)(2,1)}, u32[]{:S(2)}, u32[]{:S(2)}) collective-permute-start(bf16[72,3072]{1,0:T(8,128)(2,1)S(1)} %pack.1.refs_0_), channel_id=1, source_target_pairs={{0,2},{1,3},{2,4},{3,5},{4,6},{5,7},{6,0},{7,1},{8,10},{9,11},{10,... | collective-permute-start | bytes 1327112 | tf_op jit(solution)/shard_map/ppermute | solution.py:320
  19.4 62.1 %copy-start.5 = (bf16[72,3072]{1,0:T(8,128)(2,1)}, bf16[72,3072]{1,0:T(8,128)(2,1)S(1)}, u32[]{:S(2)}) copy-start(bf16[72,3072]{1,0:T(8,128)(2,1)S(1)} %collective-permute-done.14.refs_0_) | copy-start | bytes 1327108
  19.4 26.6 %collective-permute-start.18 = (bf16[72,3072]{1,0:T(8,128)(2,1)S(1)}, bf16[72,3072]{1,0:T(8,128)(2,1)S(1)}, u32[]{:S(2)}, u32[]{:S(2)}) collective-permute-start(bf16[72,3072]{1,0:T(8,128)(2,1)S(1)} %collective-permute-done.14.refs_0_), channel_id=1, source_target_pairs={{0,1},{1,0},{2,3},{3,2},{4,5},{5,4},{6,7},{7,6},{8,9},{9,8},{10,11... | collective-permute-start | bytes 1327112 | tf_op jit(solution)/shard_map/ppermute | solution.py:317
  42.0 39.6 %copy-start.13 = (bf16[72,3072]{1,0:T(8,128)(2,1)}, bf16[72,3072]{1,0:T(8,128)(2,1)S(1)}, u32[]{:S(2)}) copy-start(bf16[72,3072]{1,0:T(8,128)(2,1)S(1)} %collective-permute-done.6.refs_1_) | copy-start | bytes 1327108
  42.0 13.0 %collective-permute-start.17 = (bf16[72,3072]{1,0:T(8,128)(2,1)S(1)}, bf16[72,3072]{1,0:T(8,128)(2,1)S(1)}, u32[]{:S(2)}, u32[]{:S(2)}) collective-permute-start(bf16[72,3072]{1,0:T(8,128)(2,1)S(1)} %collective-permute-done.6.refs_1_), channel_id=1, source_target_pairs={{0,16},{8,24},{16,0},{24,8},{1,17},{9,25},{17,1},{25,9},{2,18},{10... | collective-permute-start | bytes 1327112 | tf_op jit(solution)/shard_map/ppermute | solution.py:314
  42.0 39.6 %copy-start.14 = (bf16[72,3072]{1,0:T(8,128)(2,1)}, bf16[72,3072]{1,0:T(8,128)(2,1)S(1)}, u32[]{:S(2)}) copy-start(bf16[72,3072]{1,0:T(8,128)(2,1)S(1)} %collective-permute-done.5.refs_0_) | copy-start | bytes 1327108
  42.0 13.0 %collective-permute-start.8 = (bf16[72,3072]{1,0:T(8,128)(2,1)S(1)}, bf16[72,3072]{1,0:T(8,128)(2,1)S(1)}, u32[]{:S(2)}, u32[]{:S(2)}) collective-permute-start(bf16[72,3072]{1,0:T(8,128)(2,1)S(1)} %collective-permute-done.6.refs_1_), channel_id=1, source_target_pairs={{0,1},{1,0},{2,3},{3,2},{4,5},{5,4},{6,7},{7,6},{8,9},{9,8},{10,11... | collective-permute-start | bytes 1327112 | tf_op jit(solution)/shard_map/ppermute | solution.py:317
  44.0 13.8 %collective-permute-start.7 = (bf16[72,3072]{1,0:T(8,128)(2,1)S(1)}, bf16[72,3072]{1,0:T(8,128)(2,1)}, u32[]{:S(2)}, u32[]{:S(2)}) collective-permute-start(bf16[72,3072]{1,0:T(8,128)(2,1)S(1)} %collective-permute-done.5.refs_0_), channel_id=1, source_target_pairs={{0,1},{1,0},{2,3},{3,2},{4,5},{5,4},{6,7},{7,6},{8,9},{9,8},{10,11... | collective-permute-start | bytes 1327112 | tf_op jit(solution)/shard_map/ppermute | solution.py:317
  44.7 17.8 %collective-permute-start.2 = (bf16[72,3072]{1,0:T(8,128)(2,1)}, bf16[72,3072]{1,0:T(8,128)(2,1)}, u32[]{:S(2)}, u32[]{:S(2)}) collective-permute-start(bf16[72,3072]{1,0:T(8,128)(2,1)} %collective-permute-done.refs_1_), channel_id=1, source_target_pairs={{0,1},{1,0},{2,3},{3,2},{4,5},{5,4},{6,7},{7,6},{8,9},{9,8},{10,11... | collective-permute-start | bytes 1327112 | tf_op jit(solution)/shard_map/ppermute | solution.py:317
  46.0 35.6 %copy-start.6 = (bf16[72,3072]{1,0:T(8,128)(2,1)}, bf16[72,3072]{1,0:T(8,128)(2,1)S(1)}, u32[]{:S(2)}) copy-start(bf16[72,3072]{1,0:T(8,128)(2,1)S(1)} %collective-permute-done.18.refs_4_) | copy-start | bytes 1327108
  46.0 35.6 %collective-permute-start.16 = (bf16[72,3072]{1,0:T(8,128)(2,1)S(1)}, bf16[72,3072]{1,0:T(8,128)(2,1)S(1)}, u32[]{:S(2)}, u32[]{:S(2)}) collective-permute-start(bf16[72,3072]{1,0:T(8,128)(2,1)S(1)} %collective-permute-done.5.refs_0_), channel_id=1, source_target_pairs={{0,16},{8,24},{16,0},{24,8},{1,17},{9,25},{17,1},{25,9},{2,18},{10... | collective-permute-start | bytes 1327112 | tf_op jit(solution)/shard_map/ppermute | solution.py:314
  55.0 26.6 %copy-start.7 = (bf16[72,3072]{1,0:T(8,128)(2,1)}, bf16[72,3072]{1,0:T(8,128)(2,1)S(1)}, u32[]{:S(2)}) copy-start(bf16[72,3072]{1,0:T(8,128)(2,1)S(1)} %collective-permute-done.17.refs_3_) | copy-start | bytes 1327108
  55.0 28.2 %collective-permute-start.15 = (bf16[72,3072]{1,0:T(8,128)(2,1)}, bf16[72,3072]{1,0:T(8,128)(2,1)S(1)}, u32[]{:S(2)}, u32[]{:S(2)}) collective-permute-start(bf16[72,3072]{1,0:T(8,128)(2,1)} %collective-permute-done.refs_1_), channel_id=1, source_target_pairs={{0,16},{8,24},{16,0},{24,8},{1,17},{9,25},{17,1},{25,9},{2,18},{10... | collective-permute-start | bytes 1327112 | tf_op jit(solution)/shard_map/ppermute | solution.py:314
  55.0 26.6 %copy-start.15 = (bf16[72,3072]{1,0:T(8,128)(2,1)}, bf16[72,3072]{1,0:T(8,128)(2,1)S(1)}, u32[]{:S(2)}) copy-start(bf16[72,3072]{1,0:T(8,128)(2,1)S(1)} %collective-permute-done.8.refs_3_) | copy-start | bytes 1327108
  55.0 28.4 %collective-permute-start.21 = (bf16[72,3072]{1,0:T(8,128)(2,1)S(1)}, bf16[72,3072]{1,0:T(8,128)(2,1)S(1)}, u32[]{:S(2)}, u32[]{:S(2)}) collective-permute-start(bf16[72,3072]{1,0:T(8,128)(2,1)S(1)} %collective-permute-done.8.refs_3_), channel_id=1, source_target_pairs={{0,16},{8,24},{16,0},{24,8},{1,17},{9,25},{17,1},{25,9},{2,18},{10... | collective-permute-start | bytes 1327112 | tf_op jit(solution)/shard_map/ppermute | solution.py:314
  57.8 34.1 %collective-permute-start.20 = (bf16[72,3072]{1,0:T(8,128)(2,1)}, bf16[72,3072]{1,0:T(8,128)(2,1)S(1)}, u32[]{:S(2)}, u32[]{:S(2)}) collective-permute-start(bf16[72,3072]{1,0:T(8,128)(2,1)} %collective-permute-done.7.refs_2_), channel_id=1, source_target_pairs={{0,16},{8,24},{16,0},{24,8},{1,17},{9,25},{17,1},{25,9},{2,18},{10... | collective-permute-start | bytes 1327112 | tf_op jit(solution)/shard_map/ppermute | solution.py:314
  62.5 34.1 %collective-permute-start.19 = (bf16[72,3072]{1,0:T(8,128)(2,1)}, bf16[72,3072]{1,0:T(8,128)(2,1)S(1)}, u32[]{:S(2)}, u32[]{:S(2)}) collective-permute-start(bf16[72,3072]{1,0:T(8,128)(2,1)} %collective-permute-done.2.refs_3_), channel_id=1, source_target_pairs={{0,16},{8,24},{16,0},{24,8},{1,17},{9,25},{17,1},{25,9},{2,18},{10... | collective-permute-start | bytes 1327112 | tf_op jit(solution)/shard_map/ppermute | solution.py:314
  81.6 15.0 %copy-start.8 = (bf16[72,3072]{1,0:T(8,128)(2,1)}, bf16[72,3072]{1,0:T(8,128)(2,1)S(1)}, u32[]{:S(2)}) copy-start(bf16[72,3072]{1,0:T(8,128)(2,1)S(1)} %collective-permute-done.16.refs_2_) | copy-start | bytes 1327108
  81.6 48.1 %collective-permute-start.3 = (bf16[72,3072]{1,0:T(8,128)(2,1)}, bf16[72,3072]{1,0:T(8,128)(2,1)S(1)}, u32[]{:S(2)}, u32[]{:S(2)}) collective-permute-start(bf16[72,3072]{1,0:T(8,128)(2,1)} %get-tuple-element.25), channel_id=1, source_target_pairs={{0,1},{1,0},{2,3},{3,2},{4,5},{5,4},{6,7},{7,6},{8,9},{9,8},{10,11... | collective-permute-start | bytes 1327112 | tf_op jit(solution)/shard_map/ppermute | solution.py:317
  83.2 13.4 %copy-start.9 = (bf16[72,3072]{1,0:T(8,128)(2,1)}, bf16[72,3072]{1,0:T(8,128)(2,1)S(1)}, u32[]{:S(2)}) copy-start(bf16[72,3072]{1,0:T(8,128)(2,1)S(1)} %collective-permute-done.15.refs_1_) | copy-start | bytes 1327108
  83.5 13.2 %copy-start.10 = (bf16[72,3072]{1,0:T(8,128)(2,1)}, bf16[72,3072]{1,0:T(8,128)(2,1)S(1)}, u32[]{:S(2)}) copy-start(bf16[72,3072]{1,0:T(8,128)(2,1)S(1)} %collective-permute-done.21.refs_7_) | copy-start | bytes 1327108
  91.9 4.8 %copy-start.11 = (bf16[72,3072]{1,0:T(8,128)(2,1)}, bf16[72,3072]{1,0:T(8,128)(2,1)S(1)}, u32[]{:S(2)}) copy-start(bf16[72,3072]{1,0:T(8,128)(2,1)S(1)} %collective-permute-done.20.refs_6_) | copy-start | bytes 1327108
  110.8 18.7 %copy-start.24 = (bf16[144,1536]{1,0:T(8,128)(2,1)S(1)}, bf16[144,1536]{1,0:T(8,128)(2,1)}, u32[]{:S(2)}) copy-start(bf16[144,1536]{1,0:T(8,128)(2,1)} %get-tuple-element.36) | copy-start | bytes 1327108
  110.8 18.9 %copy-start.3 = (bf16[72,3072]{1,0:T(8,128)(2,1)S(1)}, bf16[72,3072]{1,0:T(8,128)(2,1)}, u32[]{:S(2)}) copy-start(bf16[72,3072]{1,0:T(8,128)(2,1)} %get-tuple-element.24.keep) | copy-start | bytes 1327108
  110.8 60.5 %collective-permute-start.22 = (bf16[288,3072]{1,0:T(8,128)(2,1)}, bf16[288,3072]{1,0:T(8,128)(2,1)S(1)}, u32[]{:S(2)}, u32[]{:S(2)}) collective-permute-start(bf16[288,3072]{1,0:T(8,128)(2,1)} %get-tuple-element.34.refs_4_), channel_id=1, source_target_pairs={{0,8},{8,0},{16,24},{24,16},{1,9},{9,1},{17,25},{25,17},{2,10},{10... | collective-permute-start | bytes 5308424 | tf_op jit(solution)/shard_map/ppermute | solution.py:311
  110.9 38.8 %copy-start.19 = (bf16[288,1536]{1,0:T(8,128)(2,1)S(1)}, bf16[288,1536]{1,0:T(8,128)(2,1)}, u32[]{:S(2)}) copy-start(bf16[288,1536]{1,0:T(8,128)(2,1)} %get-tuple-element.40) | copy-start | bytes 2654212
  128.9 20.2 %copy-start.18 = (bf16[144,3072]{1,0:T(8,128)(2,1)S(1)}, bf16[144,3072]{1,0:T(8,128)(2,1)}, u32[]{:S(2)}) copy-start(bf16[144,3072]{1,0:T(8,128)(2,1)} %get-tuple-element.32.refs_0_) | copy-start | bytes 2654212
  128.9 12.8 %collective-permute-start.9 = (bf16[72,3072]{1,0:T(8,128)(2,1)}, bf16[72,3072]{1,0:T(8,128)(2,1)S(1)}, u32[]{:S(2)}, u32[]{:S(2)}) collective-permute-start(bf16[72,3072]{1,0:T(8,128)(2,1)} %get-tuple-element.29), channel_id=1, source_target_pairs={{0,1},{1,0},{2,3},{3,2},{4,5},{5,4},{6,7},{7,6},{8,9},{9,8},{10,11... | collective-permute-start | bytes 1327112 | tf_op jit(solution)/shard_map/ppermute | solution.py:317
  129.5 19.6 %collective-permute-start.23 = (bf16[144,1536]{1,0:T(8,128)(2,1)S(1)}, bf16[144,1536]{1,0:T(8,128)(2,1)S(1)}, u32[]{:S(2)}, u32[]{:S(2)}) collective-permute-start(bf16[144,1536]{1,0:T(8,128)(2,1)S(1)} %copy-done.24), channel_id=1, source_target_pairs={{0,8},{8,0},{16,24},{24,16},{1,9},{9,1},{17,25},{25,17},{2,10},{10... | collective-permute-start | bytes 1327112 | tf_op jit(solution)/shard_map/ppermute | solution.py:311
  129.8 19.8 %collective-permute-start.4 = (bf16[40,3072]{1,0:T(8,128)(2,1)S(1)}, bf16[40,3072]{1,0:T(8,128)(2,1)S(1)}, u32[]{:S(2)}, u32[]{:S(2)}) collective-permute-start(bf16[40,3072]{1,0:T(8,128)(2,1)S(1)} %get-tuple-element.27), channel_id=1, source_target_pairs={{0,6},{1,7},{2,0},{3,1},{4,2},{5,3},{6,4},{7,5},{8,14},{9,15},{10,... | collective-permute-start | bytes 737288 | tf_op jit(solution)/shard_map/ppermute | solution.py:320
  142.9 13.2 %collective-permute-start.10 = (bf16[40,3072]{1,0:T(8,128)(2,1)S(1)}, bf16[40,3072]{1,0:T(8,128)(2,1)S(1)}, u32[]{:S(2)}, u32[]{:S(2)}) collective-permute-start(bf16[40,3072]{1,0:T(8,128)(2,1)S(1)} %get-tuple-element.30), channel_id=1, source_target_pairs={{0,2},{1,3},{2,4},{3,5},{4,6},{5,7},{6,0},{7,1},{8,10},{9,11},{10,... | collective-permute-start | bytes 737288 | tf_op jit(solution)/shard_map/ppermute | solution.py:320
  149.1 22.2 %collective-permute-start.13 = (bf16[144,3072]{1,0:T(8,128)(2,1)}, bf16[144,3072]{1,0:T(8,128)(2,1)S(1)}, u32[]{:S(2)}, u32[]{:S(2)}) collective-permute-start(bf16[144,3072]{1,0:T(8,128)(2,1)} %get-tuple-element.33.refs_2_), channel_id=1, source_target_pairs={{0,8},{8,0},{16,24},{24,16},{1,9},{9,1},{17,25},{25,17},{2,10},{10... | collective-permute-start | bytes 2654216 | tf_op jit(solution)/shard_map/ppermute | solution.py:311
  149.1 22.3 %copy-start.23 = (bf16[144,1536]{1,0:T(8,128)(2,1)}, bf16[144,1536]{1,0:T(8,128)(2,1)S(1)}, u32[]{:S(2)}) copy-start(bf16[144,1536]{1,0:T(8,128)(2,1)S(1)} %collective-permute-done.23.refs_7_) | copy-start | bytes 1327108
  149.1 22.2 %collective-permute-start.12 = (bf16[144,3072]{1,0:T(8,128)(2,1)S(1)}, bf16[144,3072]{1,0:T(8,128)(2,1)S(1)}, u32[]{:S(2)}, u32[]{:S(2)}) collective-permute-start(bf16[144,3072]{1,0:T(8,128)(2,1)S(1)} %copy-done.18), channel_id=1, source_target_pairs={{0,8},{8,0},{16,24},{24,16},{1,9},{9,1},{17,25},{25,17},{2,10},{10... | collective-permute-start | bytes 2654216 | tf_op jit(solution)/shard_map/ppermute | solution.py:311
  149.7 21.7 %collective-permute-start.25 = (bf16[288,1536]{1,0:T(8,128)(2,1)S(1)}, bf16[288,1536]{1,0:T(8,128)(2,1)S(1)}, u32[]{:S(2)}, u32[]{:S(2)}) collective-permute-start(bf16[288,1536]{1,0:T(8,128)(2,1)S(1)} %copy-done.19), channel_id=1, source_target_pairs={{0,8},{8,0},{16,24},{24,16},{1,9},{9,1},{17,25},{25,17},{2,10},{10... | collective-permute-start | bytes 2654216 | tf_op jit(solution)/shard_map/ppermute | solution.py:311
  156.1 12.8 %collective-permute-start.11 = (bf16[40,3072]{1,0:T(8,128)(2,1)S(1)}, bf16[40,3072]{1,0:T(8,128)(2,1)S(1)}, u32[]{:S(2)}, u32[]{:S(2)}) collective-permute-start(bf16[40,3072]{1,0:T(8,128)(2,1)S(1)} %get-tuple-element.31), channel_id=1, source_target_pairs={{0,4},{1,5},{2,6},{3,7},{4,0},{5,1},{6,2},{7,3},{8,12},{9,13},{10,... | collective-permute-start | bytes 737288 | tf_op jit(solution)/shard_map/ppermute | solution.py:320
  168.9 2.4 %collective-permute-start.24 = (bf16[144,1536]{1,0:T(8,128)(2,1)}, bf16[144,1536]{1,0:T(8,128)(2,1)S(1)}, u32[]{:S(2)}, u32[]{:S(2)}) collective-permute-start(bf16[144,1536]{1,0:T(8,128)(2,1)} %get-tuple-element.38), channel_id=1, source_target_pairs={{0,8},{8,0},{16,24},{24,16},{1,9},{9,1},{17,25},{25,17},{2,10},{10... | collective-permute-start | bytes 1327112 | tf_op jit(solution)/shard_map/ppermute | solution.py:311
  171.3 1.2 copy-start.20
  171.3 1.3 copy-start.21
  171.3 1.6 copy-start.22
  171.3 2.2 %copy-start.17 = (bf16[288,3072]{1,0:T(8,128)(2,1)}, bf16[288,3072]{1,0:T(8,128)(2,1)S(1)}, u32[]{:S(2)}) copy-start(bf16[288,3072]{1,0:T(8,128)(2,1)S(1)} %collective-permute-done.22.refs_5_) | copy-start | bytes 5308420
  (4 other events, 3.3 us)

commit v2 on v1

--- a/solution.py
+++ b/solution.py
@@ -30,40 +30,46 @@
     return lax.dot_general(a, b, (((0,), (0,)), ((), ())), preferred_element_type=FULL)
 
 
-def chosen_slots(ids):
-    count = ids.shape[0]
-    chosen = jnp.max((ids == 0).astype(FULL), axis=1, keepdims=True)
-    chosen = jnp.broadcast_to(chosen, (count, 128))
-    earlier = lax.broadcasted_iota(jnp.int32, (count, count), 1) < lax.broadcasted_iota(
-        jnp.int32, (count, count), 0
+def earlier_count(ids):
+    count = ids.shape[1]
+    chosen = jnp.max((ids == 0).astype(FULL), axis=0, keepdims=True)
+    chosen = jnp.broadcast_to(chosen, (8, count))
+    before = lax.broadcasted_iota(jnp.int32, (count, count), 0) < lax.broadcasted_iota(
+        jnp.int32, (count, count), 1
     )
     slots = jnp.dot(
-        earlier.astype(FULL).astype(HALF), chosen.astype(HALF), preferred_element_type=FULL
+        chosen.astype(HALF), before.astype(FULL).astype(HALF), preferred_element_type=FULL
     )
     return chosen, slots
+
+
+def one_hot(places, chosen, count):
+    row = lax.broadcasted_iota(jnp.int32, (count, places.shape[1]), 0).astype(FULL)
+    return jnp.where(row == places[0:1], jnp.broadcast_to(chosen[0:1], row.shape), 0.0)
 
 
 def pack_kernel(ids, probs, tokens, cotangent, out, pick_rows, pick_cotan, share):
     @pl.when(pl.program_id(0) == 0)
     def _():
-        chosen, slots = chosen_slots(ids[...])
-        column = lax.broadcasted_iota(jnp.int32, slots.shape, 1).astype(FULL)
+        chosen, slots = earlier_count(ids[...])
         late = (slots >= MAIN).astype(FULL)
-        row_place = slots + late * MAIN
-        cotan_place = slots + MAIN + late * REST
-        pick_rows[...] = jnp.where(row_place == column, chosen, 0.0).astype(HALF)
-        pick_cotan[...] = jnp.where(cotan_place == column, chosen, 0.0).astype(HALF)
-        total = jnp.sum(jnp.where(ids[...] == 0, probs[...], 0.0), axis=1, keepdims=True)
-        share[...] = jnp.broadcast_to(total, share.shape)
-
-    scaled = (share[:, 0:1] * cotangent[...].astype(FULL)).astype(HALF)
-    packed = tn_dot(pick_rows[...], tokens[...]) + tn_dot(pick_cotan[...], scaled)
-    out[...] = packed[0 : 2 * CAP].astype(HALF)
+        depth = pick_rows.shape[0]
+        pick_rows[...] = one_hot(slots + late * MAIN, chosen, depth).astype(HALF)
+        picked = one_hot(slots + MAIN + late * REST, chosen, depth)
+        pick_cotan[...] = picked.astype(HALF)
+        total = jnp.sum(jnp.where(ids[...] == 0, probs[...], 0.0), axis=0, keepdims=True)
+        share[...] = jnp.broadcast_to(
+            jnp.sum(picked * total, axis=1, keepdims=True), share.shape
+        )
+
+    cotan = jnp.dot(pick_cotan[...], cotangent[...], preferred_element_type=FULL)
+    rows = jnp.dot(pick_rows[...], tokens[...], preferred_element_type=FULL)
+    out[...] = (rows + share[:, 0:1] * cotan)[0 : 2 * CAP].astype(HALF)
 
 
 def pack(ids, probs, tokens, cotangent):
     count, width = tokens.shape
-    step = 768
+    step = 1536
     return pl.pallas_call(
         pack_kernel,
         grid=(width // step,),
@@ -76,9 +82,9 @@
         out_specs=pl.BlockSpec((2 * CAP, step), lambda j: (0, j)),
         out_shape=shape((2 * CAP, width)),
         scratch_shapes=[
-            pltpu.VMEM((count, 128), HALF),
-            pltpu.VMEM((count, 128), HALF),
-            pltpu.VMEM((count, 128), FULL),
+            pltpu.VMEM((80, count), HALF),
+            pltpu.VMEM((80, count), HALF),
+            pltpu.VMEM((80, 128), FULL),
         ],
         compiler_params=params(32),
         name="pack",
@@ -87,19 +93,17 @@
 
 def unpack_kernel(ids, *refs):
     pieces, out = refs[:-1], refs[-1]
-    chosen, slots = chosen_slots(ids[...])
-    column = lax.broadcasted_iota(jnp.int32, slots.shape, 1).astype(FULL)
-    depth = pieces[0].shape[0]
-    place = jnp.where(slots == column, chosen, 0.0).astype(HALF)[:, 0:depth]
+    chosen, slots = earlier_count(ids[...])
+    place = one_hot(slots, chosen, pieces[0].shape[0]).astype(HALF)
     total = pieces[0][...].astype(FULL)
     for piece in pieces[1:]:
         total = total + piece[...].astype(FULL)
-    out[...] = jnp.dot(place, total.astype(HALF), preferred_element_type=FULL).astype(HALF)
+    out[...] = tn_dot(place, total.astype(HALF)).astype(HALF)
 
 
 def unpack(ids, pieces):
-    count, (depth, width) = ids.shape[0], pieces[0].shape
-    step = 1024
+    count, (depth, width) = ids.shape[1], pieces[0].shape
+    step = 1536
     return pl.pallas_call(
         unpack_kernel,
         grid=(width // step,),
@@ -115,102 +119,131 @@
 TILE = 256
 
 
-def forward_kernel(n, back, place, *refs):
-    blocks, (gate, up, down), refs = refs[:n], refs[n : n + 3], refs[n + 3 :]
-    if back:
-        acts, own, other, send, keep, rows, scaled, total = refs
-    else:
-        acts, own, other, rows, scaled = refs
-    step = pl.program_id(0)
-    width = rows.shape[1]
-    part = own.shape[1] // 2
-
-    @pl.when(step == 0)
-    def _():
-        for i, block in enumerate(blocks):
-            rows[MAIN * i : MAIN * (i + 1), :] = block[0:MAIN, :]
-            scaled[MAIN * i : MAIN * (i + 1), :] = block[MAIN : 2 * MAIN, :]
-        first = lax.broadcasted_iota(jnp.int32, (2 * REST, width), 0) < REST
-        tails = [block[2 * MAIN : 2 * CAP, :].astype(FULL) for block in blocks]
-        row_tails, scaled_tails = [], []
-        for a, b in zip(tails[0::2], tails[1::2]):
-            row_tails.append(jnp.where(first, a, pltpu.roll(b, REST, 0)))
-            scaled_tails.append(jnp.where(first, pltpu.roll(a, REST, 0), b))
-        for i in range(0, n // 2, 2):
-            here = slice(MAIN * n + 8 * i, MAIN * n + 8 * i + 16)
-            rows[here, :] = jnp.concatenate(row_tails[i : i + 2], axis=0).astype(HALF)
-            scaled[here, :] = jnp.concatenate(scaled_tails[i : i + 2], axis=0).astype(HALF)
-        for out, index in ((own, 0), (other, 1)):
-            columns = pl.ds(pl.multiple_of(place[index] * part, part), part)
-            out[:, 0:part] = rows[:, columns]
-            out[:, part : 2 * part] = scaled[:, columns]
-
-    gate_pre = jnp.dot(rows[...], gate[...], preferred_element_type=FULL)
-    up_pre = jnp.dot(rows[...], up[...], preferred_element_type=FULL)
-    hidden_back = nt_dot(scaled[...], down[...])
+def padded_rows(n):
+    return MAIN * n + -(-REST * n // 16) * 16
+
+
+def load_all(pairs, done):
+    copies = [pltpu.make_async_copy(a, b, done.at[i]) for i, (a, b) in enumerate(pairs)]
+    for copy in copies:
+        copy.start()
+    return copies
+
+
+def weight_copies(weights, buffers):
+    pairs = []
+    for j in range(buffers[0].shape[1] // TILE):
+        here = pl.ds(TILE * j, TILE)
+        for k in range(2):
+            pairs.append((weights[k].at[:, here], buffers[k].at[:, here]))
+        pairs.append((weights[2].at[here, :], buffers[2].at[here, :]))
+    return pairs
+
+
+def assemble(blocks, rows, scaled):
+    n, width = len(blocks), rows.shape[1]
+    for i, block in enumerate(blocks):
+        rows[MAIN * i : MAIN * (i + 1), :] = block[0:MAIN, :]
+        scaled[MAIN * i : MAIN * (i + 1), :] = block[MAIN : 2 * MAIN, :]
+    first = lax.broadcasted_iota(jnp.int32, (2 * REST, width), 0) < REST
+    tails = [block[2 * MAIN : 2 * CAP, :].astype(FULL) for block in blocks]
+    row_tails, scaled_tails = [], []
+    for a, b in zip(tails[0::2], tails[1::2]):
+        row_tails.append(jnp.where(first, a, pltpu.roll(b, REST, 0)))
+        scaled_tails.append(jnp.where(first, pltpu.roll(a, REST, 0), b))
+    if len(row_tails) % 2:
+        row_tails.append(jnp.zeros((2 * REST, width), FULL))
+        scaled_tails.append(jnp.zeros((2 * REST, width), FULL))
+    for i in range(0, len(row_tails), 2):
+        here = slice(MAIN * n + 8 * i, MAIN * n + 8 * i + 16)
+        rows[here, :] = jnp.concatenate(row_tails[i : i + 2], axis=0).astype(HALF)
+        scaled[here, :] = jnp.concatenate(scaled_tails[i : i + 2], axis=0).astype(HALF)
+
+
+def activations(rows, scaled, gate, up, down):
+    gate_pre = jnp.dot(rows, gate, preferred_element_type=FULL)
+    up_pre = jnp.dot(rows, up, preferred_element_type=FULL)
+    hidden_back = nt_dot(scaled, down)
     sigma = jax.nn.sigmoid(gate_pre)
     gate_act = gate_pre * sigma
     hidden = (gate_act * up_pre).astype(HALF)
     gate_back = (hidden_back * up_pre * sigma * (1.0 + gate_pre * (1.0 - sigma))).astype(HALF)
     up_back = (hidden_back * gate_act).astype(HALF)
-    acts[:, 0:TILE] = hidden
-    acts[:, TILE : 2 * TILE] = gate_back
-    acts[:, 2 * TILE : 3 * TILE] = up_back
+    return hidden, gate_back, up_back
+
+
+def forward_kernel(n, back, place, *refs):
+    blocks, weights, refs = refs[:n], refs[n : n + 3], refs[n + 3 :]
+    acts, own, other = refs[:3]
+    refs = refs[3:]
     if back:
-        term = nt_dot(gate_back, gate[...]) + nt_dot(up_back, up[...])
-
-        @pl.when(step == 0)
-        def _():
-            total[...] = term
-
-        @pl.when(step > 0)
-        def _():
-            total[...] += term
-
-        @pl.when(step == pl.num_programs(0) - 1)
-        def _():
-            mid, tail, half = MAIN * n // 2, MAIN * n, REST * n // 2
-            keep[0:mid, :] = total[0:mid, :].astype(HALF)
-            send[0:mid, :] = total[mid : 2 * mid, :].astype(HALF)
-            keep[mid : mid + half, :] = total[tail : tail + half, :].astype(HALF)
-            send[mid : mid + half, :] = total[tail + half : tail + 2 * half, :].astype(HALF)
+        send, keep = refs[:2]
+        refs = refs[2:]
+    rows, scaled, held, gate, up, down, block_done, weight_done = refs
+    width, part = rows.shape[1], own.shape[1] // 2
+    block_copies = load_all([(blocks[i], held.at[i]) for i in range(n)], block_done)
+    copies = load_all(weight_copies(weights, (gate, up, down)), weight_done)
+    for copy in block_copies:
+        copy.wait()
+    assemble([held.at[i] for i in range(n)], rows, scaled)
+    for out, index in ((own, 0), (other, 1)):
+        columns = pl.ds(pl.multiple_of(place[index] * part, part), part)
+        out[:, 0:part] = rows[:, columns]
+        out[:, part : 2 * part] = scaled[:, columns]
+    tiles = gate.shape[1] // TILE
+    for j in range(tiles):
+        for copy in copies[3 * j : 3 * j + 3]:
+            copy.wait()
+        here = slice(TILE * j, TILE * (j + 1))
+        found = activations(rows[...], scaled[...], gate[:, here], up[:, here], down[here, :])
+        for k in range(3):
+            at = TILE * (3 * j + k)
+            acts[:, at : at + TILE] = found[k]
+    if back:
+        half = n // 2
+        mid, tail, reach = MAIN * half, MAIN * n, 8 * (-(-half // 2))
+        skip = 8 * half - reach
+        gate_back = [acts[:, TILE * (3 * j + 1) : TILE * (3 * j + 2)] for j in range(tiles)]
+        up_back = [acts[:, TILE * (3 * j + 2) : TILE * (3 * j + 3)] for j in range(tiles)]
+        gate_back, up_back = jnp.concatenate(gate_back, axis=1), jnp.concatenate(up_back, axis=1)
+        for i in range(0, width, 2 * TILE):
+            here = slice(i, i + 2 * TILE)
+            total = nt_dot(gate_back, gate[here, :]) + nt_dot(up_back, up[here, :])
+            keep[0:mid, here] = total[0:mid].astype(HALF)
+            send[0:mid, here] = total[mid : 2 * mid].astype(HALF)
+            keep[mid : mid + reach, here] = total[tail : tail + reach].astype(HALF)
+            send[mid : mid + reach, here] = total[tail + skip : tail + skip + reach].astype(HALF)
 
 
 def forward(blocks, gate, up, down, place, part, back):
     n, (width, hidden) = len(blocks), gate.shape
-    count = CAP * n
-    whole = lambda j, place: (0, 0)
+    count = padded_rows(n)
+    anywhere = pl.BlockSpec(memory_space=pl.ANY)
+    in_vmem = pl.BlockSpec(memory_space=pltpu.VMEM)
     out_shape = [
         shape((count, 3 * hidden)),
         shape((count, 2 * part)),
         shape((count, 2 * part)),
     ]
-    out_specs = [
-        pl.BlockSpec((count, 3 * TILE), lambda j, place: (0, j)),
-        pl.BlockSpec((count, 2 * part), whole),
-        pl.BlockSpec((count, 2 * part), whole),
-    ]
-    scratch = [pltpu.VMEM((count, width), HALF), pltpu.VMEM((count, width), HALF)]
     if back:
-        out_shape += [shape((count // 2, width))] * 2
-        out_specs += [pl.BlockSpec((count // 2, width), whole)] * 2
-        scratch += [pltpu.VMEM((count, width), FULL)]
+        half = n // 2
+        out_shape += [shape((MAIN * half + 8 * (-(-half // 2)), width))] * 2
     matmuls = 5 if back else 3
     return pl.pallas_call(
         functools.partial(forward_kernel, n, back),
-        grid_spec=pltpu.PrefetchScalarGridSpec(
-            num_scalar_prefetch=1,
-            grid=(hidden // TILE,),
-            in_specs=[pl.BlockSpec((2 * CAP, width), whole) for _ in blocks]
-            + [
-                pl.BlockSpec((width, TILE), lambda j, place: (0, j)),
-                pl.BlockSpec((width, TILE), lambda j, place: (0, j)),
-                pl.BlockSpec((TILE, width), lambda j, place: (j, 0)),
-            ],
-            out_specs=out_specs,
-            scratch_shapes=scratch,
-        ),
+        in_specs=[pl.BlockSpec(memory_space=pltpu.SMEM)] + [anywhere] * (n + 3),
+        out_specs=[in_vmem] * len(out_shape),
         out_shape=out_shape,
+        scratch_shapes=[
+            pltpu.VMEM((count, width), HALF),
+            pltpu.VMEM((count, width), HALF),
+            pltpu.VMEM((n, 2 * CAP, width), HALF),
+            pltpu.VMEM((width, hidden), HALF),
+            pltpu.VMEM((width, hidden), HALF),
+            pltpu.VMEM((hidden, width), HALF),
+            pltpu.SemaphoreType.DMA((n,)),
+            pltpu.SemaphoreType.DMA((3 * hidden // TILE,)),
+        ],
         compiler_params=params(56),
         cost_estimate=pl.CostEstimate(
             flops=2 * matmuls * count * width * hidden,
@@ -224,17 +257,13 @@
 def grads_kernel(n, *refs):
     acts, parts, refs = refs[:n], refs[n : 2 * n], refs[2 * n :]
     gate_grad, up_grad, down_grad, act_rows, part_rows, done = refs
-    copies, start = [], 0
+    pairs, start = [], 0
     for i in range(n):
-        count = acts[i].shape[0]
-        for ref, buffer in ((acts[i], act_rows), (parts[i], part_rows)):
-            copy = pltpu.make_async_copy(
-                ref, buffer.at[pl.ds(start, count), :], done.at[len(copies)]
-            )
-            copy.start()
-            copies.append(copy)
-        start += count
-    for copy in copies:
+        here = pl.ds(start, acts[i].shape[0])
+        pairs.append((acts[i], act_rows.at[here, :]))
+        pairs.append((parts[i], part_rows.at[here, :]))
+        start += acts[i].shape[0]
+    for copy in load_all(pairs, done):
         copy.wait()
     part = part_rows.shape[1] // 2
     tiles = act_rows.shape[1] // (3 * TILE)
@@ -282,23 +311,111 @@
     )(*acts, *parts)
 
 
-def merge_kernel(keep, came, *outs):
-    total = keep[...].astype(FULL) + came[...].astype(FULL)
-    mid = MAIN * len(outs)
+def finish_kernel(n, place, *refs):
+    blocks, weights, early, refs = refs[:n], refs[n : n + 3], refs[n + 3 : n + 6], refs[n + 6 :]
+    outs, refs = refs[:3], refs[3:]
+    rows, scaled, held, gate, up, down = refs[:6]
+    sums, block_done, weight_done, sum_done, out_done = refs[6:9], *refs[9:]
+    part = outs[0].shape[0]
+    block_copies = load_all([(blocks[i], held.at[i]) for i in range(n)], block_done)
+    copies = load_all(weight_copies(weights, (gate, up, down)), weight_done)
+    sum_copies = load_all([(early[k], sums[k]) for k in range(3)], sum_done)
+    for copy in block_copies:
+        copy.wait()
+    assemble([held.at[i] for i in range(n)], rows, scaled)
+    columns = pl.ds(pl.multiple_of(place[0] * part, part), part)
+    picked, cotan = rows[:, columns].T, scaled[:, columns]
+    out_copies = []
+    for j in range(gate.shape[1] // TILE):
+        for copy in copies[3 * j : 3 * j + 3]:
+            copy.wait()
+        here = slice(TILE * j, TILE * (j + 1))
+        hidden, gate_back, up_back = activations(
+            rows[...], scaled[...], gate[:, here], up[:, here], down[here, :]
+        )
+        if j == 0:
+            for copy in sum_copies:
+                copy.wait()
+        sums[0][:, here] = (
+            sums[0][:, here].astype(FULL)
+            + jnp.dot(picked, gate_back, preferred_element_type=FULL)
+        ).astype(HALF)
+        sums[1][:, here] = (
+            sums[1][:, here].astype(FULL) + jnp.dot(picked, up_back, preferred_element_type=FULL)
+        ).astype(HALF)
+        sums[2][here, :] = (
+            sums[2][here, :].astype(FULL) + tn_dot(hidden, cotan)
+        ).astype(HALF)
+        there = pl.ds(TILE * j, TILE)
+        views = [
+            (sums[0].at[:, there], outs[0].at[:, there]),
+            (sums[1].at[:, there], outs[1].at[:, there]),
+            (sums[2].at[there, :], outs[2].at[there, :]),
+        ]
+        for source, target in views:
+            copy = pltpu.make_async_copy(source, target, out_done.at[len(out_copies)])
+            copy.start()
+            out_copies.append(copy)
+    for copy in out_copies:
+        copy.wait()
+
+
+def finish(blocks, gate, up, down, place, early):
+    n, (width, hidden) = len(blocks), gate.shape
+    count, part = padded_rows(n), early[0].shape[0]
+    anywhere = pl.BlockSpec(memory_space=pl.ANY)
+    return pl.pallas_call(
+        functools.partial(finish_kernel, n),
+        in_specs=[pl.BlockSpec(memory_space=pltpu.SMEM)] + [anywhere] * (n + 6),
+        out_specs=[anywhere] * 3,
+        out_shape=[shape(e.shape) for e in early],
+        scratch_shapes=[
+            pltpu.VMEM((count, width), HALF),
+            pltpu.VMEM((count, width), HALF),
+            pltpu.VMEM((n, 2 * CAP, width), HALF),
+            pltpu.VMEM((width, hidden), HALF),
+            pltpu.VMEM((width, hidden), HALF),
+            pltpu.VMEM((hidden, width), HALF),
+            *[pltpu.VMEM(e.shape, HALF) for e in early],
+            pltpu.SemaphoreType.DMA((n,)),
+            pltpu.SemaphoreType.DMA((3 * hidden // TILE,)),
+            pltpu.SemaphoreType.DMA((3,)),
+            pltpu.SemaphoreType.DMA((3 * hidden // TILE,)),
+        ],
+        compiler_params=params(56),
+        cost_estimate=pl.CostEstimate(
+            flops=6 * count * (width + part) * hidden,
+            bytes_accessed=6 * width * hidden + 2 * n * CAP * width + 12 * part * hidden,
+            transcendentals=count * hidden,
+        ),
+        name="finish",
+    )(place, *blocks, gate, up, down, *early)
+
+
+def merge_kernel(n, keep, came, *outs):
+    mid = MAIN * n
+    kept, other = keep[mid:, :].astype(FULL), came[mid:, :].astype(FULL)
+    if n % 2:
+        other = pltpu.roll(other, other.shape[0] - REST, 0)
+    tails = kept + other
     for i, out in enumerate(outs):
-        out[0:MAIN, :] = total[MAIN * i : MAIN * (i + 1)].astype(HALF)
-        pair = total[mid + 8 * (i // 2) : mid + 8 * (i // 2) + 8]
+        here = slice(MAIN * i, MAIN * (i + 1))
+        out[0:MAIN, :] = (keep[here, :].astype(FULL) + came[here, :].astype(FULL)).astype(HALF)
+        pair = tails[8 * (i // 2) : 8 * (i // 2) + 8]
         out[MAIN : MAIN + 8, :] = (pair if i % 2 == 0 else pltpu.roll(pair, REST, 0)).astype(HALF)
 
 
-def merge(keep, came):
-    n, width = keep.shape[0] // CAP, keep.shape[1]
+def merge(n, keep, came):
     return pl.pallas_call(
-        merge_kernel,
-        out_shape=[shape((MAIN + 8, width))] * n,
+        functools.partial(merge_kernel, n),
+        out_shape=[shape((MAIN + 8, keep.shape[1]))] * n,
         compiler_params=params(32),
         name="merge",
     )(keep, came)
+
+
+def after(value, *others):
+    return lax.optimization_barrier((value, *others))[0]
 
 
 def per_device(tokens, cotangent, route_ids, route_probs, gate_weight, up_weight, down_weight):
@@ -324,29 +441,41 @@
     part = tokens.shape[1] // n_dp
     p = lax.axis_index("dp")
     place = jnp.stack([p, p + 1 - 2 * (p % 2)]).astype(jnp.int32)
-
-    block = pack(route_ids, route_probs, tokens, cotangent)
-    mine = [block, over_z(block, 1), over_z(block, -1), over_z(block, 2)]
-    beside = [over_x(b) for b in mine]
-    far_mine = [over_y(b) for b in mine]
-    far_beside = [over_x(far_mine[0])] + [over_y(b) for b in beside[1:]]
-
-    weights = (gate_weight, up_weight, down_weight)
-    run = functools.partial(forward, gate=gate_weight, up=up_weight, down=down_weight, place=place, part=part)
-    results, pieces = [], []
-    for lo in (0, 2):
-        out = run(mine[lo : lo + 2] + beside[lo : lo + 2], back=True)
-        results.append(out[:3])
-        pieces += merge(out[4], over_x(out[3]))
-    results.append(run(far_mine + far_beside, back=False))
+    ids, probs = route_ids.T, route_probs.T
+    weights = dict(gate=gate_weight, up=up_weight, down=down_weight)
+
+    b0 = pack(ids, probs, tokens, cotangent)
+    z1 = over_z(b0, 1)
+    x0, y0 = over_x(b0), over_y(b0)
+    x1, y1 = over_x(z1), over_y(z1)
+    z3 = over_z(after(b0, z1), -1)
+    yx0 = over_x(y0)
+    z2 = over_z(after(z1, z3), 1)
+    x3, y3 = over_x(z3), over_y(z3)
+    yx1 = over_y(x1)
+    x2, y2 = over_x(z2), over_y(z2)
+    yx3, yx2 = over_y(x3), over_y(x2)
+
+    acts, parts = [], []
+
+    def share(act, own, other):
+        acts.extend([act, over_core(act)])
+        parts.extend([own, over_core(other)])
+
+    run = functools.partial(forward, place=place, part=part, **weights)
+    *first, send, keep = run([b0, z1, z3, x0, x1, x3], back=True)
+    pieces = merge(3, keep, over_x(send))
+    share(*first)
+    *second, send, keep = run([z2, x2], back=True)
+    pieces += merge(1, keep, over_x(send))
+    share(*second)
     returned = [pieces[0], over_z(pieces[1], -1), over_z(pieces[2], 1), over_z(pieces[3], 2)]
-
-    acts, parts = [], []
-    for act, own, other in results:
-        acts += [act, over_core(act)]
-        parts += [own, over_core(other)]
-    gate_grad, up_grad, down_grad = grads(acts, parts, part, gate_weight.shape[1])
-    return unpack(route_ids, returned), gate_grad, up_grad, down_grad
+    share(*run([y0, yx0, y1, yx1], back=False))
+    early = grads(acts, parts, part, gate_weight.shape[1])
+    last = [y3, y2, yx3, yx2]
+    last = last + [over_core(b) for b in last]
+    gate_grad, up_grad, down_grad = finish(last, place=place, early=early, **weights)
+    return unpack(ids, returned), gate_grad, up_grad, down_grad
 
 
 def pick_rows(placer, values):

time: 186 us -> 185 us (level); the launches traced: 185 us -> 182 us
  Pallas kernels: 65.1 us -> 84.1 us
  waiting for transfers between devices: 71.4 us -> 59.9 us
  starting transfers between devices: 38.6 us -> 28.2 us
    ppermute x7, waiting for transfers between devices: 8.58 us -> 33.2 us  [over_x(): return lax.ppermute(v, 'expert', x_pairs)]
    pallas_call x5 -> x6, Pallas kernels: 49.5 us -> 71.7 us  [the longest x3 48.4 us: forward(): pl.pallas_call(functools.partial(forward_kernel, n, back), in_specs=[pl.B...]
    ppermute x7, waiting for transfers between devices: 24.9 us -> 6.25 us  [over_y(): return lax.ppermute(v, 'dp', y_pairs)]
    ppermute x6, waiting for transfers between devices: 37.8 us -> 20.4 us  [over_z(): lax.ppermute(v, 'expert', [(i, (i + 2 * by) % n_expert) for i in range(n_...]
    ppermute x6, starting transfers between devices: 21.1 us -> 9.11 us  [over_z(): lax.ppermute(v, 'expert', [(i, (i + 2 * by) % n_expert) for i in range(n_...]
    pallas_call x1, Pallas kernels: 11.6 us -> 9.71 us  [grads(): pl.pallas_call(functools.partial(grads_kernel, n), in_specs=[anywhere] *...]
    unnamed x54 -> x62, local copies, waits for them, and re-layouts: 8.49 us -> 7.64 us
  transfers between devices with their start and end apart: 26 -> 30, of which waited for: 11 -> 8; matrix products, arithmetic and copies ran while one was open for 0% -> 0% of each run, Pallas kernels for 28% -> 33%
where the time goes in v2:
time: 185 us; the launch traced here: 182 us
  Pallas kernels  84.1 us (45%)
  waiting for transfers between devices  59.9 us (32%)
  starting transfers between devices  28.2 us (15%)
  local copies, waits for them, and re-layouts  7.64 us (4%)
    pallas_call x3, Pallas kernels, forward(): pl.pallas_call(functools.partial(forward_kernel, n, back), in_specs=[pl.B...  48.4 us
    ppermute x7, waiting for transfers between devices, over_x(): return lax.ppermute(v, 'expert', x_pairs)  33.2 us
    pallas_call x1, Pallas kernels, finish(): pl.pallas_call(functools.partial(finish_kernel, n), in_specs=[pl.BlockSpe...  23 us
    ppermute x6, waiting for transfers between devices, over_z(): lax.ppermute(v, 'expert', [(i, (i + 2 * by) % n_expert) for i in range(n_...  20.4 us
    pallas_call x1, Pallas kernels, grads(): pl.pallas_call(functools.partial(grads_kernel, n), in_specs=[anywhere] *...  9.71 us
    ppermute x6, starting transfers between devices, over_z(): lax.ppermute(v, 'expert', [(i, (i + 2 * by) % n_expert) for i in range(n_...  9.11 us
    ppermute x7, starting transfers between devices, over_y(): return lax.ppermute(v, 'dp', y_pairs)  9.04 us
    ppermute x7, starting transfers between devices, over_x(): return lax.ppermute(v, 'expert', x_pairs)  7.89 us
  transfers between devices with their start and end apart: 30, of which 8 were waited for; matrix products, arithmetic and copies ran while one was open for 0% of the time, Pallas kernels for 33%

profile of v2, /device:TPU:0, one launch (start us, length us, event | category | flops | bytes accessed | tf_op | source)
XLA Modules:
  0.0 181.5 jit_solution(9853211723397872605)
XLA Ops:
  0.6 1.1 copy-done
  1.8 1.1 copy-done.1
  2.9 0.7 copy-done.5
  3.6 0.7 copy-done.7
  4.3 1.0 pack.1.refs_0_
  5.3 3.1 %collective-permute-start = (bf16[72,3072]{1,0:T(8,128)(2,1)S(1)}, bf16[72,3072]{1,0:T(8,128)(2,1)S(1)}, u32[]{:S(2)}, u32[]{:S(2)}) collective-permute-start(bf16[72,3072]{1,0:T(8,128)(2,1)S(1)} %pack.1.refs_0_), channel_id=1, source_target_pairs={{0,2},{1,3},{2,4},{3,5},{4,6},{5,7},{6,0},{7,1},{8,10},{9,11},{10,... | collective-permute-start | bytes 1327112 | tf_op jit(solution)/shard_map/ppermute | solution.py:437
  8.3 1.5 collective-permute-start.22
  9.8 10.7 %collective-permute-done.refs_1_ = bf16[72,3072]{1,0:T(8,128)(2,1)S(1)} collective-permute-done((bf16[72,3072]{1,0:T(8,128)(2,1)S(1)}, bf16[72,3072]{1,0:T(8,128)(2,1)S(1)}, u32[]{:S(2)}, u32[]{:S(2)}) %collective-permute-start) | collective-permute-done | bytes 442400 | tf_op jit(solution)/shard_map/ppermute | solution.py:437
  20.5 1.5 collective-permute-start.3
  22.0 1.7 collective-permute-start.1
  23.8 1.5 collective-permute-start.24
  25.3 0.5 collective-permute-start.23
  25.8 7.9 %collective-permute-done.3.refs_4_ = bf16[72,3072]{1,0:T(8,128)(2,1)} collective-permute-done((bf16[72,3072]{1,0:T(8,128)(2,1)S(1)}, bf16[72,3072]{1,0:T(8,128)(2,1)}, u32[]{:S(2)}, u32[]{:S(2)}) %collective-permute-start.3) | collective-permute-done | bytes 442400 | tf_op jit(solution)/shard_map/ppermute | solution.py:434
  33.7 1.5 collective-permute-start.25
  35.3 1.5 collective-permute-start.2
  36.8 0.5 collective-permute-start.4
  37.3 0.6 pad_add_fusion.place
  37.9 5.2 %collective-permute-done.23.refs_1_ = bf16[72,3072]{1,0:T(8,128)(2,1)S(1)} collective-permute-done((bf16[72,3072]{1,0:T(8,128)(2,1)S(1)}, bf16[72,3072]{1,0:T(8,128)(2,1)S(1)}, u32[]{:S(2)}, u32[]{:S(2)}) %collective-permute-start.23) | collective-permute-done | bytes 442400 | tf_op jit(solution)/shard_map/ppermute | solution.py:434
  43.1 1.5 collective-permute-start.12
  44.8 0.8 copy-done.17
  45.6 13.0 %forward.1 = (bf16[144,3072]{1,0:T(8,128)(2,1)}, bf16[144,1536]{1,0:T(8,128)(2,1)}, bf16[144,1536]{1,0:T(8,128)(2,1)}) custom-call(s32[2]{0:T(128)} %pad_add_fusion.place, bf16[72,3072]{1,0:T(8,128)(2,1)} %copy-done.14, bf16[72,3072]{1,0:T(8,128)(2,1)} %copy-done.16, bf16[72,3072]{1,0:T(8,128)(2,1)} %copy-done.15, bf16[72,3072]{1,0:T(8,128)(2,1)} %copy-done.17, ...), custom_call_target="tpu_custom_call" | custom-call | flops 2717908992 | bytes 21086208 | tf_op jit(solution)/shard_map/forward/pallas_call | solution.py:232
  58.8 1.4 collective-permute-start.9
  60.2 0.8 collective-permute-start.13
  61.0 19.2 %forward_back.2 = (bf16[224,3072]{1,0:T(8,128)(2,1)}, bf16[224,1536]{1,0:T(8,128)(2,1)}, bf16[224,1536]{1,0:T(8,128)(2,1)}, bf16[112,3072]{1,0:T(8,128)(2,1)}, bf16[112,3072]{1,0:T(8,128)(2,1)}) custom-call(s32[2]{0:T(128)} %pad_add_fusion.place, bf16[72,3072]{1,0:T(8,128)(2,1)} %copy-done.3, bf16[72,3072]{1,0:T(8,128)(2,1)} %copy-done.29, ...), custom_call_target="tpu_custom_call" | custom-call | flops 7046430720 | bytes 22315008 | tf_op jit(solution)/shard_map/forward_back/pallas_call | solution.py:232
  80.2 0.2 collective-permute-start.20
  80.4 1.2 collective-permute-start.14
  81.6 16.2 %forward_back.3 = (bf16[80,3072]{1,0:T(8,128)(2,1)}, bf16[80,1536]{1,0:T(8,128)(2,1)}, bf16[80,1536]{1,0:T(8,128)(2,1)}, bf16[40,3072]{1,0:T(8,128)(2,1)}, bf16[40,3072]{1,0:T(8,128)(2,1)}) custom-call(s32[2]{0:T(128)} %pad_add_fusion.place, bf16[72,3072]{1,0:T(8,128)(2,1)} %copy-done.11, bf16[72,3072]{1,0:T(8,128)(2,1)} %copy-done.13, ...), custom_call_target="tpu_custom_call" | custom-call | flops 2516582400 | bytes 20103168 | tf_op jit(solution)/shard_map/forward_back/pallas_call | solution.py:232
  97.8 0.2 collective-permute-start.28
  98.0 1.8 collective-permute-start.5
  99.9 0.5 collective-permute-start.27
  100.4 0.7 collective-permute-start.10
  101.1 20.1 %collective-permute-done.10.came = bf16[40,3072]{1,0:T(8,128)(2,1)S(1)} collective-permute-done((bf16[40,3072]{1,0:T(8,128)(2,1)}, bf16[40,3072]{1,0:T(8,128)(2,1)S(1)}, u32[]{:S(2)}, u32[]{:S(2)}) %collective-permute-start.10) | collective-permute-done | bytes 245792 | tf_op jit(solution)/shard_map/ppermute | solution.py:434
  121.2 1.0 collective-permute-start.15
  122.2 0.9 copy-done.4
  123.2 0.2 merge.2
  123.4 0.5 collective-permute-start.11
  124.0 3.0 %collective-permute-start.6 = (bf16[40,3072]{1,0:T(8,128)(2,1)S(1)}, bf16[40,3072]{1,0:T(8,128)(2,1)S(1)}, u32[]{:S(2)}, u32[]{:S(2)}) collective-permute-start(bf16[40,3072]{1,0:T(8,128)(2,1)S(1)} %get-tuple-element.32), channel_id=1, source_target_pairs={{0,6},{1,7},{2,0},{3,1},{4,2},{5,3},{6,4},{7,5},{8,14},{9,15},{10,... | collective-permute-start | bytes 737288 | tf_op jit(solution)/shard_map/ppermute | solution.py:437
  127.0 6.1 %collective-permute-done.15.refs_3_ = bf16[72,3072]{1,0:T(8,128)(2,1)S(1)} collective-permute-done((bf16[72,3072]{1,0:T(8,128)(2,1)}, bf16[72,3072]{1,0:T(8,128)(2,1)S(1)}, u32[]{:S(2)}, u32[]{:S(2)}) %collective-permute-start.15) | collective-permute-done | bytes 442400 | tf_op jit(solution)/shard_map/ppermute | solution.py:431
  133.0 0.8 collective-permute-start.7
  133.8 4.8 %collective-permute-done.11.refs_3_ = bf16[40,3072]{1,0:T(8,128)(2,1)S(1)} collective-permute-done((bf16[40,3072]{1,0:T(8,128)(2,1)S(1)}, bf16[40,3072]{1,0:T(8,128)(2,1)S(1)}, u32[]{:S(2)}, u32[]{:S(2)}) %collective-permute-start.11) | collective-permute-done | bytes 245792 | tf_op jit(solution)/shard_map/ppermute | solution.py:437
  138.6 0.5 collective-permute-start.17
  139.1 4.9 %collective-permute-done.7.refs_2_ = bf16[40,3072]{1,0:T(8,128)(2,1)S(1)} collective-permute-done((bf16[40,3072]{1,0:T(8,128)(2,1)S(1)}, bf16[40,3072]{1,0:T(8,128)(2,1)S(1)}, u32[]{:S(2)}, u32[]{:S(2)}) %collective-permute-start.7) | collective-permute-done | bytes 245792 | tf_op jit(solution)/shard_map/ppermute | solution.py:437
  144.0 0.5 collective-permute-start.19
  144.5 1.7 unpack.1
  146.3 1.0 copy-done.22
  147.3 9.7 %grads.1 = (bf16[768,1024]{1,0:T(8,128)(2,1)}, bf16[768,1024]{1,0:T(8,128)(2,1)}, bf16[1024,768]{1,0:T(8,128)(2,1)}) custom-call(bf16[224,3072]{1,0:T(8,128)(2,1)} %get-tuple-element.37.refs_0_, bf16[224,3072]{1,0:T(8,128)(2,1)} %copy-done.22, bf16[80,3072]{1,0:T(8,128)(2,1)} %get-tuple-element.38.refs_2_, bf16[80,3072]{1,0:T(8,128)(2,1)} %copy-done.27, ...), custom_call_target="tpu_custom_call" | custom-call | flops 4227858432 | bytes 12976128 | tf_op jit(solution)/shard_map/grads/pallas_call | solution.py:294
  157.2 0.7 copy-done.18
  158.3 23.0 %finish.1 = (bf16[768,1024]{1,0:T(8,128)(2,1)}, bf16[768,1024]{1,0:T(8,128)(2,1)}, bf16[1024,768]{1,0:T(8,128)(2,1)}) custom-call(s32[2]{0:T(128)} %pad_add_fusion.place, bf16[72,3072]{1,0:T(8,128)(2,1)} %copy-done.8, bf16[72,3072]{1,0:T(8,128)(2,1)} %copy-done.9, bf16[72,3072]{1,0:T(8,128)(2,1)} %copy-done.10, bf16[72,3072]{1,0:T(8,128)(2,1)} %copy-done.12, ...), custom_call_target="tpu_custom_call" | custom-call | flops 6794772480 | bytes 30081024 | tf_op jit(solution)/shard_map/finish/pallas_call | solution.py:367
  (84 shorter events, 1.0 us)
Async XLA Ops:
  5.2 53.4 %copy-start.3 = (bf16[72,3072]{1,0:T(8,128)(2,1)}, bf16[72,3072]{1,0:T(8,128)(2,1)S(1)}, u32[]{:S(2)}) copy-start(bf16[72,3072]{1,0:T(8,128)(2,1)S(1)} %pack.1.refs_0_) | copy-start | bytes 1327108
  5.3 15.3 %collective-permute-start = (bf16[72,3072]{1,0:T(8,128)(2,1)S(1)}, bf16[72,3072]{1,0:T(8,128)(2,1)S(1)}, u32[]{:S(2)}, u32[]{:S(2)}) collective-permute-start(bf16[72,3072]{1,0:T(8,128)(2,1)S(1)} %pack.1.refs_0_), channel_id=1, source_target_pairs={{0,2},{1,3},{2,4},{3,5},{4,6},{5,7},{6,0},{7,1},{8,10},{9,11},{10,... | collective-permute-start | bytes 1327112 | tf_op jit(solution)/shard_map/ppermute | solution.py:437
  8.3 16.9 %collective-permute-start.22 = (bf16[72,3072]{1,0:T(8,128)(2,1)S(1)}, bf16[72,3072]{1,0:T(8,128)(2,1)S(1)}, u32[]{:S(2)}, u32[]{:S(2)}) collective-permute-start(bf16[72,3072]{1,0:T(8,128)(2,1)S(1)} %pack.1.refs_0_), channel_id=1, source_target_pairs={{0,16},{8,24},{16,0},{24,8},{1,17},{9,25},{17,1},{25,9},{2,18},{10... | collective-permute-start | bytes 1327112 | tf_op jit(solution)/shard_map/ppermute | solution.py:431
  20.5 38.1 %copy-start.29 = (bf16[72,3072]{1,0:T(8,128)(2,1)}, bf16[72,3072]{1,0:T(8,128)(2,1)S(1)}, u32[]{:S(2)}) copy-start(bf16[72,3072]{1,0:T(8,128)(2,1)S(1)} %collective-permute-done.refs_1_) | copy-start | bytes 1327108
  20.5 13.2 %collective-permute-start.3 = (bf16[72,3072]{1,0:T(8,128)(2,1)S(1)}, bf16[72,3072]{1,0:T(8,128)(2,1)}, u32[]{:S(2)}, u32[]{:S(2)}) collective-permute-start(bf16[72,3072]{1,0:T(8,128)(2,1)S(1)} %collective-permute-done.refs_1_), channel_id=1, source_target_pairs={{0,1},{1,0},{2,3},{3,2},{4,5},{5,4},{6,7},{7,6},{8,9},{9,8},{10,11... | collective-permute-start | bytes 1327112 | tf_op jit(solution)/shard_map/ppermute | solution.py:434
  22.0 13.2 %collective-permute-start.1 = (bf16[72,3072]{1,0:T(8,128)(2,1)S(1)}, bf16[72,3072]{1,0:T(8,128)(2,1)}, u32[]{:S(2)}, u32[]{:S(2)}) collective-permute-start(bf16[72,3072]{1,0:T(8,128)(2,1)S(1)} %pack.1.refs_0_), channel_id=1, source_target_pairs={{0,6},{1,7},{2,0},{3,1},{4,2},{5,3},{6,4},{7,5},{8,14},{9,15},{10,... | collective-permute-start | bytes 1327112 | tf_op jit(solution)/shard_map/ppermute | solution.py:437
  23.8 13.0 %collective-permute-start.24 = (bf16[72,3072]{1,0:T(8,128)(2,1)S(1)}, bf16[72,3072]{1,0:T(8,128)(2,1)S(1)}, u32[]{:S(2)}, u32[]{:S(2)}) collective-permute-start(bf16[72,3072]{1,0:T(8,128)(2,1)S(1)} %collective-permute-done.refs_1_), channel_id=1, source_target_pairs={{0,16},{8,24},{16,0},{24,8},{1,17},{9,25},{17,1},{25,9},{2,18},{10... | collective-permute-start | bytes 1327112 | tf_op jit(solution)/shard_map/ppermute | solution.py:431
  25.3 19.5 %copy-start.14 = (bf16[72,3072]{1,0:T(8,128)(2,1)}, bf16[72,3072]{1,0:T(8,128)(2,1)S(1)}, u32[]{:S(2)}) copy-start(bf16[72,3072]{1,0:T(8,128)(2,1)S(1)} %collective-permute-done.22.refs_0_) | copy-start | bytes 1327108
  25.3 17.8 %collective-permute-start.23 = (bf16[72,3072]{1,0:T(8,128)(2,1)S(1)}, bf16[72,3072]{1,0:T(8,128)(2,1)S(1)}, u32[]{:S(2)}, u32[]{:S(2)}) collective-permute-start(bf16[72,3072]{1,0:T(8,128)(2,1)S(1)} %collective-permute-done.22.refs_0_), channel_id=1, source_target_pairs={{0,1},{1,0},{2,3},{3,2},{4,5},{5,4},{6,7},{7,6},{8,9},{9,8},{10,11... | collective-permute-start | bytes 1327112 | tf_op jit(solution)/shard_map/ppermute | solution.py:434
  33.7 11.1 %collective-permute-start.25 = (bf16[72,3072]{1,0:T(8,128)(2,1)}, bf16[72,3072]{1,0:T(8,128)(2,1)S(1)}, u32[]{:S(2)}, u32[]{:S(2)}) collective-permute-start(bf16[72,3072]{1,0:T(8,128)(2,1)} %collective-permute-done.3.refs_4_), channel_id=1, source_target_pairs={{0,16},{8,24},{16,0},{24,8},{1,17},{9,25},{17,1},{25,9},{2,18},{10... | collective-permute-start | bytes 1327112 | tf_op jit(solution)/shard_map/ppermute | solution.py:431
  35.3 23.5 %collective-permute-start.8 = (bf16[72,3072]{1,0:T(8,128)(2,1)S(1)}, bf16[72,3072]{1,0:T(8,128)(2,1)S(1)}, u32[]{:S(2)}, u32[]{:S(2)}) collective-permute-start(bf16[72,3072]{1,0:T(8,128)(2,1)S(1)} %collective-permute-done.refs_1_), channel_id=1, source_target_pairs={{0,2},{1,3},{2,4},{3,5},{4,6},{5,7},{6,0},{7,1},{8,10},{9,11},{10,... | collective-permute-start | bytes 1327112 | tf_op jit(solution)/shard_map/ppermute | solution.py:437
  35.3 24.9 %collective-permute-start.2 = (bf16[72,3072]{1,0:T(8,128)(2,1)S(1)}, bf16[72,3072]{1,0:T(8,128)(2,1)}, u32[]{:S(2)}, u32[]{:S(2)}) collective-permute-start(bf16[72,3072]{1,0:T(8,128)(2,1)S(1)} %pack.1.refs_0_), channel_id=1, source_target_pairs={{0,1},{1,0},{2,3},{3,2},{4,5},{5,4},{6,7},{7,6},{8,9},{9,8},{10,11... | collective-permute-start | bytes 1327112 | tf_op jit(solution)/shard_map/ppermute | solution.py:434
  36.8 8.1 %copy-start.15 = (bf16[72,3072]{1,0:T(8,128)(2,1)}, bf16[72,3072]{1,0:T(8,128)(2,1)S(1)}, u32[]{:S(2)}) copy-start(bf16[72,3072]{1,0:T(8,128)(2,1)S(1)} %collective-permute-done.24.refs_2_) | copy-start | bytes 1327108
  36.8 24.2 %collective-permute-start.4 = (bf16[72,3072]{1,0:T(8,128)(2,1)}, bf16[72,3072]{1,0:T(8,128)(2,1)}, u32[]{:S(2)}, u32[]{:S(2)}) collective-permute-start(bf16[72,3072]{1,0:T(8,128)(2,1)} %collective-permute-done.1.refs_2_), channel_id=1, source_target_pairs={{0,1},{1,0},{2,3},{3,2},{4,5},{5,4},{6,7},{7,6},{8,9},{9,8},{10,11... | collective-permute-start | bytes 1327112 | tf_op jit(solution)/shard_map/ppermute | solution.py:434
  43.1 54.7 %collective-permute-start.12 = (bf16[72,3072]{1,0:T(8,128)(2,1)}, bf16[72,3072]{1,0:T(8,128)(2,1)S(1)}, u32[]{:S(2)}, u32[]{:S(2)}) collective-permute-start(bf16[72,3072]{1,0:T(8,128)(2,1)} %collective-permute-done.1.refs_2_), channel_id=1, source_target_pairs={{0,16},{8,24},{16,0},{24,8},{1,17},{9,25},{17,1},{25,9},{2,18},{10... | collective-permute-start | bytes 1327112 | tf_op jit(solution)/shard_map/ppermute | solution.py:431
  58.7 39.4 %collective-permute-start.29 = (bf16[144,1536]{1,0:T(8,128)(2,1)}, bf16[144,1536]{1,0:T(8,128)(2,1)S(1)}, u32[]{:S(2)}, u32[]{:S(2)}) collective-permute-start(bf16[144,1536]{1,0:T(8,128)(2,1)} %get-tuple-element.45), channel_id=1, source_target_pairs={{0,8},{8,0},{16,24},{24,16},{1,9},{9,1},{17,25},{25,17},{2,10},{10... | collective-permute-start | bytes 1327112 | tf_op jit(solution)/shard_map/ppermute | solution.py:428
  58.7 21.4 %copy-start.11 = (bf16[72,3072]{1,0:T(8,128)(2,1)}, bf16[72,3072]{1,0:T(8,128)(2,1)S(1)}, u32[]{:S(2)}) copy-start(bf16[72,3072]{1,0:T(8,128)(2,1)S(1)} %collective-permute-done.8.refs_0_) | copy-start | bytes 1327108
  58.8 21.7 %collective-permute-start.9 = (bf16[72,3072]{1,0:T(8,128)(2,1)S(1)}, bf16[72,3072]{1,0:T(8,128)(2,1)S(1)}, u32[]{:S(2)}, u32[]{:S(2)}) collective-permute-start(bf16[72,3072]{1,0:T(8,128)(2,1)S(1)} %collective-permute-done.8.refs_0_), channel_id=1, source_target_pairs={{0,1},{1,0},{2,3},{3,2},{4,5},{5,4},{6,7},{7,6},{8,9},{9,8},{10,11... | collective-permute-start | bytes 1327112 | tf_op jit(solution)/shard_map/ppermute | solution.py:434
  60.2 39.6 %collective-permute-start.13 = (bf16[72,3072]{1,0:T(8,128)(2,1)S(1)}, bf16[72,3072]{1,0:T(8,128)(2,1)S(1)}, u32[]{:S(2)}, u32[]{:S(2)}) collective-permute-start(bf16[72,3072]{1,0:T(8,128)(2,1)S(1)} %collective-permute-done.8.refs_0_), channel_id=1, source_target_pairs={{0,16},{8,24},{16,0},{24,8},{1,17},{9,25},{17,1},{25,9},{2,18},{10... | collective-permute-start | bytes 1327112 | tf_op jit(solution)/shard_map/ppermute | solution.py:431
  80.2 19.6 %copy-start.23 = (bf16[144,3072]{1,0:T(8,128)(2,1)S(1)}, bf16[144,3072]{1,0:T(8,128)(2,1)}, u32[]{:S(2)}) copy-start(bf16[144,3072]{1,0:T(8,128)(2,1)} %get-tuple-element.39.refs_4_) | copy-start | bytes 2654212
  80.2 19.7 %copy-start.26 = (bf16[224,1536]{1,0:T(8,128)(2,1)S(1)}, bf16[224,1536]{1,0:T(8,128)(2,1)}, u32[]{:S(2)}) copy-start(bf16[224,1536]{1,0:T(8,128)(2,1)} %get-tuple-element.41) | copy-start | bytes 2064388
  80.2 43.0 %copy-start.2 = (bf16[112,3072]{1,0:T(8,128)(2,1)S(1)}, bf16[112,3072]{1,0:T(8,128)(2,1)}, u32[]{:S(2)}) copy-start(bf16[112,3072]{1,0:T(8,128)(2,1)} %get-tuple-element.29.keep) | copy-start | bytes 2064388
  80.2 66.0 %collective-permute-start.20 = (bf16[224,3072]{1,0:T(8,128)(2,1)}, bf16[224,3072]{1,0:T(8,128)(2,1)S(1)}, u32[]{:S(2)}, u32[]{:S(2)}) collective-permute-start(bf16[224,3072]{1,0:T(8,128)(2,1)} %get-tuple-element.37.refs_0_), channel_id=1, source_target_pairs={{0,8},{8,0},{16,24},{24,16},{1,9},{9,1},{17,25},{25,17},{2,10},{10... | collective-permute-start | bytes 4128776 | tf_op jit(solution)/shard_map/ppermute | solution.py:428
  80.4 19.4 %collective-permute-start.14 = (bf16[72,3072]{1,0:T(8,128)(2,1)}, bf16[72,3072]{1,0:T(8,128)(2,1)S(1)}, u32[]{:S(2)}, u32[]{:S(2)}) collective-permute-start(bf16[72,3072]{1,0:T(8,128)(2,1)} %collective-permute-done.4.refs_5_), channel_id=1, source_target_pairs={{0,16},{8,24},{16,0},{24,8},{1,17},{9,25},{17,1},{25,9},{2,18},{10... | collective-permute-start | bytes 1327112 | tf_op jit(solution)/shard_map/ppermute | solution.py:431
  97.8 46.7 %copy-start.6 = (s32[128,2]{0,1:T(2,128)S(1)}, s32[128,2]{0,1:T(2,128)}, u32[]{:S(2)}) copy-start(s32[128,2]{0,1:T(2,128)} %param.9) | copy-start | bytes 3076
  97.8 48.4 %copy-start.8 = (bf16[72,3072]{1,0:T(8,128)(2,1)}, bf16[72,3072]{1,0:T(8,128)(2,1)S(1)}, u32[]{:S(2)}) copy-start(bf16[72,3072]{1,0:T(8,128)(2,1)S(1)} %collective-permute-done.12.refs_0_) | copy-start | bytes 1327108
  97.8 2.6 %collective-permute-start.28 = (bf16[80,1536]{1,0:T(8,128)(2,1)}, bf16[80,1536]{1,0:T(8,128)(2,1)S(1)}, u32[]{:S(2)}, u32[]{:S(2)}) collective-permute-start(bf16[80,1536]{1,0:T(8,128)(2,1)} %get-tuple-element.43), channel_id=1, source_target_pairs={{0,8},{8,0},{16,24},{24,16},{1,9},{9,1},{17,25},{25,17},{2,10},{10... | collective-permute-start | bytes 737288 | tf_op jit(solution)/shard_map/ppermute | solution.py:428
  98.0 1.8 copy-start.28
  98.0 24.2 %collective-permute-start.5 = (bf16[112,3072]{1,0:T(8,128)(2,1)}, bf16[112,3072]{1,0:T(8,128)(2,1)S(1)}, u32[]{:S(2)}, u32[]{:S(2)}) collective-permute-start(bf16[112,3072]{1,0:T(8,128)(2,1)} %get-tuple-element.30), channel_id=1, source_target_pairs={{0,1},{1,0},{2,3},{3,2},{4,5},{5,4},{6,7},{7,6},{8,9},{9,8},{10,11... | collective-permute-start | bytes 2064392 | tf_op jit(solution)/shard_map/ppermute | solution.py:434
  99.8 46.5 %copy-start.9 = (bf16[72,3072]{1,0:T(8,128)(2,1)}, bf16[72,3072]{1,0:T(8,128)(2,1)S(1)}, u32[]{:S(2)}) copy-start(bf16[72,3072]{1,0:T(8,128)(2,1)S(1)} %collective-permute-done.13.refs_1_) | copy-start | bytes 1327108
  99.8 24.2 %collective-permute-start.26 = (bf16[144,3072]{1,0:T(8,128)(2,1)S(1)}, bf16[144,3072]{1,0:T(8,128)(2,1)S(1)}, u32[]{:S(2)}, u32[]{:S(2)}) collective-permute-start(bf16[144,3072]{1,0:T(8,128)(2,1)S(1)} %copy-done.23), channel_id=1, source_target_pairs={{0,8},{8,0},{16,24},{24,16},{1,9},{9,1},{17,25},{25,17},{2,10},{10... | collective-permute-start | bytes 2654216 | tf_op jit(solution)/shard_map/ppermute | solution.py:428
  99.9 46.4 %copy-start.10 = (bf16[72,3072]{1,0:T(8,128)(2,1)}, bf16[72,3072]{1,0:T(8,128)(2,1)S(1)}, u32[]{:S(2)}) copy-start(bf16[72,3072]{1,0:T(8,128)(2,1)S(1)} %collective-permute-done.14.refs_2_) | copy-start | bytes 1327108
  99.9 23.5 %collective-permute-start.27 = (bf16[224,1536]{1,0:T(8,128)(2,1)S(1)}, bf16[224,1536]{1,0:T(8,128)(2,1)S(1)}, u32[]{:S(2)}, u32[]{:S(2)}) collective-permute-start(bf16[224,1536]{1,0:T(8,128)(2,1)S(1)} %copy-done.26), channel_id=1, source_target_pairs={{0,8},{8,0},{16,24},{24,16},{1,9},{9,1},{17,25},{25,17},{2,10},{10... | collective-permute-start | bytes 2064392 | tf_op jit(solution)/shard_map/ppermute | solution.py:428
  100.4 45.8 %copy-start.30 = (bf16[80,1536]{1,0:T(8,128)(2,1)}, bf16[80,1536]{1,0:T(8,128)(2,1)S(1)}, u32[]{:S(2)}) copy-start(bf16[80,1536]{1,0:T(8,128)(2,1)S(1)} %collective-permute-done.28.refs_9_) | copy-start | bytes 737284
  100.4 20.8 %collective-permute-start.10 = (bf16[40,3072]{1,0:T(8,128)(2,1)}, bf16[40,3072]{1,0:T(8,128)(2,1)S(1)}, u32[]{:S(2)}, u32[]{:S(2)}) collective-permute-start(bf16[40,3072]{1,0:T(8,128)(2,1)} %get-tuple-element.36), channel_id=1, source_target_pairs={{0,1},{1,0},{2,3},{3,2},{4,5},{5,4},{6,7},{7,6},{8,9},{9,8},{10,11... | collective-permute-start | bytes 737288 | tf_op jit(solution)/shard_map/ppermute | solution.py:434
  121.2 11.8 %collective-permute-start.15 = (bf16[72,3072]{1,0:T(8,128)(2,1)}, bf16[72,3072]{1,0:T(8,128)(2,1)S(1)}, u32[]{:S(2)}, u32[]{:S(2)}) collective-permute-start(bf16[72,3072]{1,0:T(8,128)(2,1)} %copy-done.13), channel_id=1, source_target_pairs={{0,16},{8,24},{16,0},{24,8},{1,17},{9,25},{17,1},{25,9},{2,18},{10... | collective-permute-start | bytes 1327112 | tf_op jit(solution)/shard_map/ppermute | solution.py:431
  122.2 21.8 %collective-permute-start.21 = (bf16[80,3072]{1,0:T(8,128)(2,1)}, bf16[80,3072]{1,0:T(8,128)(2,1)S(1)}, u32[]{:S(2)}, u32[]{:S(2)}) collective-permute-start(bf16[80,3072]{1,0:T(8,128)(2,1)} %get-tuple-element.38.refs_2_), channel_id=1, source_target_pairs={{0,8},{8,0},{16,24},{24,16},{1,9},{9,1},{17,25},{25,17},{2,10},{10... | collective-permute-start | bytes 1474568 | tf_op jit(solution)/shard_map/ppermute | solution.py:428
  123.4 22.9 %copy-start.25 = (bf16[224,1536]{1,0:T(8,128)(2,1)}, bf16[224,1536]{1,0:T(8,128)(2,1)S(1)}, u32[]{:S(2)}) copy-start(bf16[224,1536]{1,0:T(8,128)(2,1)S(1)} %collective-permute-done.27.refs_7_) | copy-start | bytes 2064388
  123.4 15.2 %collective-permute-start.11 = (bf16[40,3072]{1,0:T(8,128)(2,1)S(1)}, bf16[40,3072]{1,0:T(8,128)(2,1)S(1)}, u32[]{:S(2)}, u32[]{:S(2)}) collective-permute-start(bf16[40,3072]{1,0:T(8,128)(2,1)S(1)} %merge.3), channel_id=1, source_target_pairs={{0,4},{1,5},{2,6},{3,7},{4,0},{5,1},{6,2},{7,3},{8,12},{9,13},{10,... | collective-permute-start | bytes 737288 | tf_op jit(solution)/shard_map/ppermute | solution.py:437
  124.0 22.3 %copy-start.24 = (bf16[144,3072]{1,0:T(8,128)(2,1)}, bf16[144,3072]{1,0:T(8,128)(2,1)S(1)}, u32[]{:S(2)}) copy-start(bf16[144,3072]{1,0:T(8,128)(2,1)S(1)} %collective-permute-done.26.refs_5_) | copy-start | bytes 2654212
  124.0 14.6 %collective-permute-start.6 = (bf16[40,3072]{1,0:T(8,128)(2,1)S(1)}, bf16[40,3072]{1,0:T(8,128)(2,1)S(1)}, u32[]{:S(2)}, u32[]{:S(2)}) collective-permute-start(bf16[40,3072]{1,0:T(8,128)(2,1)S(1)} %get-tuple-element.32), channel_id=1, source_target_pairs={{0,6},{1,7},{2,0},{3,1},{4,2},{5,3},{6,4},{7,5},{8,14},{9,15},{10,... | collective-permute-start | bytes 737288 | tf_op jit(solution)/shard_map/ppermute | solution.py:437
  133.0 24.0 %copy-start.12 = (bf16[72,3072]{1,0:T(8,128)(2,1)}, bf16[72,3072]{1,0:T(8,128)(2,1)S(1)}, u32[]{:S(2)}) copy-start(bf16[72,3072]{1,0:T(8,128)(2,1)S(1)} %collective-permute-done.15.refs_3_) | copy-start | bytes 1327108
  133.0 11.0 %collective-permute-start.7 = (bf16[40,3072]{1,0:T(8,128)(2,1)S(1)}, bf16[40,3072]{1,0:T(8,128)(2,1)S(1)}, u32[]{:S(2)}, u32[]{:S(2)}) collective-permute-start(bf16[40,3072]{1,0:T(8,128)(2,1)S(1)} %get-tuple-element.33), channel_id=1, source_target_pairs={{0,2},{1,3},{2,4},{3,5},{4,6},{5,7},{6,0},{7,1},{8,10},{9,11},{10,... | collective-permute-start | bytes 737288 | tf_op jit(solution)/shard_map/ppermute | solution.py:437
  138.6 18.5 %collective-permute-start.16 = (bf16[72,3072]{1,0:T(8,128)(2,1)S(1)}, bf16[72,3072]{1,0:T(8,128)(2,1)S(1)}, u32[]{:S(2)}, u32[]{:S(2)}) collective-permute-start(bf16[72,3072]{1,0:T(8,128)(2,1)S(1)} %collective-permute-done.12.refs_0_), channel_id=1, source_target_pairs={{0,8},{8,0},{16,24},{24,16},{1,9},{9,1},{17,25},{25,17},{2,10},{10... | collective-permute-start | bytes 1327112 | tf_op jit(solution)/shard_map/ppermute | solution.py:428
  138.6 18.5 %collective-permute-start.17 = (bf16[72,3072]{1,0:T(8,128)(2,1)S(1)}, bf16[72,3072]{1,0:T(8,128)(2,1)S(1)}, u32[]{:S(2)}, u32[]{:S(2)}) collective-permute-start(bf16[72,3072]{1,0:T(8,128)(2,1)S(1)} %collective-permute-done.13.refs_1_), channel_id=1, source_target_pairs={{0,8},{8,0},{16,24},{24,16},{1,9},{9,1},{17,25},{25,17},{2,10},{10... | collective-permute-start | bytes 1327112 | tf_op jit(solution)/shard_map/ppermute | solution.py:428
  144.0 13.1 %collective-permute-start.18 = (bf16[72,3072]{1,0:T(8,128)(2,1)S(1)}, bf16[72,3072]{1,0:T(8,128)(2,1)S(1)}, u32[]{:S(2)}, u32[]{:S(2)}) collective-permute-start(bf16[72,3072]{1,0:T(8,128)(2,1)S(1)} %collective-permute-done.14.refs_2_), channel_id=1, source_target_pairs={{0,8},{8,0},{16,24},{24,16},{1,9},{9,1},{17,25},{25,17},{2,10},{10... | collective-permute-start | bytes 1327112 | tf_op jit(solution)/shard_map/ppermute | solution.py:428
  144.0 2.3 %copy-start.27 = (bf16[80,3072]{1,0:T(8,128)(2,1)}, bf16[80,3072]{1,0:T(8,128)(2,1)S(1)}, u32[]{:S(2)}) copy-start(bf16[80,3072]{1,0:T(8,128)(2,1)S(1)} %collective-permute-done.21.refs_3_) | copy-start | bytes 1474564
  144.0 13.1 %collective-permute-start.19 = (bf16[72,3072]{1,0:T(8,128)(2,1)S(1)}, bf16[72,3072]{1,0:T(8,128)(2,1)S(1)}, u32[]{:S(2)}, u32[]{:S(2)}) collective-permute-start(bf16[72,3072]{1,0:T(8,128)(2,1)S(1)} %collective-permute-done.15.refs_3_), channel_id=1, source_target_pairs={{0,8},{8,0},{16,24},{24,16},{1,9},{9,1},{17,25},{25,17},{2,10},{10... | collective-permute-start | bytes 1327112 | tf_op jit(solution)/shard_map/ppermute | solution.py:428
  (13 other events, 13.2 us)

commit v3 on v2

--- a/solution.py
+++ b/solution.py
@@ -10,6 +10,8 @@
 CAP = 36
 MAIN = 32
 REST = CAP - MAIN
+TILE = 256
+LIMIT = 20
 HALF = jnp.bfloat16
 FULL = jnp.float32
 
@@ -48,47 +50,41 @@
     return jnp.where(row == places[0:1], jnp.broadcast_to(chosen[0:1], row.shape), 0.0)
 
 
-def pack_kernel(ids, probs, tokens, cotangent, out, pick_rows, pick_cotan, share):
-    @pl.when(pl.program_id(0) == 0)
-    def _():
-        chosen, slots = earlier_count(ids[...])
-        late = (slots >= MAIN).astype(FULL)
-        depth = pick_rows.shape[0]
-        pick_rows[...] = one_hot(slots + late * MAIN, chosen, depth).astype(HALF)
-        picked = one_hot(slots + MAIN + late * REST, chosen, depth)
-        pick_cotan[...] = picked.astype(HALF)
-        total = jnp.sum(jnp.where(ids[...] == 0, probs[...], 0.0), axis=0, keepdims=True)
-        share[...] = jnp.broadcast_to(
-            jnp.sum(picked * total, axis=1, keepdims=True), share.shape
-        )
-
-    cotan = jnp.dot(pick_cotan[...], cotangent[...], preferred_element_type=FULL)
-    rows = jnp.dot(pick_rows[...], tokens[...], preferred_element_type=FULL)
-    out[...] = (rows + share[:, 0:1] * cotan)[0 : 2 * CAP].astype(HALF)
+def pack_kernel(ids_in, probs_in, tokens_in, cotangent_in, out, ids, probs, tokens, cotangent, done):
+    pairs = ((ids_in, ids), (probs_in, probs), (tokens_in, tokens), (cotangent_in, cotangent))
+    copies = [pltpu.make_async_copy(a, b, done.at[i]) for i, (a, b) in enumerate(pairs)]
+    for copy in copies:
+        copy.start()
+    copies[0].wait()
+    copies[1].wait()
+    chosen, slots = earlier_count(ids[...])
+    late = (slots >= MAIN).astype(FULL)
+    pick_rows = one_hot(slots + late * MAIN, chosen, 80).astype(HALF)
+    picked = one_hot(slots + MAIN + late * REST, chosen, 80)
+    total = jnp.sum(jnp.where(ids[...] == 0, probs[...], 0.0), axis=0, keepdims=True)
+    share = jnp.sum(picked * total, axis=1, keepdims=True)
+    picked = picked.astype(HALF)
+    copies[2].wait()
+    copies[3].wait()
+    width = out.shape[1]
+    for i in range(0, width, 768):
+        here = slice(i, i + 768)
+        cotan = jnp.dot(picked, cotangent[:, here], preferred_element_type=FULL)
+        rows = jnp.dot(pick_rows, tokens[:, here], preferred_element_type=FULL)
+        out[:, here] = (rows + share * cotan)[0 : 2 * CAP].astype(HALF)
 
 
 def pack(ids, probs, tokens, cotangent):
-    count, width = tokens.shape
-    step = 1536
+    values = (ids, probs, tokens, cotangent)
     return pl.pallas_call(
         pack_kernel,
-        grid=(width // step,),
-        in_specs=[
-            pl.BlockSpec(ids.shape, lambda j: (0, 0)),
-            pl.BlockSpec(probs.shape, lambda j: (0, 0)),
-            pl.BlockSpec((count, step), lambda j: (0, j)),
-            pl.BlockSpec((count, step), lambda j: (0, j)),
-        ],
-        out_specs=pl.BlockSpec((2 * CAP, step), lambda j: (0, j)),
-        out_shape=shape((2 * CAP, width)),
-        scratch_shapes=[
-            pltpu.VMEM((80, count), HALF),
-            pltpu.VMEM((80, count), HALF),
-            pltpu.VMEM((80, 128), FULL),
-        ],
-        compiler_params=params(32),
+        in_specs=[pl.BlockSpec(memory_space=pl.ANY)] * 4,
+        out_shape=shape((2 * CAP, tokens.shape[1])),
+        scratch_shapes=[pltpu.VMEM(v.shape, v.dtype) for v in values]
+        + [pltpu.SemaphoreType.DMA((4,))],
+        compiler_params=params(LIMIT),
         name="pack",
-    )(ids, probs, tokens, cotangent)
+    )(*values)
 
 
 def unpack_kernel(ids, *refs):
@@ -116,28 +112,8 @@
     )(ids, *pieces)
 
 
-TILE = 256
-
-
 def padded_rows(n):
     return MAIN * n + -(-REST * n // 16) * 16
-
-
-def load_all(pairs, done):
-    copies = [pltpu.make_async_copy(a, b, done.at[i]) for i, (a, b) in enumerate(pairs)]
-    for copy in copies:
-        copy.start()
-    return copies
-
-
-def weight_copies(weights, buffers):
-    pairs = []
-    for j in range(buffers[0].shape[1] // TILE):
-        here = pl.ds(TILE * j, TILE)
-        for k in range(2):
-            pairs.append((weights[k].at[:, here], buffers[k].at[:, here]))
-        pairs.append((weights[2].at[here, :], buffers[2].at[here, :]))
-    return pairs
 
 
 def assemble(blocks, rows, scaled):
@@ -179,21 +155,16 @@
     if back:
         send, keep = refs[:2]
         refs = refs[2:]
-    rows, scaled, held, gate, up, down, block_done, weight_done = refs
+    rows, scaled = refs
+    gate, up, down = weights
     width, part = rows.shape[1], own.shape[1] // 2
-    block_copies = load_all([(blocks[i], held.at[i]) for i in range(n)], block_done)
-    copies = load_all(weight_copies(weights, (gate, up, down)), weight_done)
-    for copy in block_copies:
-        copy.wait()
-    assemble([held.at[i] for i in range(n)], rows, scaled)
+    assemble(blocks, rows, scaled)
     for out, index in ((own, 0), (other, 1)):
         columns = pl.ds(pl.multiple_of(place[index] * part, part), part)
         out[:, 0:part] = rows[:, columns]
         out[:, part : 2 * part] = scaled[:, columns]
     tiles = gate.shape[1] // TILE
     for j in range(tiles):
-        for copy in copies[3 * j : 3 * j + 3]:
-            copy.wait()
         here = slice(TILE * j, TILE * (j + 1))
         found = activations(rows[...], scaled[...], gate[:, here], up[:, here], down[here, :])
         for k in range(3):
@@ -218,7 +189,6 @@
 def forward(blocks, gate, up, down, place, part, back):
     n, (width, hidden) = len(blocks), gate.shape
     count = padded_rows(n)
-    anywhere = pl.BlockSpec(memory_space=pl.ANY)
     in_vmem = pl.BlockSpec(memory_space=pltpu.VMEM)
     out_shape = [
         shape((count, 3 * hidden)),
@@ -231,20 +201,14 @@
     matmuls = 5 if back else 3
     return pl.pallas_call(
         functools.partial(forward_kernel, n, back),
-        in_specs=[pl.BlockSpec(memory_space=pltpu.SMEM)] + [anywhere] * (n + 3),
+        in_specs=[pl.BlockSpec(memory_space=pltpu.SMEM)] + [in_vmem] * (n + 3),
         out_specs=[in_vmem] * len(out_shape),
         out_shape=out_shape,
         scratch_shapes=[
             pltpu.VMEM((count, width), HALF),
             pltpu.VMEM((count, width), HALF),
-            pltpu.VMEM((n, 2 * CAP, width), HALF),
-            pltpu.VMEM((width, hidden), HALF),
-            pltpu.VMEM((width, hidden), HALF),
-            pltpu.VMEM((hidden, width), HALF),
-            pltpu.SemaphoreType.DMA((n,)),
-            pltpu.SemaphoreType.DMA((3 * hidden // TILE,)),
         ],
-        compiler_params=params(56),
+        compiler_params=params(LIMIT),
         cost_estimate=pl.CostEstimate(
             flops=2 * matmuls * count * width * hidden,
             bytes_accessed=6 * width * hidden + 4 * count * (width + part),
@@ -256,15 +220,13 @@
 
 def grads_kernel(n, *refs):
     acts, parts, refs = refs[:n], refs[n : 2 * n], refs[2 * n :]
-    gate_grad, up_grad, down_grad, act_rows, part_rows, done = refs
-    pairs, start = [], 0
-    for i in range(n):
-        here = pl.ds(start, acts[i].shape[0])
-        pairs.append((acts[i], act_rows.at[here, :]))
-        pairs.append((parts[i], part_rows.at[here, :]))
-        start += acts[i].shape[0]
-    for copy in load_all(pairs, done):
-        copy.wait()
+    gate_grad, up_grad, down_grad, act_rows, part_rows = refs
+    start = 0
+    for act, piece in zip(acts, parts):
+        here = slice(start, start + act.shape[0])
+        act_rows[here, :] = act[...]
+        part_rows[here, :] = piece[...]
+        start += act.shape[0]
     part = part_rows.shape[1] // 2
     tiles = act_rows.shape[1] // (3 * TILE)
     for i in range(part // TILE):
@@ -289,19 +251,17 @@
 
 def grads(acts, parts, part, hidden):
     n, count = len(acts), sum(a.shape[0] for a in acts)
-    anywhere = pl.BlockSpec(memory_space=pl.ANY)
     in_vmem = pl.BlockSpec(memory_space=pltpu.VMEM)
     return pl.pallas_call(
         functools.partial(grads_kernel, n),
-        in_specs=[anywhere] * (2 * n),
+        in_specs=[in_vmem] * (2 * n),
         out_specs=[in_vmem] * 3,
         out_shape=[shape((part, hidden)), shape((part, hidden)), shape((hidden, part))],
         scratch_shapes=[
             pltpu.VMEM((count, 3 * hidden), HALF),
             pltpu.VMEM((count, 2 * part), HALF),
-            pltpu.SemaphoreType.DMA((2 * n,)),
         ],
-        compiler_params=params(56),
+        compiler_params=params(LIMIT),
         cost_estimate=pl.CostEstimate(
             flops=6 * count * part * hidden,
             bytes_accessed=2 * count * (3 * hidden + 2 * part) + 6 * part * hidden,
@@ -312,77 +272,43 @@
 
 
 def finish_kernel(n, place, *refs):
-    blocks, weights, early, refs = refs[:n], refs[n : n + 3], refs[n + 3 : n + 6], refs[n + 6 :]
-    outs, refs = refs[:3], refs[3:]
-    rows, scaled, held, gate, up, down = refs[:6]
-    sums, block_done, weight_done, sum_done, out_done = refs[6:9], *refs[9:]
-    part = outs[0].shape[0]
-    block_copies = load_all([(blocks[i], held.at[i]) for i in range(n)], block_done)
-    copies = load_all(weight_copies(weights, (gate, up, down)), weight_done)
-    sum_copies = load_all([(early[k], sums[k]) for k in range(3)], sum_done)
-    for copy in block_copies:
-        copy.wait()
-    assemble([held.at[i] for i in range(n)], rows, scaled)
+    blocks, (gate, up, down), early, refs = refs[:n], refs[n : n + 3], refs[n + 3 : n + 6], refs[n + 6 :]
+    gate_grad, up_grad, down_grad, rows, scaled = refs
+    part = gate_grad.shape[0]
+    assemble(blocks, rows, scaled)
     columns = pl.ds(pl.multiple_of(place[0] * part, part), part)
     picked, cotan = rows[:, columns].T, scaled[:, columns]
-    out_copies = []
     for j in range(gate.shape[1] // TILE):
-        for copy in copies[3 * j : 3 * j + 3]:
-            copy.wait()
         here = slice(TILE * j, TILE * (j + 1))
         hidden, gate_back, up_back = activations(
             rows[...], scaled[...], gate[:, here], up[:, here], down[here, :]
         )
-        if j == 0:
-            for copy in sum_copies:
-                copy.wait()
-        sums[0][:, here] = (
-            sums[0][:, here].astype(FULL)
+        gate_grad[:, here] = (
+            early[0][:, here].astype(FULL)
             + jnp.dot(picked, gate_back, preferred_element_type=FULL)
         ).astype(HALF)
-        sums[1][:, here] = (
-            sums[1][:, here].astype(FULL) + jnp.dot(picked, up_back, preferred_element_type=FULL)
+        up_grad[:, here] = (
+            early[1][:, here].astype(FULL) + jnp.dot(picked, up_back, preferred_element_type=FULL)
         ).astype(HALF)
-        sums[2][here, :] = (
-            sums[2][here, :].astype(FULL) + tn_dot(hidden, cotan)
+        down_grad[here, :] = (
+            early[2][here, :].astype(FULL) + tn_dot(hidden, cotan)
         ).astype(HALF)
-        there = pl.ds(TILE * j, TILE)
-        views = [
-            (sums[0].at[:, there], outs[0].at[:, there]),
-            (sums[1].at[:, there], outs[1].at[:, there]),
-            (sums[2].at[there, :], outs[2].at[there, :]),
-        ]
-        for source, target in views:
-            copy = pltpu.make_async_copy(source, target, out_done.at[len(out_copies)])
-            copy.start()
-            out_copies.append(copy)
-    for copy in out_copies:
-        copy.wait()
 
 
 def finish(blocks, gate, up, down, place, early):
     n, (width, hidden) = len(blocks), gate.shape
     count, part = padded_rows(n), early[0].shape[0]
-    anywhere = pl.BlockSpec(memory_space=pl.ANY)
+    in_vmem = pl.BlockSpec(memory_space=pltpu.VMEM)
     return pl.pallas_call(
         functools.partial(finish_kernel, n),
-        in_specs=[pl.BlockSpec(memory_space=pltpu.SMEM)] + [anywhere] * (n + 6),
-        out_specs=[anywhere] * 3,
+        in_specs=[pl.BlockSpec(memory_space=pltpu.SMEM)] + [in_vmem] * (n + 6),
+        out_specs=[in_vmem] * 3,
         out_shape=[shape(e.shape) for e in early],
         scratch_shapes=[
             pltpu.VMEM((count, width), HALF),
             pltpu.VMEM((count, width), HALF),
-            pltpu.VMEM((n, 2 * CAP, width), HALF),
-            pltpu.VMEM((width, hidden), HALF),
-            pltpu.VMEM((width, hidden), HALF),
-            pltpu.VMEM((hidden, width), HALF),
-            *[pltpu.VMEM(e.shape, HALF) for e in early],
-            pltpu.SemaphoreType.DMA((n,)),
-            pltpu.SemaphoreType.DMA((3 * hidden // TILE,)),
-            pltpu.SemaphoreType.DMA((3,)),
-            pltpu.SemaphoreType.DMA((3 * hidden // TILE,)),
         ],
-        compiler_params=params(56),
+        compiler_params=params(LIMIT),
         cost_estimate=pl.CostEstimate(
             flops=6 * count * (width + part) * hidden,
             bytes_accessed=6 * width * hidden + 2 * n * CAP * width + 12 * part * hidden,

time: 185 us -> 154 us (0.83)
  the two profiles are of different devices: /device:TPU:0 before, /device:TPU:13 now
where the time goes in v3:
time: 154 us; the launch traced here: 153 us
  waiting for transfers between devices  67.2 us (44%)
  Pallas kernels  43.7 us (28%)
  starting transfers between devices  24.5 us (16%)
  local copies, waits for them, and re-layouts  16.9 us (11%)
    ppermute x7, waiting for transfers between devices, over_x(): return lax.ppermute(v, 'expert', x_pairs)  32.2 us
    ppermute x6, waiting for transfers between devices, over_z(): lax.ppermute(v, 'expert', [(i, (i + 2 * by) % n_expert) for i in range(n_...  25 us
    pallas_call x3, Pallas kernels, forward(): pl.pallas_call(functools.partial(forward_kernel, n, back), in_specs=[pl.B...  23.4 us
    unnamed x58, local copies, waits for them, and re-layouts  16.9 us
    pallas_call x1, Pallas kernels, finish(): pl.pallas_call(functools.partial(finish_kernel, n), in_specs=[pl.BlockSpe...  12.4 us
    ppermute x10, starting transfers between devices, over_core(): return lax.ppermute(v, 'dp', core_pairs)  11.6 us
    ppermute x7, waiting for transfers between devices, over_y(): return lax.ppermute(v, 'dp', y_pairs)  9.95 us
    ppermute x6, starting transfers between devices, over_z(): lax.ppermute(v, 'expert', [(i, (i + 2 * by) % n_expert) for i in range(n_...  5.47 us
  transfers between devices with their start and end apart: 30, of which 11 were waited for; matrix products, arithmetic and copies ran while one was open for 0% of the time, Pallas kernels for 20%

profile of v3, /device:TPU:13, one launch (start us, length us, event | category | flops | bytes accessed | tf_op | source)
XLA Modules:
  0.0 153.4 jit_solution(9722397090638364842)
XLA Ops:
  0.6 1.1 copy-done.4
  1.8 1.1 copy-done.5
  2.9 0.7 copy-done.8
  3.6 0.7 copy-done.10
  4.3 0.8 pack.1.refs_0_
  5.1 1.4 collective-permute-start
  6.6 9.5 %collective-permute-done.refs_1_ = bf16[72,3072]{1,0:T(8,128)(2,1)S(1)} collective-permute-done((bf16[72,3072]{1,0:T(8,128)(2,1)S(1)}, bf16[72,3072]{1,0:T(8,128)(2,1)S(1)}, u32[]{:S(2)}, u32[]{:S(2)}) %collective-permute-start) | collective-permute-done | bytes 442400 | tf_op jit(solution)/shard_map/ppermute | solution.py:363
  16.1 1.2 collective-permute-start.3
  17.4 2.1 %collective-permute-start.1 = (bf16[72,3072]{1,0:T(8,128)(2,1)S(1)}, bf16[72,3072]{1,0:T(8,128)(2,1)S(1)}, u32[]{:S(2)}, u32[]{:S(2)}) collective-permute-start(bf16[72,3072]{1,0:T(8,128)(2,1)S(1)} %pack.1.refs_0_), channel_id=1, source_target_pairs={{0,6},{1,7},{2,0},{3,1},{4,2},{5,3},{6,4},{7,5},{8,14},{9,15},{10,... | collective-permute-start | bytes 1327112 | tf_op jit(solution)/shard_map/ppermute | solution.py:363
  19.7 0.5 collective-permute-start.23
  20.2 6.2 %collective-permute-done.3.refs_4_ = bf16[72,3072]{1,0:T(8,128)(2,1)} collective-permute-done((bf16[72,3072]{1,0:T(8,128)(2,1)S(1)}, bf16[72,3072]{1,0:T(8,128)(2,1)}, u32[]{:S(2)}, u32[]{:S(2)}) %collective-permute-start.3) | collective-permute-done | bytes 442400 | tf_op jit(solution)/shard_map/ppermute | solution.py:360
  26.6 0.7 collective-permute-done.1.refs_2_
  27.3 1.3 collective-permute-start.8
  28.6 0.5 collective-permute-start.2
  29.2 0.9 collective-permute-start.4
  30.1 5.6 %collective-permute-done.23.refs_1_ = bf16[72,3072]{1,0:T(8,128)(2,1)S(1)} collective-permute-done((bf16[72,3072]{1,0:T(8,128)(2,1)S(1)}, bf16[72,3072]{1,0:T(8,128)(2,1)S(1)}, u32[]{:S(2)}, u32[]{:S(2)}) %collective-permute-start.23) | collective-permute-done | bytes 442400 | tf_op jit(solution)/shard_map/ppermute | solution.py:360
  36.0 2.5 %collective-permute-done.25.refs_3_ = bf16[72,3072]{1,0:T(8,128)(2,1)S(1)} collective-permute-done((bf16[72,3072]{1,0:T(8,128)(2,1)}, bf16[72,3072]{1,0:T(8,128)(2,1)S(1)}, u32[]{:S(2)}, u32[]{:S(2)}) %collective-permute-start.25) | collective-permute-done | bytes 442400 | tf_op jit(solution)/shard_map/ppermute | solution.py:357
  38.4 2.8 %copy-done = bf16[3072,1024]{1,0:T(8,128)(2,1)S(1)} copy-done((bf16[3072,1024]{1,0:T(8,128)(2,1)S(1)}, bf16[3072,1024]{1,0:T(8,128)(2,1)}, u32[]{:S(2)}) %copy-start) | copy-done | bytes 6291480
  41.2 2.8 %copy-done.2 = bf16[3072,1024]{1,0:T(8,128)(2,1)S(1)} copy-done((bf16[3072,1024]{1,0:T(8,128)(2,1)S(1)}, bf16[3072,1024]{1,0:T(8,128)(2,1)}, u32[]{:S(2)}) %copy-start.2) | copy-done | bytes 6291480
  44.0 2.8 %copy-done.3 = bf16[1024,3072]{1,0:T(8,128)(2,1)S(1)} copy-done((bf16[1024,3072]{1,0:T(8,128)(2,1)S(1)}, bf16[1024,3072]{1,0:T(8,128)(2,1)}, u32[]{:S(2)}) %copy-start.3) | copy-done | bytes 6291480
  46.8 4.7 %forward.1 = (bf16[144,3072]{1,0:T(8,128)(2,1)S(1)}, bf16[144,1536]{1,0:T(8,128)(2,1)S(1)}, bf16[144,1536]{1,0:T(8,128)(2,1)S(1)}) custom-call(s32[2]{0:T(128)S(1)} %pad_add_fusion.place, bf16[72,3072]{1,0:T(8,128)(2,1)S(1)} %collective-permute-done.22.refs_0_, bf16[72,3072]{1,0:T(8,128)(2,1)S(1)} %collective-permute-done.23.refs_1_, ...), custom_call_target="tpu_custom_call" | custom-call | flops 2717908992 | bytes 21086208 | tf_op jit(solution)/shard_map/forward/pallas_call | solution.py:202
  51.5 0.7 copy-done.17
  52.3 5.7 %collective-permute-start.29 = (bf16[144,1536]{1,0:T(8,128)(2,1)S(1)}, bf16[144,1536]{1,0:T(8,128)(2,1)S(1)}, u32[]{:S(2)}, u32[]{:S(2)}) collective-permute-start(bf16[144,1536]{1,0:T(8,128)(2,1)S(1)} %get-tuple-element.45), channel_id=1, source_target_pairs={{0,8},{8,0},{16,24},{24,16},{1,9},{9,1},{17,25},{25,17},{2,10},{10... | collective-permute-start | bytes 1327112 | tf_op jit(solution)/shard_map/ppermute | solution.py:354
  58.3 10.1 %forward_back.2 = (bf16[224,3072]{1,0:T(8,128)(2,1)S(1)}, bf16[224,1536]{1,0:T(8,128)(2,1)S(1)}, bf16[224,1536]{1,0:T(8,128)(2,1)S(1)}, bf16[112,3072]{1,0:T(8,128)(2,1)S(1)}, bf16[112,3072]{1,0:T(8,128)(2,1)S(1)}) custom-call(s32[2]{0:T(128)S(1)} %pad_add_fusion.place, bf16[72,3072]{1,0:T(8,128)(2,1)S(1)} %pack.1.refs_0_, ...), custom_call_target="tpu_custom_call" | custom-call | flops 7046430720 | bytes 22315008 | tf_op jit(solution)/shard_map/forward_back/pallas_call | solution.py:202
  68.8 1.0 collective-permute-done.9.refs_1_
  70.0 8.6 %forward_back.3 = (bf16[80,3072]{1,0:T(8,128)(2,1)S(1)}, bf16[80,1536]{1,0:T(8,128)(2,1)S(1)}, bf16[80,1536]{1,0:T(8,128)(2,1)S(1)}, bf16[40,3072]{1,0:T(8,128)(2,1)S(1)}, bf16[40,3072]{1,0:T(8,128)(2,1)S(1)}) custom-call(s32[2]{0:T(128)S(1)} %pad_add_fusion.place, bf16[72,3072]{1,0:T(8,128)(2,1)S(1)} %collective-permute-done.8.refs_0_, ...), custom_call_target="tpu_custom_call" | custom-call | flops 2516582400 | bytes 20103168 | tf_op jit(solution)/shard_map/forward_back/pallas_call | solution.py:202
  78.7 0.7 copy-done.21
  79.4 1.1 collective-permute-start.28
  80.5 1.0 collective-permute-start.5
  81.5 0.4 collective-permute-start.26
  81.9 0.7 collective-permute-start.27
  82.6 0.7 collective-permute-start.10
  83.3 19.5 %collective-permute-done.10.came = bf16[40,3072]{1,0:T(8,128)(2,1)S(1)} collective-permute-done((bf16[40,3072]{1,0:T(8,128)(2,1)S(1)}, bf16[40,3072]{1,0:T(8,128)(2,1)S(1)}, u32[]{:S(2)}, u32[]{:S(2)}) %collective-permute-start.10) | collective-permute-done | bytes 245792 | tf_op jit(solution)/shard_map/ppermute | solution.py:360
  102.8 1.2 collective-permute-start.15
  104.0 1.2 collective-permute-start.21
  105.5 0.6 collective-permute-start.6
  106.2 7.4 %collective-permute-done.15.refs_3_ = bf16[72,3072]{1,0:T(8,128)(2,1)S(1)} collective-permute-done((bf16[72,3072]{1,0:T(8,128)(2,1)S(1)}, bf16[72,3072]{1,0:T(8,128)(2,1)S(1)}, u32[]{:S(2)}, u32[]{:S(2)}) %collective-permute-start.15) | collective-permute-done | bytes 442400 | tf_op jit(solution)/shard_map/ppermute | solution.py:357
  113.6 8.1 %collective-permute-done.11.refs_3_ = bf16[40,3072]{1,0:T(8,128)(2,1)S(1)} collective-permute-done((bf16[40,3072]{1,0:T(8,128)(2,1)S(1)}, bf16[40,3072]{1,0:T(8,128)(2,1)S(1)}, u32[]{:S(2)}, u32[]{:S(2)}) %collective-permute-start.11) | collective-permute-done | bytes 245792 | tf_op jit(solution)/shard_map/ppermute | solution.py:363
  121.7 0.8 collective-permute-start.16
  122.5 6.7 %collective-permute-done.6.refs_1_ = bf16[40,3072]{1,0:T(8,128)(2,1)S(1)} collective-permute-done((bf16[40,3072]{1,0:T(8,128)(2,1)S(1)}, bf16[40,3072]{1,0:T(8,128)(2,1)S(1)}, u32[]{:S(2)}, u32[]{:S(2)}) %collective-permute-start.6) | collective-permute-done | bytes 245792 | tf_op jit(solution)/shard_map/ppermute | solution.py:363
  129.2 0.8 collective-permute-start.17
  130.0 0.5 collective-permute-start.19
  130.5 1.7 %unpack.1 = bf16[128,3072]{1,0:T(8,128)(2,1)} custom-call(s32[2,128]{1,0:T(2,128)S(1)} %bitcast.9, bf16[40,3072]{1,0:T(8,128)(2,1)S(1)} %get-tuple-element.31.refs_0_, bf16[40,3072]{1,0:T(8,128)(2,1)S(1)} %collective-permute-done.6.refs_1_, bf16[40,3072]{1,0:T(8,128)(2,1)S(1)} %collective-permute-done.7.refs_2_, ...), custom_call_target="tpu_custom_call" | custom-call | tf_op jit(solution)/shard_map/unpack/pallas_call | solution.py:103
  132.3 1.2 copy-done.16
  133.5 1.2 copy-done.20
  134.7 1.1 copy-done.24
  135.8 5.1 %grads.1 = (bf16[768,1024]{1,0:T(8,128)(2,1)S(1)}, bf16[768,1024]{1,0:T(8,128)(2,1)S(1)}, bf16[1024,768]{1,0:T(8,128)(2,1)S(1)}) custom-call(bf16[224,3072]{1,0:T(8,128)(2,1)S(1)} %copy-done.12, bf16[224,3072]{1,0:T(8,128)(2,1)S(1)} %collective-permute-done.20.refs_1_, bf16[80,3072]{1,0:T(8,128)(2,1)S(1)} %copy-done.16, ...), custom_call_target="tpu_custom_call" | custom-call | flops 4227858432 | bytes 12976128 | tf_op jit(solution)/shard_map/grads/pallas_call | solution.py:255
  141.0 12.4 %finish.1 = (bf16[768,1024]{1,0:T(8,128)(2,1)}, bf16[768,1024]{1,0:T(8,128)(2,1)}, bf16[1024,768]{1,0:T(8,128)(2,1)}) custom-call(s32[2]{0:T(128)S(1)} %pad_add_fusion.place, bf16[72,3072]{1,0:T(8,128)(2,1)S(1)} %copy-done.7, bf16[72,3072]{1,0:T(8,128)(2,1)} %collective-permute-done.13.refs_1_, bf16[72,3072]{1,0:T(8,128)(2,1)S(1)} %collective-permute-done.14.refs_2_, ...), custom_call_target="tpu_custom_call" | custom-call | flops 6794772480 | bytes 30081024 | tf_op jit(solution)/shard_map/finish/pallas_call | solution.py:302
  (82 shorter events, 2.5 us)
Async XLA Ops:
  5.1 11.1 %collective-permute-start = (bf16[72,3072]{1,0:T(8,128)(2,1)S(1)}, bf16[72,3072]{1,0:T(8,128)(2,1)S(1)}, u32[]{:S(2)}, u32[]{:S(2)}) collective-permute-start(bf16[72,3072]{1,0:T(8,128)(2,1)S(1)} %pack.1.refs_0_), channel_id=1, source_target_pairs={{0,2},{1,3},{2,4},{3,5},{4,6},{5,7},{6,0},{7,1},{8,10},{9,11},{10,... | collective-permute-start | bytes 1327112 | tf_op jit(solution)/shard_map/ppermute | solution.py:363
  6.4 13.3 %collective-permute-start.22 = (bf16[72,3072]{1,0:T(8,128)(2,1)S(1)}, bf16[72,3072]{1,0:T(8,128)(2,1)S(1)}, u32[]{:S(2)}, u32[]{:S(2)}) collective-permute-start(bf16[72,3072]{1,0:T(8,128)(2,1)S(1)} %pack.1.refs_0_), channel_id=1, source_target_pairs={{0,16},{8,24},{16,0},{24,8},{1,17},{9,25},{17,1},{25,9},{2,18},{10... | collective-permute-start | bytes 1327112 | tf_op jit(solution)/shard_map/ppermute | solution.py:357
  16.1 10.2 %collective-permute-start.3 = (bf16[72,3072]{1,0:T(8,128)(2,1)S(1)}, bf16[72,3072]{1,0:T(8,128)(2,1)}, u32[]{:S(2)}, u32[]{:S(2)}) collective-permute-start(bf16[72,3072]{1,0:T(8,128)(2,1)S(1)} %collective-permute-done.refs_1_), channel_id=1, source_target_pairs={{0,1},{1,0},{2,3},{3,2},{4,5},{5,4},{6,7},{7,6},{8,9},{9,8},{10,11... | collective-permute-start | bytes 1327112 | tf_op jit(solution)/shard_map/ppermute | solution.py:360
  17.4 9.9 %collective-permute-start.1 = (bf16[72,3072]{1,0:T(8,128)(2,1)S(1)}, bf16[72,3072]{1,0:T(8,128)(2,1)S(1)}, u32[]{:S(2)}, u32[]{:S(2)}) collective-permute-start(bf16[72,3072]{1,0:T(8,128)(2,1)S(1)} %pack.1.refs_0_), channel_id=1, source_target_pairs={{0,6},{1,7},{2,0},{3,1},{4,2},{5,3},{6,4},{7,5},{8,14},{9,15},{10,... | collective-permute-start | bytes 1327112 | tf_op jit(solution)/shard_map/ppermute | solution.py:363
  19.5 9.7 %collective-permute-start.24 = (bf16[72,3072]{1,0:T(8,128)(2,1)S(1)}, bf16[72,3072]{1,0:T(8,128)(2,1)S(1)}, u32[]{:S(2)}, u32[]{:S(2)}) collective-permute-start(bf16[72,3072]{1,0:T(8,128)(2,1)S(1)} %collective-permute-done.refs_1_), channel_id=1, source_target_pairs={{0,16},{8,24},{16,0},{24,8},{1,17},{9,25},{17,1},{25,9},{2,18},{10... | collective-permute-start | bytes 1327112 | tf_op jit(solution)/shard_map/ppermute | solution.py:357
  19.7 16.0 %collective-permute-start.23 = (bf16[72,3072]{1,0:T(8,128)(2,1)S(1)}, bf16[72,3072]{1,0:T(8,128)(2,1)S(1)}, u32[]{:S(2)}, u32[]{:S(2)}) collective-permute-start(bf16[72,3072]{1,0:T(8,128)(2,1)S(1)} %collective-permute-done.22.refs_0_), channel_id=1, source_target_pairs={{0,1},{1,0},{2,3},{3,2},{4,5},{5,4},{6,7},{7,6},{8,9},{9,8},{10,11... | collective-permute-start | bytes 1327112 | tf_op jit(solution)/shard_map/ppermute | solution.py:360
  26.4 12.1 %collective-permute-start.25 = (bf16[72,3072]{1,0:T(8,128)(2,1)}, bf16[72,3072]{1,0:T(8,128)(2,1)S(1)}, u32[]{:S(2)}, u32[]{:S(2)}) collective-permute-start(bf16[72,3072]{1,0:T(8,128)(2,1)} %collective-permute-done.3.refs_4_), channel_id=1, source_target_pairs={{0,16},{8,24},{16,0},{24,8},{1,17},{9,25},{17,1},{25,9},{2,18},{10... | collective-permute-start | bytes 1327112 | tf_op jit(solution)/shard_map/ppermute | solution.py:357
  27.3 30.7 %collective-permute-start.8 = (bf16[72,3072]{1,0:T(8,128)(2,1)S(1)}, bf16[72,3072]{1,0:T(8,128)(2,1)S(1)}, u32[]{:S(2)}, u32[]{:S(2)}) collective-permute-start(bf16[72,3072]{1,0:T(8,128)(2,1)S(1)} %collective-permute-done.refs_1_), channel_id=1, source_target_pairs={{0,2},{1,3},{2,4},{3,5},{4,6},{5,7},{6,0},{7,1},{8,10},{9,11},{10,... | collective-permute-start | bytes 1327112 | tf_op jit(solution)/shard_map/ppermute | solution.py:363
  28.6 29.4 %collective-permute-start.2 = (bf16[72,3072]{1,0:T(8,128)(2,1)S(1)}, bf16[72,3072]{1,0:T(8,128)(2,1)}, u32[]{:S(2)}, u32[]{:S(2)}) collective-permute-start(bf16[72,3072]{1,0:T(8,128)(2,1)S(1)} %pack.1.refs_0_), channel_id=1, source_target_pairs={{0,1},{1,0},{2,3},{3,2},{4,5},{5,4},{6,7},{7,6},{8,9},{9,8},{10,11... | collective-permute-start | bytes 1327112 | tf_op jit(solution)/shard_map/ppermute | solution.py:360
  29.2 29.1 %collective-permute-start.4 = (bf16[72,3072]{1,0:T(8,128)(2,1)S(1)}, bf16[72,3072]{1,0:T(8,128)(2,1)}, u32[]{:S(2)}, u32[]{:S(2)}) collective-permute-start(bf16[72,3072]{1,0:T(8,128)(2,1)S(1)} %collective-permute-done.1.refs_2_), channel_id=1, source_target_pairs={{0,1},{1,0},{2,3},{3,2},{4,5},{5,4},{6,7},{7,6},{8,9},{9,8},{10,11... | collective-permute-start | bytes 1327112 | tf_op jit(solution)/shard_map/ppermute | solution.py:360
  35.7 43.6 %collective-permute-start.12 = (bf16[72,3072]{1,0:T(8,128)(2,1)S(1)}, bf16[72,3072]{1,0:T(8,128)(2,1)S(1)}, u32[]{:S(2)}, u32[]{:S(2)}) collective-permute-start(bf16[72,3072]{1,0:T(8,128)(2,1)S(1)} %collective-permute-done.1.refs_2_), channel_id=1, source_target_pairs={{0,16},{8,24},{16,0},{24,8},{1,17},{9,25},{17,1},{25,9},{2,18},{10... | collective-permute-start | bytes 1327112 | tf_op jit(solution)/shard_map/ppermute | solution.py:357
  38.4 2.8 %copy-start = (bf16[3072,1024]{1,0:T(8,128)(2,1)S(1)}, bf16[3072,1024]{1,0:T(8,128)(2,1)}, u32[]{:S(2)}) copy-start(bf16[3072,1024]{1,0:T(8,128)(2,1)} %refs_8_.3) | copy-start | bytes 18874372
  46.8 11.5 %copy-start.1 = (bf16[3072,1024]{1,0:T(8,128)(2,1)S(1)}, bf16[3072,1024]{1,0:T(8,128)(2,1)}, u32[]{:S(2)}) copy-start(bf16[3072,1024]{1,0:T(8,128)(2,1)} %refs_8_.3) | copy-start | bytes 18874372
  52.3 29.2 %copy-start.13 = (bf16[144,3072]{1,0:T(8,128)(2,1)}, bf16[144,3072]{1,0:T(8,128)(2,1)S(1)}, u32[]{:S(2)}) copy-start(bf16[144,3072]{1,0:T(8,128)(2,1)S(1)} %get-tuple-element.39.refs_4_) | copy-start | bytes 2654212
  52.3 28.2 %collective-permute-start.29 = (bf16[144,1536]{1,0:T(8,128)(2,1)S(1)}, bf16[144,1536]{1,0:T(8,128)(2,1)S(1)}, u32[]{:S(2)}, u32[]{:S(2)}) collective-permute-start(bf16[144,1536]{1,0:T(8,128)(2,1)S(1)} %get-tuple-element.45), channel_id=1, source_target_pairs={{0,8},{8,0},{16,24},{24,16},{1,9},{9,1},{17,25},{25,17},{2,10},{10... | collective-permute-start | bytes 1327112 | tf_op jit(solution)/shard_map/ppermute | solution.py:354
  58.0 11.8 %collective-permute-start.9 = (bf16[72,3072]{1,0:T(8,128)(2,1)S(1)}, bf16[72,3072]{1,0:T(8,128)(2,1)S(1)}, u32[]{:S(2)}, u32[]{:S(2)}) collective-permute-start(bf16[72,3072]{1,0:T(8,128)(2,1)S(1)} %collective-permute-done.8.refs_0_), channel_id=1, source_target_pairs={{0,1},{1,0},{2,3},{3,2},{4,5},{5,4},{6,7},{7,6},{8,9},{9,8},{10,11... | collective-permute-start | bytes 1327112 | tf_op jit(solution)/shard_map/ppermute | solution.py:360
  58.0 23.5 %collective-permute-start.13 = (bf16[72,3072]{1,0:T(8,128)(2,1)S(1)}, bf16[72,3072]{1,0:T(8,128)(2,1)}, u32[]{:S(2)}, u32[]{:S(2)}) collective-permute-start(bf16[72,3072]{1,0:T(8,128)(2,1)S(1)} %collective-permute-done.8.refs_0_), channel_id=1, source_target_pairs={{0,16},{8,24},{16,0},{24,8},{1,17},{9,25},{17,1},{25,9},{2,18},{10... | collective-permute-start | bytes 1327112 | tf_op jit(solution)/shard_map/ppermute | solution.py:357
  68.4 10.3 %copy-start.11 = (bf16[224,3072]{1,0:T(8,128)(2,1)}, bf16[224,3072]{1,0:T(8,128)(2,1)S(1)}, u32[]{:S(2)}) copy-start(bf16[224,3072]{1,0:T(8,128)(2,1)S(1)} %get-tuple-element.37.refs_0_) | copy-start | bytes 4128772
  68.4 10.3 %copy-start.23 = (bf16[224,1536]{1,0:T(8,128)(2,1)}, bf16[224,1536]{1,0:T(8,128)(2,1)S(1)}, u32[]{:S(2)}) copy-start(bf16[224,1536]{1,0:T(8,128)(2,1)S(1)} %get-tuple-element.40.refs_6_) | copy-start | bytes 2064388
  68.4 63.8 %collective-permute-start.20 = (bf16[224,3072]{1,0:T(8,128)(2,1)S(1)}, bf16[224,3072]{1,0:T(8,128)(2,1)S(1)}, u32[]{:S(2)}, u32[]{:S(2)}) collective-permute-start(bf16[224,3072]{1,0:T(8,128)(2,1)S(1)} %get-tuple-element.37.refs_0_), channel_id=1, source_target_pairs={{0,8},{8,0},{16,24},{24,16},{1,9},{9,1},{17,25},{25,17},{2,10},{10... | collective-permute-start | bytes 4128776 | tf_op jit(solution)/shard_map/ppermute | solution.py:354
  69.8 12.1 %collective-permute-start.14 = (bf16[72,3072]{1,0:T(8,128)(2,1)}, bf16[72,3072]{1,0:T(8,128)(2,1)S(1)}, u32[]{:S(2)}, u32[]{:S(2)}) collective-permute-start(bf16[72,3072]{1,0:T(8,128)(2,1)} %collective-permute-done.4.refs_5_), channel_id=1, source_target_pairs={{0,16},{8,24},{16,0},{24,8},{1,17},{9,25},{17,1},{25,9},{2,18},{10... | collective-permute-start | bytes 1327112 | tf_op jit(solution)/shard_map/ppermute | solution.py:357
  79.4 52.8 %copy-start.15 = (bf16[80,3072]{1,0:T(8,128)(2,1)}, bf16[80,3072]{1,0:T(8,128)(2,1)S(1)}, u32[]{:S(2)}) copy-start(bf16[80,3072]{1,0:T(8,128)(2,1)S(1)} %get-tuple-element.38.refs_2_) | copy-start | bytes 1474564
  79.4 51.1 %copy-start.9 = (s32[128,2]{0,1:T(2,128)S(1)}, s32[128,2]{0,1:T(2,128)}, u32[]{:S(2)}) copy-start(s32[128,2]{0,1:T(2,128)} %param.9) | copy-start | bytes 3076
  79.4 52.8 %copy-start.6 = (bf16[72,3072]{1,0:T(8,128)(2,1)}, bf16[72,3072]{1,0:T(8,128)(2,1)S(1)}, u32[]{:S(2)}) copy-start(bf16[72,3072]{1,0:T(8,128)(2,1)S(1)} %collective-permute-done.12.refs_0_) | copy-start | bytes 1327108
  79.4 3.2 %collective-permute-start.28 = (bf16[80,1536]{1,0:T(8,128)(2,1)S(1)}, bf16[80,1536]{1,0:T(8,128)(2,1)S(1)}, u32[]{:S(2)}, u32[]{:S(2)}) collective-permute-start(bf16[80,1536]{1,0:T(8,128)(2,1)S(1)} %get-tuple-element.43), channel_id=1, source_target_pairs={{0,8},{8,0},{16,24},{24,16},{1,9},{9,1},{17,25},{25,17},{2,10},{10... | collective-permute-start | bytes 737288 | tf_op jit(solution)/shard_map/ppermute | solution.py:354
  80.5 49.5 %copy-start.19 = (bf16[144,1536]{1,0:T(8,128)(2,1)}, bf16[144,1536]{1,0:T(8,128)(2,1)S(1)}, u32[]{:S(2)}) copy-start(bf16[144,1536]{1,0:T(8,128)(2,1)S(1)} %collective-permute-done.29.refs_11_) | copy-start | bytes 1327108
  80.5 23.5 %collective-permute-start.5 = (bf16[112,3072]{1,0:T(8,128)(2,1)S(1)}, bf16[112,3072]{1,0:T(8,128)(2,1)S(1)}, u32[]{:S(2)}, u32[]{:S(2)}) collective-permute-start(bf16[112,3072]{1,0:T(8,128)(2,1)S(1)} %get-tuple-element.30), channel_id=1, source_target_pairs={{0,1},{1,0},{2,3},{3,2},{4,5},{5,4},{6,7},{7,6},{8,9},{9,8},{10,11... | collective-permute-start | bytes 2064392 | tf_op jit(solution)/shard_map/ppermute | solution.py:360
  81.5 24.0 %collective-permute-start.26 = (bf16[144,3072]{1,0:T(8,128)(2,1)S(1)}, bf16[144,3072]{1,0:T(8,128)(2,1)S(1)}, u32[]{:S(2)}, u32[]{:S(2)}) collective-permute-start(bf16[144,3072]{1,0:T(8,128)(2,1)S(1)} %get-tuple-element.39.refs_4_), channel_id=1, source_target_pairs={{0,8},{8,0},{16,24},{24,16},{1,9},{9,1},{17,25},{25,17},{2,10},{10... | collective-permute-start | bytes 2654216 | tf_op jit(solution)/shard_map/ppermute | solution.py:354
  81.9 23.5 %collective-permute-start.27 = (bf16[224,1536]{1,0:T(8,128)(2,1)S(1)}, bf16[224,1536]{1,0:T(8,128)(2,1)S(1)}, u32[]{:S(2)}, u32[]{:S(2)}) collective-permute-start(bf16[224,1536]{1,0:T(8,128)(2,1)S(1)} %get-tuple-element.41), channel_id=1, source_target_pairs={{0,8},{8,0},{16,24},{24,16},{1,9},{9,1},{17,25},{25,17},{2,10},{10... | collective-permute-start | bytes 2064392 | tf_op jit(solution)/shard_map/ppermute | solution.py:354
  82.6 20.2 %collective-permute-start.10 = (bf16[40,3072]{1,0:T(8,128)(2,1)S(1)}, bf16[40,3072]{1,0:T(8,128)(2,1)S(1)}, u32[]{:S(2)}, u32[]{:S(2)}) collective-permute-start(bf16[40,3072]{1,0:T(8,128)(2,1)S(1)} %get-tuple-element.36), channel_id=1, source_target_pairs={{0,1},{1,0},{2,3},{3,2},{4,5},{5,4},{6,7},{7,6},{8,9},{9,8},{10,11... | collective-permute-start | bytes 737288 | tf_op jit(solution)/shard_map/ppermute | solution.py:360
  102.8 10.8 %collective-permute-start.15 = (bf16[72,3072]{1,0:T(8,128)(2,1)S(1)}, bf16[72,3072]{1,0:T(8,128)(2,1)S(1)}, u32[]{:S(2)}, u32[]{:S(2)}) collective-permute-start(bf16[72,3072]{1,0:T(8,128)(2,1)S(1)} %collective-permute-done.9.refs_1_), channel_id=1, source_target_pairs={{0,16},{8,24},{16,0},{24,8},{1,17},{9,25},{17,1},{25,9},{2,18},{10... | collective-permute-start | bytes 1327112 | tf_op jit(solution)/shard_map/ppermute | solution.py:357
  104.0 26.0 %collective-permute-start.21 = (bf16[80,3072]{1,0:T(8,128)(2,1)S(1)}, bf16[80,3072]{1,0:T(8,128)(2,1)S(1)}, u32[]{:S(2)}, u32[]{:S(2)}) collective-permute-start(bf16[80,3072]{1,0:T(8,128)(2,1)S(1)} %get-tuple-element.38.refs_2_), channel_id=1, source_target_pairs={{0,8},{8,0},{16,24},{24,16},{1,9},{9,1},{17,25},{25,17},{2,10},{10... | collective-permute-start | bytes 1474568 | tf_op jit(solution)/shard_map/ppermute | solution.py:354
  105.1 27.1 %copy-start.18 = (bf16[144,1536]{1,0:T(8,128)(2,1)S(1)}, bf16[144,1536]{1,0:T(8,128)(2,1)}, u32[]{:S(2)}) copy-start(bf16[144,1536]{1,0:T(8,128)(2,1)} %copy-done.17) | copy-start | bytes 1327108
  105.1 27.1 %copy-start.22 = (bf16[80,1536]{1,0:T(8,128)(2,1)S(1)}, bf16[80,1536]{1,0:T(8,128)(2,1)}, u32[]{:S(2)}) copy-start(bf16[80,1536]{1,0:T(8,128)(2,1)} %copy-done.21) | copy-start | bytes 737284
  105.2 27.1 %copy-start.12 = (bf16[224,3072]{1,0:T(8,128)(2,1)S(1)}, bf16[224,3072]{1,0:T(8,128)(2,1)}, u32[]{:S(2)}) copy-start(bf16[224,3072]{1,0:T(8,128)(2,1)} %copy-done.11) | copy-start | bytes 4128772
  105.2 27.1 %copy-start.14 = (bf16[144,3072]{1,0:T(8,128)(2,1)S(1)}, bf16[144,3072]{1,0:T(8,128)(2,1)}, u32[]{:S(2)}) copy-start(bf16[144,3072]{1,0:T(8,128)(2,1)} %copy-done.13) | copy-start | bytes 2654212
  105.2 35.7 %slice-start.2 = ((s8[6291456]{0:T(1024)(128)(4,1)}), s8[4194304]{0:T(1024)(128)(4,1)S(1)}, s32[]{:S(2)}) async-start(s8[6291456]{0:T(1024)(128)(4,1)} %bitcast.6), calls=%async_computation.2 | async-start | bytes 8388608
  105.4 16.2 %collective-permute-start.11 = (bf16[40,3072]{1,0:T(8,128)(2,1)S(1)}, bf16[40,3072]{1,0:T(8,128)(2,1)S(1)}, u32[]{:S(2)}, u32[]{:S(2)}) collective-permute-start(bf16[40,3072]{1,0:T(8,128)(2,1)S(1)} %merge.3), channel_id=1, source_target_pairs={{0,4},{1,5},{2,6},{3,7},{4,0},{5,1},{6,2},{7,3},{8,12},{9,13},{10,... | collective-permute-start | bytes 737288 | tf_op jit(solution)/shard_map/ppermute | solution.py:363
  105.5 23.7 %collective-permute-start.6 = (bf16[40,3072]{1,0:T(8,128)(2,1)S(1)}, bf16[40,3072]{1,0:T(8,128)(2,1)S(1)}, u32[]{:S(2)}, u32[]{:S(2)}) collective-permute-start(bf16[40,3072]{1,0:T(8,128)(2,1)S(1)} %get-tuple-element.32), channel_id=1, source_target_pairs={{0,6},{1,7},{2,0},{3,1},{4,2},{5,3},{6,4},{7,5},{8,14},{9,15},{10,... | collective-permute-start | bytes 737288 | tf_op jit(solution)/shard_map/ppermute | solution.py:363
  113.6 16.4 %collective-permute-start.7 = (bf16[40,3072]{1,0:T(8,128)(2,1)S(1)}, bf16[40,3072]{1,0:T(8,128)(2,1)S(1)}, u32[]{:S(2)}, u32[]{:S(2)}) collective-permute-start(bf16[40,3072]{1,0:T(8,128)(2,1)S(1)} %get-tuple-element.33), channel_id=1, source_target_pairs={{0,2},{1,3},{2,4},{3,5},{4,6},{5,7},{6,0},{7,1},{8,10},{9,11},{10,... | collective-permute-start | bytes 737288 | tf_op jit(solution)/shard_map/ppermute | solution.py:363
  121.7 19.2 %collective-permute-start.16 = (bf16[72,3072]{1,0:T(8,128)(2,1)S(1)}, bf16[72,3072]{1,0:T(8,128)(2,1)S(1)}, u32[]{:S(2)}, u32[]{:S(2)}) collective-permute-start(bf16[72,3072]{1,0:T(8,128)(2,1)S(1)} %collective-permute-done.12.refs_0_), channel_id=1, source_target_pairs={{0,8},{8,0},{16,24},{24,16},{1,9},{9,1},{17,25},{25,17},{2,10},{10... | collective-permute-start | bytes 1327112 | tf_op jit(solution)/shard_map/ppermute | solution.py:354
  129.2 11.7 %collective-permute-start.17 = (bf16[72,3072]{1,0:T(8,128)(2,1)}, bf16[72,3072]{1,0:T(8,128)(2,1)S(1)}, u32[]{:S(2)}, u32[]{:S(2)}) collective-permute-start(bf16[72,3072]{1,0:T(8,128)(2,1)} %collective-permute-done.13.refs_1_), channel_id=1, source_target_pairs={{0,8},{8,0},{16,24},{24,16},{1,9},{9,1},{17,25},{25,17},{2,10},{10... | collective-permute-start | bytes 1327112 | tf_op jit(solution)/shard_map/ppermute | solution.py:354
  130.0 10.9 %collective-permute-start.18 = (bf16[72,3072]{1,0:T(8,128)(2,1)S(1)}, bf16[72,3072]{1,0:T(8,128)(2,1)S(1)}, u32[]{:S(2)}, u32[]{:S(2)}) collective-permute-start(bf16[72,3072]{1,0:T(8,128)(2,1)S(1)} %collective-permute-done.14.refs_2_), channel_id=1, source_target_pairs={{0,8},{8,0},{16,24},{24,16},{1,9},{9,1},{17,25},{25,17},{2,10},{10... | collective-permute-start | bytes 1327112 | tf_op jit(solution)/shard_map/ppermute | solution.py:354
  130.0 10.9 %collective-permute-start.19 = (bf16[72,3072]{1,0:T(8,128)(2,1)S(1)}, bf16[72,3072]{1,0:T(8,128)(2,1)S(1)}, u32[]{:S(2)}, u32[]{:S(2)}) collective-permute-start(bf16[72,3072]{1,0:T(8,128)(2,1)S(1)} %collective-permute-done.15.refs_3_), channel_id=1, source_target_pairs={{0,8},{8,0},{16,24},{24,16},{1,9},{9,1},{17,25},{25,17},{2,10},{10... | collective-permute-start | bytes 1327112 | tf_op jit(solution)/shard_map/ppermute | solution.py:354
  132.2 8.7 %slice-start = ((s8[6291456]{0:T(1024)(128)(4,1)}), s8[4194304]{0:T(1024)(128)(4,1)S(1)}, s32[]{:S(2)}) async-start(s8[6291456]{0:T(1024)(128)(4,1)} %bitcast.4), calls=%async_computation | async-start | bytes 8388608
  135.8 5.2 %slice-start.1 = ((s8[6291456]{0:T(1024)(128)(4,1)}), s8[2097152]{0:T(1024)(128)(4,1)S(1)}, s32[]{:S(2)}) async-start(s8[6291456]{0:T(1024)(128)(4,1)} %bitcast.4), calls=%async_computation.1 | async-start | bytes 4194304
  135.8 5.2 %slice-start.3 = ((s8[6291456]{0:T(1024)(128)(4,1)}), s8[2097152]{0:T(1024)(128)(4,1)S(1)}, s32[]{:S(2)}) async-start(s8[6291456]{0:T(1024)(128)(4,1)} %bitcast.6), calls=%async_computation.3 | async-start | bytes 4194304
  135.8 5.2 %copy-start.7 = (bf16[72,3072]{1,0:T(8,128)(2,1)S(1)}, bf16[72,3072]{1,0:T(8,128)(2,1)}, u32[]{:S(2)}) copy-start(bf16[72,3072]{1,0:T(8,128)(2,1)} %copy-done.6) | copy-start | bytes 1327108
  (11 other events, 14.1 us)

commit v4 on v3

--- a/solution.py
+++ b/solution.py
@@ -78,7 +78,7 @@
     values = (ids, probs, tokens, cotangent)
     return pl.pallas_call(
         pack_kernel,
-        in_specs=[pl.BlockSpec(memory_space=pl.ANY)] * 4,
+        in_specs=[pl.BlockSpec(memory_space=pltpu.HBM)] * 4,
         out_shape=shape((2 * CAP, tokens.shape[1])),
         scratch_shapes=[pltpu.VMEM(v.shape, v.dtype) for v in values]
         + [pltpu.SemaphoreType.DMA((4,))],
@@ -318,6 +318,26 @@
     )(place, *blocks, gate, up, down, *early)
 
 
+def ready_kernel(place, block, gate, up, down, out):
+    out[0] = place[0]
+    out[1] = place[1]
+
+
+def ready(place, block, gate, up, down):
+    in_vmem, in_smem = pl.BlockSpec(memory_space=pltpu.VMEM), pl.BlockSpec(memory_space=pltpu.SMEM)
+    return pl.pallas_call(
+        ready_kernel,
+        in_specs=[in_smem, in_vmem, in_vmem, in_vmem, in_vmem],
+        out_specs=in_smem,
+        out_shape=shape((2,), jnp.int32),
+        compiler_params=params(LIMIT),
+        cost_estimate=pl.CostEstimate(
+            flops=0, bytes_accessed=6 * gate.size, transcendentals=0
+        ),
+        name="ready",
+    )(place, block, gate, up, down)
+
+
 def merge_kernel(n, keep, came, *outs):
     mid = MAIN * n
     kept, other = keep[mid:, :].astype(FULL), came[mid:, :].astype(FULL)
@@ -371,16 +391,18 @@
     weights = dict(gate=gate_weight, up=up_weight, down=down_weight)
 
     b0 = pack(ids, probs, tokens, cotangent)
-    z1 = over_z(b0, 1)
-    x0, y0 = over_x(b0), over_y(b0)
-    x1, y1 = over_x(z1), over_y(z1)
-    z3 = over_z(after(b0, z1), -1)
-    yx0 = over_x(y0)
-    z2 = over_z(after(z1, z3), 1)
-    x3, y3 = over_x(z3), over_y(z3)
-    yx1 = over_y(x1)
-    x2, y2 = over_x(z2), over_y(z2)
-    yx3, yx2 = over_y(x3), over_y(x2)
+    place = ready(place, b0, **weights)
+    z1, x0, y0, z3 = over_z(b0, 1), over_x(b0), over_y(b0), over_z(b0, -1)
+    xy0 = over_y(after(x0, y0))
+    z1 = after(z1, x0, y0)
+    z2, x1, y1 = over_z(z1, 1), over_x(z1), over_y(z1)
+    x3 = over_x(z3)
+    xy1 = over_y(after(x1, y1))
+    x2 = over_x(after(z2, x1))
+    y2 = over_y(after(z2, xy0))
+    y3 = over_z(after(y0, z2), -1)
+    xy3 = over_z(after(xy0, z2), -1)
+    xy2 = over_y(after(x2, xy1))
 
     acts, parts = [], []
 
@@ -396,9 +418,9 @@
     pieces += merge(1, keep, over_x(send))
     share(*second)
     returned = [pieces[0], over_z(pieces[1], -1), over_z(pieces[2], 1), over_z(pieces[3], 2)]
-    share(*run([y0, yx0, y1, yx1], back=False))
+    share(*run([y0, xy0, y1, xy1, y3, xy3], back=False))
     early = grads(acts, parts, part, gate_weight.shape[1])
-    last = [y3, y2, yx3, yx2]
+    last = [y2, xy2]
     last = last + [over_core(b) for b in last]
     gate_grad, up_grad, down_grad = finish(last, place=place, early=early, **weights)
     return unpack(ids, returned), gate_grad, up_grad, down_grad

time: 154 us -> 145 us (0.942)
  the two profiles are of different devices: /device:TPU:13 before, /device:TPU:0 now
where the time goes in v4:
time: 145 us; the launch traced here: 144 us
  waiting for transfers between devices  51.4 us (35%)
  Pallas kernels  48.8 us (34%)
  starting transfers between devices  27.3 us (19%)
  local copies, waits for them, and re-layouts  15.3 us (11%)
    ppermute x8, waiting for transfers between devices, over_z(): lax.ppermute(v, 'expert', [(i, (i + 2 * by) % n_expert) for i in range(n_...  28.6 us
    pallas_call x3, Pallas kernels, forward(): pl.pallas_call(functools.partial(forward_kernel, n, back), in_specs=[pl.B...  26.5 us
    unnamed x42, local copies, waits for them, and re-layouts  15.3 us
    ppermute x8, starting transfers between devices, over_z(): lax.ppermute(v, 'expert', [(i, (i + 2 * by) % n_expert) for i in range(n_...  14.3 us
    ppermute x6, waiting for transfers between devices, over_y(): return lax.ppermute(v, 'dp', y_pairs)  14.1 us
    pallas_call x1, Pallas kernels, finish(): pl.pallas_call(functools.partial(finish_kernel, n), in_specs=[pl.BlockSpe...  10.9 us
    ppermute x6, waiting for transfers between devices, over_x(): return lax.ppermute(v, 'expert', x_pairs)  8.29 us
    pallas_call x1, Pallas kernels, grads(): pl.pallas_call(functools.partial(grads_kernel, n), in_specs=[in_vmem] * (...  7.48 us
  transfers between devices with their start and end apart: 28, of which 10 were waited for; matrix products, arithmetic and copies ran while one was open for 0% of the time, Pallas kernels for 26%

profile of v4, /device:TPU:0, one launch (start us, length us, event | category | flops | bytes accessed | tf_op | source)
XLA Modules:
  0.0 143.8 jit_solution(15459767019216228447)
XLA Ops:
  0.6 1.1 copy-done.6
  1.8 1.1 copy-done.7
  2.9 0.7 copy-done.8
  3.6 0.7 copy-done.10
  4.3 0.8 pack.1.block.refs_0_
  5.1 3.0 %collective-permute-start.2 = (bf16[72,3072]{1,0:T(8,128)(2,1)S(1)}, bf16[72,3072]{1,0:T(8,128)(2,1)S(1)}, u32[]{:S(2)}, u32[]{:S(2)}) collective-permute-start(bf16[72,3072]{1,0:T(8,128)(2,1)S(1)} %pack.1.block.refs_0_), channel_id=1, source_target_pairs={{0,16},{8,24},{16,0},{24,8},{1,17},{9,25},{17,1},{25,9},{2,18},{10... | collective-permute-start | bytes 1327112 | tf_op jit(solution)/shard_map/ppermute | solution.py:377
  8.1 1.5 %collective-permute-start.1 = (bf16[72,3072]{1,0:T(8,128)(2,1)S(1)}, bf16[72,3072]{1,0:T(8,128)(2,1)}, u32[]{:S(2)}, u32[]{:S(2)}) collective-permute-start(bf16[72,3072]{1,0:T(8,128)(2,1)S(1)} %pack.1.block.refs_0_), channel_id=1, source_target_pairs={{0,1},{1,0},{2,3},{3,2},{4,5},{5,4},{6,7},{7,6},{8,9},{9,8},{10,11... | collective-permute-start | bytes 1327112 | tf_op jit(solution)/shard_map/ppermute | solution.py:380
  9.6 1.6 %collective-permute-start = (bf16[72,3072]{1,0:T(8,128)(2,1)S(1)}, bf16[72,3072]{1,0:T(8,128)(2,1)}, u32[]{:S(2)}, u32[]{:S(2)}) collective-permute-start(bf16[72,3072]{1,0:T(8,128)(2,1)S(1)} %pack.1.block.refs_0_), channel_id=1, source_target_pairs={{0,2},{1,3},{2,4},{3,5},{4,6},{5,7},{6,0},{7,1},{8,10},{9,11},{10,... | collective-permute-start | bytes 1327112 | tf_op jit(solution)/shard_map/ppermute | solution.py:383
  11.2 2.2 %collective-permute-start.3 = (bf16[72,3072]{1,0:T(8,128)(2,1)S(1)}, bf16[72,3072]{1,0:T(8,128)(2,1)}, u32[]{:S(2)}, u32[]{:S(2)}) collective-permute-start(bf16[72,3072]{1,0:T(8,128)(2,1)S(1)} %pack.1.block.refs_0_), channel_id=1, source_target_pairs={{0,6},{1,7},{2,0},{3,1},{4,2},{5,3},{6,4},{7,5},{8,14},{9,15},{10,... | collective-permute-start | bytes 1327112 | tf_op jit(solution)/shard_map/ppermute | solution.py:383
  13.4 4.8 %collective-permute-done.2.refs_0_ = bf16[72,3072]{1,0:T(8,128)(2,1)S(1)} collective-permute-done((bf16[72,3072]{1,0:T(8,128)(2,1)S(1)}, bf16[72,3072]{1,0:T(8,128)(2,1)S(1)}, u32[]{:S(2)}, u32[]{:S(2)}) %collective-permute-start.2) | collective-permute-done | bytes 442400 | tf_op jit(solution)/shard_map/ppermute | solution.py:377
  18.3 1.6 %collective-permute-done.1.refs_3_ = bf16[72,3072]{1,0:T(8,128)(2,1)} collective-permute-done((bf16[72,3072]{1,0:T(8,128)(2,1)S(1)}, bf16[72,3072]{1,0:T(8,128)(2,1)}, u32[]{:S(2)}, u32[]{:S(2)}) %collective-permute-start.1) | collective-permute-done | bytes 442400 | tf_op jit(solution)/shard_map/ppermute | solution.py:380
  19.8 0.4 collective-permute-start.13
  20.2 4.5 %collective-permute-done.refs_1_ = bf16[72,3072]{1,0:T(8,128)(2,1)} collective-permute-done((bf16[72,3072]{1,0:T(8,128)(2,1)S(1)}, bf16[72,3072]{1,0:T(8,128)(2,1)}, u32[]{:S(2)}, u32[]{:S(2)}) %collective-permute-start) | collective-permute-done | bytes 442400 | tf_op jit(solution)/shard_map/ppermute | solution.py:383
  24.6 0.5 collective-permute-start.15
  25.5 7.4 %collective-permute-done.3.refs_2_ = bf16[72,3072]{1,0:T(8,128)(2,1)} collective-permute-done((bf16[72,3072]{1,0:T(8,128)(2,1)S(1)}, bf16[72,3072]{1,0:T(8,128)(2,1)}, u32[]{:S(2)}, u32[]{:S(2)}) %collective-permute-start.3) | collective-permute-done | bytes 442400 | tf_op jit(solution)/shard_map/ppermute | solution.py:383
  32.9 0.5 collective-permute-start.5
  33.5 2.8 %copy-done = bf16[3072,1024]{1,0:T(8,128)(2,1)S(1)} copy-done((bf16[3072,1024]{1,0:T(8,128)(2,1)S(1)}, bf16[3072,1024]{1,0:T(8,128)(2,1)}, u32[]{:S(2)}) %copy-start) | copy-done | bytes 6291480
  36.3 2.8 %copy-done.2 = bf16[3072,1024]{1,0:T(8,128)(2,1)S(1)} copy-done((bf16[3072,1024]{1,0:T(8,128)(2,1)S(1)}, bf16[3072,1024]{1,0:T(8,128)(2,1)}, u32[]{:S(2)}) %copy-start.2) | copy-done | bytes 6291480
  39.1 2.8 %copy-done.4 = bf16[1024,3072]{1,0:T(8,128)(2,1)S(1)} copy-done((bf16[1024,3072]{1,0:T(8,128)(2,1)S(1)}, bf16[1024,3072]{1,0:T(8,128)(2,1)}, u32[]{:S(2)}) %copy-start.4) | copy-done | bytes 6291480
  41.9 1.1 ready.1.place
  43.0 0.3 collective-permute-start.14
  43.4 3.2 %collective-permute-start.22 = (bf16[72,3072]{1,0:T(8,128)(2,1)S(1)}, bf16[72,3072]{1,0:T(8,128)(2,1)S(1)}, u32[]{:S(2)}, u32[]{:S(2)}) collective-permute-start(bf16[72,3072]{1,0:T(8,128)(2,1)S(1)} %collective-permute-done.2.refs_0_), channel_id=1, source_target_pairs={{0,6},{1,7},{2,0},{3,1},{4,2},{5,3},{6,4},{7,5},{8,14},{9,15},{10,... | collective-permute-start | bytes 1327112 | tf_op jit(solution)/shard_map/ppermute | solution.py:383
  46.6 2.0 %collective-permute-start.23 = (bf16[72,3072]{1,0:T(8,128)(2,1)S(1)}, bf16[72,3072]{1,0:T(8,128)(2,1)S(1)}, u32[]{:S(2)}, u32[]{:S(2)}) collective-permute-start(bf16[72,3072]{1,0:T(8,128)(2,1)S(1)} %collective-permute-done.13.refs_1_), channel_id=1, source_target_pairs={{0,6},{1,7},{2,0},{3,1},{4,2},{5,3},{6,4},{7,5},{8,14},{9,15},{10,... | collective-permute-start | bytes 1327112 | tf_op jit(solution)/shard_map/ppermute | solution.py:383
  49.0 0.9 collective-permute-start.16
  49.9 11.3 %forward_back.2 = (bf16[224,3072]{1,0:T(8,128)(2,1)S(1)}, bf16[224,1536]{1,0:T(8,128)(2,1)S(1)}, bf16[224,1536]{1,0:T(8,128)(2,1)}, bf16[112,3072]{1,0:T(8,128)(2,1)}, bf16[112,3072]{1,0:T(8,128)(2,1)S(1)}) custom-call(s32[2]{0:T(128)S(1)} %ready.1.place, bf16[72,3072]{1,0:T(8,128)(2,1)S(1)} %pack.1.block.refs_0_, ...), custom_call_target="tpu_custom_call" | custom-call | flops 7046430720 | bytes 22315008 | tf_op jit(solution)/shard_map/forward_back/pallas_call | solution.py:202
  61.2 0.8 copy-done.19
  62.0 1.2 collective-permute-start.6
  63.2 1.1 collective-permute-done.23.refs_5_
  64.3 0.5 collective-permute-start.20
  64.8 6.3 %forward.1 = (bf16[224,3072]{1,0:T(8,128)(2,1)S(1)}, bf16[224,1536]{1,0:T(8,128)(2,1)S(1)}, bf16[224,1536]{1,0:T(8,128)(2,1)S(1)}) custom-call(s32[2]{0:T(128)S(1)} %ready.1.place, bf16[72,3072]{1,0:T(8,128)(2,1)S(1)} %collective-permute-done.2.refs_0_, bf16[72,3072]{1,0:T(8,128)(2,1)S(1)} %collective-permute-done.13.refs_1_, ...), custom_call_target="tpu_custom_call" | custom-call | flops 4227858432 | bytes 22315008 | tf_op jit(solution)/shard_map/forward/pallas_call | solution.py:202
  71.1 0.8 copy-done.11
  72.0 0.9 copy-done.13
  72.8 8.9 %forward_back.3 = (bf16[80,3072]{1,0:T(8,128)(2,1)S(1)}, bf16[80,1536]{1,0:T(8,128)(2,1)S(1)}, bf16[80,1536]{1,0:T(8,128)(2,1)S(1)}, bf16[40,3072]{1,0:T(8,128)(2,1)S(1)}, bf16[40,3072]{1,0:T(8,128)(2,1)S(1)}) custom-call(s32[2]{0:T(128)S(1)} %ready.1.place, bf16[72,3072]{1,0:T(8,128)(2,1)} %collective-permute-done.9.refs_0_, ...), custom_call_target="tpu_custom_call" | custom-call | flops 2516582400 | bytes 20103168 | tf_op jit(solution)/shard_map/forward_back/pallas_call | solution.py:202
  81.8 1.7 %collective-permute-start.11 = (bf16[40,3072]{1,0:T(8,128)(2,1)S(1)}, bf16[40,3072]{1,0:T(8,128)(2,1)S(1)}, u32[]{:S(2)}, u32[]{:S(2)}) collective-permute-start(bf16[40,3072]{1,0:T(8,128)(2,1)S(1)} %get-tuple-element.42), channel_id=1, source_target_pairs={{0,1},{1,0},{2,3},{3,2},{4,5},{5,4},{6,7},{7,6},{8,9},{9,8},{10,11... | collective-permute-start | bytes 737288 | tf_op jit(solution)/shard_map/ppermute | solution.py:380
  83.5 6.7 %collective-permute-done.11.came = bf16[40,3072]{1,0:T(8,128)(2,1)S(1)} collective-permute-done((bf16[40,3072]{1,0:T(8,128)(2,1)S(1)}, bf16[40,3072]{1,0:T(8,128)(2,1)S(1)}, u32[]{:S(2)}, u32[]{:S(2)}) %collective-permute-start.11) | collective-permute-done | bytes 245792 | tf_op jit(solution)/shard_map/ppermute | solution.py:380
  90.4 0.8 collective-permute-start.12
  91.3 0.4 collective-permute-done.26.refs_9_
  91.8 0.7 copy-done.17
  92.5 4.4 %collective-permute-start.7 = (bf16[40,3072]{1,0:T(8,128)(2,1)S(1)}, bf16[40,3072]{1,0:T(8,128)(2,1)S(1)}, u32[]{:S(2)}, u32[]{:S(2)}) collective-permute-start(bf16[40,3072]{1,0:T(8,128)(2,1)S(1)} %get-tuple-element.38), channel_id=1, source_target_pairs={{0,6},{1,7},{2,0},{3,1},{4,2},{5,3},{6,4},{7,5},{8,14},{9,15},{10,... | collective-permute-start | bytes 737288 | tf_op jit(solution)/shard_map/ppermute | solution.py:383
  96.9 8.4 %collective-permute-done.12.refs_3_ = bf16[40,3072]{1,0:T(8,128)(2,1)S(1)} collective-permute-done((bf16[40,3072]{1,0:T(8,128)(2,1)S(1)}, bf16[40,3072]{1,0:T(8,128)(2,1)S(1)}, u32[]{:S(2)}, u32[]{:S(2)}) %collective-permute-start.12) | collective-permute-done | bytes 245792 | tf_op jit(solution)/shard_map/ppermute | solution.py:383
  105.3 0.5 collective-permute-start.21
  105.9 7.2 %collective-permute-done.8.refs_2_ = bf16[40,3072]{1,0:T(8,128)(2,1)S(1)} collective-permute-done((bf16[40,3072]{1,0:T(8,128)(2,1)S(1)}, bf16[40,3072]{1,0:T(8,128)(2,1)S(1)}, u32[]{:S(2)}, u32[]{:S(2)}) %collective-permute-start.8) | collective-permute-done | bytes 245792 | tf_op jit(solution)/shard_map/ppermute | solution.py:383
  113.0 0.8 collective-permute-start.17
  113.8 1.7 %unpack.1 = bf16[128,3072]{1,0:T(8,128)(2,1)} custom-call(s32[2,128]{1,0:T(2,128)S(1)} %bitcast.5, bf16[40,3072]{1,0:T(8,128)(2,1)S(1)} %get-tuple-element.37.refs_0_, bf16[40,3072]{1,0:T(8,128)(2,1)S(1)} %collective-permute-done.7.refs_1_, bf16[40,3072]{1,0:T(8,128)(2,1)S(1)} %collective-permute-done.8.refs_2_, ...), custom_call_target="tpu_custom_call" | custom-call | tf_op jit(solution)/shard_map/unpack/pallas_call | solution.py:103
  115.5 9.2 %collective-permute-done.17.refs_1_ = bf16[72,3072]{1,0:T(8,128)(2,1)S(1)} collective-permute-done((bf16[72,3072]{1,0:T(8,128)(2,1)S(1)}, bf16[72,3072]{1,0:T(8,128)(2,1)S(1)}, u32[]{:S(2)}, u32[]{:S(2)}) %collective-permute-start.17) | collective-permute-done | bytes 442400 | tf_op jit(solution)/shard_map/ppermute | solution.py:377
  124.8 0.5 collective-permute-start.19
  125.3 7.5 %grads.1 = (bf16[768,1024]{1,0:T(8,128)(2,1)S(1)}, bf16[768,1024]{1,0:T(8,128)(2,1)S(1)}, bf16[1024,768]{1,0:T(8,128)(2,1)S(1)}) custom-call(bf16[224,3072]{1,0:T(8,128)(2,1)S(1)} %get-tuple-element.47.refs_0_, bf16[224,3072]{1,0:T(8,128)(2,1)S(1)} %collective-permute-done.20.refs_1_, bf16[80,3072]{1,0:T(8,128)(2,1)S(1)} %get-tuple-element.48.refs_2_, ...), custom_call_target="tpu_custom_call" | custom-call | flops 4982833152 | bytes 14450688 | tf_op jit(solution)/shard_map/grads/pallas_call | solution.py:255
  132.8 10.9 %finish.1 = (bf16[768,1024]{1,0:T(8,128)(2,1)}, bf16[768,1024]{1,0:T(8,128)(2,1)}, bf16[1024,768]{1,0:T(8,128)(2,1)}) custom-call(s32[2]{0:T(128)S(1)} %ready.1.place, bf16[72,3072]{1,0:T(8,128)(2,1)S(1)} %collective-permute-done.14.refs_0_, bf16[72,3072]{1,0:T(8,128)(2,1)S(1)} %collective-permute-done.17.refs_1_, ...), custom_call_target="tpu_custom_call" | custom-call | flops 3397386240 | bytes 29196288 | tf_op jit(solution)/shard_map/finish/pallas_call | solution.py:302
  (61 shorter events, 1.1 us)
Async XLA Ops:
  0.6 1.1 copy-start.6
  1.8 1.1 copy-start.7
  2.9 0.7 copy-start.8
  5.1 13.2 %collective-permute-start.2 = (bf16[72,3072]{1,0:T(8,128)(2,1)S(1)}, bf16[72,3072]{1,0:T(8,128)(2,1)S(1)}, u32[]{:S(2)}, u32[]{:S(2)}) collective-permute-start(bf16[72,3072]{1,0:T(8,128)(2,1)S(1)} %pack.1.block.refs_0_), channel_id=1, source_target_pairs={{0,16},{8,24},{16,0},{24,8},{1,17},{9,25},{17,1},{25,9},{2,18},{10... | collective-permute-start | bytes 1327112 | tf_op jit(solution)/shard_map/ppermute | solution.py:377
  8.1 11.7 %collective-permute-start.1 = (bf16[72,3072]{1,0:T(8,128)(2,1)S(1)}, bf16[72,3072]{1,0:T(8,128)(2,1)}, u32[]{:S(2)}, u32[]{:S(2)}) collective-permute-start(bf16[72,3072]{1,0:T(8,128)(2,1)S(1)} %pack.1.block.refs_0_), channel_id=1, source_target_pairs={{0,1},{1,0},{2,3},{3,2},{4,5},{5,4},{6,7},{7,6},{8,9},{9,8},{10,11... | collective-permute-start | bytes 1327112 | tf_op jit(solution)/shard_map/ppermute | solution.py:380
  9.6 15.1 %collective-permute-start = (bf16[72,3072]{1,0:T(8,128)(2,1)S(1)}, bf16[72,3072]{1,0:T(8,128)(2,1)}, u32[]{:S(2)}, u32[]{:S(2)}) collective-permute-start(bf16[72,3072]{1,0:T(8,128)(2,1)S(1)} %pack.1.block.refs_0_), channel_id=1, source_target_pairs={{0,2},{1,3},{2,4},{3,5},{4,6},{5,7},{6,0},{7,1},{8,10},{9,11},{10,... | collective-permute-start | bytes 1327112 | tf_op jit(solution)/shard_map/ppermute | solution.py:383
  11.2 21.7 %collective-permute-start.3 = (bf16[72,3072]{1,0:T(8,128)(2,1)S(1)}, bf16[72,3072]{1,0:T(8,128)(2,1)}, u32[]{:S(2)}, u32[]{:S(2)}) collective-permute-start(bf16[72,3072]{1,0:T(8,128)(2,1)S(1)} %pack.1.block.refs_0_), channel_id=1, source_target_pairs={{0,6},{1,7},{2,0},{3,1},{4,2},{5,3},{6,4},{7,5},{8,14},{9,15},{10,... | collective-permute-start | bytes 1327112 | tf_op jit(solution)/shard_map/ppermute | solution.py:383
  19.8 23.2 %collective-permute-start.13 = (bf16[72,3072]{1,0:T(8,128)(2,1)}, bf16[72,3072]{1,0:T(8,128)(2,1)S(1)}, u32[]{:S(2)}, u32[]{:S(2)}) collective-permute-start(bf16[72,3072]{1,0:T(8,128)(2,1)} %collective-permute-done.1.refs_3_), channel_id=1, source_target_pairs={{0,16},{8,24},{16,0},{24,8},{1,17},{9,25},{17,1},{25,9},{2,18},{10... | collective-permute-start | bytes 1327112 | tf_op jit(solution)/shard_map/ppermute | solution.py:377
  24.6 18.4 %collective-permute-start.9 = (bf16[72,3072]{1,0:T(8,128)(2,1)}, bf16[72,3072]{1,0:T(8,128)(2,1)}, u32[]{:S(2)}, u32[]{:S(2)}) collective-permute-start(bf16[72,3072]{1,0:T(8,128)(2,1)} %collective-permute-done.refs_1_), channel_id=1, source_target_pairs={{0,2},{1,3},{2,4},{3,5},{4,6},{5,7},{6,0},{7,1},{8,10},{9,11},{10,... | collective-permute-start | bytes 1327112 | tf_op jit(solution)/shard_map/ppermute | solution.py:383
  24.6 22.0 %collective-permute-start.15 = (bf16[72,3072]{1,0:T(8,128)(2,1)}, bf16[72,3072]{1,0:T(8,128)(2,1)}, u32[]{:S(2)}, u32[]{:S(2)}) collective-permute-start(bf16[72,3072]{1,0:T(8,128)(2,1)} %collective-permute-done.refs_1_), channel_id=1, source_target_pairs={{0,16},{8,24},{16,0},{24,8},{1,17},{9,25},{17,1},{25,9},{2,18},{10... | collective-permute-start | bytes 1327112 | tf_op jit(solution)/shard_map/ppermute | solution.py:377
  25.1 23.5 %collective-permute-start.4 = (bf16[72,3072]{1,0:T(8,128)(2,1)}, bf16[72,3072]{1,0:T(8,128)(2,1)}, u32[]{:S(2)}, u32[]{:S(2)}) collective-permute-start(bf16[72,3072]{1,0:T(8,128)(2,1)} %collective-permute-done.refs_1_), channel_id=1, source_target_pairs={{0,1},{1,0},{2,3},{3,2},{4,5},{5,4},{6,7},{7,6},{8,9},{9,8},{10,11... | collective-permute-start | bytes 1327112 | tf_op jit(solution)/shard_map/ppermute | solution.py:380
  32.9 16.1 %collective-permute-start.5 = (bf16[72,3072]{1,0:T(8,128)(2,1)}, bf16[72,3072]{1,0:T(8,128)(2,1)}, u32[]{:S(2)}, u32[]{:S(2)}) collective-permute-start(bf16[72,3072]{1,0:T(8,128)(2,1)} %collective-permute-done.3.refs_2_), channel_id=1, source_target_pairs={{0,1},{1,0},{2,3},{3,2},{4,5},{5,4},{6,7},{7,6},{8,9},{9,8},{10,11... | collective-permute-start | bytes 1327112 | tf_op jit(solution)/shard_map/ppermute | solution.py:380
  33.5 2.8 %copy-start = (bf16[3072,1024]{1,0:T(8,128)(2,1)S(1)}, bf16[3072,1024]{1,0:T(8,128)(2,1)}, u32[]{:S(2)}) copy-start(bf16[3072,1024]{1,0:T(8,128)(2,1)} %refs_4_.3) | copy-start | bytes 18874372
  36.3 2.8 %copy-start.2 = (bf16[3072,1024]{1,0:T(8,128)(2,1)S(1)}, bf16[3072,1024]{1,0:T(8,128)(2,1)}, u32[]{:S(2)}) copy-start(bf16[3072,1024]{1,0:T(8,128)(2,1)} %refs_5_.1) | copy-start | bytes 18874372
  39.1 2.8 %copy-start.4 = (bf16[1024,3072]{1,0:T(8,128)(2,1)S(1)}, bf16[1024,3072]{1,0:T(8,128)(2,1)}, u32[]{:S(2)}) copy-start(bf16[1024,3072]{1,0:T(8,128)(2,1)} %refs_6_.5) | copy-start | bytes 18874372
  41.9 8.0 %copy-start.1 = (bf16[3072,1024]{1,0:T(8,128)(2,1)S(1)}, bf16[3072,1024]{1,0:T(8,128)(2,1)}, u32[]{:S(2)}) copy-start(bf16[3072,1024]{1,0:T(8,128)(2,1)} %refs_4_.3) | copy-start | bytes 18874372
  41.9 8.0 %copy-start.3 = (bf16[3072,1024]{1,0:T(8,128)(2,1)S(1)}, bf16[3072,1024]{1,0:T(8,128)(2,1)}, u32[]{:S(2)}) copy-start(bf16[3072,1024]{1,0:T(8,128)(2,1)} %refs_5_.1) | copy-start | bytes 18874372
  41.9 8.0 %copy-start.5 = (bf16[1024,3072]{1,0:T(8,128)(2,1)S(1)}, bf16[1024,3072]{1,0:T(8,128)(2,1)}, u32[]{:S(2)}) copy-start(bf16[1024,3072]{1,0:T(8,128)(2,1)} %refs_6_.5) | copy-start | bytes 18874372
  43.0 38.8 %collective-permute-start.14 = (bf16[72,3072]{1,0:T(8,128)(2,1)}, bf16[72,3072]{1,0:T(8,128)(2,1)S(1)}, u32[]{:S(2)}, u32[]{:S(2)}) collective-permute-start(bf16[72,3072]{1,0:T(8,128)(2,1)} %collective-permute-done.9.refs_0_), channel_id=1, source_target_pairs={{0,16},{8,24},{16,0},{24,8},{1,17},{9,25},{17,1},{25,9},{2,18},{10... | collective-permute-start | bytes 1327112 | tf_op jit(solution)/shard_map/ppermute | solution.py:377
  43.4 18.7 %collective-permute-start.22 = (bf16[72,3072]{1,0:T(8,128)(2,1)S(1)}, bf16[72,3072]{1,0:T(8,128)(2,1)S(1)}, u32[]{:S(2)}, u32[]{:S(2)}) collective-permute-start(bf16[72,3072]{1,0:T(8,128)(2,1)S(1)} %collective-permute-done.2.refs_0_), channel_id=1, source_target_pairs={{0,6},{1,7},{2,0},{3,1},{4,2},{5,3},{6,4},{7,5},{8,14},{9,15},{10,... | collective-permute-start | bytes 1327112 | tf_op jit(solution)/shard_map/ppermute | solution.py:383
  46.6 17.7 %collective-permute-start.23 = (bf16[72,3072]{1,0:T(8,128)(2,1)S(1)}, bf16[72,3072]{1,0:T(8,128)(2,1)S(1)}, u32[]{:S(2)}, u32[]{:S(2)}) collective-permute-start(bf16[72,3072]{1,0:T(8,128)(2,1)S(1)} %collective-permute-done.13.refs_1_), channel_id=1, source_target_pairs={{0,6},{1,7},{2,0},{3,1},{4,2},{5,3},{6,4},{7,5},{8,14},{9,15},{10,... | collective-permute-start | bytes 1327112 | tf_op jit(solution)/shard_map/ppermute | solution.py:383
  48.6 24.2 %collective-permute-start.10 = (bf16[72,3072]{1,0:T(8,128)(2,1)}, bf16[72,3072]{1,0:T(8,128)(2,1)S(1)}, u32[]{:S(2)}, u32[]{:S(2)}) collective-permute-start(bf16[72,3072]{1,0:T(8,128)(2,1)} %collective-permute-done.9.refs_0_), channel_id=1, source_target_pairs={{0,1},{1,0},{2,3},{3,2},{4,5},{5,4},{6,7},{7,6},{8,9},{9,8},{10,11... | collective-permute-start | bytes 1327112 | tf_op jit(solution)/shard_map/ppermute | solution.py:380
  49.0 15.3 %collective-permute-start.16 = (bf16[72,3072]{1,0:T(8,128)(2,1)}, bf16[72,3072]{1,0:T(8,128)(2,1)S(1)}, u32[]{:S(2)}, u32[]{:S(2)}) collective-permute-start(bf16[72,3072]{1,0:T(8,128)(2,1)} %collective-permute-done.4.refs_4_), channel_id=1, source_target_pairs={{0,16},{8,24},{16,0},{24,8},{1,17},{9,25},{17,1},{25,9},{2,18},{10... | collective-permute-start | bytes 1327112 | tf_op jit(solution)/shard_map/ppermute | solution.py:377
  61.2 0.8 copy-start.19
  62.0 28.3 %collective-permute-start.6 = (bf16[112,3072]{1,0:T(8,128)(2,1)}, bf16[112,3072]{1,0:T(8,128)(2,1)S(1)}, u32[]{:S(2)}, u32[]{:S(2)}) collective-permute-start(bf16[112,3072]{1,0:T(8,128)(2,1)} %get-tuple-element.36), channel_id=1, source_target_pairs={{0,1},{1,0},{2,3},{3,2},{4,5},{5,4},{6,7},{7,6},{8,9},{9,8},{10,11... | collective-permute-start | bytes 2064392 | tf_op jit(solution)/shard_map/ppermute | solution.py:380
  64.3 32.6 %collective-permute-start.25 = (bf16[224,1536]{1,0:T(8,128)(2,1)}, bf16[224,1536]{1,0:T(8,128)(2,1)}, u32[]{:S(2)}, u32[]{:S(2)}) collective-permute-start(bf16[224,1536]{1,0:T(8,128)(2,1)} %get-tuple-element.53), channel_id=1, source_target_pairs={{0,8},{8,0},{16,24},{24,16},{1,9},{9,1},{17,25},{25,17},{2,10},{10... | collective-permute-start | bytes 2064392 | tf_op jit(solution)/shard_map/ppermute | solution.py:374
  64.3 61.0 %collective-permute-start.20 = (bf16[224,3072]{1,0:T(8,128)(2,1)S(1)}, bf16[224,3072]{1,0:T(8,128)(2,1)S(1)}, u32[]{:S(2)}, u32[]{:S(2)}) collective-permute-start(bf16[224,3072]{1,0:T(8,128)(2,1)S(1)} %get-tuple-element.47.refs_0_), channel_id=1, source_target_pairs={{0,8},{8,0},{16,24},{24,16},{1,9},{9,1},{17,25},{25,17},{2,10},{10... | collective-permute-start | bytes 4128776 | tf_op jit(solution)/shard_map/ppermute | solution.py:374
  71.1 0.8 copy-start.11
  72.0 0.9 copy-start.13
  72.8 52.4 %collective-permute-start.24 = (bf16[224,3072]{1,0:T(8,128)(2,1)S(1)}, bf16[224,3072]{1,0:T(8,128)(2,1)S(1)}, u32[]{:S(2)}, u32[]{:S(2)}) collective-permute-start(bf16[224,3072]{1,0:T(8,128)(2,1)S(1)} %get-tuple-element.51.refs_4_), channel_id=1, source_target_pairs={{0,8},{8,0},{16,24},{24,16},{1,9},{9,1},{17,25},{25,17},{2,10},{10... | collective-permute-start | bytes 4128776 | tf_op jit(solution)/shard_map/ppermute | solution.py:374
  81.8 8.6 %copy-start.15 = (bf16[80,1536]{1,0:T(8,128)(2,1)}, bf16[80,1536]{1,0:T(8,128)(2,1)S(1)}, u32[]{:S(2)}) copy-start(bf16[80,1536]{1,0:T(8,128)(2,1)S(1)} %get-tuple-element.54.refs_8_) | copy-start | bytes 737284
  81.8 23.5 %copy-start.14 = (bf16[224,1536]{1,0:T(8,128)(2,1)S(1)}, bf16[224,1536]{1,0:T(8,128)(2,1)}, u32[]{:S(2)}) copy-start(bf16[224,1536]{1,0:T(8,128)(2,1)} %copy-done.13) | copy-start | bytes 2064388
  81.8 32.0 %copy-start.9 = (s32[128,2]{0,1:T(2,128)S(1)}, s32[128,2]{0,1:T(2,128)}, u32[]{:S(2)}) copy-start(s32[128,2]{0,1:T(2,128)} %param.9) | copy-start | bytes 3076
  81.8 8.4 %collective-permute-start.11 = (bf16[40,3072]{1,0:T(8,128)(2,1)S(1)}, bf16[40,3072]{1,0:T(8,128)(2,1)S(1)}, u32[]{:S(2)}, u32[]{:S(2)}) collective-permute-start(bf16[40,3072]{1,0:T(8,128)(2,1)S(1)} %get-tuple-element.42), channel_id=1, source_target_pairs={{0,1},{1,0},{2,3},{3,2},{4,5},{5,4},{6,7},{7,6},{8,9},{9,8},{10,11... | collective-permute-start | bytes 737288 | tf_op jit(solution)/shard_map/ppermute | solution.py:380
  90.3 1.5 %collective-permute-start.26 = (bf16[80,1536]{1,0:T(8,128)(2,1)S(1)}, bf16[80,1536]{1,0:T(8,128)(2,1)S(1)}, u32[]{:S(2)}, u32[]{:S(2)}) collective-permute-start(bf16[80,1536]{1,0:T(8,128)(2,1)S(1)} %get-tuple-element.55), channel_id=1, source_target_pairs={{0,8},{8,0},{16,24},{24,16},{1,9},{9,1},{17,25},{25,17},{2,10},{10... | collective-permute-start | bytes 737288 | tf_op jit(solution)/shard_map/ppermute | solution.py:374
  90.4 15.0 %collective-permute-start.12 = (bf16[40,3072]{1,0:T(8,128)(2,1)S(1)}, bf16[40,3072]{1,0:T(8,128)(2,1)S(1)}, u32[]{:S(2)}, u32[]{:S(2)}) collective-permute-start(bf16[40,3072]{1,0:T(8,128)(2,1)S(1)} %merge.3), channel_id=1, source_target_pairs={{0,4},{1,5},{2,6},{3,7},{4,0},{5,1},{6,2},{7,3},{8,12},{9,13},{10,... | collective-permute-start | bytes 737288 | tf_op jit(solution)/shard_map/ppermute | solution.py:383
  91.1 34.1 %copy-start.12 = (bf16[224,1536]{1,0:T(8,128)(2,1)S(1)}, bf16[224,1536]{1,0:T(8,128)(2,1)}, u32[]{:S(2)}) copy-start(bf16[224,1536]{1,0:T(8,128)(2,1)} %copy-done.11) | copy-start | bytes 2064388
  91.3 34.0 %copy-start.16 = (bf16[80,1536]{1,0:T(8,128)(2,1)S(1)}, bf16[80,1536]{1,0:T(8,128)(2,1)}, u32[]{:S(2)}) copy-start(bf16[80,1536]{1,0:T(8,128)(2,1)} %copy-done.15) | copy-start | bytes 737284
  91.3 34.0 %copy-start.20 = (bf16[224,1536]{1,0:T(8,128)(2,1)S(1)}, bf16[224,1536]{1,0:T(8,128)(2,1)}, u32[]{:S(2)}) copy-start(bf16[224,1536]{1,0:T(8,128)(2,1)} %copy-done.19) | copy-start | bytes 2064388
  91.8 0.7 copy-start.17
  92.5 32.8 %copy-start.18 = (bf16[80,1536]{1,0:T(8,128)(2,1)S(1)}, bf16[80,1536]{1,0:T(8,128)(2,1)}, u32[]{:S(2)}) copy-start(bf16[80,1536]{1,0:T(8,128)(2,1)} %copy-done.17) | copy-start | bytes 737284
  92.5 12.9 %collective-permute-start.7 = (bf16[40,3072]{1,0:T(8,128)(2,1)S(1)}, bf16[40,3072]{1,0:T(8,128)(2,1)S(1)}, u32[]{:S(2)}, u32[]{:S(2)}) collective-permute-start(bf16[40,3072]{1,0:T(8,128)(2,1)S(1)} %get-tuple-element.38), channel_id=1, source_target_pairs={{0,6},{1,7},{2,0},{3,1},{4,2},{5,3},{6,4},{7,5},{8,14},{9,15},{10,... | collective-permute-start | bytes 737288 | tf_op jit(solution)/shard_map/ppermute | solution.py:383
  96.9 16.1 %collective-permute-start.8 = (bf16[40,3072]{1,0:T(8,128)(2,1)S(1)}, bf16[40,3072]{1,0:T(8,128)(2,1)S(1)}, u32[]{:S(2)}, u32[]{:S(2)}) collective-permute-start(bf16[40,3072]{1,0:T(8,128)(2,1)S(1)} %get-tuple-element.39), channel_id=1, source_target_pairs={{0,2},{1,3},{2,4},{3,5},{4,6},{5,7},{6,0},{7,1},{8,10},{9,11},{10,... | collective-permute-start | bytes 737288 | tf_op jit(solution)/shard_map/ppermute | solution.py:383
  105.3 19.9 %collective-permute-start.27 = (bf16[224,1536]{1,0:T(8,128)(2,1)S(1)}, bf16[224,1536]{1,0:T(8,128)(2,1)S(1)}, u32[]{:S(2)}, u32[]{:S(2)}) collective-permute-start(bf16[224,1536]{1,0:T(8,128)(2,1)S(1)} %copy-done.14), channel_id=1, source_target_pairs={{0,8},{8,0},{16,24},{24,16},{1,9},{9,1},{17,25},{25,17},{2,10},{10... | collective-permute-start | bytes 2064392 | tf_op jit(solution)/shard_map/ppermute | solution.py:374
  105.3 19.4 %collective-permute-start.21 = (bf16[80,3072]{1,0:T(8,128)(2,1)S(1)}, bf16[80,3072]{1,0:T(8,128)(2,1)S(1)}, u32[]{:S(2)}, u32[]{:S(2)}) collective-permute-start(bf16[80,3072]{1,0:T(8,128)(2,1)S(1)} %get-tuple-element.48.refs_2_), channel_id=1, source_target_pairs={{0,8},{8,0},{16,24},{24,16},{1,9},{9,1},{17,25},{25,17},{2,10},{10... | collective-permute-start | bytes 1474568 | tf_op jit(solution)/shard_map/ppermute | solution.py:374
  113.0 11.7 %collective-permute-start.17 = (bf16[72,3072]{1,0:T(8,128)(2,1)S(1)}, bf16[72,3072]{1,0:T(8,128)(2,1)S(1)}, u32[]{:S(2)}, u32[]{:S(2)}) collective-permute-start(bf16[72,3072]{1,0:T(8,128)(2,1)S(1)} %collective-permute-done.10.refs_1_), channel_id=1, source_target_pairs={{0,16},{8,24},{16,0},{24,8},{1,17},{9,25},{17,1},{25,9},{2,18},{10... | collective-permute-start | bytes 1327112 | tf_op jit(solution)/shard_map/ppermute | solution.py:377
  124.7 8.1 %collective-permute-start.18 = (bf16[72,3072]{1,0:T(8,128)(2,1)S(1)}, bf16[72,3072]{1,0:T(8,128)(2,1)S(1)}, u32[]{:S(2)}, u32[]{:S(2)}) collective-permute-start(bf16[72,3072]{1,0:T(8,128)(2,1)S(1)} %collective-permute-done.14.refs_0_), channel_id=1, source_target_pairs={{0,8},{8,0},{16,24},{24,16},{1,9},{9,1},{17,25},{25,17},{2,10},{10... | collective-permute-start | bytes 1327112 | tf_op jit(solution)/shard_map/ppermute | solution.py:374
  124.8 8.1 %collective-permute-start.19 = (bf16[72,3072]{1,0:T(8,128)(2,1)S(1)}, bf16[72,3072]{1,0:T(8,128)(2,1)S(1)}, u32[]{:S(2)}, u32[]{:S(2)}) collective-permute-start(bf16[72,3072]{1,0:T(8,128)(2,1)S(1)} %collective-permute-done.17.refs_1_), channel_id=1, source_target_pairs={{0,8},{8,0},{16,24},{24,16},{1,9},{9,1},{17,25},{25,17},{2,10},{10... | collective-permute-start | bytes 1327112 | tf_op jit(solution)/shard_map/ppermute | solution.py:374
  (1 other events, 0.7 us)

commit v5 on v4

--- a/solution.py
+++ b/solution.py
@@ -11,7 +11,9 @@
 MAIN = 32
 REST = CAP - MAIN
 TILE = 256
-LIMIT = 20
+LIMIT = 16
+WAIT = 20 * 10**9
+COST = 10**10
 HALF = jnp.bfloat16
 FULL = jnp.float32
 
@@ -82,7 +84,7 @@
         out_shape=shape((2 * CAP, tokens.shape[1])),
         scratch_shapes=[pltpu.VMEM(v.shape, v.dtype) for v in values]
         + [pltpu.SemaphoreType.DMA((4,))],
-        compiler_params=params(LIMIT),
+        compiler_params=params(60),
         name="pack",
     )(*values)
 
@@ -150,8 +152,8 @@
 
 def forward_kernel(n, back, place, *refs):
     blocks, weights, refs = refs[:n], refs[n : n + 3], refs[n + 3 :]
-    acts, own, other = refs[:3]
-    refs = refs[3:]
+    acts, own = refs[:2]
+    refs = refs[2:]
     if back:
         send, keep = refs[:2]
         refs = refs[2:]
@@ -159,10 +161,11 @@
     gate, up, down = weights
     width, part = rows.shape[1], own.shape[1] // 2
     assemble(blocks, rows, scaled)
-    for out, index in ((own, 0), (other, 1)):
+    base = 3 * gate.shape[1]
+    for out, start, index in ((own, 0, 0), (acts, base, 1)):
         columns = pl.ds(pl.multiple_of(place[index] * part, part), part)
-        out[:, 0:part] = rows[:, columns]
-        out[:, part : 2 * part] = scaled[:, columns]
+        out[:, start : start + part] = rows[:, columns]
+        out[:, start + part : start + 2 * part] = scaled[:, columns]
     tiles = gate.shape[1] // TILE
     for j in range(tiles):
         here = slice(TILE * j, TILE * (j + 1))
@@ -191,8 +194,7 @@
     count = padded_rows(n)
     in_vmem = pl.BlockSpec(memory_space=pltpu.VMEM)
     out_shape = [
-        shape((count, 3 * hidden)),
-        shape((count, 2 * part)),
+        shape((count, 3 * hidden + 2 * part)),
         shape((count, 2 * part)),
     ]
     if back:
@@ -209,24 +211,23 @@
             pltpu.VMEM((count, width), HALF),
         ],
         compiler_params=params(LIMIT),
-        cost_estimate=pl.CostEstimate(
-            flops=2 * matmuls * count * width * hidden,
-            bytes_accessed=6 * width * hidden + 4 * count * (width + part),
-            transcendentals=count * hidden,
-        ),
+        cost_estimate=pl.CostEstimate(flops=COST, bytes_accessed=0, transcendentals=0),
         name="forward_back" if back else "forward",
     )(place, *blocks, gate, up, down)
 
 
 def grads_kernel(n, *refs):
-    acts, parts, refs = refs[:n], refs[n : 2 * n], refs[2 * n :]
+    own, parts, came, refs = refs[:n], refs[n : 2 * n], refs[2 * n : 3 * n], refs[3 * n :]
     gate_grad, up_grad, down_grad, act_rows, part_rows = refs
-    start = 0
-    for act, piece in zip(acts, parts):
-        here = slice(start, start + act.shape[0])
-        act_rows[here, :] = act[...]
+    start, reach = 0, act_rows.shape[1]
+    for mine, piece, other in zip(own, parts, came):
+        count = mine.shape[0]
+        here, there = slice(start, start + count), slice(start + count, start + 2 * count)
+        act_rows[here, :] = mine[:, 0:reach]
         part_rows[here, :] = piece[...]
-        start += act.shape[0]
+        act_rows[there, :] = other[:, 0:reach]
+        part_rows[there, :] = other[:, reach:]
+        start += 2 * count
     part = part_rows.shape[1] // 2
     tiles = act_rows.shape[1] // (3 * TILE)
     for i in range(part // TILE):
@@ -249,93 +250,42 @@
         ).astype(HALF)
 
 
-def grads(acts, parts, part, hidden):
-    n, count = len(acts), sum(a.shape[0] for a in acts)
+def grads(own, parts, came, hidden):
+    n, count, part = len(own), 2 * sum(a.shape[0] for a in own), parts[0].shape[1] // 2
     in_vmem = pl.BlockSpec(memory_space=pltpu.VMEM)
     return pl.pallas_call(
         functools.partial(grads_kernel, n),
-        in_specs=[in_vmem] * (2 * n),
+        in_specs=[in_vmem] * (3 * n),
         out_specs=[in_vmem] * 3,
         out_shape=[shape((part, hidden)), shape((part, hidden)), shape((hidden, part))],
         scratch_shapes=[
             pltpu.VMEM((count, 3 * hidden), HALF),
             pltpu.VMEM((count, 2 * part), HALF),
         ],
-        compiler_params=params(LIMIT),
-        cost_estimate=pl.CostEstimate(
-            flops=6 * count * part * hidden,
-            bytes_accessed=2 * count * (3 * hidden + 2 * part) + 6 * part * hidden,
-            transcendentals=0,
-        ),
+        compiler_params=params(24),
+        cost_estimate=pl.CostEstimate(flops=COST, bytes_accessed=0, transcendentals=0),
         name="grads",
-    )(*acts, *parts)
-
-
-def finish_kernel(n, place, *refs):
-    blocks, (gate, up, down), early, refs = refs[:n], refs[n : n + 3], refs[n + 3 : n + 6], refs[n + 6 :]
-    gate_grad, up_grad, down_grad, rows, scaled = refs
-    part = gate_grad.shape[0]
-    assemble(blocks, rows, scaled)
-    columns = pl.ds(pl.multiple_of(place[0] * part, part), part)
-    picked, cotan = rows[:, columns].T, scaled[:, columns]
-    for j in range(gate.shape[1] // TILE):
-        here = slice(TILE * j, TILE * (j + 1))
-        hidden, gate_back, up_back = activations(
-            rows[...], scaled[...], gate[:, here], up[:, here], down[here, :]
-        )
-        gate_grad[:, here] = (
-            early[0][:, here].astype(FULL)
-            + jnp.dot(picked, gate_back, preferred_element_type=FULL)
-        ).astype(HALF)
-        up_grad[:, here] = (
-            early[1][:, here].astype(FULL) + jnp.dot(picked, up_back, preferred_element_type=FULL)
-        ).astype(HALF)
-        down_grad[here, :] = (
-            early[2][here, :].astype(FULL) + tn_dot(hidden, cotan)
-        ).astype(HALF)
-
-
-def finish(blocks, gate, up, down, place, early):
-    n, (width, hidden) = len(blocks), gate.shape
-    count, part = padded_rows(n), early[0].shape[0]
-    in_vmem = pl.BlockSpec(memory_space=pltpu.VMEM)
-    return pl.pallas_call(
-        functools.partial(finish_kernel, n),
-        in_specs=[pl.BlockSpec(memory_space=pltpu.SMEM)] + [in_vmem] * (n + 6),
-        out_specs=[in_vmem] * 3,
-        out_shape=[shape(e.shape) for e in early],
-        scratch_shapes=[
-            pltpu.VMEM((count, width), HALF),
-            pltpu.VMEM((count, width), HALF),
-        ],
-        compiler_params=params(LIMIT),
-        cost_estimate=pl.CostEstimate(
-            flops=6 * count * (width + part) * hidden,
-            bytes_accessed=6 * width * hidden + 2 * n * CAP * width + 12 * part * hidden,
-            transcendentals=count * hidden,
-        ),
-        name="finish",
-    )(place, *blocks, gate, up, down, *early)
-
-
-def ready_kernel(place, block, gate, up, down, out):
+    )(*own, *parts, *came)
+
+
+def settle_kernel(place, block, out):
     out[0] = place[0]
     out[1] = place[1]
 
 
-def ready(place, block, gate, up, down):
-    in_vmem, in_smem = pl.BlockSpec(memory_space=pltpu.VMEM), pl.BlockSpec(memory_space=pltpu.SMEM)
-    return pl.pallas_call(
-        ready_kernel,
-        in_specs=[in_smem, in_vmem, in_vmem, in_vmem, in_vmem],
+def settle(place, block):
+    in_smem = pl.BlockSpec(memory_space=pltpu.SMEM)
+    return pl.pallas_call(
+        settle_kernel,
+        in_specs=[in_smem, pl.BlockSpec(memory_space=pl.ANY)],
         out_specs=in_smem,
         out_shape=shape((2,), jnp.int32),
         compiler_params=params(LIMIT),
         cost_estimate=pl.CostEstimate(
-            flops=0, bytes_accessed=6 * gate.size, transcendentals=0
+            flops=WAIT, bytes_accessed=0, transcendentals=0
         ),
-        name="ready",
-    )(place, block, gate, up, down)
+        name="settle",
+    )(place, block)
 
 
 def merge_kernel(n, keep, came, *outs):
@@ -388,42 +338,52 @@
     p = lax.axis_index("dp")
     place = jnp.stack([p, p + 1 - 2 * (p % 2)]).astype(jnp.int32)
     ids, probs = route_ids.T, route_probs.T
-    weights = dict(gate=gate_weight, up=up_weight, down=down_weight)
 
     b0 = pack(ids, probs, tokens, cotangent)
-    place = ready(place, b0, **weights)
-    z1, x0, y0, z3 = over_z(b0, 1), over_x(b0), over_y(b0), over_z(b0, -1)
-    xy0 = over_y(after(x0, y0))
-    z1 = after(z1, x0, y0)
+    place = settle(place, b0)
+    z1, x0, y0 = over_z(b0, 1), over_x(b0), over_y(b0)
+    z3 = over_z(after(b0, place), -1)
+    z1 = after(z1, x0, y0, place)
     z2, x1, y1 = over_z(z1, 1), over_x(z1), over_y(z1)
+    xy0 = over_y(after(x0, z1))
     x3 = over_x(z3)
-    xy1 = over_y(after(x1, y1))
     x2 = over_x(after(z2, x1))
-    y2 = over_y(after(z2, xy0))
-    y3 = over_z(after(y0, z2), -1)
-    xy3 = over_z(after(xy0, z2), -1)
-    xy2 = over_y(after(x2, xy1))
-
-    acts, parts = [], []
-
-    def share(act, own, other):
-        acts.extend([act, over_core(act)])
-        parts.extend([own, over_core(other)])
-
-    run = functools.partial(forward, place=place, part=part, **weights)
-    *first, send, keep = run([b0, z1, z3, x0, x1, x3], back=True)
-    pieces = merge(3, keep, over_x(send))
-    share(*first)
-    *second, send, keep = run([z2, x2], back=True)
-    pieces += merge(1, keep, over_x(send))
-    share(*second)
-    returned = [pieces[0], over_z(pieces[1], -1), over_z(pieces[2], 1), over_z(pieces[3], 2)]
-    share(*run([y0, xy0, y1, xy1, y3, xy3], back=False))
-    early = grads(acts, parts, part, gate_weight.shape[1])
-    last = [y2, xy2]
-    last = last + [over_core(b) for b in last]
-    gate_grad, up_grad, down_grad = finish(last, place=place, early=early, **weights)
-    return unpack(ids, returned), gate_grad, up_grad, down_grad
+    xy1 = over_y(after(x1, z2))
+    y2 = over_y(after(z2, x1))
+    xy2 = over_y(x2)
+
+    run = functools.partial(
+        forward, gate=gate_weight, up=up_weight, down=down_weight, place=place, part=part
+    )
+    act0, own0, send0, keep0 = run([after(b0, xy0, z2), z1, x0, x1], back=True)
+    came0 = over_x(send0)
+    y3 = over_z(after(y0, send0), -1)
+    act1, own1, send1, keep1 = run([after(z3, send0, y1), x3], back=True)
+    came1 = over_x(send1)
+    xy3 = over_z(after(xy0, send1), -1)
+    other0 = over_core(after(act0, send1))
+    act2, own2, send2, keep2 = run([after(z2, send1, xy1, y2, y3, came0), x2], back=True)
+    p0, p1 = merge(2, keep0, after(came0, send2))
+    came2, r1 = over_x(send2), over_z(p1, -1)
+    other1 = over_core(after(act1, send2))
+    y0 = after(y0, send2, p1, xy2, came1, other0)
+    act3, own3 = run([y0, xy0, y1, xy1, y3, xy3], back=False)
+    (p3,) = merge(1, keep1, after(came1, act3))
+    (p2,) = merge(1, keep2, after(came2, act3))
+    r3, r2 = over_z(p3, 1), over_z(p2, 2)
+    other2, other3 = over_core(after(act2, act3)), over_core(act3)
+    y2 = after(y2, act3, r1, other1, p2, p3)
+    act4, own4 = run([y2, xy2], back=False)
+    other4 = over_core(act4)
+    act0 = after(act0, r3)
+    gate_grad, up_grad, down_grad = grads(
+        [act0, act1, act2, act3, act4],
+        [own0, own1, own2, own3, own4],
+        [other0, other1, other2, other3, other4],
+        gate_weight.shape[1],
+    )
+    token_grad = unpack(after(ids, gate_grad), [p0, r1, r2, r3])
+    return token_grad, gate_grad, up_grad, down_grad
 
 
 def pick_rows(placer, values):

time: 145 us -> 121 us (0.83)
  waiting for transfers between devices: 51.4 us -> 35.7 us
  local copies, waits for them, and re-layouts: 15.3 us -> 4.97 us
  starting transfers between devices: 27.3 us -> 30.3 us
    pallas_call x2 -> x1, Pallas kernels: 12.1 us -> 1.14 us  [settle(): pl.pallas_call(settle_kernel, in_specs=[in_smem, pl.BlockSpec(memory_spac...]
    unnamed x42 -> x36, local copies, waits for them, and re-layouts: 15.3 us -> 4.97 us
    ppermute x6, waiting for transfers between devices: 14.1 us -> 4.76 us  [over_y(): return lax.ppermute(v, 'dp', y_pairs)]
    pallas_call x3 -> x5, Pallas kernels: 26.5 us -> 35.2 us  [forward(): pl.pallas_call(functools.partial(forward_kernel, n, back), in_specs=[pl.B...]
    ppermute x8, waiting for transfers between devices: 28.6 us -> 24.6 us  [over_z(): lax.ppermute(v, 'expert', [(i, (i + 2 * by) % n_expert) for i in range(n_...]
    ppermute x6 -> x7, starting transfers between devices: 5.57 us -> 8.71 us  [over_x(): return lax.ppermute(v, 'expert', x_pairs)]
    ppermute x6 -> x7, waiting for transfers between devices: 8.29 us -> 6.31 us  [over_x(): return lax.ppermute(v, 'expert', x_pairs)]
    pallas_call x1, Pallas kernels: 0.79 us -> 2.62 us  [pack(): pl.pallas_call(pack_kernel, in_specs=[pl.BlockSpec(memory_space=pltpu.HBM...]
  transfers between devices with their start and end apart: 28 -> 26, of which waited for: 10 -> 9; matrix products, arithmetic and copies ran while one was open for 0% -> 0% of each run, Pallas kernels for 26% -> 37%
where the time goes in v5:
time: 121 us
  Pallas kernels  49.2 us (41%)
  waiting for transfers between devices  35.7 us (30%)
  starting transfers between devices  30.3 us (25%)
  local copies, waits for them, and re-layouts  4.97 us (4%)
    pallas_call x5, Pallas kernels, forward(): pl.pallas_call(functools.partial(forward_kernel, n, back), in_specs=[pl.B...  35.2 us
    ppermute x8, waiting for transfers between devices, over_z(): lax.ppermute(v, 'expert', [(i, (i + 2 * by) % n_expert) for i in range(n_...  24.6 us
    ppermute x8, starting transfers between devices, over_z(): lax.ppermute(v, 'expert', [(i, (i + 2 * by) % n_expert) for i in range(n_...  13.3 us
    ppermute x7, starting transfers between devices, over_x(): return lax.ppermute(v, 'expert', x_pairs)  8.71 us
    pallas_call x1, Pallas kernels, grads(): pl.pallas_call(functools.partial(grads_kernel, n), in_specs=[in_vmem] * (...  8.26 us
    ppermute x6, starting transfers between devices, over_y(): return lax.ppermute(v, 'dp', y_pairs)  7.58 us
    ppermute x7, waiting for transfers between devices, over_x(): return lax.ppermute(v, 'expert', x_pairs)  6.31 us
    unnamed x36, local copies, waits for them, and re-layouts  4.97 us
  transfers between devices with their start and end apart: 26, of which 9 were waited for; matrix products, arithmetic and copies ran while one was open for 0% of the time, Pallas kernels for 37%

profile of v5, /device:TPU:0, one launch (start us, length us, event | category | flops | bytes accessed | tf_op | source)
XLA Modules:
  0.0 121.2 jit_solution(3052443481008209975)
XLA Ops:
  0.6 2.6 %pack.1.block.refs_0_ = bf16[72,3072]{1,0:T(8,128)(2,1)} custom-call(s32[2,128]{1,0:T(2,128)} %bitcast.4, f32[2,128]{1,0:T(2,128)} %bitcast.6, bf16[128,3072]{1,0:T(8,128)(2,1)} %tokens_in.1, bf16[128,3072]{1,0:T(8,128)(2,1)} %cotangent_in.1), custom_call_target="tpu_custom_call" | custom-call | tf_op jit(solution)/shard_map/pack/pallas_call | solution.py:81
  3.3 3.0 %collective-permute-start.2 = (bf16[72,3072]{1,0:T(8,128)(2,1)}, bf16[72,3072]{1,0:T(8,128)(2,1)S(1)}, u32[]{:S(2)}, u32[]{:S(2)}) collective-permute-start(bf16[72,3072]{1,0:T(8,128)(2,1)} %pack.1.block.refs_0_), channel_id=1, source_target_pairs={{0,16},{8,24},{16,0},{24,8},{1,17},{9,25},{17,1},{25,9},{2,18},{10... | collective-permute-start | bytes 1327112 | tf_op jit(solution)/shard_map/ppermute | solution.py:327
  6.3 1.6 %collective-permute-start.1 = (bf16[72,3072]{1,0:T(8,128)(2,1)}, bf16[72,3072]{1,0:T(8,128)(2,1)S(1)}, u32[]{:S(2)}, u32[]{:S(2)}) collective-permute-start(bf16[72,3072]{1,0:T(8,128)(2,1)} %pack.1.block.refs_0_), channel_id=1, source_target_pairs={{0,2},{1,3},{2,4},{3,5},{4,6},{5,7},{6,0},{7,1},{8,10},{9,11},{10,... | collective-permute-start | bytes 1327112 | tf_op jit(solution)/shard_map/ppermute | solution.py:333
  7.9 1.5 %collective-permute-start = (bf16[72,3072]{1,0:T(8,128)(2,1)}, bf16[72,3072]{1,0:T(8,128)(2,1)S(1)}, u32[]{:S(2)}, u32[]{:S(2)}) collective-permute-start(bf16[72,3072]{1,0:T(8,128)(2,1)} %pack.1.block.refs_0_), channel_id=1, source_target_pairs={{0,1},{1,0},{2,3},{3,2},{4,5},{5,4},{6,7},{7,6},{8,9},{9,8},{10,11... | collective-permute-start | bytes 1327112 | tf_op jit(solution)/shard_map/ppermute | solution.py:330
  9.4 0.1 pad_add_fusion.place
  9.4 1.0 copy-done
  10.5 1.1 settle.1.place
  11.6 2.3 %collective-permute-start.6 = (bf16[72,3072]{1,0:T(8,128)(2,1)S(1)}, bf16[72,3072]{1,0:T(8,128)(2,1)S(1)}, u32[]{:S(2)}, u32[]{:S(2)}) collective-permute-start(bf16[72,3072]{1,0:T(8,128)(2,1)S(1)} %copy-done), channel_id=1, source_target_pairs={{0,6},{1,7},{2,0},{3,1},{4,2},{5,3},{6,4},{7,5},{8,14},{9,15},{10,... | collective-permute-start | bytes 1327112 | tf_op jit(solution)/shard_map/ppermute | solution.py:333
  13.9 2.8 %collective-permute-done.2.refs_0_ = bf16[72,3072]{1,0:T(8,128)(2,1)S(1)} collective-permute-done((bf16[72,3072]{1,0:T(8,128)(2,1)}, bf16[72,3072]{1,0:T(8,128)(2,1)S(1)}, u32[]{:S(2)}, u32[]{:S(2)}) %collective-permute-start.2) | collective-permute-done | bytes 442400 | tf_op jit(solution)/shard_map/ppermute | solution.py:327
  16.7 4.8 %collective-permute-done.1.refs_1_ = bf16[72,3072]{1,0:T(8,128)(2,1)S(1)} collective-permute-done((bf16[72,3072]{1,0:T(8,128)(2,1)}, bf16[72,3072]{1,0:T(8,128)(2,1)S(1)}, u32[]{:S(2)}, u32[]{:S(2)}) %collective-permute-start.1) | collective-permute-done | bytes 442400 | tf_op jit(solution)/shard_map/ppermute | solution.py:333
  21.4 1.5 %collective-permute-start.5 = (bf16[72,3072]{1,0:T(8,128)(2,1)S(1)}, bf16[72,3072]{1,0:T(8,128)(2,1)S(1)}, u32[]{:S(2)}, u32[]{:S(2)}) collective-permute-start(bf16[72,3072]{1,0:T(8,128)(2,1)S(1)} %collective-permute-done.1.refs_1_), channel_id=1, source_target_pairs={{0,1},{1,0},{2,3},{3,2},{4,5},{5,4},{6,7},{7,6},{8,9},{9,8},{10,11... | collective-permute-start | bytes 1327112 | tf_op jit(solution)/shard_map/ppermute | solution.py:330
  22.9 0.5 collective-permute-start.3
  23.4 1.5 %collective-permute-start.7 = (bf16[72,3072]{1,0:T(8,128)(2,1)S(1)}, bf16[72,3072]{1,0:T(8,128)(2,1)S(1)}, u32[]{:S(2)}, u32[]{:S(2)}) collective-permute-start(bf16[72,3072]{1,0:T(8,128)(2,1)S(1)} %collective-permute-done.1.refs_1_), channel_id=1, source_target_pairs={{0,16},{8,24},{16,0},{24,8},{1,17},{9,25},{17,1},{25,9},{2,18},{10... | collective-permute-start | bytes 1327112 | tf_op jit(solution)/shard_map/ppermute | solution.py:327
  25.0 5.9 %collective-permute-done.6.refs_0_ = bf16[72,3072]{1,0:T(8,128)(2,1)S(1)} collective-permute-done((bf16[72,3072]{1,0:T(8,128)(2,1)S(1)}, bf16[72,3072]{1,0:T(8,128)(2,1)S(1)}, u32[]{:S(2)}, u32[]{:S(2)}) %collective-permute-start.6) | collective-permute-done | bytes 442400 | tf_op jit(solution)/shard_map/ppermute | solution.py:333
  30.8 1.5 %collective-permute-start.8 = (bf16[72,3072]{1,0:T(8,128)(2,1)S(1)}, bf16[72,3072]{1,0:T(8,128)(2,1)S(1)}, u32[]{:S(2)}, u32[]{:S(2)}) collective-permute-start(bf16[72,3072]{1,0:T(8,128)(2,1)S(1)} %collective-permute-done.6.refs_0_), channel_id=1, source_target_pairs={{0,1},{1,0},{2,3},{3,2},{4,5},{5,4},{6,7},{7,6},{8,9},{9,8},{10,11... | collective-permute-start | bytes 1327112 | tf_op jit(solution)/shard_map/ppermute | solution.py:330
  32.3 6.7 %collective-permute-done.4.refs_0_ = bf16[72,3072]{1,0:T(8,128)(2,1)S(1)} collective-permute-done((bf16[72,3072]{1,0:T(8,128)(2,1)S(1)}, bf16[72,3072]{1,0:T(8,128)(2,1)S(1)}, u32[]{:S(2)}, u32[]{:S(2)}) %collective-permute-start.4) | collective-permute-done | bytes 442400 | tf_op jit(solution)/shard_map/ppermute | solution.py:333
  39.0 1.5 %collective-permute-start.14 = (bf16[72,3072]{1,0:T(8,128)(2,1)S(1)}, bf16[72,3072]{1,0:T(8,128)(2,1)S(1)}, u32[]{:S(2)}, u32[]{:S(2)}) collective-permute-start(bf16[72,3072]{1,0:T(8,128)(2,1)S(1)} %collective-permute-done.4.refs_0_), channel_id=1, source_target_pairs={{0,1},{1,0},{2,3},{3,2},{4,5},{5,4},{6,7},{7,6},{8,9},{9,8},{10,11... | collective-permute-start | bytes 1327112 | tf_op jit(solution)/shard_map/ppermute | solution.py:330
  40.5 0.5 collective-permute-start.11
  41.1 8.0 %forward_back.3 = (bf16[144,4608]{1,0:T(8,128)(2,1)S(1)}, bf16[144,1536]{1,0:T(8,128)(2,1)S(1)}, bf16[72,3072]{1,0:T(8,128)(2,1)S(1)}, bf16[72,3072]{1,0:T(8,128)(2,1)S(1)}) custom-call(s32[2]{0:T(128)S(1)} %settle.1.place, bf16[72,3072]{1,0:T(8,128)(2,1)S(1)} %copy-done.1, bf16[72,3072]{1,0:T(8,128)(2,1)S(1)} %collective-permute-done.1.refs_1_, ...), custom_call_target="tpu_custom_call" | custom-call | flops 10000000000 | tf_op jit(solution)/shard_map/forward_back/pallas_call | solution.py:204
  49.1 0.6 collective-permute-start.13
  49.7 1.5 %collective-permute-start.10 = (bf16[72,3072]{1,0:T(8,128)(2,1)S(1)}, bf16[72,3072]{1,0:T(8,128)(2,1)S(1)}, u32[]{:S(2)}, u32[]{:S(2)}) collective-permute-start(bf16[72,3072]{1,0:T(8,128)(2,1)S(1)} %collective-permute-done.5.refs_3_), channel_id=1, source_target_pairs={{0,16},{8,24},{16,0},{24,8},{1,17},{9,25},{17,1},{25,9},{2,18},{10... | collective-permute-start | bytes 1327112 | tf_op jit(solution)/shard_map/ppermute | solution.py:327
  51.2 4.0 %collective-permute-start.12 = (bf16[72,3072]{1,0:T(8,128)(2,1)S(1)}, bf16[72,3072]{1,0:T(8,128)(2,1)S(1)}, u32[]{:S(2)}, u32[]{:S(2)}) collective-permute-start(bf16[72,3072]{1,0:T(8,128)(2,1)S(1)} %collective-permute-done.2.refs_0_), channel_id=1, source_target_pairs={{0,6},{1,7},{2,0},{3,1},{4,2},{5,3},{6,4},{7,5},{8,14},{9,15},{10,... | collective-permute-start | bytes 1327112 | tf_op jit(solution)/shard_map/ppermute | solution.py:333
  55.2 8.5 %forward_back.4 = (bf16[80,4608]{1,0:T(8,128)(2,1)S(1)}, bf16[80,1536]{1,0:T(8,128)(2,1)S(1)}, bf16[40,3072]{1,0:T(8,128)(2,1)S(1)}, bf16[40,3072]{1,0:T(8,128)(2,1)S(1)}) custom-call(s32[2]{0:T(128)S(1)} %settle.1.place, bf16[72,3072]{1,0:T(8,128)(2,1)S(1)} %collective-permute-done.6.refs_0_, bf16[72,3072]{1,0:T(8,128)(2,1)S(1)} %collective-permute-done.8.refs_1_, ...), custom_call_target="tpu_custom_call" | custom-call | flops 10000000000 | tf_op jit(solution)/shard_map/forward_back/pallas_call | solution.py:204
  63.7 0.1 collective-permute-start.16
  63.7 1.5 %collective-permute-start.9 = (bf16[40,3072]{1,0:T(8,128)(2,1)S(1)}, bf16[40,3072]{1,0:T(8,128)(2,1)S(1)}, u32[]{:S(2)}, u32[]{:S(2)}) collective-permute-start(bf16[40,3072]{1,0:T(8,128)(2,1)S(1)} %get-tuple-element.53), channel_id=1, source_target_pairs={{0,1},{1,0},{2,3},{3,2},{4,5},{5,4},{6,7},{7,6},{8,9},{9,8},{10,11... | collective-permute-start | bytes 737288 | tf_op jit(solution)/shard_map/ppermute | solution.py:330
  65.2 0.4 collective-permute-start.17
  65.6 0.5 collective-permute-start.15
  66.1 8.5 %forward_back.5 = (bf16[80,4608]{1,0:T(8,128)(2,1)S(1)}, bf16[80,1536]{1,0:T(8,128)(2,1)S(1)}, bf16[40,3072]{1,0:T(8,128)(2,1)S(1)}, bf16[40,3072]{1,0:T(8,128)(2,1)S(1)}) custom-call(s32[2]{0:T(128)S(1)} %settle.1.place, bf16[72,3072]{1,0:T(8,128)(2,1)S(1)} %collective-permute-done.4.refs_0_, bf16[72,3072]{1,0:T(8,128)(2,1)S(1)} %collective-permute-done.14.refs_1_, ...), custom_call_target="tpu_custom_call" | custom-call | flops 10000000000 | tf_op jit(solution)/shard_map/forward_back/pallas_call | solution.py:204
  74.6 0.9 copy-done.10
  75.4 0.1 merge.3
  75.5 2.0 %collective-permute-done.15.refs_1_ = bf16[72,3072]{1,0:T(8,128)(2,1)S(1)} collective-permute-done((bf16[72,3072]{1,0:T(8,128)(2,1)S(1)}, bf16[72,3072]{1,0:T(8,128)(2,1)S(1)}, u32[]{:S(2)}, u32[]{:S(2)}) %collective-permute-start.15) | collective-permute-done | bytes 442400 | tf_op jit(solution)/shard_map/ppermute | solution.py:327
  77.5 1.1 copy-done.6
  78.6 5.6 %forward.2 = (bf16[224,4608]{1,0:T(8,128)(2,1)S(1)}, bf16[224,1536]{1,0:T(8,128)(2,1)S(1)}) custom-call(s32[2]{0:T(128)S(1)} %settle.1.place, bf16[72,3072]{1,0:T(8,128)(2,1)S(1)} %collective-permute-done.2.refs_0_, bf16[72,3072]{1,0:T(8,128)(2,1)S(1)} %collective-permute-done.3.refs_1_, bf16[72,3072]{1,0:T(8,128)(2,1)S(1)} %collective-permute-done.7.refs_2_, ...), custom_call_target="tpu_custom_call" | custom-call | flops 10000000000 | tf_op jit(solution)/shard_map/forward/pallas_call | solution.py:204
  84.3 0.7 collective-permute-start.21
  85.0 1.4 %collective-permute-start.19 = (bf16[40,3072]{1,0:T(8,128)(2,1)S(1)}, bf16[40,3072]{1,0:T(8,128)(2,1)S(1)}, u32[]{:S(2)}, u32[]{:S(2)}) collective-permute-start(bf16[40,3072]{1,0:T(8,128)(2,1)S(1)} %get-tuple-element.61), channel_id=1, source_target_pairs={{0,6},{1,7},{2,0},{3,1},{4,2},{5,3},{6,4},{7,5},{8,14},{9,15},{10,... | collective-permute-start | bytes 737288 | tf_op jit(solution)/shard_map/ppermute | solution.py:333
  86.4 6.3 %collective-permute-done.21.came = bf16[40,3072]{1,0:T(8,128)(2,1)S(1)} collective-permute-done((bf16[40,3072]{1,0:T(8,128)(2,1)S(1)}, bf16[40,3072]{1,0:T(8,128)(2,1)S(1)}, u32[]{:S(2)}, u32[]{:S(2)}) %collective-permute-start.21) | collective-permute-done | bytes 245792 | tf_op jit(solution)/shard_map/ppermute | solution.py:330
  92.9 0.1 collective-permute-done.19.refs_1_
  93.1 0.9 copy-done.12
  93.9 4.7 %forward.3 = (bf16[80,4608]{1,0:T(8,128)(2,1)S(1)}, bf16[80,1536]{1,0:T(8,128)(2,1)S(1)}) custom-call(s32[2]{0:T(128)S(1)} %settle.1.place, bf16[72,3072]{1,0:T(8,128)(2,1)S(1)} %collective-permute-done.11.refs_0_, bf16[72,3072]{1,0:T(8,128)(2,1)S(1)} %collective-permute-done.15.refs_1_, bf16[3072,1024]{1,0:T(8,128)(2,1)S(1)} %copy-done.3, ...), custom_call_target="tpu_custom_call" | custom-call | flops 10000000000 | tf_op jit(solution)/shard_map/forward/pallas_call | solution.py:204
  98.6 0.1 collective-permute-start.24
  98.7 0.5 collective-permute-start.22
  99.2 1.7 %collective-permute-start.18 = (bf16[40,3072]{1,0:T(8,128)(2,1)S(1)}, bf16[40,3072]{1,0:T(8,128)(2,1)S(1)}, u32[]{:S(2)}, u32[]{:S(2)}) collective-permute-start(bf16[40,3072]{1,0:T(8,128)(2,1)S(1)} %merge.4), channel_id=1, source_target_pairs={{0,2},{1,3},{2,4},{3,5},{4,6},{5,7},{6,0},{7,1},{8,10},{9,11},{10,... | collective-permute-start | bytes 737288 | tf_op jit(solution)/shard_map/ppermute | solution.py:333
  100.8 2.1 %collective-permute-start.25 = (bf16[40,3072]{1,0:T(8,128)(2,1)S(1)}, bf16[40,3072]{1,0:T(8,128)(2,1)S(1)}, u32[]{:S(2)}, u32[]{:S(2)}) collective-permute-start(bf16[40,3072]{1,0:T(8,128)(2,1)S(1)} %merge.5), channel_id=1, source_target_pairs={{0,4},{1,5},{2,6},{3,7},{4,0},{5,1},{6,2},{7,3},{8,12},{9,13},{10,... | collective-permute-start | bytes 737288 | tf_op jit(solution)/shard_map/ppermute | solution.py:333
  102.9 7.0 %collective-permute-done.18.refs_3_ = bf16[40,3072]{1,0:T(8,128)(2,1)S(1)} collective-permute-done((bf16[40,3072]{1,0:T(8,128)(2,1)S(1)}, bf16[40,3072]{1,0:T(8,128)(2,1)S(1)}, u32[]{:S(2)}, u32[]{:S(2)}) %collective-permute-start.18) | collective-permute-done | bytes 245792 | tf_op jit(solution)/shard_map/ppermute | solution.py:333
  109.9 1.1 copy-done.13
  111.0 8.3 %grads.1 = (bf16[768,1024]{1,0:T(8,128)(2,1)}, bf16[768,1024]{1,0:T(8,128)(2,1)}, bf16[1024,768]{1,0:T(8,128)(2,1)}) custom-call(bf16[144,4608]{1,0:T(8,128)(2,1)S(1)} %get-tuple-element.67.refs_0_, bf16[80,4608]{1,0:T(8,128)(2,1)S(1)} %copy-done.9, bf16[80,4608]{1,0:T(8,128)(2,1)S(1)} %copy-done.11, bf16[224,4608]{1,0:T(8,128)(2,1)S(1)} %get-tuple-element.65.refs_3_, ...), custom_call_target="tpu_custom_call" | custom-call | flops 10000000000 | tf_op jit(solution)/shard_map/grads/pallas_call | solution.py:256
  119.3 0.1 collective-permute-done.25.refs_2_
  119.4 1.7 %unpack.1 = bf16[128,3072]{1,0:T(8,128)(2,1)} custom-call(s32[2,128]{1,0:T(2,128)S(1)} %bitcast.5, bf16[40,3072]{1,0:T(8,128)(2,1)S(1)} %get-tuple-element.83.refs_0_, bf16[40,3072]{1,0:T(8,128)(2,1)S(1)} %collective-permute-done.19.refs_1_, bf16[40,3072]{1,0:T(8,128)(2,1)S(1)} %collective-permute-done.25.refs_2_, ...), custom_call_target="tpu_custom_call" | custom-call | tf_op jit(solution)/shard_map/unpack/pallas_call | solution.py:105
  (53 shorter events, 0.3 us)
Async XLA Ops:
  3.3 13.4 %collective-permute-start.2 = (bf16[72,3072]{1,0:T(8,128)(2,1)}, bf16[72,3072]{1,0:T(8,128)(2,1)S(1)}, u32[]{:S(2)}, u32[]{:S(2)}) collective-permute-start(bf16[72,3072]{1,0:T(8,128)(2,1)} %pack.1.block.refs_0_), channel_id=1, source_target_pairs={{0,16},{8,24},{16,0},{24,8},{1,17},{9,25},{17,1},{25,9},{2,18},{10... | collective-permute-start | bytes 1327112 | tf_op jit(solution)/shard_map/ppermute | solution.py:327
  6.3 15.1 %collective-permute-start.1 = (bf16[72,3072]{1,0:T(8,128)(2,1)}, bf16[72,3072]{1,0:T(8,128)(2,1)S(1)}, u32[]{:S(2)}, u32[]{:S(2)}) collective-permute-start(bf16[72,3072]{1,0:T(8,128)(2,1)} %pack.1.block.refs_0_), channel_id=1, source_target_pairs={{0,2},{1,3},{2,4},{3,5},{4,6},{5,7},{6,0},{7,1},{8,10},{9,11},{10,... | collective-permute-start | bytes 1327112 | tf_op jit(solution)/shard_map/ppermute | solution.py:333
  7.9 13.6 %collective-permute-start = (bf16[72,3072]{1,0:T(8,128)(2,1)}, bf16[72,3072]{1,0:T(8,128)(2,1)S(1)}, u32[]{:S(2)}, u32[]{:S(2)}) collective-permute-start(bf16[72,3072]{1,0:T(8,128)(2,1)} %pack.1.block.refs_0_), channel_id=1, source_target_pairs={{0,1},{1,0},{2,3},{3,2},{4,5},{5,4},{6,7},{7,6},{8,9},{9,8},{10,11... | collective-permute-start | bytes 1327112 | tf_op jit(solution)/shard_map/ppermute | solution.py:330
  9.4 1.0 copy-start
  10.4 30.6 %copy-start.1 = (bf16[72,3072]{1,0:T(8,128)(2,1)S(1)}, bf16[72,3072]{1,0:T(8,128)(2,1)}, u32[]{:S(2)}) copy-start(bf16[72,3072]{1,0:T(8,128)(2,1)} %pack.1.block.refs_0_) | copy-start | bytes 1327108
  10.5 30.6 %copy-start.3 = (bf16[3072,1024]{1,0:T(8,128)(2,1)S(1)}, bf16[3072,1024]{1,0:T(8,128)(2,1)}, u32[]{:S(2)}) copy-start(bf16[3072,1024]{1,0:T(8,128)(2,1)} %refs_2_.5) | copy-start | bytes 18874372
  10.5 30.6 %copy-start.4 = (bf16[3072,1024]{1,0:T(8,128)(2,1)S(1)}, bf16[3072,1024]{1,0:T(8,128)(2,1)}, u32[]{:S(2)}) copy-start(bf16[3072,1024]{1,0:T(8,128)(2,1)} %refs_3_.5) | copy-start | bytes 18874372
  10.5 30.6 %copy-start.5 = (bf16[1024,3072]{1,0:T(8,128)(2,1)S(1)}, bf16[1024,3072]{1,0:T(8,128)(2,1)}, u32[]{:S(2)}) copy-start(bf16[1024,3072]{1,0:T(8,128)(2,1)} %refs_4_.7) | copy-start | bytes 18874372
  11.6 19.2 %collective-permute-start.6 = (bf16[72,3072]{1,0:T(8,128)(2,1)S(1)}, bf16[72,3072]{1,0:T(8,128)(2,1)S(1)}, u32[]{:S(2)}, u32[]{:S(2)}) collective-permute-start(bf16[72,3072]{1,0:T(8,128)(2,1)S(1)} %copy-done), channel_id=1, source_target_pairs={{0,6},{1,7},{2,0},{3,1},{4,2},{5,3},{6,4},{7,5},{8,14},{9,15},{10,... | collective-permute-start | bytes 1327112 | tf_op jit(solution)/shard_map/ppermute | solution.py:333
  21.4 10.9 %collective-permute-start.5 = (bf16[72,3072]{1,0:T(8,128)(2,1)S(1)}, bf16[72,3072]{1,0:T(8,128)(2,1)S(1)}, u32[]{:S(2)}, u32[]{:S(2)}) collective-permute-start(bf16[72,3072]{1,0:T(8,128)(2,1)S(1)} %collective-permute-done.1.refs_1_), channel_id=1, source_target_pairs={{0,1},{1,0},{2,3},{3,2},{4,5},{5,4},{6,7},{7,6},{8,9},{9,8},{10,11... | collective-permute-start | bytes 1327112 | tf_op jit(solution)/shard_map/ppermute | solution.py:330
  22.9 16.1 %collective-permute-start.4 = (bf16[72,3072]{1,0:T(8,128)(2,1)S(1)}, bf16[72,3072]{1,0:T(8,128)(2,1)S(1)}, u32[]{:S(2)}, u32[]{:S(2)}) collective-permute-start(bf16[72,3072]{1,0:T(8,128)(2,1)S(1)} %collective-permute-done.1.refs_1_), channel_id=1, source_target_pairs={{0,2},{1,3},{2,4},{3,5},{4,6},{5,7},{6,0},{7,1},{8,10},{9,11},{10,... | collective-permute-start | bytes 1327112 | tf_op jit(solution)/shard_map/ppermute | solution.py:333
  22.9 18.1 %collective-permute-start.3 = (bf16[72,3072]{1,0:T(8,128)(2,1)S(1)}, bf16[72,3072]{1,0:T(8,128)(2,1)S(1)}, u32[]{:S(2)}, u32[]{:S(2)}) collective-permute-start(bf16[72,3072]{1,0:T(8,128)(2,1)S(1)} %collective-permute-done.refs_2_), channel_id=1, source_target_pairs={{0,16},{8,24},{16,0},{24,8},{1,17},{9,25},{17,1},{25,9},{2,18},{10... | collective-permute-start | bytes 1327112 | tf_op jit(solution)/shard_map/ppermute | solution.py:327
  23.4 26.2 %collective-permute-start.7 = (bf16[72,3072]{1,0:T(8,128)(2,1)S(1)}, bf16[72,3072]{1,0:T(8,128)(2,1)S(1)}, u32[]{:S(2)}, u32[]{:S(2)}) collective-permute-start(bf16[72,3072]{1,0:T(8,128)(2,1)S(1)} %collective-permute-done.1.refs_1_), channel_id=1, source_target_pairs={{0,16},{8,24},{16,0},{24,8},{1,17},{9,25},{17,1},{25,9},{2,18},{10... | collective-permute-start | bytes 1327112 | tf_op jit(solution)/shard_map/ppermute | solution.py:327
  30.8 20.4 %collective-permute-start.8 = (bf16[72,3072]{1,0:T(8,128)(2,1)S(1)}, bf16[72,3072]{1,0:T(8,128)(2,1)S(1)}, u32[]{:S(2)}, u32[]{:S(2)}) collective-permute-start(bf16[72,3072]{1,0:T(8,128)(2,1)S(1)} %collective-permute-done.6.refs_0_), channel_id=1, source_target_pairs={{0,1},{1,0},{2,3},{3,2},{4,5},{5,4},{6,7},{7,6},{8,9},{9,8},{10,11... | collective-permute-start | bytes 1327112 | tf_op jit(solution)/shard_map/ppermute | solution.py:330
  39.0 26.5 %collective-permute-start.14 = (bf16[72,3072]{1,0:T(8,128)(2,1)S(1)}, bf16[72,3072]{1,0:T(8,128)(2,1)S(1)}, u32[]{:S(2)}, u32[]{:S(2)}) collective-permute-start(bf16[72,3072]{1,0:T(8,128)(2,1)S(1)} %collective-permute-done.4.refs_0_), channel_id=1, source_target_pairs={{0,1},{1,0},{2,3},{3,2},{4,5},{5,4},{6,7},{7,6},{8,9},{9,8},{10,11... | collective-permute-start | bytes 1327112 | tf_op jit(solution)/shard_map/ppermute | solution.py:330
  40.5 23.2 %collective-permute-start.11 = (bf16[72,3072]{1,0:T(8,128)(2,1)S(1)}, bf16[72,3072]{1,0:T(8,128)(2,1)S(1)}, u32[]{:S(2)}, u32[]{:S(2)}) collective-permute-start(bf16[72,3072]{1,0:T(8,128)(2,1)S(1)} %collective-permute-done.4.refs_0_), channel_id=1, source_target_pairs={{0,16},{8,24},{16,0},{24,8},{1,17},{9,25},{17,1},{25,9},{2,18},{10... | collective-permute-start | bytes 1327112 | tf_op jit(solution)/shard_map/ppermute | solution.py:327
  49.1 14.6 %copy-start.16 = (bf16[144,1536]{1,0:T(8,128)(2,1)}, bf16[144,1536]{1,0:T(8,128)(2,1)S(1)}, u32[]{:S(2)}) copy-start(bf16[144,1536]{1,0:T(8,128)(2,1)S(1)} %get-tuple-element.75.refs_5_) | copy-start | bytes 1327108
  49.1 16.5 %collective-permute-start.13 = (bf16[72,3072]{1,0:T(8,128)(2,1)S(1)}, bf16[72,3072]{1,0:T(8,128)(2,1)S(1)}, u32[]{:S(2)}, u32[]{:S(2)}) collective-permute-start(bf16[72,3072]{1,0:T(8,128)(2,1)S(1)} %get-tuple-element.50), channel_id=1, source_target_pairs={{0,1},{1,0},{2,3},{3,2},{4,5},{5,4},{6,7},{7,6},{8,9},{9,8},{10,11... | collective-permute-start | bytes 1327112 | tf_op jit(solution)/shard_map/ppermute | solution.py:330
  49.7 14.0 %collective-permute-start.10 = (bf16[72,3072]{1,0:T(8,128)(2,1)S(1)}, bf16[72,3072]{1,0:T(8,128)(2,1)S(1)}, u32[]{:S(2)}, u32[]{:S(2)}) collective-permute-start(bf16[72,3072]{1,0:T(8,128)(2,1)S(1)} %collective-permute-done.5.refs_3_), channel_id=1, source_target_pairs={{0,16},{8,24},{16,0},{24,8},{1,17},{9,25},{17,1},{25,9},{2,18},{10... | collective-permute-start | bytes 1327112 | tf_op jit(solution)/shard_map/ppermute | solution.py:327
  51.2 14.0 %collective-permute-start.12 = (bf16[72,3072]{1,0:T(8,128)(2,1)S(1)}, bf16[72,3072]{1,0:T(8,128)(2,1)S(1)}, u32[]{:S(2)}, u32[]{:S(2)}) collective-permute-start(bf16[72,3072]{1,0:T(8,128)(2,1)S(1)} %collective-permute-done.2.refs_0_), channel_id=1, source_target_pairs={{0,6},{1,7},{2,0},{3,1},{4,2},{5,3},{6,4},{7,5},{8,14},{9,15},{10,... | collective-permute-start | bytes 1327112 | tf_op jit(solution)/shard_map/ppermute | solution.py:333
  63.6 11.8 %copy-start.8 = (bf16[80,4608]{1,0:T(8,128)(2,1)}, bf16[80,4608]{1,0:T(8,128)(2,1)S(1)}, u32[]{:S(2)}) copy-start(bf16[80,4608]{1,0:T(8,128)(2,1)S(1)} %get-tuple-element.70.refs_1_) | copy-start | bytes 2211844
  63.7 13.9 %collective-permute-start.16 = (bf16[144,4608]{1,0:T(8,128)(2,1)S(1)}, bf16[144,4608]{1,0:T(8,128)(2,1)S(1)}, u32[]{:S(2)}, u32[]{:S(2)}) collective-permute-start(bf16[144,4608]{1,0:T(8,128)(2,1)S(1)} %get-tuple-element.67.refs_0_), channel_id=1, source_target_pairs={{0,8},{8,0},{16,24},{24,16},{1,9},{9,1},{17,25},{25,17},{2,10},{10... | collective-permute-start | bytes 3981320 | tf_op jit(solution)/shard_map/ppermute | solution.py:324
  63.7 11.8 %collective-permute-start.9 = (bf16[40,3072]{1,0:T(8,128)(2,1)S(1)}, bf16[40,3072]{1,0:T(8,128)(2,1)S(1)}, u32[]{:S(2)}, u32[]{:S(2)}) collective-permute-start(bf16[40,3072]{1,0:T(8,128)(2,1)S(1)} %get-tuple-element.53), channel_id=1, source_target_pairs={{0,1},{1,0},{2,3},{3,2},{4,5},{5,4},{6,7},{7,6},{8,9},{9,8},{10,11... | collective-permute-start | bytes 737288 | tf_op jit(solution)/shard_map/ppermute | solution.py:330
  65.2 13.4 %collective-permute-start.17 = (bf16[72,3072]{1,0:T(8,128)(2,1)S(1)}, bf16[72,3072]{1,0:T(8,128)(2,1)S(1)}, u32[]{:S(2)}, u32[]{:S(2)}) collective-permute-start(bf16[72,3072]{1,0:T(8,128)(2,1)S(1)} %collective-permute-done.3.refs_1_), channel_id=1, source_target_pairs={{0,6},{1,7},{2,0},{3,1},{4,2},{5,3},{6,4},{7,5},{8,14},{9,15},{10,... | collective-permute-start | bytes 1327112 | tf_op jit(solution)/shard_map/ppermute | solution.py:333
  65.6 12.0 %collective-permute-start.15 = (bf16[72,3072]{1,0:T(8,128)(2,1)S(1)}, bf16[72,3072]{1,0:T(8,128)(2,1)S(1)}, u32[]{:S(2)}, u32[]{:S(2)}) collective-permute-start(bf16[72,3072]{1,0:T(8,128)(2,1)S(1)} %collective-permute-done.14.refs_1_), channel_id=1, source_target_pairs={{0,16},{8,24},{16,0},{24,8},{1,17},{9,25},{17,1},{25,9},{2,18},{10... | collective-permute-start | bytes 1327112 | tf_op jit(solution)/shard_map/ppermute | solution.py:327
  74.5 0.9 copy-start.10
  75.4 17.6 %collective-permute-start.20 = (bf16[80,4608]{1,0:T(8,128)(2,1)S(1)}, bf16[80,4608]{1,0:T(8,128)(2,1)S(1)}, u32[]{:S(2)}, u32[]{:S(2)}) collective-permute-start(bf16[80,4608]{1,0:T(8,128)(2,1)S(1)} %get-tuple-element.70.refs_1_), channel_id=1, source_target_pairs={{0,8},{8,0},{16,24},{24,16},{1,9},{9,1},{17,25},{25,17},{2,10},{10... | collective-permute-start | bytes 2211848 | tf_op jit(solution)/shard_map/ppermute | solution.py:324
  77.5 1.1 copy-start.6
  84.2 8.5 %copy-start.14 = (bf16[224,1536]{1,0:T(8,128)(2,1)}, bf16[224,1536]{1,0:T(8,128)(2,1)S(1)}, u32[]{:S(2)}) copy-start(bf16[224,1536]{1,0:T(8,128)(2,1)S(1)} %get-tuple-element.78.refs_8_) | copy-start | bytes 2064388
  84.2 25.6 %collective-permute-start.23 = (bf16[224,4608]{1,0:T(8,128)(2,1)S(1)}, bf16[224,4608]{1,0:T(8,128)(2,1)S(1)}, u32[]{:S(2)}, u32[]{:S(2)}) collective-permute-start(bf16[224,4608]{1,0:T(8,128)(2,1)S(1)} %get-tuple-element.65.refs_3_), channel_id=1, source_target_pairs={{0,8},{8,0},{16,24},{24,16},{1,9},{9,1},{17,25},{25,17},{2,10},{10... | collective-permute-start | bytes 6193160 | tf_op jit(solution)/shard_map/ppermute | solution.py:324
  84.3 8.4 %collective-permute-start.21 = (bf16[40,3072]{1,0:T(8,128)(2,1)S(1)}, bf16[40,3072]{1,0:T(8,128)(2,1)S(1)}, u32[]{:S(2)}, u32[]{:S(2)}) collective-permute-start(bf16[40,3072]{1,0:T(8,128)(2,1)S(1)} %get-tuple-element.58), channel_id=1, source_target_pairs={{0,1},{1,0},{2,3},{3,2},{4,5},{5,4},{6,7},{7,6},{8,9},{9,8},{10,11... | collective-permute-start | bytes 737288 | tf_op jit(solution)/shard_map/ppermute | solution.py:330
  85.0 8.0 %collective-permute-start.19 = (bf16[40,3072]{1,0:T(8,128)(2,1)S(1)}, bf16[40,3072]{1,0:T(8,128)(2,1)S(1)}, u32[]{:S(2)}, u32[]{:S(2)}) collective-permute-start(bf16[40,3072]{1,0:T(8,128)(2,1)S(1)} %get-tuple-element.61), channel_id=1, source_target_pairs={{0,6},{1,7},{2,0},{3,1},{4,2},{5,3},{6,4},{7,5},{8,14},{9,15},{10,... | collective-permute-start | bytes 737288 | tf_op jit(solution)/shard_map/ppermute | solution.py:333
  92.8 5.8 %copy-start.11 = (bf16[80,4608]{1,0:T(8,128)(2,1)S(1)}, bf16[80,4608]{1,0:T(8,128)(2,1)}, u32[]{:S(2)}) copy-start(bf16[80,4608]{1,0:T(8,128)(2,1)} %copy-done.10) | copy-start | bytes 2211844
  92.9 17.0 %copy-start.7 = (bf16[144,4608]{1,0:T(8,128)(2,1)S(1)}, bf16[144,4608]{1,0:T(8,128)(2,1)}, u32[]{:S(2)}) copy-start(bf16[144,4608]{1,0:T(8,128)(2,1)} %copy-done.6) | copy-start | bytes 3981316
  92.9 17.0 %copy-start.9 = (bf16[80,4608]{1,0:T(8,128)(2,1)S(1)}, bf16[80,4608]{1,0:T(8,128)(2,1)}, u32[]{:S(2)}) copy-start(bf16[80,4608]{1,0:T(8,128)(2,1)} %copy-done.8) | copy-start | bytes 2211844
  92.9 17.0 %copy-start.15 = (bf16[224,1536]{1,0:T(8,128)(2,1)S(1)}, bf16[224,1536]{1,0:T(8,128)(2,1)}, u32[]{:S(2)}) copy-start(bf16[224,1536]{1,0:T(8,128)(2,1)} %copy-done.14) | copy-start | bytes 2064388
  92.9 17.0 %copy-start.17 = (bf16[144,1536]{1,0:T(8,128)(2,1)S(1)}, bf16[144,1536]{1,0:T(8,128)(2,1)}, u32[]{:S(2)}) copy-start(bf16[144,1536]{1,0:T(8,128)(2,1)} %copy-done.16) | copy-start | bytes 1327108
  93.0 0.9 copy-start.12
  98.6 11.3 %collective-permute-start.24 = (bf16[80,4608]{1,0:T(8,128)(2,1)S(1)}, bf16[80,4608]{1,0:T(8,128)(2,1)S(1)}, u32[]{:S(2)}, u32[]{:S(2)}) collective-permute-start(bf16[80,4608]{1,0:T(8,128)(2,1)S(1)} %get-tuple-element.74.refs_4_), channel_id=1, source_target_pairs={{0,8},{8,0},{16,24},{24,16},{1,9},{9,1},{17,25},{25,17},{2,10},{10... | collective-permute-start | bytes 2211848 | tf_op jit(solution)/shard_map/ppermute | solution.py:324
  98.7 11.2 %collective-permute-start.22 = (bf16[80,4608]{1,0:T(8,128)(2,1)S(1)}, bf16[80,4608]{1,0:T(8,128)(2,1)S(1)}, u32[]{:S(2)}, u32[]{:S(2)}) collective-permute-start(bf16[80,4608]{1,0:T(8,128)(2,1)S(1)} %copy-done.11), channel_id=1, source_target_pairs={{0,8},{8,0},{16,24},{24,16},{1,9},{9,1},{17,25},{25,17},{2,10},{10... | collective-permute-start | bytes 2211848 | tf_op jit(solution)/shard_map/ppermute | solution.py:324
  99.2 10.7 %collective-permute-start.18 = (bf16[40,3072]{1,0:T(8,128)(2,1)S(1)}, bf16[40,3072]{1,0:T(8,128)(2,1)S(1)}, u32[]{:S(2)}, u32[]{:S(2)}) collective-permute-start(bf16[40,3072]{1,0:T(8,128)(2,1)S(1)} %merge.4), channel_id=1, source_target_pairs={{0,2},{1,3},{2,4},{3,5},{4,6},{5,7},{6,0},{7,1},{8,10},{9,11},{10,... | collective-permute-start | bytes 737288 | tf_op jit(solution)/shard_map/ppermute | solution.py:333
  100.8 18.6 %collective-permute-start.25 = (bf16[40,3072]{1,0:T(8,128)(2,1)S(1)}, bf16[40,3072]{1,0:T(8,128)(2,1)S(1)}, u32[]{:S(2)}, u32[]{:S(2)}) collective-permute-start(bf16[40,3072]{1,0:T(8,128)(2,1)S(1)} %merge.5), channel_id=1, source_target_pairs={{0,4},{1,5},{2,6},{3,7},{4,0},{5,1},{6,2},{7,3},{8,12},{9,13},{10,... | collective-permute-start | bytes 737288 | tf_op jit(solution)/shard_map/ppermute | solution.py:333
  109.9 1.1 copy-start.13
  111.0 8.4 %copy-start.2 = (s32[128,2]{0,1:T(2,128)S(1)}, s32[128,2]{0,1:T(2,128)}, u32[]{:S(2)}) copy-start(s32[128,2]{0,1:T(2,128)} %param.9) | copy-start | bytes 3076

commit v6 on v5

--- a/solution.py
+++ b/solution.py
@@ -11,7 +11,8 @@
 MAIN = 32
 REST = CAP - MAIN
 TILE = 256
-LIMIT = 16
+LIMIT = 9
+GRADS_LIMIT = 14
 WAIT = 20 * 10**9
 COST = 10**10
 HALF = jnp.bfloat16
@@ -189,7 +190,7 @@
             send[mid : mid + reach, here] = total[tail + skip : tail + skip + reach].astype(HALF)
 
 
-def forward(blocks, gate, up, down, place, part, back):
+def forward(blocks, gate, up, down, place, part, back, cost=COST):
     n, (width, hidden) = len(blocks), gate.shape
     count = padded_rows(n)
     in_vmem = pl.BlockSpec(memory_space=pltpu.VMEM)
@@ -211,13 +212,14 @@
             pltpu.VMEM((count, width), HALF),
         ],
         compiler_params=params(LIMIT),
-        cost_estimate=pl.CostEstimate(flops=COST, bytes_accessed=0, transcendentals=0),
+        cost_estimate=pl.CostEstimate(flops=cost, bytes_accessed=0, transcendentals=0),
         name="forward_back" if back else "forward",
     )(place, *blocks, gate, up, down)
 
 
-def grads_kernel(n, *refs):
+def grads_kernel(n, early, *refs):
     own, parts, came, refs = refs[:n], refs[n : 2 * n], refs[2 * n : 3 * n], refs[3 * n :]
+    sums, refs = refs[:early], refs[early:]
     gate_grad, up_grad, down_grad, act_rows, part_rows = refs
     start, reach = 0, act_rows.shape[1]
     for mine, piece, other in zip(own, parts, came):
@@ -230,42 +232,47 @@
         start += 2 * count
     part = part_rows.shape[1] // 2
     tiles = act_rows.shape[1] // (3 * TILE)
+
+    def put(k, out, rows, columns, value):
+        if early:
+            value = value + sums[k][rows, columns].astype(FULL)
+        out[rows, columns] = value.astype(HALF)
+
     for i in range(part // TILE):
         picked = part_rows[:, i * TILE : (i + 1) * TILE].T
         here = slice(i * TILE, (i + 1) * TILE)
         for j in range(tiles):
             at = 3 * TILE * j
             there = slice(j * TILE, (j + 1) * TILE)
-            gate_grad[here, there] = jnp.dot(
-                picked, act_rows[:, at + TILE : at + 2 * TILE], preferred_element_type=FULL
-            ).astype(HALF)
-            up_grad[here, there] = jnp.dot(
-                picked, act_rows[:, at + 2 * TILE : at + 3 * TILE], preferred_element_type=FULL
-            ).astype(HALF)
+            gate_back = act_rows[:, at + TILE : at + 2 * TILE]
+            up_back = act_rows[:, at + 2 * TILE : at + 3 * TILE]
+            put(0, gate_grad, here, there, jnp.dot(picked, gate_back, preferred_element_type=FULL))
+            put(1, up_grad, here, there, jnp.dot(picked, up_back, preferred_element_type=FULL))
+    cotan = part_rows[:, part : 2 * part]
     for j in range(tiles):
         at = 3 * TILE * j
         hidden = act_rows[:, at : at + TILE].T
-        down_grad[j * TILE : (j + 1) * TILE, :] = jnp.dot(
-            hidden, part_rows[:, part : 2 * part], preferred_element_type=FULL
-        ).astype(HALF)
-
-
-def grads(own, parts, came, hidden):
+        here = slice(j * TILE, (j + 1) * TILE)
+        value = jnp.dot(hidden, cotan, preferred_element_type=FULL)
+        put(2, down_grad, here, slice(0, part), value)
+
+
+def grads(own, parts, came, hidden, early=(), cost=COST):
     n, count, part = len(own), 2 * sum(a.shape[0] for a in own), parts[0].shape[1] // 2
     in_vmem = pl.BlockSpec(memory_space=pltpu.VMEM)
     return pl.pallas_call(
-        functools.partial(grads_kernel, n),
-        in_specs=[in_vmem] * (3 * n),
+        functools.partial(grads_kernel, n, len(early)),
+        in_specs=[in_vmem] * (3 * n + len(early)),
         out_specs=[in_vmem] * 3,
         out_shape=[shape((part, hidden)), shape((part, hidden)), shape((hidden, part))],
         scratch_shapes=[
             pltpu.VMEM((count, 3 * hidden), HALF),
             pltpu.VMEM((count, 2 * part), HALF),
         ],
-        compiler_params=params(24),
-        cost_estimate=pl.CostEstimate(flops=COST, bytes_accessed=0, transcendentals=0),
+        compiler_params=params(GRADS_LIMIT),
+        cost_estimate=pl.CostEstimate(flops=cost, bytes_accessed=0, transcendentals=0),
         name="grads",
-    )(*own, *parts, *came)
+    )(*own, *parts, *came, *early)
 
 
 def settle_kernel(place, block, out):
@@ -357,31 +364,25 @@
     )
     act0, own0, send0, keep0 = run([after(b0, xy0, z2), z1, x0, x1], back=True)
     came0 = over_x(send0)
-    y3 = over_z(after(y0, send0), -1)
-    act1, own1, send1, keep1 = run([after(z3, send0, y1), x3], back=True)
+    y3 = over_z(after(y0, z2), -1)
+    xy3 = over_z(after(xy0, send0), -1)
+    act1, own1, send1, keep1 = run([after(z3, send0, y1, y3), x3], back=True)
     came1 = over_x(send1)
-    xy3 = over_z(after(xy0, send1), -1)
     other0 = over_core(after(act0, send1))
-    act2, own2, send2, keep2 = run([after(z2, send1, xy1, y2, y3, came0), x2], back=True)
-    p0, p1 = merge(2, keep0, after(came0, send2))
-    came2, r1 = over_x(send2), over_z(p1, -1)
+    p0, p1 = merge(2, keep0, came0)
+    r1 = over_z(p1, -1)
+    act2, own2, send2, keep2 = run([after(z2, send1, xy1, y2, xy3, p1), x2], back=True)
+    (p3,) = merge(1, keep1, after(came1, send2))
+    came2, r3 = over_x(send2), over_z(p3, 1)
     other1 = over_core(after(act1, send2))
-    y0 = after(y0, send2, p1, xy2, came1, other0)
-    act3, own3 = run([y0, xy0, y1, xy1, y3, xy3], back=False)
-    (p3,) = merge(1, keep1, after(came1, act3))
-    (p2,) = merge(1, keep2, after(came2, act3))
-    r3, r2 = over_z(p3, 1), over_z(p2, 2)
-    other2, other3 = over_core(after(act2, act3)), over_core(act3)
-    y2 = after(y2, act3, r1, other1, p2, p3)
-    act4, own4 = run([y2, xy2], back=False)
-    other4 = over_core(act4)
-    act0 = after(act0, r3)
-    gate_grad, up_grad, down_grad = grads(
-        [act0, act1, act2, act3, act4],
-        [own0, own1, own2, own3, own4],
-        [other0, other1, other2, other3, other4],
-        gate_weight.shape[1],
-    )
+    y0 = after(y0, send2, r1, p3, xy2, other0)
+    act3, own3 = run([y0, xy0, y1, xy1, y3, xy3, y2, xy2], back=False)
+    (p2,) = merge(1, keep2, after(came2, act3, r3, other1))
+    r2 = over_z(p2, 2)
+    other2, other3 = over_core(act2), over_core(act3)
+    hidden = gate_weight.shape[1]
+    early = grads([act0, act1, act2], [own0, own1, own2], [other0, other1, other2], hidden, cost=4 * COST)
+    gate_grad, up_grad, down_grad = grads([act3], [own3], [other3], hidden, early, cost=10**6)
     token_grad = unpack(after(ids, gate_grad), [p0, r1, r2, r3])
     return token_grad, gate_grad, up_grad, down_grad
 

time: 121 us -> 107 us (0.88)
  waiting for transfers between devices: 35.7 us -> 26 us
  starting transfers between devices: 30.3 us -> 27.1 us
  Pallas kernels: 49.2 us -> 46.2 us
  local copies, waits for them, and re-layouts: 4.97 us -> 6.21 us
    ppermute x6, waiting for transfers between devices: 4.76 us -> 0.02 us  [over_y(): return lax.ppermute(v, 'dp', y_pairs)]
    ppermute x7, waiting for transfers between devices: 6.31 us -> 2.75 us  [over_x(): return lax.ppermute(v, 'expert', x_pairs)]
    pallas_call x5 -> x4, Pallas kernels: 35.2 us -> 31.6 us  [forward(): pl.pallas_call(functools.partial(forward_kernel, n, back), in_specs=[pl.B...]
    ppermute x8, starting transfers between devices: 13.3 us -> 10.3 us  [over_z(): lax.ppermute(v, 'expert', [(i, (i + 2 * by) % n_expert) for i in range(n_...]
    ppermute x8, waiting for transfers between devices: 24.6 us -> 23.2 us  [over_z(): lax.ppermute(v, 'expert', [(i, (i + 2 * by) % n_expert) for i in range(n_...]
    unnamed x36 -> x28, local copies, waits for them, and re-layouts: 4.97 us -> 6.21 us
    pallas_call x1 -> x2, Pallas kernels: 8.26 us -> 8.85 us  [grads(): pl.pallas_call(functools.partial(grads_kernel, n, len(early)), in_specs=[...]
  transfers between devices with their start and end apart: 26 -> 25, of which waited for: 9 -> 6; matrix products, arithmetic and copies ran while one was open for 0% -> 0% of each run, Pallas kernels for 37% -> 39%
where the time goes in v6:
time: 107 us; the launch traced here: 106 us
  Pallas kernels  46.2 us (43%)
  starting transfers between devices  27.1 us (25%)
  waiting for transfers between devices  26 us (24%)
  local copies, waits for them, and re-layouts  6.21 us (6%)
    pallas_call x4, Pallas kernels, forward(): pl.pallas_call(functools.partial(forward_kernel, n, back), in_specs=[pl.B...  31.6 us
    ppermute x8, waiting for transfers between devices, over_z(): lax.ppermute(v, 'expert', [(i, (i + 2 * by) % n_expert) for i in range(n_...  23.2 us
    ppermute x8, starting transfers between devices, over_z(): lax.ppermute(v, 'expert', [(i, (i + 2 * by) % n_expert) for i in range(n_...  10.3 us
    pallas_call x2, Pallas kernels, grads(): pl.pallas_call(functools.partial(grads_kernel, n, len(early)), in_specs=[...  8.85 us
    ppermute x7, starting transfers between devices, over_x(): return lax.ppermute(v, 'expert', x_pairs)  8.38 us
    ppermute x6, starting transfers between devices, over_y(): return lax.ppermute(v, 'dp', y_pairs)  7.66 us
    unnamed x28, local copies, waits for them, and re-layouts  6.21 us
    ppermute x7, waiting for transfers between devices, over_x(): return lax.ppermute(v, 'expert', x_pairs)  2.75 us
  transfers between devices with their start and end apart: 25, of which 6 were waited for; matrix products, arithmetic and copies ran while one was open for 0% of the time, Pallas kernels for 39%

profile of v6, /device:TPU:0, one launch (start us, length us, event | category | flops | bytes accessed | tf_op | source)
XLA Modules:
  0.0 106.4 jit_solution(52791561383611247)
XLA Ops:
  0.6 2.6 %pack.1.block.refs_0_ = bf16[72,3072]{1,0:T(8,128)(2,1)} custom-call(s32[2,128]{1,0:T(2,128)} %bitcast.4, f32[2,128]{1,0:T(2,128)} %bitcast.6, bf16[128,3072]{1,0:T(8,128)(2,1)} %tokens_in.1, bf16[128,3072]{1,0:T(8,128)(2,1)} %cotangent_in.1), custom_call_target="tpu_custom_call" | custom-call | tf_op jit(solution)/shard_map/pack/pallas_call | solution.py:82
  3.3 3.0 %collective-permute-start.2 = (bf16[72,3072]{1,0:T(8,128)(2,1)}, bf16[72,3072]{1,0:T(8,128)(2,1)S(1)}, u32[]{:S(2)}, u32[]{:S(2)}) collective-permute-start(bf16[72,3072]{1,0:T(8,128)(2,1)} %pack.1.block.refs_0_), channel_id=1, source_target_pairs={{0,1},{1,0},{2,3},{3,2},{4,5},{5,4},{6,7},{7,6},{8,9},{9,8},{10,11... | collective-permute-start | bytes 1327112 | tf_op jit(solution)/shard_map/ppermute | solution.py:337
  6.3 1.6 %collective-permute-start.1 = (bf16[72,3072]{1,0:T(8,128)(2,1)}, bf16[72,3072]{1,0:T(8,128)(2,1)S(1)}, u32[]{:S(2)}, u32[]{:S(2)}) collective-permute-start(bf16[72,3072]{1,0:T(8,128)(2,1)} %pack.1.block.refs_0_), channel_id=1, source_target_pairs={{0,2},{1,3},{2,4},{3,5},{4,6},{5,7},{6,0},{7,1},{8,10},{9,11},{10,... | collective-permute-start | bytes 1327112 | tf_op jit(solution)/shard_map/ppermute | solution.py:340
  7.8 1.5 %collective-permute-start = (bf16[72,3072]{1,0:T(8,128)(2,1)}, bf16[72,3072]{1,0:T(8,128)(2,1)S(1)}, u32[]{:S(2)}, u32[]{:S(2)}) collective-permute-start(bf16[72,3072]{1,0:T(8,128)(2,1)} %pack.1.block.refs_0_), channel_id=1, source_target_pairs={{0,16},{8,24},{16,0},{24,8},{1,17},{9,25},{17,1},{25,9},{2,18},{10... | collective-permute-start | bytes 1327112 | tf_op jit(solution)/shard_map/ppermute | solution.py:334
  9.4 0.1 pad_add_fusion.place
  9.4 1.0 copy-done
  10.5 1.1 %settle.1.place = s32[2]{0:T(128)S(1)} custom-call(s32[2]{0:T(128)S(1)} %pad_add_fusion.place, bf16[72,3072]{1,0:T(8,128)(2,1)S(1)} %copy-done), custom_call_target="tpu_custom_call" | custom-call | flops 20000000000 | tf_op jit(solution)/shard_map/settle/pallas_call | solution.py:285
  11.6 2.3 %collective-permute-start.4 = (bf16[72,3072]{1,0:T(8,128)(2,1)S(1)}, bf16[72,3072]{1,0:T(8,128)(2,1)S(1)}, u32[]{:S(2)}, u32[]{:S(2)}) collective-permute-start(bf16[72,3072]{1,0:T(8,128)(2,1)S(1)} %copy-done), channel_id=1, source_target_pairs={{0,6},{1,7},{2,0},{3,1},{4,2},{5,3},{6,4},{7,5},{8,14},{9,15},{10,... | collective-permute-start | bytes 1327112 | tf_op jit(solution)/shard_map/ppermute | solution.py:340
  13.9 2.7 %collective-permute-done.2.refs_2_ = bf16[72,3072]{1,0:T(8,128)(2,1)S(1)} collective-permute-done((bf16[72,3072]{1,0:T(8,128)(2,1)}, bf16[72,3072]{1,0:T(8,128)(2,1)S(1)}, u32[]{:S(2)}, u32[]{:S(2)}) %collective-permute-start.2) | collective-permute-done | bytes 442400 | tf_op jit(solution)/shard_map/ppermute | solution.py:337
  16.6 4.8 %collective-permute-done.1.refs_1_ = bf16[72,3072]{1,0:T(8,128)(2,1)S(1)} collective-permute-done((bf16[72,3072]{1,0:T(8,128)(2,1)}, bf16[72,3072]{1,0:T(8,128)(2,1)S(1)}, u32[]{:S(2)}, u32[]{:S(2)}) %collective-permute-start.1) | collective-permute-done | bytes 442400 | tf_op jit(solution)/shard_map/ppermute | solution.py:340
  21.4 0.3 collective-permute-start.6
  21.7 1.7 %collective-permute-start.5 = (bf16[72,3072]{1,0:T(8,128)(2,1)S(1)}, bf16[72,3072]{1,0:T(8,128)(2,1)S(1)}, u32[]{:S(2)}, u32[]{:S(2)}) collective-permute-start(bf16[72,3072]{1,0:T(8,128)(2,1)S(1)} %collective-permute-done.2.refs_2_), channel_id=1, source_target_pairs={{0,16},{8,24},{16,0},{24,8},{1,17},{9,25},{17,1},{25,9},{2,18},{10... | collective-permute-start | bytes 1327112 | tf_op jit(solution)/shard_map/ppermute | solution.py:334
  23.5 0.3 collective-permute-start.7
  23.8 7.0 %collective-permute-done.4.refs_0_ = bf16[72,3072]{1,0:T(8,128)(2,1)S(1)} collective-permute-done((bf16[72,3072]{1,0:T(8,128)(2,1)S(1)}, bf16[72,3072]{1,0:T(8,128)(2,1)S(1)}, u32[]{:S(2)}, u32[]{:S(2)}) %collective-permute-start.4) | collective-permute-done | bytes 442400 | tf_op jit(solution)/shard_map/ppermute | solution.py:340
  30.8 0.3 collective-permute-start.9
  31.1 7.9 %collective-permute-done.3.refs_0_ = bf16[72,3072]{1,0:T(8,128)(2,1)S(1)} collective-permute-done((bf16[72,3072]{1,0:T(8,128)(2,1)S(1)}, bf16[72,3072]{1,0:T(8,128)(2,1)S(1)}, u32[]{:S(2)}, u32[]{:S(2)}) %collective-permute-start.3) | collective-permute-done | bytes 442400 | tf_op jit(solution)/shard_map/ppermute | solution.py:340
  39.0 0.5 collective-permute-start.14
  39.5 1.5 %collective-permute-start.11 = (bf16[72,3072]{1,0:T(8,128)(2,1)S(1)}, bf16[72,3072]{1,0:T(8,128)(2,1)S(1)}, u32[]{:S(2)}, u32[]{:S(2)}) collective-permute-start(bf16[72,3072]{1,0:T(8,128)(2,1)S(1)} %collective-permute-done.3.refs_0_), channel_id=1, source_target_pairs={{0,16},{8,24},{16,0},{24,8},{1,17},{9,25},{17,1},{25,9},{2,18},{10... | collective-permute-start | bytes 1327112 | tf_op jit(solution)/shard_map/ppermute | solution.py:334
  41.1 4.0 %collective-permute-start.8 = (bf16[72,3072]{1,0:T(8,128)(2,1)S(1)}, bf16[72,3072]{1,0:T(8,128)(2,1)S(1)}, u32[]{:S(2)}, u32[]{:S(2)}) collective-permute-start(bf16[72,3072]{1,0:T(8,128)(2,1)S(1)} %collective-permute-done.refs_0_), channel_id=1, source_target_pairs={{0,6},{1,7},{2,0},{3,1},{4,2},{5,3},{6,4},{7,5},{8,14},{9,15},{10,... | collective-permute-start | bytes 1327112 | tf_op jit(solution)/shard_map/ppermute | solution.py:340
  45.0 7.8 %forward_back.3 = (bf16[144,4608]{1,0:T(8,128)(2,1)S(1)}, bf16[144,1536]{1,0:T(8,128)(2,1)S(1)}, bf16[72,3072]{1,0:T(8,128)(2,1)S(1)}, bf16[72,3072]{1,0:T(8,128)(2,1)S(1)}) custom-call(s32[2]{0:T(128)S(1)} %settle.1.place, bf16[72,3072]{1,0:T(8,128)(2,1)S(1)} %copy-done.1, bf16[72,3072]{1,0:T(8,128)(2,1)S(1)} %collective-permute-done.1.refs_1_, ...), custom_call_target="tpu_custom_call" | custom-call | flops 10000000000 | tf_op jit(solution)/shard_map/forward_back/pallas_call | solution.py:205
  52.8 0.8 copy-done.8
  53.6 1.4 %collective-permute-start.13 = (bf16[72,3072]{1,0:T(8,128)(2,1)S(1)}, bf16[72,3072]{1,0:T(8,128)(2,1)S(1)}, u32[]{:S(2)}, u32[]{:S(2)}) collective-permute-start(bf16[72,3072]{1,0:T(8,128)(2,1)S(1)} %get-tuple-element.46), channel_id=1, source_target_pairs={{0,1},{1,0},{2,3},{3,2},{4,5},{5,4},{6,7},{7,6},{8,9},{9,8},{10,11... | collective-permute-start | bytes 1327112 | tf_op jit(solution)/shard_map/ppermute | solution.py:337
  55.0 0.5 collective-permute-start.10
  55.5 0.6 collective-permute-start.12
  56.1 8.4 %forward_back.4 = (bf16[80,4608]{1,0:T(8,128)(2,1)S(1)}, bf16[80,1536]{1,0:T(8,128)(2,1)S(1)}, bf16[40,3072]{1,0:T(8,128)(2,1)S(1)}, bf16[40,3072]{1,0:T(8,128)(2,1)S(1)}) custom-call(s32[2]{0:T(128)S(1)} %settle.1.place, bf16[72,3072]{1,0:T(8,128)(2,1)S(1)} %collective-permute-done.4.refs_0_, bf16[72,3072]{1,0:T(8,128)(2,1)S(1)} %collective-permute-done.9.refs_1_, ...), custom_call_target="tpu_custom_call" | custom-call | flops 10000000000 | tf_op jit(solution)/shard_map/forward_back/pallas_call | solution.py:205
  64.5 0.1 collective-permute-start.18
  64.6 0.1 merge.3
  64.7 2.5 %collective-permute-start.16 = (bf16[40,3072]{1,0:T(8,128)(2,1)S(1)}, bf16[40,3072]{1,0:T(8,128)(2,1)S(1)}, u32[]{:S(2)}, u32[]{:S(2)}) collective-permute-start(bf16[40,3072]{1,0:T(8,128)(2,1)S(1)} %get-tuple-element.49), channel_id=1, source_target_pairs={{0,1},{1,0},{2,3},{3,2},{4,5},{5,4},{6,7},{7,6},{8,9},{9,8},{10,11... | collective-permute-start | bytes 737288 | tf_op jit(solution)/shard_map/ppermute | solution.py:337
  67.3 2.1 %collective-permute-start.17 = (bf16[72,3072]{1,0:T(8,128)(2,1)S(1)}, bf16[72,3072]{1,0:T(8,128)(2,1)S(1)}, u32[]{:S(2)}, u32[]{:S(2)}) collective-permute-start(bf16[72,3072]{1,0:T(8,128)(2,1)S(1)} %collective-permute-done.14.refs_1_), channel_id=1, source_target_pairs={{0,16},{8,24},{16,0},{24,8},{1,17},{9,25},{17,1},{25,9},{2,18},{10... | collective-permute-start | bytes 1327112 | tf_op jit(solution)/shard_map/ppermute | solution.py:334
  69.3 9.1 %forward_back.5 = (bf16[80,4608]{1,0:T(8,128)(2,1)S(1)}, bf16[80,1536]{1,0:T(8,128)(2,1)S(1)}, bf16[40,3072]{1,0:T(8,128)(2,1)}, bf16[40,3072]{1,0:T(8,128)(2,1)S(1)}) custom-call(s32[2]{0:T(128)S(1)} %settle.1.place, bf16[72,3072]{1,0:T(8,128)(2,1)S(1)} %collective-permute-done.3.refs_0_, bf16[72,3072]{1,0:T(8,128)(2,1)S(1)} %collective-permute-done.14.refs_1_, ...), custom_call_target="tpu_custom_call" | custom-call | flops 10000000000 | tf_op jit(solution)/shard_map/forward_back/pallas_call | solution.py:205
  78.4 0.7 copy-done.12
  79.1 0.3 collective-permute-start.22
  79.4 0.1 merge.4
  79.5 0.6 collective-permute-start.21
  80.1 0.8 copy-done.6
  80.8 1.8 %collective-permute-start.23 = (bf16[40,3072]{1,0:T(8,128)(2,1)S(1)}, bf16[40,3072]{1,0:T(8,128)(2,1)S(1)}, u32[]{:S(2)}, u32[]{:S(2)}) collective-permute-start(bf16[40,3072]{1,0:T(8,128)(2,1)S(1)} %merge.4), channel_id=1, source_target_pairs={{0,2},{1,3},{2,4},{3,5},{4,6},{5,7},{6,0},{7,1},{8,10},{9,11},{10,... | collective-permute-start | bytes 737288 | tf_op jit(solution)/shard_map/ppermute | solution.py:340
  82.6 1.0 copy-done.7
  83.6 6.4 %forward.1 = (bf16[288,4608]{1,0:T(8,128)(2,1)S(1)}, bf16[288,1536]{1,0:T(8,128)(2,1)S(1)}) custom-call(s32[2]{0:T(128)S(1)} %settle.1.place, bf16[72,3072]{1,0:T(8,128)(2,1)S(1)} %collective-permute-done.refs_0_, bf16[72,3072]{1,0:T(8,128)(2,1)S(1)} %collective-permute-done.5.refs_1_, bf16[72,3072]{1,0:T(8,128)(2,1)S(1)} %collective-permute-done.7.refs_2_, ...), custom_call_target="tpu_custom_call" | custom-call | flops 10000000000 | tf_op jit(solution)/shard_map/forward/pallas_call | solution.py:205
  90.1 0.1 collective-permute-start.19
  90.1 0.4 collective-permute-done.23.refs_3_
  90.5 0.1 merge.5
  90.6 0.1 collective-permute-start.24
  90.7 1.0 copy-done.9
  91.7 0.9 copy-done.13
  92.6 3.8 %grads.2 = (bf16[768,1024]{1,0:T(8,128)(2,1)S(1)}, bf16[768,1024]{1,0:T(8,128)(2,1)S(1)}, bf16[1024,768]{1,0:T(8,128)(2,1)S(1)}) custom-call(bf16[144,4608]{1,0:T(8,128)(2,1)S(1)} %get-tuple-element.60.refs_0_, bf16[80,4608]{1,0:T(8,128)(2,1)S(1)} %get-tuple-element.69.refs_1_, bf16[80,4608]{1,0:T(8,128)(2,1)S(1)} %get-tuple-element.65.refs_2_, ...), custom_call_target="tpu_custom_call" | custom-call | flops 40000000000 | tf_op jit(solution)/shard_map/grads/pallas_call | solution.py:263
  96.5 5.0 %grads.3 = (bf16[768,1024]{1,0:T(8,128)(2,1)}, bf16[768,1024]{1,0:T(8,128)(2,1)}, bf16[1024,768]{1,0:T(8,128)(2,1)}) custom-call(bf16[288,4608]{1,0:T(8,128)(2,1)S(1)} %get-tuple-element.62.refs_0_, bf16[288,1536]{1,0:T(8,128)(2,1)S(1)} %get-tuple-element.63.refs_1_, bf16[288,4608]{1,0:T(8,128)(2,1)S(1)} %collective-permute-done.19.refs_2_, ...), custom_call_target="tpu_custom_call" | custom-call | flops 1000000 | tf_op jit(solution)/shard_map/grads/pallas_call | solution.py:263
  101.5 3.2 %collective-permute-done.24.refs_2_ = bf16[40,3072]{1,0:T(8,128)(2,1)S(1)} collective-permute-done((bf16[40,3072]{1,0:T(8,128)(2,1)S(1)}, bf16[40,3072]{1,0:T(8,128)(2,1)S(1)}, u32[]{:S(2)}, u32[]{:S(2)}) %collective-permute-start.24) | collective-permute-done | bytes 245792 | tf_op jit(solution)/shard_map/ppermute | solution.py:340
  104.7 1.7 %unpack.1 = bf16[128,3072]{1,0:T(8,128)(2,1)} custom-call(s32[2,128]{1,0:T(2,128)S(1)} %bitcast.5, bf16[40,3072]{1,0:T(8,128)(2,1)S(1)} %get-tuple-element.75.refs_0_, bf16[40,3072]{1,0:T(8,128)(2,1)S(1)} %collective-permute-done.15.refs_1_, bf16[40,3072]{1,0:T(8,128)(2,1)S(1)} %collective-permute-done.24.refs_2_, ...), custom_call_target="tpu_custom_call" | custom-call | tf_op jit(solution)/shard_map/unpack/pallas_call | solution.py:106
  (43 shorter events, 0.1 us)
Async XLA Ops:
  3.3 13.4 %collective-permute-start.2 = (bf16[72,3072]{1,0:T(8,128)(2,1)}, bf16[72,3072]{1,0:T(8,128)(2,1)S(1)}, u32[]{:S(2)}, u32[]{:S(2)}) collective-permute-start(bf16[72,3072]{1,0:T(8,128)(2,1)} %pack.1.block.refs_0_), channel_id=1, source_target_pairs={{0,1},{1,0},{2,3},{3,2},{4,5},{5,4},{6,7},{7,6},{8,9},{9,8},{10,11... | collective-permute-start | bytes 1327112 | tf_op jit(solution)/shard_map/ppermute | solution.py:337
  6.3 15.1 %collective-permute-start.1 = (bf16[72,3072]{1,0:T(8,128)(2,1)}, bf16[72,3072]{1,0:T(8,128)(2,1)S(1)}, u32[]{:S(2)}, u32[]{:S(2)}) collective-permute-start(bf16[72,3072]{1,0:T(8,128)(2,1)} %pack.1.block.refs_0_), channel_id=1, source_target_pairs={{0,2},{1,3},{2,4},{3,5},{4,6},{5,7},{6,0},{7,1},{8,10},{9,11},{10,... | collective-permute-start | bytes 1327112 | tf_op jit(solution)/shard_map/ppermute | solution.py:340
  7.8 13.6 %collective-permute-start = (bf16[72,3072]{1,0:T(8,128)(2,1)}, bf16[72,3072]{1,0:T(8,128)(2,1)S(1)}, u32[]{:S(2)}, u32[]{:S(2)}) collective-permute-start(bf16[72,3072]{1,0:T(8,128)(2,1)} %pack.1.block.refs_0_), channel_id=1, source_target_pairs={{0,16},{8,24},{16,0},{24,8},{1,17},{9,25},{17,1},{25,9},{2,18},{10... | collective-permute-start | bytes 1327112 | tf_op jit(solution)/shard_map/ppermute | solution.py:334
  9.4 1.0 copy-start
  10.4 34.6 %copy-start.1 = (bf16[72,3072]{1,0:T(8,128)(2,1)S(1)}, bf16[72,3072]{1,0:T(8,128)(2,1)}, u32[]{:S(2)}) copy-start(bf16[72,3072]{1,0:T(8,128)(2,1)} %pack.1.block.refs_0_) | copy-start | bytes 1327108
  10.5 34.6 %copy-start.3 = (bf16[3072,1024]{1,0:T(8,128)(2,1)S(1)}, bf16[3072,1024]{1,0:T(8,128)(2,1)}, u32[]{:S(2)}) copy-start(bf16[3072,1024]{1,0:T(8,128)(2,1)} %refs_8_.1) | copy-start | bytes 18874372
  10.5 34.6 %copy-start.4 = (bf16[3072,1024]{1,0:T(8,128)(2,1)S(1)}, bf16[3072,1024]{1,0:T(8,128)(2,1)}, u32[]{:S(2)}) copy-start(bf16[3072,1024]{1,0:T(8,128)(2,1)} %refs_9_.1) | copy-start | bytes 18874372
  10.5 34.6 %copy-start.5 = (bf16[1024,3072]{1,0:T(8,128)(2,1)S(1)}, bf16[1024,3072]{1,0:T(8,128)(2,1)}, u32[]{:S(2)}) copy-start(bf16[1024,3072]{1,0:T(8,128)(2,1)} %refs_10_.1) | copy-start | bytes 18874372
  11.6 19.2 %collective-permute-start.4 = (bf16[72,3072]{1,0:T(8,128)(2,1)S(1)}, bf16[72,3072]{1,0:T(8,128)(2,1)S(1)}, u32[]{:S(2)}, u32[]{:S(2)}) collective-permute-start(bf16[72,3072]{1,0:T(8,128)(2,1)S(1)} %copy-done), channel_id=1, source_target_pairs={{0,6},{1,7},{2,0},{3,1},{4,2},{5,3},{6,4},{7,5},{8,14},{9,15},{10,... | collective-permute-start | bytes 1327112 | tf_op jit(solution)/shard_map/ppermute | solution.py:340
  21.4 9.7 %collective-permute-start.6 = (bf16[72,3072]{1,0:T(8,128)(2,1)S(1)}, bf16[72,3072]{1,0:T(8,128)(2,1)S(1)}, u32[]{:S(2)}, u32[]{:S(2)}) collective-permute-start(bf16[72,3072]{1,0:T(8,128)(2,1)S(1)} %collective-permute-done.1.refs_1_), channel_id=1, source_target_pairs={{0,1},{1,0},{2,3},{3,2},{4,5},{5,4},{6,7},{7,6},{8,9},{9,8},{10,11... | collective-permute-start | bytes 1327112 | tf_op jit(solution)/shard_map/ppermute | solution.py:337
  21.7 17.3 %collective-permute-start.3 = (bf16[72,3072]{1,0:T(8,128)(2,1)S(1)}, bf16[72,3072]{1,0:T(8,128)(2,1)S(1)}, u32[]{:S(2)}, u32[]{:S(2)}) collective-permute-start(bf16[72,3072]{1,0:T(8,128)(2,1)S(1)} %collective-permute-done.1.refs_1_), channel_id=1, source_target_pairs={{0,2},{1,3},{2,4},{3,5},{4,6},{5,7},{6,0},{7,1},{8,10},{9,11},{10,... | collective-permute-start | bytes 1327112 | tf_op jit(solution)/shard_map/ppermute | solution.py:340
  21.7 19.3 %collective-permute-start.5 = (bf16[72,3072]{1,0:T(8,128)(2,1)S(1)}, bf16[72,3072]{1,0:T(8,128)(2,1)S(1)}, u32[]{:S(2)}, u32[]{:S(2)}) collective-permute-start(bf16[72,3072]{1,0:T(8,128)(2,1)S(1)} %collective-permute-done.2.refs_2_), channel_id=1, source_target_pairs={{0,16},{8,24},{16,0},{24,8},{1,17},{9,25},{17,1},{25,9},{2,18},{10... | collective-permute-start | bytes 1327112 | tf_op jit(solution)/shard_map/ppermute | solution.py:334
  23.5 30.1 %collective-permute-start.7 = (bf16[72,3072]{1,0:T(8,128)(2,1)S(1)}, bf16[72,3072]{1,0:T(8,128)(2,1)S(1)}, u32[]{:S(2)}, u32[]{:S(2)}) collective-permute-start(bf16[72,3072]{1,0:T(8,128)(2,1)S(1)} %collective-permute-done.1.refs_1_), channel_id=1, source_target_pairs={{0,16},{8,24},{16,0},{24,8},{1,17},{9,25},{17,1},{25,9},{2,18},{10... | collective-permute-start | bytes 1327112 | tf_op jit(solution)/shard_map/ppermute | solution.py:334
  30.8 24.7 %collective-permute-start.9 = (bf16[72,3072]{1,0:T(8,128)(2,1)S(1)}, bf16[72,3072]{1,0:T(8,128)(2,1)S(1)}, u32[]{:S(2)}, u32[]{:S(2)}) collective-permute-start(bf16[72,3072]{1,0:T(8,128)(2,1)S(1)} %collective-permute-done.4.refs_0_), channel_id=1, source_target_pairs={{0,1},{1,0},{2,3},{3,2},{4,5},{5,4},{6,7},{7,6},{8,9},{9,8},{10,11... | collective-permute-start | bytes 1327112 | tf_op jit(solution)/shard_map/ppermute | solution.py:337
  39.0 28.2 %collective-permute-start.14 = (bf16[72,3072]{1,0:T(8,128)(2,1)S(1)}, bf16[72,3072]{1,0:T(8,128)(2,1)S(1)}, u32[]{:S(2)}, u32[]{:S(2)}) collective-permute-start(bf16[72,3072]{1,0:T(8,128)(2,1)S(1)} %collective-permute-done.3.refs_0_), channel_id=1, source_target_pairs={{0,1},{1,0},{2,3},{3,2},{4,5},{5,4},{6,7},{7,6},{8,9},{9,8},{10,11... | collective-permute-start | bytes 1327112 | tf_op jit(solution)/shard_map/ppermute | solution.py:337
  39.5 27.7 %collective-permute-start.11 = (bf16[72,3072]{1,0:T(8,128)(2,1)S(1)}, bf16[72,3072]{1,0:T(8,128)(2,1)S(1)}, u32[]{:S(2)}, u32[]{:S(2)}) collective-permute-start(bf16[72,3072]{1,0:T(8,128)(2,1)S(1)} %collective-permute-done.3.refs_0_), channel_id=1, source_target_pairs={{0,16},{8,24},{16,0},{24,8},{1,17},{9,25},{17,1},{25,9},{2,18},{10... | collective-permute-start | bytes 1327112 | tf_op jit(solution)/shard_map/ppermute | solution.py:334
  41.1 13.9 %collective-permute-start.8 = (bf16[72,3072]{1,0:T(8,128)(2,1)S(1)}, bf16[72,3072]{1,0:T(8,128)(2,1)S(1)}, u32[]{:S(2)}, u32[]{:S(2)}) collective-permute-start(bf16[72,3072]{1,0:T(8,128)(2,1)S(1)} %collective-permute-done.refs_0_), channel_id=1, source_target_pairs={{0,6},{1,7},{2,0},{3,1},{4,2},{5,3},{6,4},{7,5},{8,14},{9,15},{10,... | collective-permute-start | bytes 1327112 | tf_op jit(solution)/shard_map/ppermute | solution.py:340
  52.8 0.8 copy-start.8
  53.6 10.9 %collective-permute-start.13 = (bf16[72,3072]{1,0:T(8,128)(2,1)S(1)}, bf16[72,3072]{1,0:T(8,128)(2,1)S(1)}, u32[]{:S(2)}, u32[]{:S(2)}) collective-permute-start(bf16[72,3072]{1,0:T(8,128)(2,1)S(1)} %get-tuple-element.46), channel_id=1, source_target_pairs={{0,1},{1,0},{2,3},{3,2},{4,5},{5,4},{6,7},{7,6},{8,9},{9,8},{10,11... | collective-permute-start | bytes 1327112 | tf_op jit(solution)/shard_map/ppermute | solution.py:337
  55.0 9.7 %collective-permute-start.10 = (bf16[72,3072]{1,0:T(8,128)(2,1)S(1)}, bf16[72,3072]{1,0:T(8,128)(2,1)S(1)}, u32[]{:S(2)}, u32[]{:S(2)}) collective-permute-start(bf16[72,3072]{1,0:T(8,128)(2,1)S(1)} %collective-permute-done.6.refs_3_), channel_id=1, source_target_pairs={{0,16},{8,24},{16,0},{24,8},{1,17},{9,25},{17,1},{25,9},{2,18},{10... | collective-permute-start | bytes 1327112 | tf_op jit(solution)/shard_map/ppermute | solution.py:334
  55.5 11.7 %collective-permute-start.12 = (bf16[72,3072]{1,0:T(8,128)(2,1)S(1)}, bf16[72,3072]{1,0:T(8,128)(2,1)S(1)}, u32[]{:S(2)}, u32[]{:S(2)}) collective-permute-start(bf16[72,3072]{1,0:T(8,128)(2,1)S(1)} %collective-permute-done.5.refs_1_), channel_id=1, source_target_pairs={{0,6},{1,7},{2,0},{3,1},{4,2},{5,3},{6,4},{7,5},{8,14},{9,15},{10,... | collective-permute-start | bytes 1327112 | tf_op jit(solution)/shard_map/ppermute | solution.py:340
  64.5 2.7 %copy-start.10 = (bf16[80,1536]{1,0:T(8,128)(2,1)}, bf16[80,1536]{1,0:T(8,128)(2,1)S(1)}, u32[]{:S(2)}) copy-start(bf16[80,1536]{1,0:T(8,128)(2,1)S(1)} %get-tuple-element.67.refs_4_) | copy-start | bytes 737284
  64.5 18.1 %collective-permute-start.18 = (bf16[144,4608]{1,0:T(8,128)(2,1)S(1)}, bf16[144,4608]{1,0:T(8,128)(2,1)S(1)}, u32[]{:S(2)}, u32[]{:S(2)}) collective-permute-start(bf16[144,4608]{1,0:T(8,128)(2,1)S(1)} %get-tuple-element.60.refs_0_), channel_id=1, source_target_pairs={{0,8},{8,0},{16,24},{24,16},{1,9},{9,1},{17,25},{25,17},{2,10},{10... | collective-permute-start | bytes 3981320 | tf_op jit(solution)/shard_map/ppermute | solution.py:331
  64.7 14.7 %collective-permute-start.16 = (bf16[40,3072]{1,0:T(8,128)(2,1)S(1)}, bf16[40,3072]{1,0:T(8,128)(2,1)S(1)}, u32[]{:S(2)}, u32[]{:S(2)}) collective-permute-start(bf16[40,3072]{1,0:T(8,128)(2,1)S(1)} %get-tuple-element.49), channel_id=1, source_target_pairs={{0,1},{1,0},{2,3},{3,2},{4,5},{5,4},{6,7},{7,6},{8,9},{9,8},{10,11... | collective-permute-start | bytes 737288 | tf_op jit(solution)/shard_map/ppermute | solution.py:337
  67.2 12.3 %collective-permute-start.15 = (bf16[40,3072]{1,0:T(8,128)(2,1)S(1)}, bf16[40,3072]{1,0:T(8,128)(2,1)S(1)}, u32[]{:S(2)}, u32[]{:S(2)}) collective-permute-start(bf16[40,3072]{1,0:T(8,128)(2,1)S(1)} %get-tuple-element.54), channel_id=1, source_target_pairs={{0,6},{1,7},{2,0},{3,1},{4,2},{5,3},{6,4},{7,5},{8,14},{9,15},{10,... | collective-permute-start | bytes 737288 | tf_op jit(solution)/shard_map/ppermute | solution.py:340
  67.3 12.8 %collective-permute-start.17 = (bf16[72,3072]{1,0:T(8,128)(2,1)S(1)}, bf16[72,3072]{1,0:T(8,128)(2,1)S(1)}, u32[]{:S(2)}, u32[]{:S(2)}) collective-permute-start(bf16[72,3072]{1,0:T(8,128)(2,1)S(1)} %collective-permute-done.14.refs_1_), channel_id=1, source_target_pairs={{0,16},{8,24},{16,0},{24,8},{1,17},{9,25},{17,1},{25,9},{2,18},{10... | collective-permute-start | bytes 1327112 | tf_op jit(solution)/shard_map/ppermute | solution.py:334
  78.4 0.7 copy-start.12
  79.1 11.0 %collective-permute-start.22 = (bf16[40,3072]{1,0:T(8,128)(2,1)}, bf16[40,3072]{1,0:T(8,128)(2,1)S(1)}, u32[]{:S(2)}, u32[]{:S(2)}) collective-permute-start(bf16[40,3072]{1,0:T(8,128)(2,1)} %get-tuple-element.56), channel_id=1, source_target_pairs={{0,1},{1,0},{2,3},{3,2},{4,5},{5,4},{6,7},{7,6},{8,9},{9,8},{10,11... | collective-permute-start | bytes 737288 | tf_op jit(solution)/shard_map/ppermute | solution.py:337
  79.4 11.1 %collective-permute-start.20 = (bf16[80,4608]{1,0:T(8,128)(2,1)S(1)}, bf16[80,4608]{1,0:T(8,128)(2,1)S(1)}, u32[]{:S(2)}, u32[]{:S(2)}) collective-permute-start(bf16[80,4608]{1,0:T(8,128)(2,1)S(1)} %get-tuple-element.69.refs_1_), channel_id=1, source_target_pairs={{0,8},{8,0},{16,24},{24,16},{1,9},{9,1},{17,25},{25,17},{2,10},{10... | collective-permute-start | bytes 2211848 | tf_op jit(solution)/shard_map/ppermute | solution.py:331
  79.4 11.3 %copy-start.11 = (bf16[80,1536]{1,0:T(8,128)(2,1)S(1)}, bf16[80,1536]{1,0:T(8,128)(2,1)}, u32[]{:S(2)}) copy-start(bf16[80,1536]{1,0:T(8,128)(2,1)} %copy-done.10) | copy-start | bytes 737284
  79.5 11.2 %collective-permute-start.21 = (bf16[80,4608]{1,0:T(8,128)(2,1)S(1)}, bf16[80,4608]{1,0:T(8,128)(2,1)S(1)}, u32[]{:S(2)}, u32[]{:S(2)}) collective-permute-start(bf16[80,4608]{1,0:T(8,128)(2,1)S(1)} %get-tuple-element.65.refs_2_), channel_id=1, source_target_pairs={{0,8},{8,0},{16,24},{24,16},{1,9},{9,1},{17,25},{25,17},{2,10},{10... | collective-permute-start | bytes 2211848 | tf_op jit(solution)/shard_map/ppermute | solution.py:331
  80.1 0.8 copy-start.6
  80.8 9.7 %collective-permute-start.23 = (bf16[40,3072]{1,0:T(8,128)(2,1)S(1)}, bf16[40,3072]{1,0:T(8,128)(2,1)S(1)}, u32[]{:S(2)}, u32[]{:S(2)}) collective-permute-start(bf16[40,3072]{1,0:T(8,128)(2,1)S(1)} %merge.4), channel_id=1, source_target_pairs={{0,2},{1,3},{2,4},{3,5},{4,6},{5,7},{6,0},{7,1},{8,10},{9,11},{10,... | collective-permute-start | bytes 737288 | tf_op jit(solution)/shard_map/ppermute | solution.py:340
  82.6 1.0 copy-start.7
  90.1 6.4 %collective-permute-start.19 = (bf16[288,4608]{1,0:T(8,128)(2,1)S(1)}, bf16[288,4608]{1,0:T(8,128)(2,1)S(1)}, u32[]{:S(2)}, u32[]{:S(2)}) collective-permute-start(bf16[288,4608]{1,0:T(8,128)(2,1)S(1)} %get-tuple-element.62.refs_0_), channel_id=1, source_target_pairs={{0,8},{8,0},{16,24},{24,16},{1,9},{9,1},{17,25},{25,17},{2,10},{10... | collective-permute-start | bytes 7962632 | tf_op jit(solution)/shard_map/ppermute | solution.py:331
  90.6 14.1 %collective-permute-start.24 = (bf16[40,3072]{1,0:T(8,128)(2,1)S(1)}, bf16[40,3072]{1,0:T(8,128)(2,1)S(1)}, u32[]{:S(2)}, u32[]{:S(2)}) collective-permute-start(bf16[40,3072]{1,0:T(8,128)(2,1)S(1)} %merge.5), channel_id=1, source_target_pairs={{0,4},{1,5},{2,6},{3,7},{4,0},{5,1},{6,2},{7,3},{8,12},{9,13},{10,... | collective-permute-start | bytes 737288 | tf_op jit(solution)/shard_map/ppermute | solution.py:340
  90.7 1.0 copy-start.9
  91.7 0.9 copy-start.13
  96.5 8.2 %copy-start.2 = (s32[128,2]{0,1:T(2,128)S(1)}, s32[128,2]{0,1:T(2,128)}, u32[]{:S(2)}) copy-start(s32[128,2]{0,1:T(2,128)} %param.9) | copy-start | bytes 3076

commit v7 on v6

--- a/solution.py
+++ b/solution.py
@@ -15,6 +15,7 @@
 GRADS_LIMIT = 14
 WAIT = 20 * 10**9
 COST = 10**10
+COSTS = (10**10, 10**10, 10**6, 10**10, 4 * 10**10, 10**6)
 HALF = jnp.bfloat16
 FULL = jnp.float32
 
@@ -110,7 +111,7 @@
         + [pl.BlockSpec((depth, step), lambda j: (0, j)) for _ in pieces],
         out_specs=pl.BlockSpec((count, step), lambda j: (0, j)),
         out_shape=shape((count, width)),
-        compiler_params=params(32),
+        compiler_params=params(LIMIT),
         name="unpack",
     )(ids, *pieces)
 
@@ -152,12 +153,18 @@
 
 
 def forward_kernel(n, back, place, *refs):
-    blocks, weights, refs = refs[:n], refs[n : n + 3], refs[n + 3 :]
+    arrays, weights, refs = refs[:n], refs[n : n + 3], refs[n + 3 :]
+    blocks = []
+    for array in arrays:
+        blocks += [array] if len(array.shape) == 2 else [array.at[0], array.at[1]]
+    n = len(blocks)
     acts, own = refs[:2]
     refs = refs[2:]
-    if back:
+    if back == "halves":
         send, keep = refs[:2]
         refs = refs[2:]
+    elif back == "pieces":
+        pieces, refs = refs[:n], refs[n:]
     rows, scaled = refs
     gate, up, down = weights
     width, part = rows.shape[1], own.shape[1] // 2
@@ -184,6 +191,13 @@
         for i in range(0, width, 2 * TILE):
             here = slice(i, i + 2 * TILE)
             total = nt_dot(gate_back, gate[here, :]) + nt_dot(up_back, up[here, :])
+            if back == "pieces":
+                for k, piece in enumerate(pieces):
+                    piece[0:MAIN, here] = total[MAIN * k : MAIN * (k + 1)].astype(HALF)
+                    pair = total[tail + 8 * (k // 2) : tail + 8 * (k // 2) + 8]
+                    pair = pair if k % 2 == 0 else pltpu.roll(pair, REST, 0)
+                    piece[MAIN : MAIN + 8, here] = pair.astype(HALF)
+                continue
             keep[0:mid, here] = total[0:mid].astype(HALF)
             send[0:mid, here] = total[mid : 2 * mid].astype(HALF)
             keep[mid : mid + reach, here] = total[tail : tail + reach].astype(HALF)
@@ -191,20 +205,23 @@
 
 
 def forward(blocks, gate, up, down, place, part, back, cost=COST):
-    n, (width, hidden) = len(blocks), gate.shape
+    given, (width, hidden) = len(blocks), gate.shape
+    n = sum(1 if len(block.shape) == 2 else 2 for block in blocks)
     count = padded_rows(n)
     in_vmem = pl.BlockSpec(memory_space=pltpu.VMEM)
     out_shape = [
         shape((count, 3 * hidden + 2 * part)),
         shape((count, 2 * part)),
     ]
-    if back:
+    if back == "pieces":
+        out_shape += [shape((MAIN + 8, width))] * n
+    elif back:
         half = n // 2
         out_shape += [shape((MAIN * half + 8 * (-(-half // 2)), width))] * 2
     matmuls = 5 if back else 3
     return pl.pallas_call(
-        functools.partial(forward_kernel, n, back),
-        in_specs=[pl.BlockSpec(memory_space=pltpu.SMEM)] + [in_vmem] * (n + 3),
+        functools.partial(forward_kernel, given, back),
+        in_specs=[pl.BlockSpec(memory_space=pltpu.SMEM)] + [in_vmem] * (given + 3),
         out_specs=[in_vmem] * len(out_shape),
         out_shape=out_shape,
         scratch_shapes=[
@@ -312,9 +329,34 @@
     return pl.pallas_call(
         functools.partial(merge_kernel, n),
         out_shape=[shape((MAIN + 8, keep.shape[1]))] * n,
-        compiler_params=params(32),
+        compiler_params=params(LIMIT),
         name="merge",
     )(keep, came)
+
+
+def pair_kernel(a, b, out):
+    out[0] = a[...]
+    out[1] = b[...]
+
+
+def pair(a, b):
+    return pl.pallas_call(
+        pair_kernel,
+        out_shape=shape((2,) + a.shape),
+        compiler_params=params(LIMIT),
+        cost_estimate=pl.CostEstimate(flops=10**6, bytes_accessed=0, transcendentals=0),
+        name="pair",
+    )(a, b)
+
+
+def add_kernel(a, b, out):
+    out[...] = (a[...].astype(FULL) + b[...].astype(FULL)).astype(HALF)
+
+
+def add(a, b):
+    return pl.pallas_call(
+        add_kernel, out_shape=shape(a.shape), compiler_params=params(LIMIT), name="add"
+    )(a, b)
 
 
 def after(value, *others):
@@ -355,35 +397,42 @@
     xy0 = over_y(after(x0, z1))
     x3 = over_x(z3)
     x2 = over_x(after(z2, x1))
-    xy1 = over_y(after(x1, z2))
+    xy1 = over_y(x1)
     y2 = over_y(after(z2, x1))
     xy2 = over_y(x2)
+    y3 = over_z(after(y0, z2), -1)
 
     run = functools.partial(
         forward, gate=gate_weight, up=up_weight, down=down_weight, place=place, part=part
     )
-    act0, own0, send0, keep0 = run([after(b0, xy0, z2), z1, x0, x1], back=True)
+    act0, own0, send0, keep0 = run(
+        [after(z1, xy0, z2, y1), z3, x1, x3], back="halves", cost=COSTS[0]
+    )
     came0 = over_x(send0)
-    y3 = over_z(after(y0, z2), -1)
     xy3 = over_z(after(xy0, send0), -1)
-    act1, own1, send1, keep1 = run([after(z3, send0, y1, y3), x3], back=True)
-    came1 = over_x(send1)
-    other0 = over_core(after(act0, send1))
-    p0, p1 = merge(2, keep0, came0)
-    r1 = over_z(p1, -1)
-    act2, own2, send2, keep2 = run([after(z2, send1, xy1, y2, xy3, p1), x2], back=True)
-    (p3,) = merge(1, keep1, after(came1, send2))
-    came2, r3 = over_x(send2), over_z(p3, 1)
-    other1 = over_core(after(act1, send2))
-    y0 = after(y0, send2, r1, p3, xy2, other0)
-    act3, own3 = run([y0, xy0, y1, xy1, y3, xy3, y2, xy2], back=False)
-    (p2,) = merge(1, keep2, after(came2, act3, r3, other1))
+    act1, own1, keep2, near, send2, aside = run(
+        [after(z2, send0, xy1, y3), b0, x2, x0], back="pieces", cost=COSTS[1]
+    )
+    came2 = over_x(send2)
+    other0 = over_core(act0)
+    p1, p3 = merge(2, keep0, after(came0, send2))
+    r1, r3 = over_z(p1, -1), over_z(p3, 1)
+    other1 = over_core(act1)
+    y0 = after(y0, p1, other0, y2, xy3)
+    act2, own2 = run([y0, xy0, y1, xy1], back=False, cost=COSTS[2])
+    other2 = over_core(act2)
+    y2 = after(y2, act2)
+    act3, own3 = run([y2, xy2, y3, xy3], back=False, cost=COSTS[3])
+    other3 = over_core(act3)
+    p2 = add(keep2, after(came2, act3, r1, r3))
     r2 = over_z(p2, 2)
-    other2, other3 = over_core(act2), over_core(act3)
+    beside = over_x(after(aside, act3))
     hidden = gate_weight.shape[1]
-    early = grads([act0, act1, act2], [own0, own1, own2], [other0, other1, other2], hidden, cost=4 * COST)
-    gate_grad, up_grad, down_grad = grads([act3], [own3], [other3], hidden, early, cost=10**6)
-    token_grad = unpack(after(ids, gate_grad), [p0, r1, r2, r3])
+    early = grads([act0, act1], [own0, own1], [other0, other1], hidden, cost=COSTS[4])
+    gate_grad, up_grad, down_grad = grads(
+        [act2, act3], [own2, own3], [other2, other3], hidden, early, cost=COSTS[5]
+    )
+    token_grad = unpack(after(ids, gate_grad), [near, beside, r1, r2, r3])
     return token_grad, gate_grad, up_grad, down_grad
 
 

time: 107 us -> 103 us (0.963)
  Pallas kernels: 46.2 us -> 40.4 us
  starting transfers between devices: 27.1 us -> 32.5 us
  local copies, waits for them, and re-layouts: 6.21 us -> 1.04 us
  waiting for transfers between devices: 26 us -> 28.2 us
    ppermute x8, starting transfers between devices: 10.3 us -> 17.9 us  [over_z(): lax.ppermute(v, 'expert', [(i, (i + 2 * by) % n_expert) for i in range(n_...]
    pallas_call x4 -> x5, Pallas kernels: 31.6 us -> 25.4 us  [the longest x4 25.3 us: forward(): pl.pallas_call(functools.partial(forward_kernel, given, back), in_specs=[...]
    unnamed x28 -> x14, local copies, waits for them, and re-layouts: 6.21 us -> 1.04 us
    ppermute x6, waiting for transfers between devices: 0.02 us -> 1.98 us  [over_y(): return lax.ppermute(v, 'dp', y_pairs)]
    ppermute x6, starting transfers between devices: 7.66 us -> 6.15 us  [over_y(): return lax.ppermute(v, 'dp', y_pairs)]
    ppermute x7, waiting for transfers between devices: 2.75 us -> 3.91 us  [over_x(): return lax.ppermute(v, 'expert', x_pairs)]
  transfers between devices with their start and end apart: 25 -> 25, of which waited for: 6 -> 8; matrix products, arithmetic and copies ran while one was open for 0% -> 0% of each run, Pallas kernels for 39% -> 35%
where the time goes in v7:
time: 103 us
  Pallas kernels  40.4 us (39%)
  starting transfers between devices  32.5 us (32%)
  waiting for transfers between devices  28.2 us (27%)
  local copies, waits for them, and re-layouts  1.04 us (1%)
    pallas_call x4, Pallas kernels, forward(): pl.pallas_call(functools.partial(forward_kernel, given, back), in_specs=[...  25.3 us
    ppermute x8, waiting for transfers between devices, over_z(): lax.ppermute(v, 'expert', [(i, (i + 2 * by) % n_expert) for i in range(n_...  22.3 us
    ppermute x8, starting transfers between devices, over_z(): lax.ppermute(v, 'expert', [(i, (i + 2 * by) % n_expert) for i in range(n_...  17.9 us
    pallas_call x2, Pallas kernels, grads(): pl.pallas_call(functools.partial(grads_kernel, n, len(early)), in_specs=[...  9.32 us
    ppermute x7, starting transfers between devices, over_x(): return lax.ppermute(v, 'expert', x_pairs)  7.75 us
    ppermute x6, starting transfers between devices, over_y(): return lax.ppermute(v, 'dp', y_pairs)  6.15 us
    ppermute x7, waiting for transfers between devices, over_x(): return lax.ppermute(v, 'expert', x_pairs)  3.91 us
    pallas_call x1, Pallas kernels, pack(): pl.pallas_call(pack_kernel, in_specs=[pl.BlockSpec(memory_space=pltpu.HBM...  2.77 us
  transfers between devices with their start and end apart: 25, of which 8 were waited for; matrix products, arithmetic and copies ran while one was open for 0% of the time, Pallas kernels for 35%

profile of v7, /device:TPU:0, one launch (start us, length us, event | category | flops | bytes accessed | tf_op | source)
XLA Modules:
  0.0 103.1 jit_solution(11329830283240865580)
XLA Ops:
  0.6 0.0 slice-start
  0.6 2.8 %pack.1.block.refs_1_ = bf16[72,3072]{1,0:T(8,128)(2,1)} custom-call(s32[2,128]{1,0:T(2,128)} %bitcast.6, f32[2,128]{1,0:T(2,128)} %bitcast.8, bf16[128,3072]{1,0:T(8,128)(2,1)} %tokens_in.1, bf16[128,3072]{1,0:T(8,128)(2,1)} %cotangent_in.1), custom_call_target="tpu_custom_call" | custom-call | tf_op jit(solution)/shard_map/pack/pallas_call | solution.py:83
  3.4 3.0 %collective-permute-start.2 = (bf16[72,3072]{1,0:T(8,128)(2,1)}, bf16[72,3072]{1,0:T(8,128)(2,1)S(1)}, u32[]{:S(2)}, u32[]{:S(2)}) collective-permute-start(bf16[72,3072]{1,0:T(8,128)(2,1)} %pack.1.block.refs_1_), channel_id=1, source_target_pairs={{0,1},{1,0},{2,3},{3,2},{4,5},{5,4},{6,7},{7,6},{8,9},{9,8},{10,11... | collective-permute-start | bytes 1327112 | tf_op jit(solution)/shard_map/ppermute | solution.py:379
  6.4 1.6 %collective-permute-start.1 = (bf16[72,3072]{1,0:T(8,128)(2,1)}, bf16[72,3072]{1,0:T(8,128)(2,1)S(1)}, u32[]{:S(2)}, u32[]{:S(2)}) collective-permute-start(bf16[72,3072]{1,0:T(8,128)(2,1)} %pack.1.block.refs_1_), channel_id=1, source_target_pairs={{0,2},{1,3},{2,4},{3,5},{4,6},{5,7},{6,0},{7,1},{8,10},{9,11},{10,... | collective-permute-start | bytes 1327112 | tf_op jit(solution)/shard_map/ppermute | solution.py:382
  8.0 1.5 %collective-permute-start = (bf16[72,3072]{1,0:T(8,128)(2,1)}, bf16[72,3072]{1,0:T(8,128)(2,1)S(1)}, u32[]{:S(2)}, u32[]{:S(2)}) collective-permute-start(bf16[72,3072]{1,0:T(8,128)(2,1)} %pack.1.block.refs_1_), channel_id=1, source_target_pairs={{0,16},{8,24},{16,0},{24,8},{1,17},{9,25},{17,1},{25,9},{2,18},{10... | collective-permute-start | bytes 1327112 | tf_op jit(solution)/shard_map/ppermute | solution.py:376
  9.5 0.1 pad_add_fusion.place
  9.6 1.0 copy-done.2
  10.6 1.1 %settle.1.place = s32[2]{0:T(128)S(1)} custom-call(s32[2]{0:T(128)S(1)} %pad_add_fusion.place, bf16[72,3072]{1,0:T(8,128)(2,1)S(1)} %copy-done.2), custom_call_target="tpu_custom_call" | custom-call | flops 20000000000 | tf_op jit(solution)/shard_map/settle/pallas_call | solution.py:302
  11.8 0.0 copy-start.3
  11.8 2.3 %collective-permute-start.6 = (bf16[72,3072]{1,0:T(8,128)(2,1)S(1)}, bf16[72,3072]{1,0:T(8,128)(2,1)S(1)}, u32[]{:S(2)}, u32[]{:S(2)}) collective-permute-start(bf16[72,3072]{1,0:T(8,128)(2,1)S(1)} %copy-done.2), channel_id=1, source_target_pairs={{0,6},{1,7},{2,0},{3,1},{4,2},{5,3},{6,4},{7,5},{8,14},{9,15},{10,... | collective-permute-start | bytes 1327112 | tf_op jit(solution)/shard_map/ppermute | solution.py:382
  14.1 2.7 %collective-permute-done.2.refs_3_ = bf16[72,3072]{1,0:T(8,128)(2,1)S(1)} collective-permute-done((bf16[72,3072]{1,0:T(8,128)(2,1)}, bf16[72,3072]{1,0:T(8,128)(2,1)S(1)}, u32[]{:S(2)}, u32[]{:S(2)}) %collective-permute-start.2) | collective-permute-done | bytes 442400 | tf_op jit(solution)/shard_map/ppermute | solution.py:379
  16.8 4.8 %collective-permute-done.1.refs_0_ = bf16[72,3072]{1,0:T(8,128)(2,1)S(1)} collective-permute-done((bf16[72,3072]{1,0:T(8,128)(2,1)}, bf16[72,3072]{1,0:T(8,128)(2,1)S(1)}, u32[]{:S(2)}, u32[]{:S(2)}) %collective-permute-start.1) | collective-permute-done | bytes 442400 | tf_op jit(solution)/shard_map/ppermute | solution.py:382
  21.6 0.0 collective-permute-done.refs_0_
  21.6 0.3 collective-permute-start.7
  21.9 1.7 %collective-permute-start.3 = (bf16[72,3072]{1,0:T(8,128)(2,1)S(1)}, bf16[72,3072]{1,0:T(8,128)(2,1)S(1)}, u32[]{:S(2)}, u32[]{:S(2)}) collective-permute-start(bf16[72,3072]{1,0:T(8,128)(2,1)S(1)} %collective-permute-done.2.refs_3_), channel_id=1, source_target_pairs={{0,16},{8,24},{16,0},{24,8},{1,17},{9,25},{17,1},{25,9},{2,18},{10... | collective-permute-start | bytes 1327112 | tf_op jit(solution)/shard_map/ppermute | solution.py:376
  23.6 0.3 collective-permute-start.5
  23.9 7.0 %collective-permute-done.6.refs_1_ = bf16[72,3072]{1,0:T(8,128)(2,1)S(1)} collective-permute-done((bf16[72,3072]{1,0:T(8,128)(2,1)S(1)}, bf16[72,3072]{1,0:T(8,128)(2,1)S(1)}, u32[]{:S(2)}, u32[]{:S(2)}) %collective-permute-start.6) | collective-permute-done | bytes 442400 | tf_op jit(solution)/shard_map/ppermute | solution.py:382
  31.0 0.3 collective-permute-start.8
  31.3 7.9 %collective-permute-done.4.refs_0_ = bf16[72,3072]{1,0:T(8,128)(2,1)S(1)} collective-permute-done((bf16[72,3072]{1,0:T(8,128)(2,1)S(1)}, bf16[72,3072]{1,0:T(8,128)(2,1)S(1)}, u32[]{:S(2)}, u32[]{:S(2)}) %collective-permute-start.4) | collective-permute-done | bytes 442400 | tf_op jit(solution)/shard_map/ppermute | solution.py:382
  39.2 1.9 %collective-permute-done.5.refs_2_ = bf16[72,3072]{1,0:T(8,128)(2,1)S(1)} collective-permute-done((bf16[72,3072]{1,0:T(8,128)(2,1)S(1)}, bf16[72,3072]{1,0:T(8,128)(2,1)S(1)}, u32[]{:S(2)}, u32[]{:S(2)}) %collective-permute-start.5) | collective-permute-done | bytes 442400 | tf_op jit(solution)/shard_map/ppermute | solution.py:376
  41.0 7.0 %collective-permute-start.11 = (bf16[72,3072]{1,0:T(8,128)(2,1)S(1)}, bf16[72,3072]{1,0:T(8,128)(2,1)S(1)}, u32[]{:S(2)}, u32[]{:S(2)}) collective-permute-start(bf16[72,3072]{1,0:T(8,128)(2,1)S(1)} %collective-permute-done.refs_0_), channel_id=1, source_target_pairs={{0,6},{1,7},{2,0},{3,1},{4,2},{5,3},{6,4},{7,5},{8,14},{9,15},{10,... | collective-permute-start | bytes 1327112 | tf_op jit(solution)/shard_map/ppermute | solution.py:382
  48.0 0.8 collective-permute-start.12
  48.8 1.5 %collective-permute-start.10 = (bf16[72,3072]{1,0:T(8,128)(2,1)S(1)}, bf16[72,3072]{1,0:T(8,128)(2,1)S(1)}, u32[]{:S(2)}, u32[]{:S(2)}) collective-permute-start(bf16[72,3072]{1,0:T(8,128)(2,1)S(1)} %collective-permute-done.7.refs_2_), channel_id=1, source_target_pairs={{0,16},{8,24},{16,0},{24,8},{1,17},{9,25},{17,1},{25,9},{2,18},{10... | collective-permute-start | bytes 1327112 | tf_op jit(solution)/shard_map/ppermute | solution.py:376
  50.4 8.0 %forward_back.2 = (bf16[144,4608]{1,0:T(8,128)(2,1)S(1)}, bf16[144,1536]{1,0:T(8,128)(2,1)S(1)}, bf16[72,3072]{1,0:T(8,128)(2,1)S(1)}, bf16[72,3072]{1,0:T(8,128)(2,1)S(1)}) custom-call(s32[2]{0:T(128)S(1)} %settle.1.place, bf16[72,3072]{1,0:T(8,128)(2,1)S(1)} %collective-permute-done.1.refs_0_, bf16[72,3072]{1,0:T(8,128)(2,1)S(1)} %collective-permute-done.6.refs_1_, ...), custom_call_target="tpu_custom_call" | custom-call | flops 10000000000 | tf_op jit(solution)/shard_map/forward_back/pallas_call | solution.py:222
  58.3 0.1 collective-permute-start.13
  58.4 0.6 collective-permute-start.14
  59.0 1.2 %collective-permute-start.9 = (bf16[72,3072]{1,0:T(8,128)(2,1)S(1)}, bf16[72,3072]{1,0:T(8,128)(2,1)S(1)}, u32[]{:S(2)}, u32[]{:S(2)}) collective-permute-start(bf16[72,3072]{1,0:T(8,128)(2,1)S(1)} %get-tuple-element.45), channel_id=1, source_target_pairs={{0,1},{1,0},{2,3},{3,2},{4,5},{5,4},{6,7},{7,6},{8,9},{9,8},{10,11... | collective-permute-start | bytes 1327112 | tf_op jit(solution)/shard_map/ppermute | solution.py:379
  60.2 1.3 %collective-permute-start.15 = (bf16[72,3072]{1,0:T(8,128)(2,1)S(1)}, bf16[72,3072]{1,0:T(8,128)(2,1)S(1)}, u32[]{:S(2)}, u32[]{:S(2)}) collective-permute-start(bf16[72,3072]{1,0:T(8,128)(2,1)S(1)} %collective-permute-done.3.refs_1_), channel_id=1, source_target_pairs={{0,6},{1,7},{2,0},{3,1},{4,2},{5,3},{6,4},{7,5},{8,14},{9,15},{10,... | collective-permute-start | bytes 1327112 | tf_op jit(solution)/shard_map/ppermute | solution.py:382
  61.5 0.5 collective-permute-start.16
  62.1 8.0 %forward_back.3 = (bf16[144,4608]{1,0:T(8,128)(2,1)S(1)}, bf16[144,1536]{1,0:T(8,128)(2,1)S(1)}, bf16[40,3072]{1,0:T(8,128)(2,1)S(1)}, bf16[40,3072]{1,0:T(8,128...) custom-call(s32[2]{0:T(128)S(1)} %settle.1.place, ...), custom_call_target="tpu_custom_call" | custom-call | flops 10000000000 | tf_op jit(solution)/shard_map/forward_back/pallas_call | solution.py:222
  70.0 1.2 %collective-permute-done.9.came = bf16[72,3072]{1,0:T(8,128)(2,1)S(1)} collective-permute-done((bf16[72,3072]{1,0:T(8,128)(2,1)S(1)}, bf16[72,3072]{1,0:T(8,128)(2,1)S(1)}, u32[]{:S(2)}, u32[]{:S(2)}) %collective-permute-start.9) | collective-permute-done | bytes 442400 | tf_op jit(solution)/shard_map/ppermute | solution.py:379
  71.2 0.1 merge.1
  71.3 0.1 collective-permute-done.14.refs_0_
  71.4 1.2 %collective-permute-start.22 = (bf16[40,3072]{1,0:T(8,128)(2,1)S(1)}, bf16[40,3072]{1,0:T(8,128)(2,1)S(1)}, u32[]{:S(2)}, u32[]{:S(2)}) collective-permute-start(bf16[40,3072]{1,0:T(8,128)(2,1)S(1)} %get-tuple-element.49), channel_id=1, source_target_pairs={{0,1},{1,0},{2,3},{3,2},{4,5},{5,4},{6,7},{7,6},{8,9},{9,8},{10,11... | collective-permute-start | bytes 737288 | tf_op jit(solution)/shard_map/ppermute | solution.py:379
  72.6 0.2 collective-permute-start.23
  72.8 3.6 %collective-permute-start.21 = (bf16[40,3072]{1,0:T(8,128)(2,1)S(1)}, bf16[40,3072]{1,0:T(8,128)(2,1)S(1)}, u32[]{:S(2)}, u32[]{:S(2)}) collective-permute-start(bf16[40,3072]{1,0:T(8,128)(2,1)S(1)} %get-tuple-element.51), channel_id=1, source_target_pairs={{0,6},{1,7},{2,0},{3,1},{4,2},{5,3},{6,4},{7,5},{8,14},{9,15},{10,... | collective-permute-start | bytes 737288 | tf_op jit(solution)/shard_map/ppermute | solution.py:382
  76.5 4.7 %forward.2 = (bf16[144,4608]{1,0:T(8,128)(2,1)S(1)}, bf16[144,1536]{1,0:T(8,128)(2,1)S(1)}) custom-call(s32[2]{0:T(128)S(1)} %settle.1.place, bf16[72,3072]{1,0:T(8,128)(2,1)S(1)} %collective-permute-done.refs_0_, bf16[72,3072]{1,0:T(8,128)(2,1)S(1)} %collective-permute-done.3.refs_1_, bf16[72,3072]{1,0:T(8,128)(2,1)S(1)} %collective-permute-done.5.refs_2_, ...), custom_call_target="tpu_custom_call" | custom-call | flops 1000000 | tf_op jit(solution)/shard_map/forward/pallas_call | solution.py:222
  81.2 0.1 collective-permute-start.17
  81.2 4.7 %forward.3 = (bf16[144,4608]{1,0:T(8,128)(2,1)S(1)}, bf16[144,1536]{1,0:T(8,128)(2,1)S(1)}) custom-call(s32[2]{0:T(128)S(1)} %settle.1.place, bf16[72,3072]{1,0:T(8,128)(2,1)S(1)} %collective-permute-done.14.refs_0_, bf16[72,3072]{1,0:T(8,128)(2,1)S(1)} %collective-permute-done.16.refs_1_, bf16[72,3072]{1,0:T(8,128)(2,1)S(1)} %collective-permute-done.11.refs_2_, ...), custom_call_target="tpu_custom_call" | custom-call | flops 10000000000 | tf_op jit(solution)/shard_map/forward/pallas_call | solution.py:222
  86.0 0.6 collective-permute-start.18
  86.5 0.9 collective-permute-start.20
  87.4 0.1 add.12
  87.5 1.9 %collective-permute-start.24 = (bf16[40,3072]{1,0:T(8,128)(2,1)S(1)}, bf16[40,3072]{1,0:T(8,128)(2,1)S(1)}, u32[]{:S(2)}, u32[]{:S(2)}) collective-permute-start(bf16[40,3072]{1,0:T(8,128)(2,1)S(1)} %add.12), channel_id=1, source_target_pairs={{0,4},{1,5},{2,6},{3,7},{4,0},{5,1},{6,2},{7,3},{8,12},{9,13},{10,... | collective-permute-start | bytes 737288 | tf_op jit(solution)/shard_map/ppermute | solution.py:382
  89.3 3.9 %grads.2 = (bf16[768,1024]{1,0:T(8,128)(2,1)S(1)}, bf16[768,1024]{1,0:T(8,128)(2,1)S(1)}, bf16[1024,768]{1,0:T(8,128)(2,1)S(1)}) custom-call(bf16[144,4608]{1,0:T(8,128)(2,1)S(1)} %get-tuple-element.52.refs_0_, bf16[144,4608]{1,0:T(8,128)(2,1)S(1)} %get-tuple-element.60.refs_1_, bf16[144,1536]{1,0:T(8,128)(2,1)S(1)} %get-tuple-element.61.refs_2_, ...), custom_call_target="tpu_custom_call" | custom-call | flops 40000000000 | tf_op jit(solution)/shard_map/grads/pallas_call | solution.py:280
  93.2 0.0 copy-start.4
  93.2 5.5 %grads.3 = (bf16[768,1024]{1,0:T(8,128)(2,1)}, bf16[768,1024]{1,0:T(8,128)(2,1)}, bf16[1024,768]{1,0:T(8,128)(2,1)}) custom-call(bf16[144,4608]{1,0:T(8,128)(2,1)S(1)} %get-tuple-element.55.refs_0_, bf16[144,4608]{1,0:T(8,128)(2,1)S(1)} %get-tuple-element.57.refs_1_, bf16[144,1536]{1,0:T(8,128)(2,1)S(1)} %get-tuple-element.58.refs_2_, ...), custom_call_target="tpu_custom_call" | custom-call | flops 1000000 | tf_op jit(solution)/shard_map/grads/pallas_call | solution.py:280
  98.7 2.6 %collective-permute-done.24.refs_3_ = bf16[40,3072]{1,0:T(8,128)(2,1)S(1)} collective-permute-done((bf16[40,3072]{1,0:T(8,128)(2,1)S(1)}, bf16[40,3072]{1,0:T(8,128)(2,1)S(1)}, u32[]{:S(2)}, u32[]{:S(2)}) %collective-permute-start.24) | collective-permute-done | bytes 245792 | tf_op jit(solution)/shard_map/ppermute | solution.py:382
  101.3 1.7 %unpack.1 = bf16[128,3072]{1,0:T(8,128)(2,1)} custom-call(s32[2,128]{1,0:T(2,128)S(1)} %bitcast.7, bf16[40,3072]{1,0:T(8,128)(2,1)S(1)} %get-tuple-element.68.refs_0_, bf16[40,3072]{1,0:T(8,128)(2,1)S(1)} %collective-permute-done.20.refs_1_, bf16[40,3072]{1,0:T(8,128)(2,1)S(1)} %collective-permute-done.21.refs_2_, ...), custom_call_target="tpu_custom_call" | custom-call | tf_op jit(solution)/shard_map/unpack/pallas_call | solution.py:107
  (29 shorter events, 0.1 us)
Async XLA Ops:
  0.6 49.7 %slice-start = ((s8[6291456]{0:T(1024)(128)(4,1)}), s8[2097152]{0:T(1024)(128)(4,1)S(1)}, s32[]{:S(2)}) async-start(s8[6291456]{0:T(1024)(128)(4,1)} %bitcast.4), calls=%async_computation | async-start | bytes 4194304
  3.4 13.4 %collective-permute-start.2 = (bf16[72,3072]{1,0:T(8,128)(2,1)}, bf16[72,3072]{1,0:T(8,128)(2,1)S(1)}, u32[]{:S(2)}, u32[]{:S(2)}) collective-permute-start(bf16[72,3072]{1,0:T(8,128)(2,1)} %pack.1.block.refs_1_), channel_id=1, source_target_pairs={{0,1},{1,0},{2,3},{3,2},{4,5},{5,4},{6,7},{7,6},{8,9},{9,8},{10,11... | collective-permute-start | bytes 1327112 | tf_op jit(solution)/shard_map/ppermute | solution.py:379
  6.4 15.1 %collective-permute-start.1 = (bf16[72,3072]{1,0:T(8,128)(2,1)}, bf16[72,3072]{1,0:T(8,128)(2,1)S(1)}, u32[]{:S(2)}, u32[]{:S(2)}) collective-permute-start(bf16[72,3072]{1,0:T(8,128)(2,1)} %pack.1.block.refs_1_), channel_id=1, source_target_pairs={{0,2},{1,3},{2,4},{3,5},{4,6},{5,7},{6,0},{7,1},{8,10},{9,11},{10,... | collective-permute-start | bytes 1327112 | tf_op jit(solution)/shard_map/ppermute | solution.py:382
  8.0 13.6 %collective-permute-start = (bf16[72,3072]{1,0:T(8,128)(2,1)}, bf16[72,3072]{1,0:T(8,128)(2,1)S(1)}, u32[]{:S(2)}, u32[]{:S(2)}) collective-permute-start(bf16[72,3072]{1,0:T(8,128)(2,1)} %pack.1.block.refs_1_), channel_id=1, source_target_pairs={{0,16},{8,24},{16,0},{24,8},{1,17},{9,25},{17,1},{25,9},{2,18},{10... | collective-permute-start | bytes 1327112 | tf_op jit(solution)/shard_map/ppermute | solution.py:376
  9.6 1.0 copy-start.2
  10.6 39.7 %slice-start.1 = ((s8[6291456]{0:T(1024)(128)(4,1)}), s8[4194304]{0:T(1024)(128)(4,1)S(1)}, s32[]{:S(2)}) async-start(s8[6291456]{0:T(1024)(128)(4,1)} %bitcast.4), calls=%async_computation.1 | async-start | bytes 8388608
  10.6 39.7 %copy-start = (bf16[3072,1024]{1,0:T(8,128)(2,1)S(1)}, bf16[3072,1024]{1,0:T(8,128)(2,1)}, u32[]{:S(2)}) copy-start(bf16[3072,1024]{1,0:T(8,128)(2,1)} %refs_5_.7) | copy-start | bytes 18874372
  10.6 39.7 %copy-start.1 = (bf16[1024,3072]{1,0:T(8,128)(2,1)S(1)}, bf16[1024,3072]{1,0:T(8,128)(2,1)}, u32[]{:S(2)}) copy-start(bf16[1024,3072]{1,0:T(8,128)(2,1)} %refs_6_.7) | copy-start | bytes 18874372
  11.8 50.3 %copy-start.3 = (bf16[72,3072]{1,0:T(8,128)(2,1)S(1)}, bf16[72,3072]{1,0:T(8,128)(2,1)}, u32[]{:S(2)}) copy-start(bf16[72,3072]{1,0:T(8,128)(2,1)} %pack.1.block.refs_1_) | copy-start | bytes 1327108
  11.8 19.2 %collective-permute-start.6 = (bf16[72,3072]{1,0:T(8,128)(2,1)S(1)}, bf16[72,3072]{1,0:T(8,128)(2,1)S(1)}, u32[]{:S(2)}, u32[]{:S(2)}) collective-permute-start(bf16[72,3072]{1,0:T(8,128)(2,1)S(1)} %copy-done.2), channel_id=1, source_target_pairs={{0,6},{1,7},{2,0},{3,1},{4,2},{5,3},{6,4},{7,5},{8,14},{9,15},{10,... | collective-permute-start | bytes 1327112 | tf_op jit(solution)/shard_map/ppermute | solution.py:382
  21.6 9.7 %collective-permute-start.7 = (bf16[72,3072]{1,0:T(8,128)(2,1)S(1)}, bf16[72,3072]{1,0:T(8,128)(2,1)S(1)}, u32[]{:S(2)}, u32[]{:S(2)}) collective-permute-start(bf16[72,3072]{1,0:T(8,128)(2,1)S(1)} %collective-permute-done.1.refs_0_), channel_id=1, source_target_pairs={{0,1},{1,0},{2,3},{3,2},{4,5},{5,4},{6,7},{7,6},{8,9},{9,8},{10,11... | collective-permute-start | bytes 1327112 | tf_op jit(solution)/shard_map/ppermute | solution.py:379
  21.9 17.3 %collective-permute-start.4 = (bf16[72,3072]{1,0:T(8,128)(2,1)S(1)}, bf16[72,3072]{1,0:T(8,128)(2,1)S(1)}, u32[]{:S(2)}, u32[]{:S(2)}) collective-permute-start(bf16[72,3072]{1,0:T(8,128)(2,1)S(1)} %collective-permute-done.1.refs_0_), channel_id=1, source_target_pairs={{0,2},{1,3},{2,4},{3,5},{4,6},{5,7},{6,0},{7,1},{8,10},{9,11},{10,... | collective-permute-start | bytes 1327112 | tf_op jit(solution)/shard_map/ppermute | solution.py:382
  21.9 17.3 %collective-permute-start.3 = (bf16[72,3072]{1,0:T(8,128)(2,1)S(1)}, bf16[72,3072]{1,0:T(8,128)(2,1)S(1)}, u32[]{:S(2)}, u32[]{:S(2)}) collective-permute-start(bf16[72,3072]{1,0:T(8,128)(2,1)S(1)} %collective-permute-done.2.refs_3_), channel_id=1, source_target_pairs={{0,16},{8,24},{16,0},{24,8},{1,17},{9,25},{17,1},{25,9},{2,18},{10... | collective-permute-start | bytes 1327112 | tf_op jit(solution)/shard_map/ppermute | solution.py:376
  23.6 17.4 %collective-permute-start.5 = (bf16[72,3072]{1,0:T(8,128)(2,1)S(1)}, bf16[72,3072]{1,0:T(8,128)(2,1)S(1)}, u32[]{:S(2)}, u32[]{:S(2)}) collective-permute-start(bf16[72,3072]{1,0:T(8,128)(2,1)S(1)} %collective-permute-done.1.refs_0_), channel_id=1, source_target_pairs={{0,16},{8,24},{16,0},{24,8},{1,17},{9,25},{17,1},{25,9},{2,18},{10... | collective-permute-start | bytes 1327112 | tf_op jit(solution)/shard_map/ppermute | solution.py:376
  31.0 19.4 %collective-permute-start.8 = (bf16[72,3072]{1,0:T(8,128)(2,1)S(1)}, bf16[72,3072]{1,0:T(8,128)(2,1)S(1)}, u32[]{:S(2)}, u32[]{:S(2)}) collective-permute-start(bf16[72,3072]{1,0:T(8,128)(2,1)S(1)} %collective-permute-done.6.refs_1_), channel_id=1, source_target_pairs={{0,1},{1,0},{2,3},{3,2},{4,5},{5,4},{6,7},{7,6},{8,9},{9,8},{10,11... | collective-permute-start | bytes 1327112 | tf_op jit(solution)/shard_map/ppermute | solution.py:379
  41.0 19.2 %collective-permute-start.11 = (bf16[72,3072]{1,0:T(8,128)(2,1)S(1)}, bf16[72,3072]{1,0:T(8,128)(2,1)S(1)}, u32[]{:S(2)}, u32[]{:S(2)}) collective-permute-start(bf16[72,3072]{1,0:T(8,128)(2,1)S(1)} %collective-permute-done.refs_0_), channel_id=1, source_target_pairs={{0,6},{1,7},{2,0},{3,1},{4,2},{5,3},{6,4},{7,5},{8,14},{9,15},{10,... | collective-permute-start | bytes 1327112 | tf_op jit(solution)/shard_map/ppermute | solution.py:382
  48.0 13.5 %collective-permute-start.12 = (bf16[72,3072]{1,0:T(8,128)(2,1)S(1)}, bf16[72,3072]{1,0:T(8,128)(2,1)S(1)}, u32[]{:S(2)}, u32[]{:S(2)}) collective-permute-start(bf16[72,3072]{1,0:T(8,128)(2,1)S(1)} %collective-permute-done.4.refs_0_), channel_id=1, source_target_pairs={{0,1},{1,0},{2,3},{3,2},{4,5},{5,4},{6,7},{7,6},{8,9},{9,8},{10,11... | collective-permute-start | bytes 1327112 | tf_op jit(solution)/shard_map/ppermute | solution.py:379
  48.8 10.2 %collective-permute-start.10 = (bf16[72,3072]{1,0:T(8,128)(2,1)S(1)}, bf16[72,3072]{1,0:T(8,128)(2,1)S(1)}, u32[]{:S(2)}, u32[]{:S(2)}) collective-permute-start(bf16[72,3072]{1,0:T(8,128)(2,1)S(1)} %collective-permute-done.7.refs_2_), channel_id=1, source_target_pairs={{0,16},{8,24},{16,0},{24,8},{1,17},{9,25},{17,1},{25,9},{2,18},{10... | collective-permute-start | bytes 1327112 | tf_op jit(solution)/shard_map/ppermute | solution.py:376
  58.3 14.5 %collective-permute-start.13 = (bf16[144,4608]{1,0:T(8,128)(2,1)S(1)}, bf16[144,4608]{1,0:T(8,128)(2,1)S(1)}, u32[]{:S(2)}, u32[]{:S(2)}) collective-permute-start(bf16[144,4608]{1,0:T(8,128)(2,1)S(1)} %get-tuple-element.52.refs_0_), channel_id=1, source_target_pairs={{0,8},{8,0},{16,24},{24,16},{1,9},{9,1},{17,25},{25,17},{2,10},{10... | collective-permute-start | bytes 3981320 | tf_op jit(solution)/shard_map/ppermute | solution.py:373
  58.4 13.0 %collective-permute-start.14 = (bf16[72,3072]{1,0:T(8,128)(2,1)S(1)}, bf16[72,3072]{1,0:T(8,128)(2,1)S(1)}, u32[]{:S(2)}, u32[]{:S(2)}) collective-permute-start(bf16[72,3072]{1,0:T(8,128)(2,1)S(1)} %collective-permute-done.4.refs_0_), channel_id=1, source_target_pairs={{0,16},{8,24},{16,0},{24,8},{1,17},{9,25},{17,1},{25,9},{2,18},{10... | collective-permute-start | bytes 1327112 | tf_op jit(solution)/shard_map/ppermute | solution.py:376
  59.0 12.2 %collective-permute-start.9 = (bf16[72,3072]{1,0:T(8,128)(2,1)S(1)}, bf16[72,3072]{1,0:T(8,128)(2,1)S(1)}, u32[]{:S(2)}, u32[]{:S(2)}) collective-permute-start(bf16[72,3072]{1,0:T(8,128)(2,1)S(1)} %get-tuple-element.45), channel_id=1, source_target_pairs={{0,1},{1,0},{2,3},{3,2},{4,5},{5,4},{6,7},{7,6},{8,9},{9,8},{10,11... | collective-permute-start | bytes 1327112 | tf_op jit(solution)/shard_map/ppermute | solution.py:379
  60.2 12.4 %collective-permute-start.15 = (bf16[72,3072]{1,0:T(8,128)(2,1)S(1)}, bf16[72,3072]{1,0:T(8,128)(2,1)S(1)}, u32[]{:S(2)}, u32[]{:S(2)}) collective-permute-start(bf16[72,3072]{1,0:T(8,128)(2,1)S(1)} %collective-permute-done.3.refs_1_), channel_id=1, source_target_pairs={{0,6},{1,7},{2,0},{3,1},{4,2},{5,3},{6,4},{7,5},{8,14},{9,15},{10,... | collective-permute-start | bytes 1327112 | tf_op jit(solution)/shard_map/ppermute | solution.py:382
  61.5 19.6 %collective-permute-start.16 = (bf16[72,3072]{1,0:T(8,128)(2,1)S(1)}, bf16[72,3072]{1,0:T(8,128)(2,1)S(1)}, u32[]{:S(2)}, u32[]{:S(2)}) collective-permute-start(bf16[72,3072]{1,0:T(8,128)(2,1)S(1)} %collective-permute-done.12.refs_2_), channel_id=1, source_target_pairs={{0,16},{8,24},{16,0},{24,8},{1,17},{9,25},{17,1},{25,9},{2,18},{10... | collective-permute-start | bytes 1327112 | tf_op jit(solution)/shard_map/ppermute | solution.py:376
  71.2 18.1 %collective-permute-start.19 = (bf16[144,4608]{1,0:T(8,128)(2,1)S(1)}, bf16[144,4608]{1,0:T(8,128)(2,1)S(1)}, u32[]{:S(2)}, u32[]{:S(2)}) collective-permute-start(bf16[144,4608]{1,0:T(8,128)(2,1)S(1)} %get-tuple-element.60.refs_1_), channel_id=1, source_target_pairs={{0,8},{8,0},{16,24},{24,16},{1,9},{9,1},{17,25},{25,17},{2,10},{10... | collective-permute-start | bytes 3981320 | tf_op jit(solution)/shard_map/ppermute | solution.py:373
  71.4 15.1 %collective-permute-start.22 = (bf16[40,3072]{1,0:T(8,128)(2,1)S(1)}, bf16[40,3072]{1,0:T(8,128)(2,1)S(1)}, u32[]{:S(2)}, u32[]{:S(2)}) collective-permute-start(bf16[40,3072]{1,0:T(8,128)(2,1)S(1)} %get-tuple-element.49), channel_id=1, source_target_pairs={{0,1},{1,0},{2,3},{3,2},{4,5},{5,4},{6,7},{7,6},{8,9},{9,8},{10,11... | collective-permute-start | bytes 737288 | tf_op jit(solution)/shard_map/ppermute | solution.py:379
  72.6 13.3 %collective-permute-start.23 = (bf16[40,3072]{1,0:T(8,128)(2,1)S(1)}, bf16[40,3072]{1,0:T(8,128)(2,1)S(1)}, u32[]{:S(2)}, u32[]{:S(2)}) collective-permute-start(bf16[40,3072]{1,0:T(8,128)(2,1)S(1)} %get-tuple-element.72), channel_id=1, source_target_pairs={{0,2},{1,3},{2,4},{3,5},{4,6},{5,7},{6,0},{7,1},{8,10},{9,11},{10,... | collective-permute-start | bytes 737288 | tf_op jit(solution)/shard_map/ppermute | solution.py:382
  72.8 13.7 %collective-permute-start.21 = (bf16[40,3072]{1,0:T(8,128)(2,1)S(1)}, bf16[40,3072]{1,0:T(8,128)(2,1)S(1)}, u32[]{:S(2)}, u32[]{:S(2)}) collective-permute-start(bf16[40,3072]{1,0:T(8,128)(2,1)S(1)} %get-tuple-element.51), channel_id=1, source_target_pairs={{0,6},{1,7},{2,0},{3,1},{4,2},{5,3},{6,4},{7,5},{8,14},{9,15},{10,... | collective-permute-start | bytes 737288 | tf_op jit(solution)/shard_map/ppermute | solution.py:382
  81.2 12.0 %collective-permute-start.17 = (bf16[144,4608]{1,0:T(8,128)(2,1)S(1)}, bf16[144,4608]{1,0:T(8,128)(2,1)S(1)}, u32[]{:S(2)}, u32[]{:S(2)}) collective-permute-start(bf16[144,4608]{1,0:T(8,128)(2,1)S(1)} %get-tuple-element.55.refs_0_), channel_id=1, source_target_pairs={{0,8},{8,0},{16,24},{24,16},{1,9},{9,1},{17,25},{25,17},{2,10},{10... | collective-permute-start | bytes 3981320 | tf_op jit(solution)/shard_map/ppermute | solution.py:373
  86.0 7.2 %collective-permute-start.18 = (bf16[144,4608]{1,0:T(8,128)(2,1)S(1)}, bf16[144,4608]{1,0:T(8,128)(2,1)S(1)}, u32[]{:S(2)}, u32[]{:S(2)}) collective-permute-start(bf16[144,4608]{1,0:T(8,128)(2,1)S(1)} %get-tuple-element.57.refs_1_), channel_id=1, source_target_pairs={{0,8},{8,0},{16,24},{24,16},{1,9},{9,1},{17,25},{25,17},{2,10},{10... | collective-permute-start | bytes 3981320 | tf_op jit(solution)/shard_map/ppermute | solution.py:373
  86.5 12.2 %collective-permute-start.20 = (bf16[40,3072]{1,0:T(8,128)(2,1)S(1)}, bf16[40,3072]{1,0:T(8,128)(2,1)S(1)}, u32[]{:S(2)}, u32[]{:S(2)}) collective-permute-start(bf16[40,3072]{1,0:T(8,128)(2,1)S(1)} %get-tuple-element.70), channel_id=1, source_target_pairs={{0,1},{1,0},{2,3},{3,2},{4,5},{5,4},{6,7},{7,6},{8,9},{9,8},{10,11... | collective-permute-start | bytes 737288 | tf_op jit(solution)/shard_map/ppermute | solution.py:379
  87.5 13.8 %collective-permute-start.24 = (bf16[40,3072]{1,0:T(8,128)(2,1)S(1)}, bf16[40,3072]{1,0:T(8,128)(2,1)S(1)}, u32[]{:S(2)}, u32[]{:S(2)}) collective-permute-start(bf16[40,3072]{1,0:T(8,128)(2,1)S(1)} %add.12), channel_id=1, source_target_pairs={{0,4},{1,5},{2,6},{3,7},{4,0},{5,1},{6,2},{7,3},{8,12},{9,13},{10,... | collective-permute-start | bytes 737288 | tf_op jit(solution)/shard_map/ppermute | solution.py:382
  93.2 8.1 %copy-start.4 = (s32[128,2]{0,1:T(2,128)S(1)}, s32[128,2]{0,1:T(2,128)}, u32[]{:S(2)}) copy-start(s32[128,2]{0,1:T(2,128)} %param.9) | copy-start | bytes 3076

commit v8 on v7

--- a/solution.py
+++ b/solution.py
@@ -393,40 +393,40 @@
     z1, x0, y0 = over_z(b0, 1), over_x(b0), over_y(b0)
     z3 = over_z(after(b0, place), -1)
     z1 = after(z1, x0, y0, place)
-    z2, x1, y1 = over_z(z1, 1), over_x(z1), over_y(z1)
+    z2, x1 = over_z(z1, 1), over_x(z1)
     xy0 = over_y(after(x0, z1))
     x3 = over_x(z3)
     x2 = over_x(after(z2, x1))
-    xy1 = over_y(x1)
+    y3, xy3 = over_y(z3), over_y(x3)
     y2 = over_y(after(z2, x1))
     xy2 = over_y(x2)
-    y3 = over_z(after(y0, z2), -1)
+    y1 = over_z(after(y0, z2), 1)
 
     run = functools.partial(
         forward, gate=gate_weight, up=up_weight, down=down_weight, place=place, part=part
     )
     act0, own0, send0, keep0 = run(
-        [after(z1, xy0, z2, y1), z3, x1, x3], back="halves", cost=COSTS[0]
+        [after(z1, xy0, z2), z3, x1, x3], back="halves", cost=COSTS[0]
     )
     came0 = over_x(send0)
-    xy3 = over_z(after(xy0, send0), -1)
+    xy1 = over_z(after(xy0, send0), 1)
     act1, own1, keep2, near, send2, aside = run(
-        [after(z2, send0, xy1, y3), b0, x2, x0], back="pieces", cost=COSTS[1]
+        [after(z2, send0, y3, y1, y2), b0, x2, x0], back="pieces", cost=COSTS[1]
     )
     came2 = over_x(send2)
     other0 = over_core(act0)
     p1, p3 = merge(2, keep0, after(came0, send2))
     r1, r3 = over_z(p1, -1), over_z(p3, 1)
     other1 = over_core(act1)
-    y0 = after(y0, p1, other0, y2, xy3)
-    act2, own2 = run([y0, xy0, y1, xy1], back=False, cost=COSTS[2])
+    y0 = after(y0, p1, other0, y2, xy1)
+    act2, own2 = run([y0, xy0, y3, xy3], back=False, cost=COSTS[2])
     other2 = over_core(act2)
     y2 = after(y2, act2)
-    act3, own3 = run([y2, xy2, y3, xy3], back=False, cost=COSTS[3])
+    act3, own3 = run([y2, xy2, y1, xy1], back=False, cost=COSTS[3])
     other3 = over_core(act3)
     p2 = add(keep2, after(came2, act3, r1, r3))
     r2 = over_z(p2, 2)
-    beside = over_x(after(aside, act3))
+    beside = over_x(after(aside, p2))
     hidden = gate_weight.shape[1]
     early = grads([act0, act1], [own0, own1], [other0, other1], hidden, cost=COSTS[4])
     gate_grad, up_grad, down_grad = grads(

time: 103 us -> 102 us (level)
  starting transfers between devices: 32.5 us -> 27.4 us
  waiting for transfers between devices: 28.2 us -> 32.6 us
    ppermute x8, starting transfers between devices: 17.9 us -> 11.2 us  [over_z(): lax.ppermute(v, 'expert', [(i, (i + 2 * by) % n_expert) for i in range(n_...]
    ppermute x8, waiting for transfers between devices: 22.3 us -> 28.1 us  [over_z(): lax.ppermute(v, 'expert', [(i, (i + 2 * by) % n_expert) for i in range(n_...]
    ppermute x6, starting transfers between devices: 6.15 us -> 8.54 us  [over_y(): return lax.ppermute(v, 'dp', y_pairs)]
    ppermute x6, waiting for transfers between devices: 1.98 us -> 0.02 us  [over_y(): return lax.ppermute(v, 'dp', y_pairs)]
  transfers between devices with their start and end apart: 25 -> 25, of which waited for: 8 -> 9; matrix products, arithmetic and copies ran while one was open for 0% -> 0% of each run, Pallas kernels for 35% -> 35%
where the time goes in v8:
time: 102 us
  Pallas kernels  39.8 us (39%)
  waiting for transfers between devices  32.6 us (32%)
  starting transfers between devices  27.4 us (27%)
  local copies, waits for them, and re-layouts  1.04 us (1%)
    ppermute x8, waiting for transfers between devices, over_z(): lax.ppermute(v, 'expert', [(i, (i + 2 * by) % n_expert) for i in range(n_...  28.1 us
    pallas_call x4, Pallas kernels, forward(): pl.pallas_call(functools.partial(forward_kernel, given, back), in_specs=[...  24.7 us
    ppermute x8, starting transfers between devices, over_z(): lax.ppermute(v, 'expert', [(i, (i + 2 * by) % n_expert) for i in range(n_...  11.2 us
    pallas_call x2, Pallas kernels, grads(): pl.pallas_call(functools.partial(grads_kernel, n, len(early)), in_specs=[...  9.28 us
    ppermute x6, starting transfers between devices, over_y(): return lax.ppermute(v, 'dp', y_pairs)  8.54 us
    ppermute x7, starting transfers between devices, over_x(): return lax.ppermute(v, 'expert', x_pairs)  7.54 us
    ppermute x7, waiting for transfers between devices, over_x(): return lax.ppermute(v, 'expert', x_pairs)  4.42 us
    pallas_call x1, Pallas kernels, pack(): pl.pallas_call(pack_kernel, in_specs=[pl.BlockSpec(memory_space=pltpu.HBM...  2.77 us
  transfers between devices with their start and end apart: 25, of which 9 were waited for; matrix products, arithmetic and copies ran while one was open for 0% of the time, Pallas kernels for 35%

profile of v8, /device:TPU:0, one launch (start us, length us, event | category | flops | bytes accessed | tf_op | source)
XLA Modules:
  0.0 101.7 jit_solution(10761555573568849268)
XLA Ops:
  0.6 0.0 slice-start
  0.6 2.8 %pack.1.block.refs_1_ = bf16[72,3072]{1,0:T(8,128)(2,1)} custom-call(s32[2,128]{1,0:T(2,128)} %bitcast.6, f32[2,128]{1,0:T(2,128)} %bitcast.8, bf16[128,3072]{1,0:T(8,128)(2,1)} %tokens_in.1, bf16[128,3072]{1,0:T(8,128)(2,1)} %cotangent_in.1), custom_call_target="tpu_custom_call" | custom-call | tf_op jit(solution)/shard_map/pack/pallas_call | solution.py:83
  3.4 3.0 %collective-permute-start.2 = (bf16[72,3072]{1,0:T(8,128)(2,1)}, bf16[72,3072]{1,0:T(8,128)(2,1)S(1)}, u32[]{:S(2)}, u32[]{:S(2)}) collective-permute-start(bf16[72,3072]{1,0:T(8,128)(2,1)} %pack.1.block.refs_1_), channel_id=1, source_target_pairs={{0,1},{1,0},{2,3},{3,2},{4,5},{5,4},{6,7},{7,6},{8,9},{9,8},{10,11... | collective-permute-start | bytes 1327112 | tf_op jit(solution)/shard_map/ppermute | solution.py:379
  6.4 1.6 %collective-permute-start.1 = (bf16[72,3072]{1,0:T(8,128)(2,1)}, bf16[72,3072]{1,0:T(8,128)(2,1)S(1)}, u32[]{:S(2)}, u32[]{:S(2)}) collective-permute-start(bf16[72,3072]{1,0:T(8,128)(2,1)} %pack.1.block.refs_1_), channel_id=1, source_target_pairs={{0,2},{1,3},{2,4},{3,5},{4,6},{5,7},{6,0},{7,1},{8,10},{9,11},{10,... | collective-permute-start | bytes 1327112 | tf_op jit(solution)/shard_map/ppermute | solution.py:382
  8.0 1.5 %collective-permute-start = (bf16[72,3072]{1,0:T(8,128)(2,1)}, bf16[72,3072]{1,0:T(8,128)(2,1)S(1)}, u32[]{:S(2)}, u32[]{:S(2)}) collective-permute-start(bf16[72,3072]{1,0:T(8,128)(2,1)} %pack.1.block.refs_1_), channel_id=1, source_target_pairs={{0,16},{8,24},{16,0},{24,8},{1,17},{9,25},{17,1},{25,9},{2,18},{10... | collective-permute-start | bytes 1327112 | tf_op jit(solution)/shard_map/ppermute | solution.py:376
  9.5 0.1 pad_add_fusion.place
  9.6 1.0 copy-done.2
  10.6 1.1 %settle.1.place = s32[2]{0:T(128)S(1)} custom-call(s32[2]{0:T(128)S(1)} %pad_add_fusion.place, bf16[72,3072]{1,0:T(8,128)(2,1)S(1)} %copy-done.2), custom_call_target="tpu_custom_call" | custom-call | flops 20000000000 | tf_op jit(solution)/shard_map/settle/pallas_call | solution.py:302
  11.8 0.0 copy-start.3
  11.8 2.3 %collective-permute-start.5 = (bf16[72,3072]{1,0:T(8,128)(2,1)S(1)}, bf16[72,3072]{1,0:T(8,128)(2,1)S(1)}, u32[]{:S(2)}, u32[]{:S(2)}) collective-permute-start(bf16[72,3072]{1,0:T(8,128)(2,1)S(1)} %copy-done.2), channel_id=1, source_target_pairs={{0,6},{1,7},{2,0},{3,1},{4,2},{5,3},{6,4},{7,5},{8,14},{9,15},{10,... | collective-permute-start | bytes 1327112 | tf_op jit(solution)/shard_map/ppermute | solution.py:382
  14.1 2.7 %collective-permute-done.2.refs_3_ = bf16[72,3072]{1,0:T(8,128)(2,1)S(1)} collective-permute-done((bf16[72,3072]{1,0:T(8,128)(2,1)}, bf16[72,3072]{1,0:T(8,128)(2,1)S(1)}, u32[]{:S(2)}, u32[]{:S(2)}) %collective-permute-start.2) | collective-permute-done | bytes 442400 | tf_op jit(solution)/shard_map/ppermute | solution.py:379
  16.8 4.8 %collective-permute-done.1.refs_0_ = bf16[72,3072]{1,0:T(8,128)(2,1)S(1)} collective-permute-done((bf16[72,3072]{1,0:T(8,128)(2,1)}, bf16[72,3072]{1,0:T(8,128)(2,1)S(1)}, u32[]{:S(2)}, u32[]{:S(2)}) %collective-permute-start.1) | collective-permute-done | bytes 442400 | tf_op jit(solution)/shard_map/ppermute | solution.py:382
  21.6 0.0 collective-permute-done.refs_0_
  21.6 0.3 collective-permute-start.6
  21.9 1.7 %collective-permute-start.3 = (bf16[72,3072]{1,0:T(8,128)(2,1)S(1)}, bf16[72,3072]{1,0:T(8,128)(2,1)S(1)}, u32[]{:S(2)}, u32[]{:S(2)}) collective-permute-start(bf16[72,3072]{1,0:T(8,128)(2,1)S(1)} %collective-permute-done.2.refs_3_), channel_id=1, source_target_pairs={{0,16},{8,24},{16,0},{24,8},{1,17},{9,25},{17,1},{25,9},{2,18},{10... | collective-permute-start | bytes 1327112 | tf_op jit(solution)/shard_map/ppermute | solution.py:376
  23.6 7.3 %collective-permute-done.5.refs_1_ = bf16[72,3072]{1,0:T(8,128)(2,1)S(1)} collective-permute-done((bf16[72,3072]{1,0:T(8,128)(2,1)S(1)}, bf16[72,3072]{1,0:T(8,128)(2,1)S(1)}, u32[]{:S(2)}, u32[]{:S(2)}) %collective-permute-start.5) | collective-permute-done | bytes 442400 | tf_op jit(solution)/shard_map/ppermute | solution.py:382
  31.0 0.3 collective-permute-start.7
  31.3 1.7 %collective-permute-start.9 = (bf16[72,3072]{1,0:T(8,128)(2,1)S(1)}, bf16[72,3072]{1,0:T(8,128)(2,1)S(1)}, u32[]{:S(2)}, u32[]{:S(2)}) collective-permute-start(bf16[72,3072]{1,0:T(8,128)(2,1)S(1)} %collective-permute-done.5.refs_1_), channel_id=1, source_target_pairs={{0,16},{8,24},{16,0},{24,8},{1,17},{9,25},{17,1},{25,9},{2,18},{10... | collective-permute-start | bytes 1327112 | tf_op jit(solution)/shard_map/ppermute | solution.py:376
  33.0 6.1 %collective-permute-done.4.refs_0_ = bf16[72,3072]{1,0:T(8,128)(2,1)S(1)} collective-permute-done((bf16[72,3072]{1,0:T(8,128)(2,1)S(1)}, bf16[72,3072]{1,0:T(8,128)(2,1)S(1)}, u32[]{:S(2)}, u32[]{:S(2)}) %collective-permute-start.4) | collective-permute-done | bytes 442400 | tf_op jit(solution)/shard_map/ppermute | solution.py:382
  39.2 0.5 collective-permute-start.12
  39.7 1.5 %collective-permute-start.11 = (bf16[72,3072]{1,0:T(8,128)(2,1)S(1)}, bf16[72,3072]{1,0:T(8,128)(2,1)S(1)}, u32[]{:S(2)}, u32[]{:S(2)}) collective-permute-start(bf16[72,3072]{1,0:T(8,128)(2,1)S(1)} %collective-permute-done.4.refs_0_), channel_id=1, source_target_pairs={{0,16},{8,24},{16,0},{24,8},{1,17},{9,25},{17,1},{25,9},{2,18},{10... | collective-permute-start | bytes 1327112 | tf_op jit(solution)/shard_map/ppermute | solution.py:376
  41.2 1.4 %collective-permute-start.10 = (bf16[72,3072]{1,0:T(8,128)(2,1)S(1)}, bf16[72,3072]{1,0:T(8,128)(2,1)S(1)}, u32[]{:S(2)}, u32[]{:S(2)}) collective-permute-start(bf16[72,3072]{1,0:T(8,128)(2,1)S(1)} %collective-permute-done.refs_0_), channel_id=1, source_target_pairs={{0,2},{1,3},{2,4},{3,5},{4,6},{5,7},{6,0},{7,1},{8,10},{9,11},{10,... | collective-permute-start | bytes 1327112 | tf_op jit(solution)/shard_map/ppermute | solution.py:382
  42.6 1.4 %collective-permute-done.7.refs_3_ = bf16[72,3072]{1,0:T(8,128)(2,1)S(1)} collective-permute-done((bf16[72,3072]{1,0:T(8,128)(2,1)S(1)}, bf16[72,3072]{1,0:T(8,128)(2,1)S(1)}, u32[]{:S(2)}, u32[]{:S(2)}) %collective-permute-start.7) | collective-permute-done | bytes 442400 | tf_op jit(solution)/shard_map/ppermute | solution.py:379
  44.0 7.8 %forward_back.2 = (bf16[144,4608]{1,0:T(8,128)(2,1)S(1)}, bf16[144,1536]{1,0:T(8,128)(2,1)S(1)}, bf16[72,3072]{1,0:T(8,128)(2,1)S(1)}, bf16[72,3072]{1,0:T(8,128)(2,1)S(1)}) custom-call(s32[2]{0:T(128)S(1)} %settle.1.place, bf16[72,3072]{1,0:T(8,128)(2,1)S(1)} %collective-permute-done.1.refs_0_, bf16[72,3072]{1,0:T(8,128)(2,1)S(1)} %collective-permute-done.5.refs_1_, ...), custom_call_target="tpu_custom_call" | custom-call | flops 10000000000 | tf_op jit(solution)/shard_map/forward_back/pallas_call | solution.py:222
  51.8 0.1 collective-permute-start.13
  51.9 0.4 collective-permute-start.8
  52.3 2.1 %collective-permute-start.14 = (bf16[72,3072]{1,0:T(8,128)(2,1)S(1)}, bf16[72,3072]{1,0:T(8,128)(2,1)S(1)}, u32[]{:S(2)}, u32[]{:S(2)}) collective-permute-start(bf16[72,3072]{1,0:T(8,128)(2,1)S(1)} %collective-permute-done.3.refs_1_), channel_id=1, source_target_pairs={{0,2},{1,3},{2,4},{3,5},{4,6},{5,7},{6,0},{7,1},{8,10},{9,11},{10,... | collective-permute-start | bytes 1327112 | tf_op jit(solution)/shard_map/ppermute | solution.py:382
  54.3 1.5 %collective-permute-start.15 = (bf16[72,3072]{1,0:T(8,128)(2,1)S(1)}, bf16[72,3072]{1,0:T(8,128)(2,1)S(1)}, u32[]{:S(2)}, u32[]{:S(2)}) collective-permute-start(bf16[72,3072]{1,0:T(8,128)(2,1)S(1)} %collective-permute-done.7.refs_3_), channel_id=1, source_target_pairs={{0,16},{8,24},{16,0},{24,8},{1,17},{9,25},{17,1},{25,9},{2,18},{10... | collective-permute-start | bytes 1327112 | tf_op jit(solution)/shard_map/ppermute | solution.py:376
  55.9 0.5 collective-permute-start.16
  56.4 7.8 %forward_back.3 = (bf16[144,4608]{1,0:T(8,128)(2,1)S(1)}, bf16[144,1536]{1,0:T(8,128)(2,1)S(1)}, bf16[40,3072]{1,0:T(8,128)(2,1)S(1)}, bf16[40,3072]{1,0:T(8,128...) custom-call(s32[2]{0:T(128)S(1)} %settle.1.place, ...), custom_call_target="tpu_custom_call" | custom-call | flops 10000000000 | tf_op jit(solution)/shard_map/forward_back/pallas_call | solution.py:222
  64.2 0.3 collective-permute-done.8.came
  64.5 0.1 merge.1
  64.6 5.7 %collective-permute-done.14.refs_3_ = bf16[72,3072]{1,0:T(8,128)(2,1)S(1)} collective-permute-done((bf16[72,3072]{1,0:T(8,128)(2,1)S(1)}, bf16[72,3072]{1,0:T(8,128)(2,1)S(1)}, u32[]{:S(2)}, u32[]{:S(2)}) %collective-permute-start.14) | collective-permute-done | bytes 442400 | tf_op jit(solution)/shard_map/ppermute | solution.py:382
  70.3 1.5 %collective-permute-start.20 = (bf16[40,3072]{1,0:T(8,128)(2,1)S(1)}, bf16[40,3072]{1,0:T(8,128)(2,1)S(1)}, u32[]{:S(2)}, u32[]{:S(2)}) collective-permute-start(bf16[40,3072]{1,0:T(8,128)(2,1)S(1)} %get-tuple-element.49), channel_id=1, source_target_pairs={{0,1},{1,0},{2,3},{3,2},{4,5},{5,4},{6,7},{7,6},{8,9},{9,8},{10,11... | collective-permute-start | bytes 737288 | tf_op jit(solution)/shard_map/ppermute | solution.py:379
  71.8 1.7 %collective-permute-start.21 = (bf16[40,3072]{1,0:T(8,128)(2,1)S(1)}, bf16[40,3072]{1,0:T(8,128)(2,1)S(1)}, u32[]{:S(2)}, u32[]{:S(2)}) collective-permute-start(bf16[40,3072]{1,0:T(8,128)(2,1)S(1)} %get-tuple-element.51), channel_id=1, source_target_pairs={{0,6},{1,7},{2,0},{3,1},{4,2},{5,3},{6,4},{7,5},{8,14},{9,15},{10,... | collective-permute-start | bytes 737288 | tf_op jit(solution)/shard_map/ppermute | solution.py:382
  73.6 0.3 collective-permute-start.22
  73.9 4.6 %forward.2 = (bf16[144,4608]{1,0:T(8,128)(2,1)S(1)}, bf16[144,1536]{1,0:T(8,128)(2,1)S(1)}) custom-call(s32[2]{0:T(128)S(1)} %settle.1.place, bf16[72,3072]{1,0:T(8,128)(2,1)S(1)} %collective-permute-done.refs_0_, bf16[72,3072]{1,0:T(8,128)(2,1)S(1)} %collective-permute-done.3.refs_1_, bf16[72,3072]{1,0:T(8,128)(2,1)S(1)} %collective-permute-done.9.refs_2_, ...), custom_call_target="tpu_custom_call" | custom-call | flops 1000000 | tf_op jit(solution)/shard_map/forward/pallas_call | solution.py:222
  78.4 0.1 collective-permute-start.17
  78.5 4.6 %forward.3 = (bf16[144,4608]{1,0:T(8,128)(2,1)S(1)}, bf16[144,1536]{1,0:T(8,128)(2,1)S(1)}) custom-call(s32[2]{0:T(128)S(1)} %settle.1.place, bf16[72,3072]{1,0:T(8,128)(2,1)S(1)} %collective-permute-done.11.refs_0_, bf16[72,3072]{1,0:T(8,128)(2,1)S(1)} %collective-permute-done.16.refs_1_, bf16[72,3072]{1,0:T(8,128)(2,1)S(1)} %collective-permute-done.10.refs_2_, ...), custom_call_target="tpu_custom_call" | custom-call | flops 10000000000 | tf_op jit(solution)/shard_map/forward/pallas_call | solution.py:222
  83.1 2.2 %collective-permute-done.22.refs_4_ = bf16[40,3072]{1,0:T(8,128)(2,1)S(1)} collective-permute-done((bf16[40,3072]{1,0:T(8,128)(2,1)S(1)}, bf16[40,3072]{1,0:T(8,128)(2,1)S(1)}, u32[]{:S(2)}, u32[]{:S(2)}) %collective-permute-start.22) | collective-permute-done | bytes 245792 | tf_op jit(solution)/shard_map/ppermute | solution.py:382
  85.3 0.1 add.12
  85.3 1.8 %collective-permute-start.24 = (bf16[40,3072]{1,0:T(8,128)(2,1)S(1)}, bf16[40,3072]{1,0:T(8,128)(2,1)S(1)}, u32[]{:S(2)}, u32[]{:S(2)}) collective-permute-start(bf16[40,3072]{1,0:T(8,128)(2,1)S(1)} %add.12), channel_id=1, source_target_pairs={{0,4},{1,5},{2,6},{3,7},{4,0},{5,1},{6,2},{7,3},{8,12},{9,13},{10,... | collective-permute-start | bytes 737288 | tf_op jit(solution)/shard_map/ppermute | solution.py:382
  87.1 1.5 %collective-permute-start.23 = (bf16[40,3072]{1,0:T(8,128)(2,1)S(1)}, bf16[40,3072]{1,0:T(8,128)(2,1)S(1)}, u32[]{:S(2)}, u32[]{:S(2)}) collective-permute-start(bf16[40,3072]{1,0:T(8,128)(2,1)S(1)} %get-tuple-element.73), channel_id=1, source_target_pairs={{0,1},{1,0},{2,3},{3,2},{4,5},{5,4},{6,7},{7,6},{8,9},{9,8},{10,11... | collective-permute-start | bytes 737288 | tf_op jit(solution)/shard_map/ppermute | solution.py:379
  88.6 3.8 %grads.2 = (bf16[768,1024]{1,0:T(8,128)(2,1)S(1)}, bf16[768,1024]{1,0:T(8,128)(2,1)S(1)}, bf16[1024,768]{1,0:T(8,128)(2,1)S(1)}) custom-call(bf16[144,4608]{1,0:T(8,128)(2,1)S(1)} %get-tuple-element.52.refs_0_, bf16[144,4608]{1,0:T(8,128)(2,1)S(1)} %get-tuple-element.60.refs_1_, bf16[144,1536]{1,0:T(8,128)(2,1)S(1)} %get-tuple-element.61.refs_2_, ...), custom_call_target="tpu_custom_call" | custom-call | flops 40000000000 | tf_op jit(solution)/shard_map/grads/pallas_call | solution.py:280
  92.5 0.0 copy-start.4
  92.5 5.4 %grads.3 = (bf16[768,1024]{1,0:T(8,128)(2,1)}, bf16[768,1024]{1,0:T(8,128)(2,1)}, bf16[1024,768]{1,0:T(8,128)(2,1)}) custom-call(bf16[144,4608]{1,0:T(8,128)(2,1)S(1)} %get-tuple-element.55.refs_0_, bf16[144,4608]{1,0:T(8,128)(2,1)S(1)} %get-tuple-element.57.refs_1_, bf16[144,1536]{1,0:T(8,128)(2,1)S(1)} %get-tuple-element.58.refs_2_, ...), custom_call_target="tpu_custom_call" | custom-call | flops 1000000 | tf_op jit(solution)/shard_map/grads/pallas_call | solution.py:280
  97.9 2.0 %collective-permute-done.24.refs_3_ = bf16[40,3072]{1,0:T(8,128)(2,1)S(1)} collective-permute-done((bf16[40,3072]{1,0:T(8,128)(2,1)S(1)}, bf16[40,3072]{1,0:T(8,128)(2,1)S(1)}, u32[]{:S(2)}, u32[]{:S(2)}) %collective-permute-start.24) | collective-permute-done | bytes 245792 | tf_op jit(solution)/shard_map/ppermute | solution.py:382
  99.9 1.7 %unpack.1 = bf16[128,3072]{1,0:T(8,128)(2,1)} custom-call(s32[2,128]{1,0:T(2,128)S(1)} %bitcast.7, bf16[40,3072]{1,0:T(8,128)(2,1)S(1)} %get-tuple-element.68.refs_0_, bf16[40,3072]{1,0:T(8,128)(2,1)S(1)} %collective-permute-done.23.refs_1_, bf16[40,3072]{1,0:T(8,128)(2,1)S(1)} %collective-permute-done.21.refs_2_, ...), custom_call_target="tpu_custom_call" | custom-call | tf_op jit(solution)/shard_map/unpack/pallas_call | solution.py:107
  (29 shorter events, 0.1 us)
Async XLA Ops:
  0.6 43.4 %slice-start = ((s8[6291456]{0:T(1024)(128)(4,1)}), s8[2097152]{0:T(1024)(128)(4,1)S(1)}, s32[]{:S(2)}) async-start(s8[6291456]{0:T(1024)(128)(4,1)} %bitcast.4), calls=%async_computation | async-start | bytes 4194304
  3.4 13.4 %collective-permute-start.2 = (bf16[72,3072]{1,0:T(8,128)(2,1)}, bf16[72,3072]{1,0:T(8,128)(2,1)S(1)}, u32[]{:S(2)}, u32[]{:S(2)}) collective-permute-start(bf16[72,3072]{1,0:T(8,128)(2,1)} %pack.1.block.refs_1_), channel_id=1, source_target_pairs={{0,1},{1,0},{2,3},{3,2},{4,5},{5,4},{6,7},{7,6},{8,9},{9,8},{10,11... | collective-permute-start | bytes 1327112 | tf_op jit(solution)/shard_map/ppermute | solution.py:379
  6.4 15.1 %collective-permute-start.1 = (bf16[72,3072]{1,0:T(8,128)(2,1)}, bf16[72,3072]{1,0:T(8,128)(2,1)S(1)}, u32[]{:S(2)}, u32[]{:S(2)}) collective-permute-start(bf16[72,3072]{1,0:T(8,128)(2,1)} %pack.1.block.refs_1_), channel_id=1, source_target_pairs={{0,2},{1,3},{2,4},{3,5},{4,6},{5,7},{6,0},{7,1},{8,10},{9,11},{10,... | collective-permute-start | bytes 1327112 | tf_op jit(solution)/shard_map/ppermute | solution.py:382
  8.0 13.6 %collective-permute-start = (bf16[72,3072]{1,0:T(8,128)(2,1)}, bf16[72,3072]{1,0:T(8,128)(2,1)S(1)}, u32[]{:S(2)}, u32[]{:S(2)}) collective-permute-start(bf16[72,3072]{1,0:T(8,128)(2,1)} %pack.1.block.refs_1_), channel_id=1, source_target_pairs={{0,16},{8,24},{16,0},{24,8},{1,17},{9,25},{17,1},{25,9},{2,18},{10... | collective-permute-start | bytes 1327112 | tf_op jit(solution)/shard_map/ppermute | solution.py:376
  9.6 1.0 copy-start.2
  10.6 33.4 %slice-start.1 = ((s8[6291456]{0:T(1024)(128)(4,1)}), s8[4194304]{0:T(1024)(128)(4,1)S(1)}, s32[]{:S(2)}) async-start(s8[6291456]{0:T(1024)(128)(4,1)} %bitcast.4), calls=%async_computation.1 | async-start | bytes 8388608
  10.6 33.4 %copy-start = (bf16[3072,1024]{1,0:T(8,128)(2,1)S(1)}, bf16[3072,1024]{1,0:T(8,128)(2,1)}, u32[]{:S(2)}) copy-start(bf16[3072,1024]{1,0:T(8,128)(2,1)} %refs_5_.7) | copy-start | bytes 18874372
  10.6 33.4 %copy-start.1 = (bf16[1024,3072]{1,0:T(8,128)(2,1)S(1)}, bf16[1024,3072]{1,0:T(8,128)(2,1)}, u32[]{:S(2)}) copy-start(bf16[1024,3072]{1,0:T(8,128)(2,1)} %refs_6_.7) | copy-start | bytes 18874372
  11.8 44.6 %copy-start.3 = (bf16[72,3072]{1,0:T(8,128)(2,1)S(1)}, bf16[72,3072]{1,0:T(8,128)(2,1)}, u32[]{:S(2)}) copy-start(bf16[72,3072]{1,0:T(8,128)(2,1)} %pack.1.block.refs_1_) | copy-start | bytes 1327108
  11.8 19.2 %collective-permute-start.5 = (bf16[72,3072]{1,0:T(8,128)(2,1)S(1)}, bf16[72,3072]{1,0:T(8,128)(2,1)S(1)}, u32[]{:S(2)}, u32[]{:S(2)}) collective-permute-start(bf16[72,3072]{1,0:T(8,128)(2,1)S(1)} %copy-done.2), channel_id=1, source_target_pairs={{0,6},{1,7},{2,0},{3,1},{4,2},{5,3},{6,4},{7,5},{8,14},{9,15},{10,... | collective-permute-start | bytes 1327112 | tf_op jit(solution)/shard_map/ppermute | solution.py:382
  21.6 11.4 %collective-permute-start.6 = (bf16[72,3072]{1,0:T(8,128)(2,1)S(1)}, bf16[72,3072]{1,0:T(8,128)(2,1)S(1)}, u32[]{:S(2)}, u32[]{:S(2)}) collective-permute-start(bf16[72,3072]{1,0:T(8,128)(2,1)S(1)} %collective-permute-done.1.refs_0_), channel_id=1, source_target_pairs={{0,1},{1,0},{2,3},{3,2},{4,5},{5,4},{6,7},{7,6},{8,9},{9,8},{10,11... | collective-permute-start | bytes 1327112 | tf_op jit(solution)/shard_map/ppermute | solution.py:379
  21.9 17.3 %collective-permute-start.4 = (bf16[72,3072]{1,0:T(8,128)(2,1)S(1)}, bf16[72,3072]{1,0:T(8,128)(2,1)S(1)}, u32[]{:S(2)}, u32[]{:S(2)}) collective-permute-start(bf16[72,3072]{1,0:T(8,128)(2,1)S(1)} %collective-permute-done.1.refs_0_), channel_id=1, source_target_pairs={{0,2},{1,3},{2,4},{3,5},{4,6},{5,7},{6,0},{7,1},{8,10},{9,11},{10,... | collective-permute-start | bytes 1327112 | tf_op jit(solution)/shard_map/ppermute | solution.py:382
  21.9 19.3 %collective-permute-start.3 = (bf16[72,3072]{1,0:T(8,128)(2,1)S(1)}, bf16[72,3072]{1,0:T(8,128)(2,1)S(1)}, u32[]{:S(2)}, u32[]{:S(2)}) collective-permute-start(bf16[72,3072]{1,0:T(8,128)(2,1)S(1)} %collective-permute-done.2.refs_3_), channel_id=1, source_target_pairs={{0,16},{8,24},{16,0},{24,8},{1,17},{9,25},{17,1},{25,9},{2,18},{10... | collective-permute-start | bytes 1327112 | tf_op jit(solution)/shard_map/ppermute | solution.py:376
  31.0 13.1 %collective-permute-start.7 = (bf16[72,3072]{1,0:T(8,128)(2,1)S(1)}, bf16[72,3072]{1,0:T(8,128)(2,1)S(1)}, u32[]{:S(2)}, u32[]{:S(2)}) collective-permute-start(bf16[72,3072]{1,0:T(8,128)(2,1)S(1)} %collective-permute-done.5.refs_1_), channel_id=1, source_target_pairs={{0,1},{1,0},{2,3},{3,2},{4,5},{5,4},{6,7},{7,6},{8,9},{9,8},{10,11... | collective-permute-start | bytes 1327112 | tf_op jit(solution)/shard_map/ppermute | solution.py:379
  31.3 20.6 %collective-permute-start.9 = (bf16[72,3072]{1,0:T(8,128)(2,1)S(1)}, bf16[72,3072]{1,0:T(8,128)(2,1)S(1)}, u32[]{:S(2)}, u32[]{:S(2)}) collective-permute-start(bf16[72,3072]{1,0:T(8,128)(2,1)S(1)} %collective-permute-done.5.refs_1_), channel_id=1, source_target_pairs={{0,16},{8,24},{16,0},{24,8},{1,17},{9,25},{17,1},{25,9},{2,18},{10... | collective-permute-start | bytes 1327112 | tf_op jit(solution)/shard_map/ppermute | solution.py:376
  39.2 16.7 %collective-permute-start.12 = (bf16[72,3072]{1,0:T(8,128)(2,1)S(1)}, bf16[72,3072]{1,0:T(8,128)(2,1)S(1)}, u32[]{:S(2)}, u32[]{:S(2)}) collective-permute-start(bf16[72,3072]{1,0:T(8,128)(2,1)S(1)} %collective-permute-done.4.refs_0_), channel_id=1, source_target_pairs={{0,1},{1,0},{2,3},{3,2},{4,5},{5,4},{6,7},{7,6},{8,9},{9,8},{10,11... | collective-permute-start | bytes 1327112 | tf_op jit(solution)/shard_map/ppermute | solution.py:379
  39.7 14.7 %collective-permute-start.11 = (bf16[72,3072]{1,0:T(8,128)(2,1)S(1)}, bf16[72,3072]{1,0:T(8,128)(2,1)S(1)}, u32[]{:S(2)}, u32[]{:S(2)}) collective-permute-start(bf16[72,3072]{1,0:T(8,128)(2,1)S(1)} %collective-permute-done.4.refs_0_), channel_id=1, source_target_pairs={{0,16},{8,24},{16,0},{24,8},{1,17},{9,25},{17,1},{25,9},{2,18},{10... | collective-permute-start | bytes 1327112 | tf_op jit(solution)/shard_map/ppermute | solution.py:376
  41.2 11.1 %collective-permute-start.10 = (bf16[72,3072]{1,0:T(8,128)(2,1)S(1)}, bf16[72,3072]{1,0:T(8,128)(2,1)S(1)}, u32[]{:S(2)}, u32[]{:S(2)}) collective-permute-start(bf16[72,3072]{1,0:T(8,128)(2,1)S(1)} %collective-permute-done.refs_0_), channel_id=1, source_target_pairs={{0,2},{1,3},{2,4},{3,5},{4,6},{5,7},{6,0},{7,1},{8,10},{9,11},{10,... | collective-permute-start | bytes 1327112 | tf_op jit(solution)/shard_map/ppermute | solution.py:382
  51.8 20.0 %collective-permute-start.13 = (bf16[144,4608]{1,0:T(8,128)(2,1)S(1)}, bf16[144,4608]{1,0:T(8,128)(2,1)S(1)}, u32[]{:S(2)}, u32[]{:S(2)}) collective-permute-start(bf16[144,4608]{1,0:T(8,128)(2,1)S(1)} %get-tuple-element.52.refs_0_), channel_id=1, source_target_pairs={{0,8},{8,0},{16,24},{24,16},{1,9},{9,1},{17,25},{25,17},{2,10},{10... | collective-permute-start | bytes 3981320 | tf_op jit(solution)/shard_map/ppermute | solution.py:373
  51.9 12.6 %collective-permute-start.8 = (bf16[72,3072]{1,0:T(8,128)(2,1)S(1)}, bf16[72,3072]{1,0:T(8,128)(2,1)S(1)}, u32[]{:S(2)}, u32[]{:S(2)}) collective-permute-start(bf16[72,3072]{1,0:T(8,128)(2,1)S(1)} %get-tuple-element.45), channel_id=1, source_target_pairs={{0,1},{1,0},{2,3},{3,2},{4,5},{5,4},{6,7},{7,6},{8,9},{9,8},{10,11... | collective-permute-start | bytes 1327112 | tf_op jit(solution)/shard_map/ppermute | solution.py:379
  52.3 18.1 %collective-permute-start.14 = (bf16[72,3072]{1,0:T(8,128)(2,1)S(1)}, bf16[72,3072]{1,0:T(8,128)(2,1)S(1)}, u32[]{:S(2)}, u32[]{:S(2)}) collective-permute-start(bf16[72,3072]{1,0:T(8,128)(2,1)S(1)} %collective-permute-done.3.refs_1_), channel_id=1, source_target_pairs={{0,2},{1,3},{2,4},{3,5},{4,6},{5,7},{6,0},{7,1},{8,10},{9,11},{10,... | collective-permute-start | bytes 1327112 | tf_op jit(solution)/shard_map/ppermute | solution.py:382
  54.3 19.2 %collective-permute-start.15 = (bf16[72,3072]{1,0:T(8,128)(2,1)S(1)}, bf16[72,3072]{1,0:T(8,128)(2,1)S(1)}, u32[]{:S(2)}, u32[]{:S(2)}) collective-permute-start(bf16[72,3072]{1,0:T(8,128)(2,1)S(1)} %collective-permute-done.7.refs_3_), channel_id=1, source_target_pairs={{0,16},{8,24},{16,0},{24,8},{1,17},{9,25},{17,1},{25,9},{2,18},{10... | collective-permute-start | bytes 1327112 | tf_op jit(solution)/shard_map/ppermute | solution.py:376
  55.9 22.6 %collective-permute-start.16 = (bf16[72,3072]{1,0:T(8,128)(2,1)S(1)}, bf16[72,3072]{1,0:T(8,128)(2,1)S(1)}, u32[]{:S(2)}, u32[]{:S(2)}) collective-permute-start(bf16[72,3072]{1,0:T(8,128)(2,1)S(1)} %collective-permute-done.12.refs_2_), channel_id=1, source_target_pairs={{0,16},{8,24},{16,0},{24,8},{1,17},{9,25},{17,1},{25,9},{2,18},{10... | collective-permute-start | bytes 1327112 | tf_op jit(solution)/shard_map/ppermute | solution.py:376
  64.5 24.1 %collective-permute-start.19 = (bf16[144,4608]{1,0:T(8,128)(2,1)S(1)}, bf16[144,4608]{1,0:T(8,128)(2,1)S(1)}, u32[]{:S(2)}, u32[]{:S(2)}) collective-permute-start(bf16[144,4608]{1,0:T(8,128)(2,1)S(1)} %get-tuple-element.60.refs_1_), channel_id=1, source_target_pairs={{0,8},{8,0},{16,24},{24,16},{1,9},{9,1},{17,25},{25,17},{2,10},{10... | collective-permute-start | bytes 3981320 | tf_op jit(solution)/shard_map/ppermute | solution.py:373
  70.3 14.9 %collective-permute-start.20 = (bf16[40,3072]{1,0:T(8,128)(2,1)S(1)}, bf16[40,3072]{1,0:T(8,128)(2,1)S(1)}, u32[]{:S(2)}, u32[]{:S(2)}) collective-permute-start(bf16[40,3072]{1,0:T(8,128)(2,1)S(1)} %get-tuple-element.49), channel_id=1, source_target_pairs={{0,1},{1,0},{2,3},{3,2},{4,5},{5,4},{6,7},{7,6},{8,9},{9,8},{10,11... | collective-permute-start | bytes 737288 | tf_op jit(solution)/shard_map/ppermute | solution.py:379
  71.8 13.4 %collective-permute-start.21 = (bf16[40,3072]{1,0:T(8,128)(2,1)S(1)}, bf16[40,3072]{1,0:T(8,128)(2,1)S(1)}, u32[]{:S(2)}, u32[]{:S(2)}) collective-permute-start(bf16[40,3072]{1,0:T(8,128)(2,1)S(1)} %get-tuple-element.51), channel_id=1, source_target_pairs={{0,6},{1,7},{2,0},{3,1},{4,2},{5,3},{6,4},{7,5},{8,14},{9,15},{10,... | collective-permute-start | bytes 737288 | tf_op jit(solution)/shard_map/ppermute | solution.py:382
  73.6 11.7 %collective-permute-start.22 = (bf16[40,3072]{1,0:T(8,128)(2,1)S(1)}, bf16[40,3072]{1,0:T(8,128)(2,1)S(1)}, u32[]{:S(2)}, u32[]{:S(2)}) collective-permute-start(bf16[40,3072]{1,0:T(8,128)(2,1)S(1)} %get-tuple-element.71), channel_id=1, source_target_pairs={{0,2},{1,3},{2,4},{3,5},{4,6},{5,7},{6,0},{7,1},{8,10},{9,11},{10,... | collective-permute-start | bytes 737288 | tf_op jit(solution)/shard_map/ppermute | solution.py:382
  78.4 14.0 %collective-permute-start.17 = (bf16[144,4608]{1,0:T(8,128)(2,1)S(1)}, bf16[144,4608]{1,0:T(8,128)(2,1)S(1)}, u32[]{:S(2)}, u32[]{:S(2)}) collective-permute-start(bf16[144,4608]{1,0:T(8,128)(2,1)S(1)} %get-tuple-element.55.refs_0_), channel_id=1, source_target_pairs={{0,8},{8,0},{16,24},{24,16},{1,9},{9,1},{17,25},{25,17},{2,10},{10... | collective-permute-start | bytes 3981320 | tf_op jit(solution)/shard_map/ppermute | solution.py:373
  85.3 7.2 %collective-permute-start.18 = (bf16[144,4608]{1,0:T(8,128)(2,1)S(1)}, bf16[144,4608]{1,0:T(8,128)(2,1)S(1)}, u32[]{:S(2)}, u32[]{:S(2)}) collective-permute-start(bf16[144,4608]{1,0:T(8,128)(2,1)S(1)} %get-tuple-element.57.refs_1_), channel_id=1, source_target_pairs={{0,8},{8,0},{16,24},{24,16},{1,9},{9,1},{17,25},{25,17},{2,10},{10... | collective-permute-start | bytes 3981320 | tf_op jit(solution)/shard_map/ppermute | solution.py:373
  85.3 14.6 %collective-permute-start.24 = (bf16[40,3072]{1,0:T(8,128)(2,1)S(1)}, bf16[40,3072]{1,0:T(8,128)(2,1)S(1)}, u32[]{:S(2)}, u32[]{:S(2)}) collective-permute-start(bf16[40,3072]{1,0:T(8,128)(2,1)S(1)} %add.12), channel_id=1, source_target_pairs={{0,4},{1,5},{2,6},{3,7},{4,0},{5,1},{6,2},{7,3},{8,12},{9,13},{10,... | collective-permute-start | bytes 737288 | tf_op jit(solution)/shard_map/ppermute | solution.py:382
  87.1 10.8 %collective-permute-start.23 = (bf16[40,3072]{1,0:T(8,128)(2,1)S(1)}, bf16[40,3072]{1,0:T(8,128)(2,1)S(1)}, u32[]{:S(2)}, u32[]{:S(2)}) collective-permute-start(bf16[40,3072]{1,0:T(8,128)(2,1)S(1)} %get-tuple-element.73), channel_id=1, source_target_pairs={{0,1},{1,0},{2,3},{3,2},{4,5},{5,4},{6,7},{7,6},{8,9},{9,8},{10,11... | collective-permute-start | bytes 737288 | tf_op jit(solution)/shard_map/ppermute | solution.py:379
  92.5 7.4 %copy-start.4 = (s32[128,2]{0,1:T(2,128)S(1)}, s32[128,2]{0,1:T(2,128)}, u32[]{:S(2)}) copy-start(s32[128,2]{0,1:T(2,128)} %param.9) | copy-start | bytes 3076

commit v9 on v8

--- a/solution.py
+++ b/solution.py
@@ -91,29 +91,49 @@
     )(*values)
 
 
-def unpack_kernel(ids, *refs):
+def settle_rows_kernel(ids, *refs):
+    pieces, (place, total) = refs[:-2], refs[-2:]
+    chosen, slots = earlier_count(ids[...])
+    place[...] = one_hot(slots, chosen, place.shape[0]).astype(HALF)
+    found = pieces[0][...].astype(FULL)
+    for piece in pieces[1:]:
+        found = found + piece[...].astype(FULL)
+    total[...] = found
+
+
+def settle_rows(ids, pieces):
+    depth, width = pieces[0].shape
+    return pl.pallas_call(
+        settle_rows_kernel,
+        out_shape=[shape((depth, ids.shape[1])), shape((depth, width), FULL)],
+        compiler_params=params(LIMIT),
+        cost_estimate=pl.CostEstimate(flops=10**6, bytes_accessed=0, transcendentals=0),
+        name="settle_rows",
+    )(ids, *pieces)
+
+
+def unpack_kernel(place, total, *refs):
     pieces, out = refs[:-1], refs[-1]
-    chosen, slots = earlier_count(ids[...])
-    place = one_hot(slots, chosen, pieces[0].shape[0]).astype(HALF)
-    total = pieces[0][...].astype(FULL)
-    for piece in pieces[1:]:
-        total = total + piece[...].astype(FULL)
-    out[...] = tn_dot(place, total.astype(HALF)).astype(HALF)
-
-
-def unpack(ids, pieces):
-    count, (depth, width) = ids.shape[1], pieces[0].shape
+    found = total[...]
+    for piece in pieces:
+        found = found + piece[...].astype(FULL)
+    out[...] = tn_dot(place[...], found.astype(HALF)).astype(HALF)
+
+
+def unpack(place, total, pieces):
+    (depth, width), count = total.shape, place.shape[1]
     step = 1536
+    column = lambda j: (0, j)
     return pl.pallas_call(
         unpack_kernel,
         grid=(width // step,),
-        in_specs=[pl.BlockSpec(ids.shape, lambda j: (0, 0))]
-        + [pl.BlockSpec((depth, step), lambda j: (0, j)) for _ in pieces],
-        out_specs=pl.BlockSpec((count, step), lambda j: (0, j)),
+        in_specs=[pl.BlockSpec(place.shape, lambda j: (0, 0))]
+        + [pl.BlockSpec((depth, step), column) for _ in range(1 + len(pieces))],
+        out_specs=pl.BlockSpec((count, step), column),
         out_shape=shape((count, width)),
         compiler_params=params(LIMIT),
         name="unpack",
-    )(ids, *pieces)
+    )(place, total, *pieces)
 
 
 def padded_rows(n):
@@ -432,7 +452,8 @@
     gate_grad, up_grad, down_grad = grads(
         [act2, act3], [own2, own3], [other2, other3], hidden, early, cost=COSTS[5]
     )
-    token_grad = unpack(after(ids, gate_grad), [near, beside, r1, r2, r3])
+    row_place, row_total = settle_rows(after(ids, gate_grad), [near, r1, r3])
+    token_grad = unpack(row_place, row_total, [beside, r2])
     return token_grad, gate_grad, up_grad, down_grad
 
 

time: 102 us -> 102 us (level)
  transfers between devices with their start and end apart: 25 -> 25, of which waited for: 9 -> 9; matrix products, arithmetic and copies ran while one was open for 0% -> 0% of each run, Pallas kernels for 35% -> 36%
where the time goes in v9:
time: 102 us
  Pallas kernels  40.3 us (40%)
  waiting for transfers between devices  31.8 us (31%)
  starting transfers between devices  27.5 us (27%)
  local copies, waits for them, and re-layouts  1.04 us (1%)
    ppermute x8, waiting for transfers between devices, over_z(): lax.ppermute(v, 'expert', [(i, (i + 2 * by) % n_expert) for i in range(n_...  27.5 us
    pallas_call x4, Pallas kernels, forward(): pl.pallas_call(functools.partial(forward_kernel, given, back), in_specs=[...  25.3 us
    ppermute x8, starting transfers between devices, over_z(): lax.ppermute(v, 'expert', [(i, (i + 2 * by) % n_expert) for i in range(n_...  11.3 us
    pallas_call x2, Pallas kernels, grads(): pl.pallas_call(functools.partial(grads_kernel, n, len(early)), in_specs=[...  9.32 us
    ppermute x6, starting transfers between devices, over_y(): return lax.ppermute(v, 'dp', y_pairs)  8.54 us
    ppermute x7, starting transfers between devices, over_x(): return lax.ppermute(v, 'expert', x_pairs)  7.55 us
    ppermute x7, waiting for transfers between devices, over_x(): return lax.ppermute(v, 'expert', x_pairs)  4.24 us
    pallas_call x1, Pallas kernels, pack(): pl.pallas_call(pack_kernel, in_specs=[pl.BlockSpec(memory_space=pltpu.HBM...  2.77 us
  transfers between devices with their start and end apart: 25, of which 9 were waited for; matrix products, arithmetic and copies ran while one was open for 0% of the time, Pallas kernels for 36%

profile of v9, /device:TPU:0, one launch (start us, length us, event | category | flops | bytes accessed | tf_op | source)
XLA Modules:
  0.0 101.5 jit_solution(14259437606763592496)
XLA Ops:
  0.6 0.0 slice-start
  0.6 2.8 %pack.1.block.refs_1_ = bf16[72,3072]{1,0:T(8,128)(2,1)} custom-call(s32[2,128]{1,0:T(2,128)} %bitcast.6, f32[2,128]{1,0:T(2,128)} %bitcast.8, bf16[128,3072]{1,0:T(8,128)(2,1)} %tokens_in.1, bf16[128,3072]{1,0:T(8,128)(2,1)} %cotangent_in.1), custom_call_target="tpu_custom_call" | custom-call | tf_op jit(solution)/shard_map/pack/pallas_call | solution.py:83
  3.4 3.0 %collective-permute-start.2 = (bf16[72,3072]{1,0:T(8,128)(2,1)}, bf16[72,3072]{1,0:T(8,128)(2,1)S(1)}, u32[]{:S(2)}, u32[]{:S(2)}) collective-permute-start(bf16[72,3072]{1,0:T(8,128)(2,1)} %pack.1.block.refs_1_), channel_id=1, source_target_pairs={{0,1},{1,0},{2,3},{3,2},{4,5},{5,4},{6,7},{7,6},{8,9},{9,8},{10,11... | collective-permute-start | bytes 1327112 | tf_op jit(solution)/shard_map/ppermute | solution.py:399
  6.4 1.6 %collective-permute-start.1 = (bf16[72,3072]{1,0:T(8,128)(2,1)}, bf16[72,3072]{1,0:T(8,128)(2,1)S(1)}, u32[]{:S(2)}, u32[]{:S(2)}) collective-permute-start(bf16[72,3072]{1,0:T(8,128)(2,1)} %pack.1.block.refs_1_), channel_id=1, source_target_pairs={{0,2},{1,3},{2,4},{3,5},{4,6},{5,7},{6,0},{7,1},{8,10},{9,11},{10,... | collective-permute-start | bytes 1327112 | tf_op jit(solution)/shard_map/ppermute | solution.py:402
  8.0 1.5 %collective-permute-start = (bf16[72,3072]{1,0:T(8,128)(2,1)}, bf16[72,3072]{1,0:T(8,128)(2,1)S(1)}, u32[]{:S(2)}, u32[]{:S(2)}) collective-permute-start(bf16[72,3072]{1,0:T(8,128)(2,1)} %pack.1.block.refs_1_), channel_id=1, source_target_pairs={{0,16},{8,24},{16,0},{24,8},{1,17},{9,25},{17,1},{25,9},{2,18},{10... | collective-permute-start | bytes 1327112 | tf_op jit(solution)/shard_map/ppermute | solution.py:396
  9.5 0.1 pad_add_fusion.place
  9.6 1.0 copy-done.2
  10.6 1.1 %settle.1.place = s32[2]{0:T(128)S(1)} custom-call(s32[2]{0:T(128)S(1)} %pad_add_fusion.place, bf16[72,3072]{1,0:T(8,128)(2,1)S(1)} %copy-done.2), custom_call_target="tpu_custom_call" | custom-call | flops 20000000000 | tf_op jit(solution)/shard_map/settle/pallas_call | solution.py:322
  11.8 0.0 copy-start.3
  11.8 2.3 %collective-permute-start.5 = (bf16[72,3072]{1,0:T(8,128)(2,1)S(1)}, bf16[72,3072]{1,0:T(8,128)(2,1)S(1)}, u32[]{:S(2)}, u32[]{:S(2)}) collective-permute-start(bf16[72,3072]{1,0:T(8,128)(2,1)S(1)} %copy-done.2), channel_id=1, source_target_pairs={{0,6},{1,7},{2,0},{3,1},{4,2},{5,3},{6,4},{7,5},{8,14},{9,15},{10,... | collective-permute-start | bytes 1327112 | tf_op jit(solution)/shard_map/ppermute | solution.py:402
  14.1 2.7 %collective-permute-done.2.refs_3_ = bf16[72,3072]{1,0:T(8,128)(2,1)S(1)} collective-permute-done((bf16[72,3072]{1,0:T(8,128)(2,1)}, bf16[72,3072]{1,0:T(8,128)(2,1)S(1)}, u32[]{:S(2)}, u32[]{:S(2)}) %collective-permute-start.2) | collective-permute-done | bytes 442400 | tf_op jit(solution)/shard_map/ppermute | solution.py:399
  16.8 4.8 %collective-permute-done.1.refs_0_ = bf16[72,3072]{1,0:T(8,128)(2,1)S(1)} collective-permute-done((bf16[72,3072]{1,0:T(8,128)(2,1)}, bf16[72,3072]{1,0:T(8,128)(2,1)S(1)}, u32[]{:S(2)}, u32[]{:S(2)}) %collective-permute-start.1) | collective-permute-done | bytes 442400 | tf_op jit(solution)/shard_map/ppermute | solution.py:402
  21.6 0.3 collective-permute-start.6
  21.9 1.7 %collective-permute-start.3 = (bf16[72,3072]{1,0:T(8,128)(2,1)S(1)}, bf16[72,3072]{1,0:T(8,128)(2,1)S(1)}, u32[]{:S(2)}, u32[]{:S(2)}) collective-permute-start(bf16[72,3072]{1,0:T(8,128)(2,1)S(1)} %collective-permute-done.2.refs_3_), channel_id=1, source_target_pairs={{0,16},{8,24},{16,0},{24,8},{1,17},{9,25},{17,1},{25,9},{2,18},{10... | collective-permute-start | bytes 1327112 | tf_op jit(solution)/shard_map/ppermute | solution.py:396
  23.6 7.3 %collective-permute-done.5.refs_1_ = bf16[72,3072]{1,0:T(8,128)(2,1)S(1)} collective-permute-done((bf16[72,3072]{1,0:T(8,128)(2,1)S(1)}, bf16[72,3072]{1,0:T(8,128)(2,1)S(1)}, u32[]{:S(2)}, u32[]{:S(2)}) %collective-permute-start.5) | collective-permute-done | bytes 442400 | tf_op jit(solution)/shard_map/ppermute | solution.py:402
  31.0 0.3 collective-permute-start.7
  31.3 1.7 %collective-permute-start.9 = (bf16[72,3072]{1,0:T(8,128)(2,1)S(1)}, bf16[72,3072]{1,0:T(8,128)(2,1)S(1)}, u32[]{:S(2)}, u32[]{:S(2)}) collective-permute-start(bf16[72,3072]{1,0:T(8,128)(2,1)S(1)} %collective-permute-done.5.refs_1_), channel_id=1, source_target_pairs={{0,16},{8,24},{16,0},{24,8},{1,17},{9,25},{17,1},{25,9},{2,18},{10... | collective-permute-start | bytes 1327112 | tf_op jit(solution)/shard_map/ppermute | solution.py:396
  33.0 6.1 %collective-permute-done.4.refs_0_ = bf16[72,3072]{1,0:T(8,128)(2,1)S(1)} collective-permute-done((bf16[72,3072]{1,0:T(8,128)(2,1)S(1)}, bf16[72,3072]{1,0:T(8,128)(2,1)S(1)}, u32[]{:S(2)}, u32[]{:S(2)}) %collective-permute-start.4) | collective-permute-done | bytes 442400 | tf_op jit(solution)/shard_map/ppermute | solution.py:402
  39.2 0.5 collective-permute-start.12
  39.7 1.5 %collective-permute-start.11 = (bf16[72,3072]{1,0:T(8,128)(2,1)S(1)}, bf16[72,3072]{1,0:T(8,128)(2,1)S(1)}, u32[]{:S(2)}, u32[]{:S(2)}) collective-permute-start(bf16[72,3072]{1,0:T(8,128)(2,1)S(1)} %collective-permute-done.4.refs_0_), channel_id=1, source_target_pairs={{0,16},{8,24},{16,0},{24,8},{1,17},{9,25},{17,1},{25,9},{2,18},{10... | collective-permute-start | bytes 1327112 | tf_op jit(solution)/shard_map/ppermute | solution.py:396
  41.2 1.4 %collective-permute-start.10 = (bf16[72,3072]{1,0:T(8,128)(2,1)S(1)}, bf16[72,3072]{1,0:T(8,128)(2,1)S(1)}, u32[]{:S(2)}, u32[]{:S(2)}) collective-permute-start(bf16[72,3072]{1,0:T(8,128)(2,1)S(1)} %collective-permute-done.refs_0_), channel_id=1, source_target_pairs={{0,2},{1,3},{2,4},{3,5},{4,6},{5,7},{6,0},{7,1},{8,10},{9,11},{10,... | collective-permute-start | bytes 1327112 | tf_op jit(solution)/shard_map/ppermute | solution.py:402
  42.6 1.4 %collective-permute-done.7.refs_3_ = bf16[72,3072]{1,0:T(8,128)(2,1)S(1)} collective-permute-done((bf16[72,3072]{1,0:T(8,128)(2,1)S(1)}, bf16[72,3072]{1,0:T(8,128)(2,1)S(1)}, u32[]{:S(2)}, u32[]{:S(2)}) %collective-permute-start.7) | collective-permute-done | bytes 442400 | tf_op jit(solution)/shard_map/ppermute | solution.py:399
  44.0 8.0 %forward_back.2 = (bf16[144,4608]{1,0:T(8,128)(2,1)S(1)}, bf16[144,1536]{1,0:T(8,128)(2,1)S(1)}, bf16[72,3072]{1,0:T(8,128)(2,1)S(1)}, bf16[72,3072]{1,0:T(8,128)(2,1)S(1)}) custom-call(s32[2]{0:T(128)S(1)} %settle.1.place, bf16[72,3072]{1,0:T(8,128)(2,1)S(1)} %collective-permute-done.1.refs_0_, bf16[72,3072]{1,0:T(8,128)(2,1)S(1)} %collective-permute-done.5.refs_1_, ...), custom_call_target="tpu_custom_call" | custom-call | flops 10000000000 | tf_op jit(solution)/shard_map/forward_back/pallas_call | solution.py:242
  52.0 0.1 collective-permute-start.13
  52.1 0.4 collective-permute-start.8
  52.5 2.0 %collective-permute-start.14 = (bf16[72,3072]{1,0:T(8,128)(2,1)S(1)}, bf16[72,3072]{1,0:T(8,128)(2,1)S(1)}, u32[]{:S(2)}, u32[]{:S(2)}) collective-permute-start(bf16[72,3072]{1,0:T(8,128)(2,1)S(1)} %collective-permute-done.3.refs_1_), channel_id=1, source_target_pairs={{0,2},{1,3},{2,4},{3,5},{4,6},{5,7},{6,0},{7,1},{8,10},{9,11},{10,... | collective-permute-start | bytes 1327112 | tf_op jit(solution)/shard_map/ppermute | solution.py:402
  54.5 1.5 %collective-permute-start.15 = (bf16[72,3072]{1,0:T(8,128)(2,1)S(1)}, bf16[72,3072]{1,0:T(8,128)(2,1)S(1)}, u32[]{:S(2)}, u32[]{:S(2)}) collective-permute-start(bf16[72,3072]{1,0:T(8,128)(2,1)S(1)} %collective-permute-done.7.refs_3_), channel_id=1, source_target_pairs={{0,16},{8,24},{16,0},{24,8},{1,17},{9,25},{17,1},{25,9},{2,18},{10... | collective-permute-start | bytes 1327112 | tf_op jit(solution)/shard_map/ppermute | solution.py:396
  56.0 0.5 collective-permute-start.16
  56.6 8.0 %forward_back.3 = (bf16[144,4608]{1,0:T(8,128)(2,1)S(1)}, bf16[144,1536]{1,0:T(8,128)(2,1)S(1)}, bf16[40,3072]{1,0:T(8,128)(2,1)S(1)}, bf16[40,3072]{1,0:T(8,128...) custom-call(s32[2]{0:T(128)S(1)} %settle.1.place, ...), custom_call_target="tpu_custom_call" | custom-call | flops 10000000000 | tf_op jit(solution)/shard_map/forward_back/pallas_call | solution.py:242
  64.5 0.1 collective-permute-done.8.came
  64.7 0.1 merge.1
  64.8 5.7 %collective-permute-done.14.refs_3_ = bf16[72,3072]{1,0:T(8,128)(2,1)S(1)} collective-permute-done((bf16[72,3072]{1,0:T(8,128)(2,1)S(1)}, bf16[72,3072]{1,0:T(8,128)(2,1)S(1)}, u32[]{:S(2)}, u32[]{:S(2)}) %collective-permute-start.14) | collective-permute-done | bytes 442400 | tf_op jit(solution)/shard_map/ppermute | solution.py:402
  70.5 1.5 %collective-permute-start.22 = (bf16[40,3072]{1,0:T(8,128)(2,1)S(1)}, bf16[40,3072]{1,0:T(8,128)(2,1)S(1)}, u32[]{:S(2)}, u32[]{:S(2)}) collective-permute-start(bf16[40,3072]{1,0:T(8,128)(2,1)S(1)} %get-tuple-element.51), channel_id=1, source_target_pairs={{0,1},{1,0},{2,3},{3,2},{4,5},{5,4},{6,7},{7,6},{8,9},{9,8},{10,11... | collective-permute-start | bytes 737288 | tf_op jit(solution)/shard_map/ppermute | solution.py:399
  72.0 1.7 %collective-permute-start.20 = (bf16[40,3072]{1,0:T(8,128)(2,1)S(1)}, bf16[40,3072]{1,0:T(8,128)(2,1)S(1)}, u32[]{:S(2)}, u32[]{:S(2)}) collective-permute-start(bf16[40,3072]{1,0:T(8,128)(2,1)S(1)} %get-tuple-element.53), channel_id=1, source_target_pairs={{0,6},{1,7},{2,0},{3,1},{4,2},{5,3},{6,4},{7,5},{8,14},{9,15},{10,... | collective-permute-start | bytes 737288 | tf_op jit(solution)/shard_map/ppermute | solution.py:402
  73.8 0.3 collective-permute-start.21
  74.1 4.7 %forward.2 = (bf16[144,4608]{1,0:T(8,128)(2,1)S(1)}, bf16[144,1536]{1,0:T(8,128)(2,1)S(1)}) custom-call(s32[2]{0:T(128)S(1)} %settle.1.place, bf16[72,3072]{1,0:T(8,128)(2,1)S(1)} %collective-permute-done.refs_0_, bf16[72,3072]{1,0:T(8,128)(2,1)S(1)} %collective-permute-done.3.refs_1_, bf16[72,3072]{1,0:T(8,128)(2,1)S(1)} %collective-permute-done.9.refs_2_, ...), custom_call_target="tpu_custom_call" | custom-call | flops 1000000 | tf_op jit(solution)/shard_map/forward/pallas_call | solution.py:242
  78.8 0.1 collective-permute-start.17
  78.8 4.7 %forward.3 = (bf16[144,4608]{1,0:T(8,128)(2,1)S(1)}, bf16[144,1536]{1,0:T(8,128)(2,1)S(1)}) custom-call(s32[2]{0:T(128)S(1)} %settle.1.place, bf16[72,3072]{1,0:T(8,128)(2,1)S(1)} %collective-permute-done.11.refs_0_, bf16[72,3072]{1,0:T(8,128)(2,1)S(1)} %collective-permute-done.16.refs_1_, bf16[72,3072]{1,0:T(8,128)(2,1)S(1)} %collective-permute-done.10.refs_2_, ...), custom_call_target="tpu_custom_call" | custom-call | flops 10000000000 | tf_op jit(solution)/shard_map/forward/pallas_call | solution.py:242
  83.5 1.9 %collective-permute-done.21.refs_2_ = bf16[40,3072]{1,0:T(8,128)(2,1)S(1)} collective-permute-done((bf16[40,3072]{1,0:T(8,128)(2,1)S(1)}, bf16[40,3072]{1,0:T(8,128)(2,1)S(1)}, u32[]{:S(2)}, u32[]{:S(2)}) %collective-permute-start.21) | collective-permute-done | bytes 245792 | tf_op jit(solution)/shard_map/ppermute | solution.py:402
  85.5 0.1 add.12
  85.5 1.9 %collective-permute-start.24 = (bf16[40,3072]{1,0:T(8,128)(2,1)S(1)}, bf16[40,3072]{1,0:T(8,128)(2,1)S(1)}, u32[]{:S(2)}, u32[]{:S(2)}) collective-permute-start(bf16[40,3072]{1,0:T(8,128)(2,1)S(1)} %add.12), channel_id=1, source_target_pairs={{0,4},{1,5},{2,6},{3,7},{4,0},{5,1},{6,2},{7,3},{8,12},{9,13},{10,... | collective-permute-start | bytes 737288 | tf_op jit(solution)/shard_map/ppermute | solution.py:402
  87.4 1.5 %collective-permute-start.23 = (bf16[40,3072]{1,0:T(8,128)(2,1)S(1)}, bf16[40,3072]{1,0:T(8,128)(2,1)S(1)}, u32[]{:S(2)}, u32[]{:S(2)}) collective-permute-start(bf16[40,3072]{1,0:T(8,128)(2,1)S(1)} %get-tuple-element.77), channel_id=1, source_target_pairs={{0,1},{1,0},{2,3},{3,2},{4,5},{5,4},{6,7},{7,6},{8,9},{9,8},{10,11... | collective-permute-start | bytes 737288 | tf_op jit(solution)/shard_map/ppermute | solution.py:399
  88.9 3.9 %grads.2 = (bf16[768,1024]{1,0:T(8,128)(2,1)S(1)}, bf16[768,1024]{1,0:T(8,128)(2,1)S(1)}, bf16[1024,768]{1,0:T(8,128)(2,1)S(1)}) custom-call(bf16[144,4608]{1,0:T(8,128)(2,1)S(1)} %get-tuple-element.54.refs_0_, bf16[144,4608]{1,0:T(8,128)(2,1)S(1)} %get-tuple-element.62.refs_1_, bf16[144,1536]{1,0:T(8,128)(2,1)S(1)} %get-tuple-element.63.refs_2_, ...), custom_call_target="tpu_custom_call" | custom-call | flops 40000000000 | tf_op jit(solution)/shard_map/grads/pallas_call | solution.py:300
  92.8 0.0 copy-start.4
  92.9 5.5 %grads.3 = (bf16[768,1024]{1,0:T(8,128)(2,1)}, bf16[768,1024]{1,0:T(8,128)(2,1)}, bf16[1024,768]{1,0:T(8,128)(2,1)}) custom-call(bf16[144,4608]{1,0:T(8,128)(2,1)S(1)} %get-tuple-element.57.refs_0_, bf16[144,4608]{1,0:T(8,128)(2,1)S(1)} %get-tuple-element.59.refs_1_, bf16[144,1536]{1,0:T(8,128)(2,1)S(1)} %get-tuple-element.60.refs_2_, ...), custom_call_target="tpu_custom_call" | custom-call | flops 1000000 | tf_op jit(solution)/shard_map/grads/pallas_call | solution.py:300
  98.3 0.2 settle_rows.1
  98.5 1.6 %collective-permute-done.24.refs_1_ = bf16[40,3072]{1,0:T(8,128)(2,1)S(1)} collective-permute-done((bf16[40,3072]{1,0:T(8,128)(2,1)S(1)}, bf16[40,3072]{1,0:T(8,128)(2,1)S(1)}, u32[]{:S(2)}, u32[]{:S(2)}) %collective-permute-start.24) | collective-permute-done | bytes 245792 | tf_op jit(solution)/shard_map/ppermute | solution.py:402
  100.1 1.4 %unpack.1 = bf16[128,3072]{1,0:T(8,128)(2,1)} custom-call(bf16[40,128]{1,0:T(8,128)(2,1)S(1)} %get-tuple-element.72.place, f32[40,3072]{1,0:T(8,128)S(1)} %get-tuple-element.73.total, bf16[40,3072]{1,0:T(8,128)(2,1)S(1)} %collective-permute-done.23.refs_0_, bf16[40,3072]{1,0:T(8,128)(2,1)S(1)} %collective-permute-done.24.refs_1_), custom_call_target="tpu_custom_call" | custom-call | tf_op jit(solution)/shard_map/unpack/pallas_call | solution.py:127
  (30 shorter events, 0.1 us)
Async XLA Ops:
  0.6 43.4 %slice-start = ((s8[6291456]{0:T(1024)(128)(4,1)}), s8[2097152]{0:T(1024)(128)(4,1)S(1)}, s32[]{:S(2)}) async-start(s8[6291456]{0:T(1024)(128)(4,1)} %bitcast.4), calls=%async_computation | async-start | bytes 4194304
  3.4 13.4 %collective-permute-start.2 = (bf16[72,3072]{1,0:T(8,128)(2,1)}, bf16[72,3072]{1,0:T(8,128)(2,1)S(1)}, u32[]{:S(2)}, u32[]{:S(2)}) collective-permute-start(bf16[72,3072]{1,0:T(8,128)(2,1)} %pack.1.block.refs_1_), channel_id=1, source_target_pairs={{0,1},{1,0},{2,3},{3,2},{4,5},{5,4},{6,7},{7,6},{8,9},{9,8},{10,11... | collective-permute-start | bytes 1327112 | tf_op jit(solution)/shard_map/ppermute | solution.py:399
  6.4 15.1 %collective-permute-start.1 = (bf16[72,3072]{1,0:T(8,128)(2,1)}, bf16[72,3072]{1,0:T(8,128)(2,1)S(1)}, u32[]{:S(2)}, u32[]{:S(2)}) collective-permute-start(bf16[72,3072]{1,0:T(8,128)(2,1)} %pack.1.block.refs_1_), channel_id=1, source_target_pairs={{0,2},{1,3},{2,4},{3,5},{4,6},{5,7},{6,0},{7,1},{8,10},{9,11},{10,... | collective-permute-start | bytes 1327112 | tf_op jit(solution)/shard_map/ppermute | solution.py:402
  8.0 13.6 %collective-permute-start = (bf16[72,3072]{1,0:T(8,128)(2,1)}, bf16[72,3072]{1,0:T(8,128)(2,1)S(1)}, u32[]{:S(2)}, u32[]{:S(2)}) collective-permute-start(bf16[72,3072]{1,0:T(8,128)(2,1)} %pack.1.block.refs_1_), channel_id=1, source_target_pairs={{0,16},{8,24},{16,0},{24,8},{1,17},{9,25},{17,1},{25,9},{2,18},{10... | collective-permute-start | bytes 1327112 | tf_op jit(solution)/shard_map/ppermute | solution.py:396
  9.6 1.0 copy-start.2
  10.6 33.4 %slice-start.1 = ((s8[6291456]{0:T(1024)(128)(4,1)}), s8[4194304]{0:T(1024)(128)(4,1)S(1)}, s32[]{:S(2)}) async-start(s8[6291456]{0:T(1024)(128)(4,1)} %bitcast.4), calls=%async_computation.1 | async-start | bytes 8388608
  10.6 33.4 %copy-start = (bf16[3072,1024]{1,0:T(8,128)(2,1)S(1)}, bf16[3072,1024]{1,0:T(8,128)(2,1)}, u32[]{:S(2)}) copy-start(bf16[3072,1024]{1,0:T(8,128)(2,1)} %refs_5_.7) | copy-start | bytes 18874372
  10.6 33.4 %copy-start.1 = (bf16[1024,3072]{1,0:T(8,128)(2,1)S(1)}, bf16[1024,3072]{1,0:T(8,128)(2,1)}, u32[]{:S(2)}) copy-start(bf16[1024,3072]{1,0:T(8,128)(2,1)} %refs_6_.7) | copy-start | bytes 18874372
  11.8 44.8 %copy-start.3 = (bf16[72,3072]{1,0:T(8,128)(2,1)S(1)}, bf16[72,3072]{1,0:T(8,128)(2,1)}, u32[]{:S(2)}) copy-start(bf16[72,3072]{1,0:T(8,128)(2,1)} %pack.1.block.refs_1_) | copy-start | bytes 1327108
  11.8 19.2 %collective-permute-start.5 = (bf16[72,3072]{1,0:T(8,128)(2,1)S(1)}, bf16[72,3072]{1,0:T(8,128)(2,1)S(1)}, u32[]{:S(2)}, u32[]{:S(2)}) collective-permute-start(bf16[72,3072]{1,0:T(8,128)(2,1)S(1)} %copy-done.2), channel_id=1, source_target_pairs={{0,6},{1,7},{2,0},{3,1},{4,2},{5,3},{6,4},{7,5},{8,14},{9,15},{10,... | collective-permute-start | bytes 1327112 | tf_op jit(solution)/shard_map/ppermute | solution.py:402
  21.6 11.4 %collective-permute-start.6 = (bf16[72,3072]{1,0:T(8,128)(2,1)S(1)}, bf16[72,3072]{1,0:T(8,128)(2,1)S(1)}, u32[]{:S(2)}, u32[]{:S(2)}) collective-permute-start(bf16[72,3072]{1,0:T(8,128)(2,1)S(1)} %collective-permute-done.1.refs_0_), channel_id=1, source_target_pairs={{0,1},{1,0},{2,3},{3,2},{4,5},{5,4},{6,7},{7,6},{8,9},{9,8},{10,11... | collective-permute-start | bytes 1327112 | tf_op jit(solution)/shard_map/ppermute | solution.py:399
  21.9 17.3 %collective-permute-start.4 = (bf16[72,3072]{1,0:T(8,128)(2,1)S(1)}, bf16[72,3072]{1,0:T(8,128)(2,1)S(1)}, u32[]{:S(2)}, u32[]{:S(2)}) collective-permute-start(bf16[72,3072]{1,0:T(8,128)(2,1)S(1)} %collective-permute-done.1.refs_0_), channel_id=1, source_target_pairs={{0,2},{1,3},{2,4},{3,5},{4,6},{5,7},{6,0},{7,1},{8,10},{9,11},{10,... | collective-permute-start | bytes 1327112 | tf_op jit(solution)/shard_map/ppermute | solution.py:402
  21.9 19.3 %collective-permute-start.3 = (bf16[72,3072]{1,0:T(8,128)(2,1)S(1)}, bf16[72,3072]{1,0:T(8,128)(2,1)S(1)}, u32[]{:S(2)}, u32[]{:S(2)}) collective-permute-start(bf16[72,3072]{1,0:T(8,128)(2,1)S(1)} %collective-permute-done.2.refs_3_), channel_id=1, source_target_pairs={{0,16},{8,24},{16,0},{24,8},{1,17},{9,25},{17,1},{25,9},{2,18},{10... | collective-permute-start | bytes 1327112 | tf_op jit(solution)/shard_map/ppermute | solution.py:396
  31.0 13.1 %collective-permute-start.7 = (bf16[72,3072]{1,0:T(8,128)(2,1)S(1)}, bf16[72,3072]{1,0:T(8,128)(2,1)S(1)}, u32[]{:S(2)}, u32[]{:S(2)}) collective-permute-start(bf16[72,3072]{1,0:T(8,128)(2,1)S(1)} %collective-permute-done.5.refs_1_), channel_id=1, source_target_pairs={{0,1},{1,0},{2,3},{3,2},{4,5},{5,4},{6,7},{7,6},{8,9},{9,8},{10,11... | collective-permute-start | bytes 1327112 | tf_op jit(solution)/shard_map/ppermute | solution.py:399
  31.3 20.8 %collective-permute-start.9 = (bf16[72,3072]{1,0:T(8,128)(2,1)S(1)}, bf16[72,3072]{1,0:T(8,128)(2,1)S(1)}, u32[]{:S(2)}, u32[]{:S(2)}) collective-permute-start(bf16[72,3072]{1,0:T(8,128)(2,1)S(1)} %collective-permute-done.5.refs_1_), channel_id=1, source_target_pairs={{0,16},{8,24},{16,0},{24,8},{1,17},{9,25},{17,1},{25,9},{2,18},{10... | collective-permute-start | bytes 1327112 | tf_op jit(solution)/shard_map/ppermute | solution.py:396
  39.2 16.9 %collective-permute-start.12 = (bf16[72,3072]{1,0:T(8,128)(2,1)S(1)}, bf16[72,3072]{1,0:T(8,128)(2,1)S(1)}, u32[]{:S(2)}, u32[]{:S(2)}) collective-permute-start(bf16[72,3072]{1,0:T(8,128)(2,1)S(1)} %collective-permute-done.4.refs_0_), channel_id=1, source_target_pairs={{0,1},{1,0},{2,3},{3,2},{4,5},{5,4},{6,7},{7,6},{8,9},{9,8},{10,11... | collective-permute-start | bytes 1327112 | tf_op jit(solution)/shard_map/ppermute | solution.py:399
  39.7 14.8 %collective-permute-start.11 = (bf16[72,3072]{1,0:T(8,128)(2,1)S(1)}, bf16[72,3072]{1,0:T(8,128)(2,1)S(1)}, u32[]{:S(2)}, u32[]{:S(2)}) collective-permute-start(bf16[72,3072]{1,0:T(8,128)(2,1)S(1)} %collective-permute-done.4.refs_0_), channel_id=1, source_target_pairs={{0,16},{8,24},{16,0},{24,8},{1,17},{9,25},{17,1},{25,9},{2,18},{10... | collective-permute-start | bytes 1327112 | tf_op jit(solution)/shard_map/ppermute | solution.py:396
  41.2 11.3 %collective-permute-start.10 = (bf16[72,3072]{1,0:T(8,128)(2,1)S(1)}, bf16[72,3072]{1,0:T(8,128)(2,1)S(1)}, u32[]{:S(2)}, u32[]{:S(2)}) collective-permute-start(bf16[72,3072]{1,0:T(8,128)(2,1)S(1)} %collective-permute-done.refs_0_), channel_id=1, source_target_pairs={{0,2},{1,3},{2,4},{3,5},{4,6},{5,7},{6,0},{7,1},{8,10},{9,11},{10,... | collective-permute-start | bytes 1327112 | tf_op jit(solution)/shard_map/ppermute | solution.py:402
  52.0 20.0 %collective-permute-start.13 = (bf16[144,4608]{1,0:T(8,128)(2,1)S(1)}, bf16[144,4608]{1,0:T(8,128)(2,1)S(1)}, u32[]{:S(2)}, u32[]{:S(2)}) collective-permute-start(bf16[144,4608]{1,0:T(8,128)(2,1)S(1)} %get-tuple-element.54.refs_0_), channel_id=1, source_target_pairs={{0,8},{8,0},{16,24},{24,16},{1,9},{9,1},{17,25},{25,17},{2,10},{10... | collective-permute-start | bytes 3981320 | tf_op jit(solution)/shard_map/ppermute | solution.py:393
  52.1 12.6 %collective-permute-start.8 = (bf16[72,3072]{1,0:T(8,128)(2,1)S(1)}, bf16[72,3072]{1,0:T(8,128)(2,1)S(1)}, u32[]{:S(2)}, u32[]{:S(2)}) collective-permute-start(bf16[72,3072]{1,0:T(8,128)(2,1)S(1)} %get-tuple-element.47), channel_id=1, source_target_pairs={{0,1},{1,0},{2,3},{3,2},{4,5},{5,4},{6,7},{7,6},{8,9},{9,8},{10,11... | collective-permute-start | bytes 1327112 | tf_op jit(solution)/shard_map/ppermute | solution.py:399
  52.5 18.1 %collective-permute-start.14 = (bf16[72,3072]{1,0:T(8,128)(2,1)S(1)}, bf16[72,3072]{1,0:T(8,128)(2,1)S(1)}, u32[]{:S(2)}, u32[]{:S(2)}) collective-permute-start(bf16[72,3072]{1,0:T(8,128)(2,1)S(1)} %collective-permute-done.3.refs_1_), channel_id=1, source_target_pairs={{0,2},{1,3},{2,4},{3,5},{4,6},{5,7},{6,0},{7,1},{8,10},{9,11},{10,... | collective-permute-start | bytes 1327112 | tf_op jit(solution)/shard_map/ppermute | solution.py:402
  54.5 19.3 %collective-permute-start.15 = (bf16[72,3072]{1,0:T(8,128)(2,1)S(1)}, bf16[72,3072]{1,0:T(8,128)(2,1)S(1)}, u32[]{:S(2)}, u32[]{:S(2)}) collective-permute-start(bf16[72,3072]{1,0:T(8,128)(2,1)S(1)} %collective-permute-done.7.refs_3_), channel_id=1, source_target_pairs={{0,16},{8,24},{16,0},{24,8},{1,17},{9,25},{17,1},{25,9},{2,18},{10... | collective-permute-start | bytes 1327112 | tf_op jit(solution)/shard_map/ppermute | solution.py:396
  56.0 22.7 %collective-permute-start.16 = (bf16[72,3072]{1,0:T(8,128)(2,1)S(1)}, bf16[72,3072]{1,0:T(8,128)(2,1)S(1)}, u32[]{:S(2)}, u32[]{:S(2)}) collective-permute-start(bf16[72,3072]{1,0:T(8,128)(2,1)S(1)} %collective-permute-done.12.refs_2_), channel_id=1, source_target_pairs={{0,16},{8,24},{16,0},{24,8},{1,17},{9,25},{17,1},{25,9},{2,18},{10... | collective-permute-start | bytes 1327112 | tf_op jit(solution)/shard_map/ppermute | solution.py:396
  64.7 24.3 %collective-permute-start.19 = (bf16[144,4608]{1,0:T(8,128)(2,1)S(1)}, bf16[144,4608]{1,0:T(8,128)(2,1)S(1)}, u32[]{:S(2)}, u32[]{:S(2)}) collective-permute-start(bf16[144,4608]{1,0:T(8,128)(2,1)S(1)} %get-tuple-element.62.refs_1_), channel_id=1, source_target_pairs={{0,8},{8,0},{16,24},{24,16},{1,9},{9,1},{17,25},{25,17},{2,10},{10... | collective-permute-start | bytes 3981320 | tf_op jit(solution)/shard_map/ppermute | solution.py:393
  70.5 14.9 %collective-permute-start.22 = (bf16[40,3072]{1,0:T(8,128)(2,1)S(1)}, bf16[40,3072]{1,0:T(8,128)(2,1)S(1)}, u32[]{:S(2)}, u32[]{:S(2)}) collective-permute-start(bf16[40,3072]{1,0:T(8,128)(2,1)S(1)} %get-tuple-element.51), channel_id=1, source_target_pairs={{0,1},{1,0},{2,3},{3,2},{4,5},{5,4},{6,7},{7,6},{8,9},{9,8},{10,11... | collective-permute-start | bytes 737288 | tf_op jit(solution)/shard_map/ppermute | solution.py:399
  72.0 13.4 %collective-permute-start.20 = (bf16[40,3072]{1,0:T(8,128)(2,1)S(1)}, bf16[40,3072]{1,0:T(8,128)(2,1)S(1)}, u32[]{:S(2)}, u32[]{:S(2)}) collective-permute-start(bf16[40,3072]{1,0:T(8,128)(2,1)S(1)} %get-tuple-element.53), channel_id=1, source_target_pairs={{0,6},{1,7},{2,0},{3,1},{4,2},{5,3},{6,4},{7,5},{8,14},{9,15},{10,... | collective-permute-start | bytes 737288 | tf_op jit(solution)/shard_map/ppermute | solution.py:402
  73.8 11.7 %collective-permute-start.21 = (bf16[40,3072]{1,0:T(8,128)(2,1)S(1)}, bf16[40,3072]{1,0:T(8,128)(2,1)S(1)}, u32[]{:S(2)}, u32[]{:S(2)}) collective-permute-start(bf16[40,3072]{1,0:T(8,128)(2,1)S(1)} %get-tuple-element.71), channel_id=1, source_target_pairs={{0,2},{1,3},{2,4},{3,5},{4,6},{5,7},{6,0},{7,1},{8,10},{9,11},{10,... | collective-permute-start | bytes 737288 | tf_op jit(solution)/shard_map/ppermute | solution.py:402
  78.8 14.1 %collective-permute-start.17 = (bf16[144,4608]{1,0:T(8,128)(2,1)S(1)}, bf16[144,4608]{1,0:T(8,128)(2,1)S(1)}, u32[]{:S(2)}, u32[]{:S(2)}) collective-permute-start(bf16[144,4608]{1,0:T(8,128)(2,1)S(1)} %get-tuple-element.57.refs_0_), channel_id=1, source_target_pairs={{0,8},{8,0},{16,24},{24,16},{1,9},{9,1},{17,25},{25,17},{2,10},{10... | collective-permute-start | bytes 3981320 | tf_op jit(solution)/shard_map/ppermute | solution.py:393
  85.4 7.4 %collective-permute-start.18 = (bf16[144,4608]{1,0:T(8,128)(2,1)S(1)}, bf16[144,4608]{1,0:T(8,128)(2,1)S(1)}, u32[]{:S(2)}, u32[]{:S(2)}) collective-permute-start(bf16[144,4608]{1,0:T(8,128)(2,1)S(1)} %get-tuple-element.59.refs_1_), channel_id=1, source_target_pairs={{0,8},{8,0},{16,24},{24,16},{1,9},{9,1},{17,25},{25,17},{2,10},{10... | collective-permute-start | bytes 3981320 | tf_op jit(solution)/shard_map/ppermute | solution.py:393
  85.5 14.6 %collective-permute-start.24 = (bf16[40,3072]{1,0:T(8,128)(2,1)S(1)}, bf16[40,3072]{1,0:T(8,128)(2,1)S(1)}, u32[]{:S(2)}, u32[]{:S(2)}) collective-permute-start(bf16[40,3072]{1,0:T(8,128)(2,1)S(1)} %add.12), channel_id=1, source_target_pairs={{0,4},{1,5},{2,6},{3,7},{4,0},{5,1},{6,2},{7,3},{8,12},{9,13},{10,... | collective-permute-start | bytes 737288 | tf_op jit(solution)/shard_map/ppermute | solution.py:402
  87.4 11.0 %collective-permute-start.23 = (bf16[40,3072]{1,0:T(8,128)(2,1)S(1)}, bf16[40,3072]{1,0:T(8,128)(2,1)S(1)}, u32[]{:S(2)}, u32[]{:S(2)}) collective-permute-start(bf16[40,3072]{1,0:T(8,128)(2,1)S(1)} %get-tuple-element.77), channel_id=1, source_target_pairs={{0,1},{1,0},{2,3},{3,2},{4,5},{5,4},{6,7},{7,6},{8,9},{9,8},{10,11... | collective-permute-start | bytes 737288 | tf_op jit(solution)/shard_map/ppermute | solution.py:399
  92.8 5.5 %copy-start.4 = (s32[128,2]{0,1:T(2,128)S(1)}, s32[128,2]{0,1:T(2,128)}, u32[]{:S(2)}) copy-start(s32[128,2]{0,1:T(2,128)} %param.9) | copy-start | bytes 3076
